TPU v7x, 32 devices: a whole 2x2x4 slice. The times are simulated.
32 devices in a mesh: grp: 4 (over y, x), dev: 8 (over z, core).
Axes of the slice: x: 2, y: 2, z: 4, core: 2. Of those that a mesh axis runs over, the one named last changes fastest.
Arguments:
- batch_rows: bfloat16 [1024, 512], P(('grp', 'dev')), may hold values from -30 to 30
- batch_labels: int32 [1024], P(('grp', 'dev')), may hold values from 0 to 1023, as said below
- memory: bfloat16 [65536, 512], P(('grp', 'dev')), may hold values from -30 to 30
- memory_labels: int32 [65536], P(('grp', 'dev')), may hold values from 0 to 1023
- keep_bits: int32 [65536], P(('grp', 'dev')), may hold values from 0 to 1
- step_index: int32 [1], replicated, may hold values from 0 to 999999
Outputs:
- grad_batch: float32 [1024, 512], P(('grp', 'dev'))
- anchor_loss: float32 [1024], P(('grp', 'dev'))
- new_memory: bfloat16 [65536, 512], P(('grp', 'dev'))
- new_labels: int32 [65536], P(('grp', 'dev'))
Inputs may be any that keep to these rules, and one draw needn't show every extreme that they name: `batch_labels`: labels of batch and memory rows are class numbers below 1024.
All inputs are finite; a program needn't handle non-finite values.
Results may differ from a plain program's by a relative error of at most 0.0034.
Values may be sent and summed in bfloat16 or wider, within the bound.
No kernel may reach another device: no remote copies, remote signals or barrier semaphores. Data moves between devices by JAX's collectives and lax.ppermute only.
A program may use at most 128 MiB of HBM per device.

v0:
```python
import jax
import jax.numpy as jnp
from jax import lax
from jax.sharding import PartitionSpec as P

pos_scale = 2.0
neg_scale = 50.0
margin = 0.5


def normalize(values):
    floats = values.astype(jnp.float32)
    radius = jnp.sqrt(jnp.sum(floats * floats, axis=1, keepdims=True) + 1e-06)
    return (floats / radius, radius)


def per_device(batch_rows, batch_labels, memory, memory_labels, keep_bits, step_index):
    group_size = lax.axis_size("dev")
    devices_all = lax.axis_size("grp") * group_size
    my_index = lax.axis_index("grp") * group_size + lax.axis_index("dev")
    local_rows = batch_rows.shape[0]
    width = batch_rows.shape[1]
    unit_rows, radius = normalize(batch_rows)
    local_anchors = unit_rows.astype(jnp.bfloat16)
    first_section = (
        lax.all_gather(local_anchors, "dev", axis=0, tiled=True),
        lax.all_gather(batch_labels, "dev", axis=0, tiled=True),
    )
    anchors, labels_all = (
        lax.all_gather(first_section[0], "grp", axis=0, tiled=True),
        lax.all_gather(first_section[1], "grp", axis=0, tiled=True),
    )
    memory_keys = normalize(memory)[0].astype(jnp.bfloat16)
    kept_rows = (keep_bits > 0)[None, :]
    row_count = anchors.shape[0]
    block_rows = min(512, row_count)
    blocks = row_count // block_rows

    def score_block(inputs):
        block_anchors, block_labels = inputs
        scores = lax.dot_general(
            block_anchors, memory_keys, (((1,), (1,)), ((), ())), preferred_element_type=jnp.float32
        )
        same_class = block_labels[:, None] == memory_labels[None, :]
        positive = jnp.logical_and(same_class, kept_rows)
        negative = jnp.logical_and(jnp.logical_not(same_class), kept_rows)
        pos_term = jnp.where(positive, jnp.exp(-pos_scale * (scores - margin)), 0.0)
        neg_term = jnp.where(negative, jnp.exp(neg_scale * (scores - margin)), 0.0)
        pull = jnp.dot(
            pos_term.astype(jnp.bfloat16), memory_keys, preferred_element_type=jnp.float32
        )
        push = jnp.dot(
            neg_term.astype(jnp.bfloat16), memory_keys, preferred_element_type=jnp.float32
        )
        return (jnp.sum(pos_term, axis=1), jnp.sum(neg_term, axis=1), pull, push)

    pos_sum, neg_sum, pull, push = lax.map(
        score_block,
        (anchors.reshape(blocks, block_rows, width), labels_all.reshape(blocks, block_rows)),
    )
    pos_sum = pos_sum.reshape(row_count)
    neg_sum = neg_sum.reshape(row_count)
    pull = pull.reshape(row_count, width)
    push = push.reshape(row_count, width)
    pos_total, neg_total = lax.psum((pos_sum, neg_sum), ("grp", "dev"))
    combined = push / (1.0 + neg_total)[:, None] - pull / (1.0 + pos_total)[:, None]
    grad_unit = lax.psum_scatter(combined, ("grp", "dev"), scatter_dimension=0, tiled=True)
    own_pos = lax.dynamic_slice_in_dim(pos_total, my_index * local_rows, local_rows, 0)
    own_neg = lax.dynamic_slice_in_dim(neg_total, my_index * local_rows, local_rows, 0)
    anchor_loss = jnp.log(1.0 + own_pos) / pos_scale + jnp.log(1.0 + own_neg) / neg_scale
    along = jnp.sum(unit_rows * grad_unit, axis=1, keepdims=True)
    grad_batch = (grad_unit - unit_rows * along) / radius
    step_value = step_index[0]
    slot_index = step_value % (memory.shape[0] // local_rows)
    source = (my_index - step_value) % devices_all
    moved_rows = lax.dynamic_slice_in_dim(anchors, source * local_rows, local_rows, 0)
    moved_labels = lax.dynamic_slice_in_dim(labels_all, source * local_rows, local_rows, 0)
    new_memory = lax.dynamic_update_slice_in_dim(memory, moved_rows, slot_index * local_rows, 0)
    new_labels = lax.dynamic_update_slice_in_dim(
        memory_labels, moved_labels, slot_index * local_rows, 0
    )
    return (grad_batch, anchor_loss, new_memory, new_labels)


def solution(mesh):
    placed = (
        P(("grp", "dev"), None),
        P(("grp", "dev")),
        P(("grp", "dev"), None),
        P(("grp", "dev")),
        P(("grp", "dev")),
        P(),
    )
    return jax.shard_map(
        per_device,
        mesh=mesh,
        in_specs=placed,
        out_specs=(
            P(("grp", "dev"), None),
            P(("grp", "dev")),
            P(("grp", "dev"), None),
            P(("grp", "dev")),
        ),
        check_vma=False,
    )
```

profile of v0, /device:TPU:0, one launch (start us, length us, event | category | flops | bytes accessed | tf_op | source)
XLA Modules:
  0.0 275.1 jit_solution(7357091025150657136)
XLA Ops:
  7.2 0.0 all-gather.3.cloned.1.call-start
  7.3 1.6 copy.37
  8.9 0.1 fusion.42
  9.0 0.1 fusion.43
  9.1 17.0 %all_gather.14 = bf16[256,512]{1,0:T(8,128)(2,1)} all-gather(bf16[32,512]{1,0:T(8,128)(2,1)S(1)} %fusion.43), channel_id=1, replica_groups=mesh['grp'=4,'dev'=8] {'dev'}, dimensions={0}, use_global_device_ids=true | all-gather | bytes 294912 | tf_op jit(solution)/shard_map/all_gather | solution.py:26
  26.1 0.0 all-gather.3.cloned.1.call-update
  26.1 0.0 reduce-scatter.2.cloned.1.call-start
  26.2 0.6 dynamic-slice
  27.4 0.2 dynamic-update-slice
  27.7 9.0 %all-reduce = s32[256]{0:T(256)S(1)} all-reduce(s32[256]{0:T(256)S(1)} %dynamic-update-slice), channel_id=1, replica_groups=mesh['grp'=4,'dev'=8] {'dev'}, use_global_device_ids=true, to_apply=%add | all-reduce | flops 256 | bytes 2048
  36.6 8.1 %all-gather = s32[4,1,256]{2,1,0:T(1,128)S(1)} all-gather(s32[1,1,256]{2,1,0:T(1,128)S(1)} %bitcast.66), channel_id=1, replica_groups=mesh['grp'=4,'dev'=8] {'grp'}, dimensions={0}, use_global_device_ids=true | all-gather | bytes 5120 | tf_op jit(solution)/shard_map/all_gather | solution.py:31
  44.8 0.5 fusion.39
  45.3 1.8 fusion.40
  47.1 6.8 %all-gather.3.cloned.1.call-done = bf16[1024,512]{1,0:T(8,128)(2,1)} async-done(((bf16[256,512]{1,0:T(8,128)(2,1)}), bf16[1024,512]{1,0:T(8,128)(2,1)}) %all-gather.3.cloned.1.call-update) | async-done | bytes 1048592 | tf_op jit(solution)/shard_map/all_gather | solution.py:30
  53.9 30.1 %while.18 = (s32[]{:T(128)}, f32[2,512]{1,0:T(2,128)S(1)}, f32[2,512]{1,0:T(2,128)S(1)}, f32[2,512,512]{2,1,0:T(8,128)}, f32[2,512,512]{2,1,0:T(8,128)}, /*index...) while((s32[]{:T(128)}, f32[2,512]{1,0:T(2,128)S(1)}, ...), condition=%wide.region_5.6_spmd, body=%wide.region_2.5_spmd.sunk | while | flops 3246390272 | bytes 63496460 | solution.py:57
  54.0 6.7 %fusion.60 = (f32[512]{0:T(512)S(1)}, f32[512]{0:T(512)S(1)}, f32[512,2048]{1,0:T(8,128)}) fusion(s32[2048]{0:T(1024)S(1)} %get-tuple-element.262, s32[512]{0:T(512)S(1)} %bitcast.58, pred[2048]{0:T(1024)(128)(4,1)S(1)} %reduce.3, bf16[2048,512]{1,0:T(8,128)(2,1)} %get-tuple-element.265, bf16[2,512,512]{2,1,0:T(8,128)(2,1)} %get-tuple-element.264, ...), kind=kOutput, calls=%fused_computation.8.clone.1 | convolution fusion | flops 1085275136 | bytes 6832132 | tf_op jit(solution)/shard_map/while/body/eval_jaxpr/dot_general | solution.py:41
  60.8 5.4 %fusion.61 = f32[2,512,512]{2,1,0:T(8,128)} fusion(f32[2,512,512]{2,1,0:T(8,128)} %get-tuple-element.246, s32[]{:T(128)S(6)} %copy.22, bf16[2048,512]{1,0:T(8,128)(2,1)} %get-tuple-element.265, f32[512,2048]{1,0:T(8,128)} %get-tuple-element.229, s32[2048]{0:T(1024)S(1)} %get-tuple-element.262, s32[512]{0:T(512)S(1)} %bitcast.59, ...), kind=kOutput, calls=%fused_computation.22.clone.1 | convolution fusion | flops 1080033280 | bytes 7352324 | tf_op jit(solution)/shard_map/while/body/eval_jaxpr/dot_general | solution.py:49
  66.1 1.5 fusion.62
  67.7 1.3 copy-done.3
  69.0 6.7 %fusion.60 = (f32[512]{0:T(512)S(1)}, f32[512]{0:T(512)S(1)}, f32[512,2048]{1,0:T(8,128)}) fusion(s32[2048]{0:T(1024)S(1)} %get-tuple-element.262, s32[512]{0:T(512)S(1)} %bitcast.58, pred[2048]{0:T(1024)(128)(4,1)S(1)} %reduce.3, bf16[2048,512]{1,0:T(8,128)(2,1)} %get-tuple-element.265, bf16[2,512,512]{2,1,0:T(8,128)(2,1)} %get-tuple-element.264, ...), kind=kOutput, calls=%fused_computation.8.clone.1 | convolution fusion | flops 1085275136 | bytes 6832132 | tf_op jit(solution)/shard_map/while/body/eval_jaxpr/dot_general | solution.py:41
  75.8 5.3 %fusion.61 = f32[2,512,512]{2,1,0:T(8,128)} fusion(f32[2,512,512]{2,1,0:T(8,128)} %get-tuple-element.246, s32[]{:T(128)S(6)} %copy.22, bf16[2048,512]{1,0:T(8,128)(2,1)} %get-tuple-element.265, f32[512,2048]{1,0:T(8,128)} %get-tuple-element.229, s32[2048]{0:T(1024)S(1)} %get-tuple-element.262, s32[512]{0:T(512)S(1)} %bitcast.59, ...), kind=kOutput, calls=%fused_computation.22.clone.1 | convolution fusion | flops 1080033280 | bytes 7352324 | tf_op jit(solution)/shard_map/while/body/eval_jaxpr/dot_general | solution.py:49
  81.2 1.5 fusion.62
  82.7 1.3 copy-done.3
  84.0 39.4 %all-reduce.1 = (f32[1024]{0:T(1024)S(1)}, f32[1024]{0:T(1024)S(1)}) all-reduce(f32[1024]{0:T(1024)S(1)} %bitcast.64, f32[1024]{0:T(1024)S(1)} %bitcast.65), channel_id=1, replica_groups=mesh['grp'=4,'dev'=8] {'grp','dev'}, use_global_device_ids=true, to_apply=%region_7.8 | all-reduce | flops 2048 | bytes 16384 | tf_op jit(solution)/shard_map/psum | solution.py:65
  123.4 4.0 %fusion.41 = f32[1024,512]{1,0:T(8,128)} fusion(f32[2,512,512]{2,1,0:T(8,128)} %get-tuple-element.134, f32[2,512,512]{2,1,0:T(8,128)} %get-tuple-element.132, f32[1024]{0:T(1024)S(1)} %get-tuple-element.161, f32[1024]{0:T(1024)S(1)} %get-tuple-element.162), kind=kLoop, calls=%fused_computation.39 | loop fusion | flops 1572864 | bytes 6299648 | tf_op jit(solution)/shard_map/sub | solution.py:66
  127.4 0.0 reduce-scatter.2.cloned.1.call-update
  128.1 0.6 multiply_add_fusion
  128.7 0.2 dynamic-slice_dynamic-update-slice_fusion.1
  128.9 0.8 dynamic-slice_dynamic-update-slice_fusion
  129.7 136.0 %reduce-scatter.2.cloned.1.call-done = f32[32,512]{1,0:T(8,128)} async-done(((f32[1024,512]{1,0:T(8,128)}), f32[32,512]{1,0:T(8,128)}) %reduce-scatter.2.cloned.1.call-update) | async-done | bytes 65552 | tf_op jit(solution)/shard_map/reduce_scatter | solution.py:67
  265.7 1.0 multiply_reduce_fusion
  266.7 1.6 subtract_divide_fusion
  (50 shorter events, 0.4 us)
Async XLA Ops:
  7.2 46.8 %all-gather.3.cloned.1.call-start = ((), (), s32[]{:S(2)}) async-start(), calls=%async_computation.1 | async-start | bytes 1310720 | tf_op jit(solution)/shard_map/all_gather | solution.py:30
  7.2 1.7 copy-start.4
  7.2 19.0 %copy-start.9 = (u32[32]{0:T(128)S(1)}, u32[32]{0:T(128)}, u32[]{:S(2)}) copy-start(u32[32]{0:T(128)} %constant.101) | copy-start | bytes 388
  7.2 20.2 %copy-start.8 = (s32[32]{0:T(128)S(1)}, s32[32]{0:T(128)}, u32[]{:S(2)}) copy-start(s32[32]{0:T(128)} %param.9) | copy-start | bytes 388
  7.2 37.5 %copy-start.5 = (s32[2048]{0:T(1024)S(1)}, s32[2048]{0:T(1024)}, u32[]{:S(2)}) copy-start(s32[2048]{0:T(1024)} %param.12) | copy-start | bytes 24580
  26.1 239.6 %reduce-scatter.2.cloned.1.call-start = ((), (), s32[]{:S(2)}) async-start(), calls=%async_computation.2 | async-start | bytes 2162688 | tf_op jit(solution)/shard_map/reduce_scatter | solution.py:67
  45.3 8.7 %copy-start.7 = (s32[2048]{0:T(1024)S(1)}, s32[2048]{0:T(1024)}, u32[]{:S(2)}) copy-start(s32[2048]{0:T(1024)} %param.11) | copy-start | bytes 24580
  60.7 5.4 %copy-start.1 = (bf16[2048,512]{1,0:T(8,128)(2,1)S(1)}, bf16[2048,512]{1,0:T(8,128)(2,1)}, u32[]{:S(2)}) copy-start(bf16[2048,512]{1,0:T(8,128)(2,1)} %get-tuple-element.265) | copy-start | bytes 6291460 | tf_op jit(solution)/shard_map/while
  60.7 5.4 %copy-start.2 = (f32[2,512,512]{2,1,0:T(8,128)S(1)}, f32[2,512,512]{2,1,0:T(8,128)}, u32[]{:S(2)}) copy-start(f32[2,512,512]{2,1,0:T(8,128)} %get-tuple-element.247) | copy-start | bytes 6291460 | tf_op jit(solution)/shard_map/while
  60.8 5.4 %copy-start.10 = (f32[512,2048]{1,0:T(8,128)S(1)}, f32[512,2048]{1,0:T(8,128)}, u32[]{:S(2)}) copy-start(f32[512,2048]{1,0:T(8,128)} %get-tuple-element.229) | copy-start | bytes 12582916 | tf_op jit(solution)/shard_map/while
  67.7 1.3 copy-start.3
  75.8 5.4 %copy-start.1 = (bf16[2048,512]{1,0:T(8,128)(2,1)S(1)}, bf16[2048,512]{1,0:T(8,128)(2,1)}, u32[]{:S(2)}) copy-start(bf16[2048,512]{1,0:T(8,128)(2,1)} %get-tuple-element.265) | copy-start | bytes 6291460 | tf_op jit(solution)/shard_map/while
  75.8 5.4 %copy-start.2 = (f32[2,512,512]{2,1,0:T(8,128)S(1)}, f32[2,512,512]{2,1,0:T(8,128)}, u32[]{:S(2)}) copy-start(f32[2,512,512]{2,1,0:T(8,128)} %get-tuple-element.247) | copy-start | bytes 6291460 | tf_op jit(solution)/shard_map/while
  75.8 5.4 %copy-start.10 = (f32[512,2048]{1,0:T(8,128)S(1)}, f32[512,2048]{1,0:T(8,128)}, u32[]{:S(2)}) copy-start(f32[512,2048]{1,0:T(8,128)} %get-tuple-element.229) | copy-start | bytes 12582916 | tf_op jit(solution)/shard_map/while
  82.7 1.3 copy-start.3
  128.9 139.4 %copy-start.6 = (s32[2048]{0:T(1024)}, s32[2048]{0:T(1024)S(1)}, u32[]{:S(2)}) copy-start(s32[2048]{0:T(1024)S(1)} %dynamic-slice_dynamic-update-slice_fusion.1) | copy-start | bytes 24580
  129.7 138.6 %copy-start = (bf16[2048,512]{1,0:T(8,128)(2,1)}, bf16[2048,512]{1,0:T(8,128)(2,1)S(1)}, u32[]{:S(2)}) copy-start(bf16[2048,512]{1,0:T(8,128)(2,1)S(1)} %dynamic-slice_dynamic-update-slice_fusion) | copy-start | bytes 6291460
Sparse Core Ops, SparseCore 0:
  26.2 27.7 all-gather.2
  127.6 138.0 reduce-scatter.1
where the time goes:
time: 276 us; the launch traced here: 275 us
  waiting for transfers between devices  143 us (52%)
  blocking collectives  73.4 us (27%)
  matrix products  27.1 us (10%)
  between operations  15.5 us (6%)
  other arithmetic  9.78 us (4%)
  local copies, waits for them, and re-layouts  6.29 us (2%)
    reduce_scatter x1, waiting for transfers between devices, per_device(): lax.psum_scatter(combined, ('grp', 'dev'), scatter_dimension=0, tiled=True)  136 us
    psum x1, blocking collectives, per_device(): pos_total, neg_total = lax.psum((pos_sum, neg_sum), ('grp', 'dev'))  39.4 us
    all_gather x1, blocking collectives, per_device(): lax.all_gather(local_anchors, 'dev', axis=0, tiled=True)  17 us
    dot_general x2, matrix products, score_block(): lax.dot_general(block_anchors, memory_keys, (((1,), (1,)), ((), ())), pre...  13.3 us
    dot_general x2, matrix products, score_block(): jnp.dot(pos_term.astype(jnp.bfloat16), memory_keys, preferred_element_typ...  10.7 us
    unnamed x1, blocking collectives  8.96 us
    all_gather x1, blocking collectives, per_device(): lax.all_gather(first_section[1], 'grp', axis=0, tiled=True)  8.06 us
    all_gather x1, waiting for transfers between devices, per_device(): lax.all_gather(first_section[0], 'grp', axis=0, tiled=True)  6.83 us
  transfers between devices with their start and end apart: 2, of which 2 were waited for; matrix products, arithmetic and copies ran while one was open for 2% of the time, Pallas kernels for 0%

commit v1 on v0

v1 whole, which is shorter than its diff:
```python
import functools
import math

import jax
import jax.numpy as jnp
from jax import lax
from jax.experimental import pallas as pl
from jax.experimental.pallas import tpu as pltpu
from jax.sharding import PartitionSpec as P

pos_scale = 2.0
neg_scale = 50.0
margin = 0.5
lanes = 128
log2e = math.log2(math.e)
vmem_bytes = 56 * 1024 * 1024
f32 = jnp.float32
bf16 = jnp.bfloat16


def owner(index, step, count):
    if count & (count - 1) == 0:
        return index ^ step
    return (index - step) % count


def place_of(index, member, count):
    if count & (count - 1) == 0:
        return index ^ member
    return (index - member) % count


def whole(shape):
    return pl.BlockSpec(shape, lambda *_: (0,) * len(shape))


def call(body, outs, *args, flops=0, **kw):
    moved = sum(a.size * a.dtype.itemsize for a in args)
    moved += sum(math.prod(o.shape) * o.dtype.itemsize for o in outs)
    return pl.pallas_call(
        body,
        out_shape=outs,
        compiler_params=pltpu.CompilerParams(vmem_limit_bytes=vmem_bytes),
        cost_estimate=pl.CostEstimate(flops=flops, bytes_accessed=moved, transcendentals=0),
        **kw,
    )(*args)


def shaped(shape, dtype):
    return jax.ShapeDtypeStruct(shape, dtype)


def prepare_kernel(rows_ref, labels_ref, packed_ref, unit_ref, radius_ref):
    rows = rows_ref[...].astype(f32)
    count, width = rows.shape
    radius = jnp.sqrt(jnp.sum(rows * rows, axis=1, keepdims=True) + 1e-06)
    unit = rows / radius
    unit_ref[...] = unit
    radius_ref[...] = jnp.broadcast_to(radius, radius_ref.shape)
    packed_ref[:, :width] = unit.astype(bf16)
    labels = jnp.broadcast_to(labels_ref[...], (count, count))
    across = lax.broadcasted_iota(jnp.int32, (count, count), 1)
    down = lax.broadcasted_iota(jnp.int32, (count, count), 0)
    column = jnp.sum(jnp.where(across == down, labels, 0).astype(f32), axis=1, keepdims=True)
    high = jnp.floor(column * (1.0 / 256.0))
    low = column - high * 256.0
    lane = lax.broadcasted_iota(jnp.int32, (count, lanes), 1)
    digits = jnp.where(lane == 0, high, jnp.where(lane == 1, low, 0.0))
    packed_ref[:, width:] = digits.astype(bf16)


def keys_kernel(memory_ref, keys_ref, turned_ref):
    rows = memory_ref[...].astype(f32)
    radius = jnp.sqrt(jnp.sum(rows * rows, axis=1, keepdims=True) + 1e-06)
    keys = rows / radius
    keys_ref[...] = keys.astype(bf16)
    turned_ref[...] = keys.T.astype(bf16)


def pack_stats(pos, neg):
    rows = pos.shape[0]
    lane = lax.broadcasted_iota(jnp.int32, (rows, lanes), 1)
    parts = []
    for value in (pos, neg):
        high = value.astype(bf16).astype(f32)
        parts += [high, value - high]
    stats = jnp.zeros((rows, lanes), f32)
    for at, part in enumerate(parts):
        stats = jnp.where(lane == at, part, stats)
    return stats


def unpack_stats(stats):
    lane = lax.broadcasted_iota(jnp.int32, stats.shape, 1)
    pos = jnp.sum(jnp.where(lane < 2, stats, 0.0), axis=1, keepdims=True)
    neg = jnp.sum(jnp.where((lane >= 2) & (lane < 4), stats, 0.0), axis=1, keepdims=True)
    return pos, neg


def score_kernel(chunk, rows_ref, keys_ref, turned_ref, labels_ref, keep_ref, out_ref, pos_ref, neg_ref):
    width = keys_ref.shape[1]
    slots = keys_ref.shape[0]
    anchors = rows_ref[:, :width]
    digits = rows_ref[:, width:].astype(f32)
    lane = lax.broadcasted_iota(jnp.int32, digits.shape, 1)
    weight = jnp.where(lane == 0, 256.0, jnp.where(lane == 1, 1.0, 0.0))
    labels = jnp.sum(digits * weight, axis=1, keepdims=True)
    kept = keep_ref[...] > 0
    slot_labels = jnp.where(kept, labels_ref[...], -1).astype(f32)
    neg_shift = jnp.where(kept, -neg_scale * margin * log2e, -1e30)
    pos_sum = jnp.zeros((anchors.shape[0], 1), f32)
    neg_sum = jnp.zeros((anchors.shape[0], 1), f32)
    for start in range(0, slots, chunk):
        part = slice(start, start + chunk)
        scores = jnp.dot(anchors, turned_ref[:, part], preferred_element_type=f32)
        same = labels == slot_labels[:, part]
        slope = jnp.where(same, -pos_scale * log2e, neg_scale * log2e)
        shift = jnp.where(same, pos_scale * margin * log2e, neg_shift[:, part])
        term = jnp.exp2(scores * slope + shift)
        pos = jnp.where(same, term, 0.0)
        neg = jnp.where(same, 0.0, term)
        pos_sum += jnp.sum(pos, axis=1, keepdims=True)
        neg_sum += jnp.sum(neg, axis=1, keepdims=True)
        pos_ref[:, part] = pos.astype(bf16)
        neg_ref[:, part] = neg.astype(bf16)
    push = jnp.dot(neg_ref[...], keys_ref[...], preferred_element_type=f32)
    out_ref[:, :width] = push.astype(out_ref.dtype)
    pull = jnp.dot(pos_ref[...], keys_ref[...], preferred_element_type=f32)
    out_ref[:, width : 2 * width] = pull.astype(out_ref.dtype)
    out_ref[:, 2 * width :] = pack_stats(pos_sum, neg_sum).astype(out_ref.dtype)


def score(rows, first, count, keys, turned, labels, keep, dtype):
    width = keys.shape[1]
    slots = keys.shape[0]
    tile = math.gcd(256, math.gcd(first, count))
    chunk = math.gcd(512, slots)
    columns = 2 * width + lanes
    return call(
        functools.partial(score_kernel, chunk),
        [shaped((count, columns), dtype)],
        rows, keys, turned, labels, keep,
        flops=6 * count * slots * width,
        grid=(count // tile,),
        in_specs=[
            pl.BlockSpec((tile, rows.shape[1]), lambda i: (i + first // tile, 0)),
            whole(keys.shape),
            whole(turned.shape),
            whole(labels.shape),
            whole(keep.shape),
        ],
        out_specs=[pl.BlockSpec((tile, columns), lambda i: (i, 0))],
        scratch_shapes=[pltpu.VMEM((tile, slots), bf16), pltpu.VMEM((tile, slots), bf16)],
    )[0]


def add_kernel(width, held, arrived, refs):
    held_refs, arrived_refs, out_refs = refs[:held], refs[held : held + arrived], refs[held + arrived :]
    rows = out_refs[0].shape[0]
    for block, out_ref in enumerate(out_refs):
        first = block * rows
        total = None
        for group in (held_refs, arrived_refs):
            size = group[0].shape[0]
            for ref in group if group is arrived_refs else [group[first // size]]:
                inside = first % size
                value = ref[inside : inside + rows, :].astype(f32)
                total = value if total is None else total + value
        out_ref[:, : 2 * width] = total[:, : 2 * width].astype(out_ref.dtype)
        pos, neg = unpack_stats(total[:, 2 * width :])
        out_ref[:, 2 * width :] = pack_stats(pos, neg).astype(out_ref.dtype)


def add(width, held, arrived, blocks):
    rows = sum(h.shape[0] for h in held) // blocks
    columns = held[0].shape[1]
    outs = [shaped((rows, columns), f32 if b == 0 else bf16) for b in range(blocks)]

    def body(*refs):
        add_kernel(width, len(held), len(arrived), refs)

    return call(body, outs, *held, *arrived)


def finish_kernel(arrived, *refs):
    held_ref, arrived_refs = refs[0], refs[1 : 1 + arrived]
    unit_ref, radius_ref, grad_ref, loss_ref = refs[1 + arrived :]
    width = unit_ref.shape[1]
    total = held_ref[...]
    for ref in arrived_refs:
        total = total + ref[...].astype(f32)
    pos, neg = unpack_stats(total[:, 2 * width :])
    loss = jnp.log(1.0 + pos) / pos_scale + jnp.log(1.0 + neg) / neg_scale
    grad_unit = total[:, :width] / (1.0 + neg) - total[:, width : 2 * width] / (1.0 + pos)
    unit = unit_ref[...]
    along = jnp.sum(unit * grad_unit, axis=1, keepdims=True)
    grad_ref[...] = (grad_unit - unit * along) / radius_ref[:, :1]
    loss_ref[...] = loss


def per_device(batch_rows, batch_labels, memory, memory_labels, keep_bits, step_index):
    groups = lax.axis_size("grp")
    members = lax.axis_size("dev")
    cores = 2 if members % 2 == 0 else 1
    line = members // cores
    devices_all = groups * members
    my_grp = lax.axis_index("grp")
    my_dev = lax.axis_index("dev")
    count, width = batch_rows.shape
    slots = memory.shape[0]

    def pairs(axis, step):
        if axis == "grp":
            return [(owner(i, step, groups), i) for i in range(groups)]
        out = []
        for z in range(line):
            for c in range(cores):
                source = (owner(z, step, line), c) if axis == "line" else (z, owner(c, step, cores))
                out.append((source[0] * cores + source[1], z * cores + c))
        return out

    def fetch(value, axis, step):
        return lax.ppermute(value, "grp" if axis == "grp" else "dev", pairs(axis, step))

    def hand_back(value, axis, step):
        back = [(b, a) for a, b in pairs(axis, step)]
        return lax.ppermute(value, "grp" if axis == "grp" else "dev", back)

    packed, unit, radius = call(
        prepare_kernel,
        [shaped((count, width + lanes), bf16), shaped((count, width), f32), shaped((count, lanes), f32)],
        batch_rows,
        batch_labels.reshape(1, count),
    )

    block = math.gcd(256, slots)
    keys, turned = call(
        keys_kernel,
        [shaped((slots, width), bf16), shaped((width, slots), bf16)],
        memory,
        grid=(slots // block,),
        in_specs=[pl.BlockSpec((block, width), lambda i: (i, 0))],
        out_specs=[pl.BlockSpec((block, width), lambda i: (i, 0)), pl.BlockSpec((width, block), lambda i: (0, i))],
    )
    label_row = memory_labels.reshape(1, slots)
    keep_row = keep_bits.reshape(1, slots)

    part = jnp.concatenate([packed] + [fetch(packed, "line", s) for s in range(1, line)])
    near = jnp.concatenate([part] + [fetch(part, "grp", s) for s in range(1, groups)])
    halves = [near] + [fetch(near, "core", s) for s in range(1, cores)]
    near_rows = near.shape[0]
    split = near_rows // 2

    sides = (keys, turned, label_row, keep_row)
    early = score(near, 0, split, *sides, f32)
    arrived = [hand_back(score(halves[s], 0, near_rows, *sides, bf16), "core", s) for s in range(1, cores)]
    late = score(near, split, near_rows - split, *sides, f32)

    sums = add(width, [early, late], arrived, groups)
    arrived = [hand_back(sums[s], "grp", s) for s in range(1, groups)]
    sums = add(width, [sums[0]], arrived, line)
    arrived = [hand_back(sums[s], "line", s) for s in range(1, line)]
    grad_batch, loss = call(
        functools.partial(finish_kernel, len(arrived)),
        [shaped((count, width), f32), shaped((count, 1), f32)],
        sums[0], *arrived, unit, radius,
    )

    step_value = step_index[0]
    first_slot = (step_value % (slots // count)) * count
    source = (my_grp * members + my_dev - step_value) % devices_all
    source_grp, source_dev = source // members, source % members
    grp_place = place_of(my_grp, source_grp, groups)
    line_place = place_of(my_dev // cores, source_dev // cores, line)
    core_place = place_of(my_dev % cores, source_dev % cores, cores)
    at = (grp_place * line + line_place) * count
    moved = lax.dynamic_slice_in_dim(halves[0], at, count, 0)
    for s in range(1, cores):
        moved = jnp.where(core_place == s, lax.dynamic_slice_in_dim(halves[s], at, count, 0), moved)
    digits = moved[:, width : width + 2].astype(jnp.int32)
    moved_labels = digits[:, 0] * 256 + digits[:, 1]
    new_memory = lax.dynamic_update_slice_in_dim(memory, moved[:, :width], first_slot, 0)
    new_labels = lax.dynamic_update_slice_in_dim(memory_labels, moved_labels, first_slot, 0)
    return (grad_batch, loss.reshape(count), new_memory, new_labels)


def solution(mesh):
    placed = (
        P(("grp", "dev"), None),
        P(("grp", "dev")),
        P(("grp", "dev"), None),
        P(("grp", "dev")),
        P(("grp", "dev")),
        P(),
    )
    return jax.shard_map(
        per_device,
        mesh=mesh,
        in_specs=placed,
        out_specs=(
            P(("grp", "dev"), None),
            P(("grp", "dev")),
            P(("grp", "dev"), None),
            P(("grp", "dev")),
        ),
        check_vma=False,
    )
```

time: 276 us -> 92.9 us (0.34)
  waiting for transfers between devices: 143 us -> 25.2 us
  blocking collectives: 73.4 us -> 0 us
  Pallas kernels: 0 us -> 35 us
  matrix products: 27.1 us -> 0 us
  starting transfers between devices: 0.08 us -> 17.4 us
  between operations: 15.5 us -> 1.49 us
  other arithmetic: 9.78 us -> 2.34 us
  local copies, waits for them, and re-layouts: 6.29 us -> 10.7 us
    reduce_scatter x1 -> x0, waiting for transfers between devices: 136 us -> none  [per_device(): lax.psum_scatter(combined, ('grp', 'dev'), scatter_dimension=0, tiled=True)]
    psum x1 -> x0, blocking collectives: 39.4 us -> none  [per_device(): pos_total, neg_total = lax.psum((pos_sum, neg_sum), ('grp', 'dev'))]
    pallas_call x0 -> x8, Pallas kernels: none -> 35 us  [call(): pl.pallas_call(body, out_shape=outs, compiler_params=pltpu.CompilerParams...]
    dot_general x6 -> x0, matrix products: 27.1 us -> none  [the longest x2 13.3 us: score_block(): lax.dot_general(block_anchors, memory_keys, (((1,), (1,)), ((), ())), pre...]
    ppermute x0 -> x14, waiting for transfers between devices: none -> 25.2 us  [the longest x7 15.1 us: hand_back(): return lax.ppermute(value, 'grp' if axis == 'grp' else 'dev', back)]
    all_gather x2 -> x0, blocking collectives: 25 us -> none  [the longest x1 17 us: per_device(): lax.all_gather(local_anchors, 'dev', axis=0, tiled=True)]
    ppermute x0 -> x14, starting transfers between devices: none -> 17.4 us  [the longest x7 9.24 us: fetch(): lax.ppermute(value, 'grp' if axis == 'grp' else 'dev', pairs(axis, step))]
    unnamed x1 -> x0, blocking collectives: 8.96 us -> none
  transfers between devices with their start and end apart: 2 -> 14, of which waited for: 2 -> 8; matrix products, arithmetic and copies ran while one was open for 2% -> 4% of each run, Pallas kernels for 0% -> 20%
where the time goes in v1:
time: 92.9 us; the launch traced here: 92.2 us
  Pallas kernels  35 us (38%)
  waiting for transfers between devices  25.2 us (27%)
  starting transfers between devices  17.4 us (19%)
  local copies, waits for them, and re-layouts  10.7 us (12%)
  other arithmetic  2.34 us (3%)
  between operations  1.49 us (2%)
    pallas_call x8, Pallas kernels, call(): pl.pallas_call(body, out_shape=outs, compiler_params=pltpu.CompilerParams...  35 us
    ppermute x7, waiting for transfers between devices, hand_back(): return lax.ppermute(value, 'grp' if axis == 'grp' else 'dev', back)  15.1 us
    ppermute x7, waiting for transfers between devices, fetch(): lax.ppermute(value, 'grp' if axis == 'grp' else 'dev', pairs(axis, step))  10.1 us
    ppermute x7, starting transfers between devices, fetch(): lax.ppermute(value, 'grp' if axis == 'grp' else 'dev', pairs(axis, step))  9.24 us
    unnamed x25, local copies, waits for them, and re-layouts  8.59 us
    ppermute x7, starting transfers between devices, hand_back(): return lax.ppermute(value, 'grp' if axis == 'grp' else 'dev', back)  8.21 us
  transfers between devices with their start and end apart: 14, of which 8 were waited for; matrix products, arithmetic and copies ran while one was open for 4% of the time, Pallas kernels for 20%

profile of v1, /device:TPU:0, one launch (start us, length us, event | category | flops | bytes accessed | tf_op | source)
XLA Modules:
  0.0 92.2 jit_solution(14729015195381415842)
XLA Ops:
  0.6 1.3 %copy.25 = s32[2048]{0:T(1024)} copy(s32[2048]{0:T(1024)} %param.9) | data formatting | bytes 16384
  1.9 3.0 %copy.24.memory_ref = bf16[2048,512]{1,0:T(8,128)(2,1)} copy(bf16[2048,512]{1,0:T(8,128)(2,1)} %param.8) | data formatting | bytes 4194304
  5.0 1.5 %shard_map.93 = (bf16[32,640]{1,0:T(8,128)(2,1)}, f32[32,512]{1,0:T(8,128)}, f32[32,128]{1,0:T(8,128)}) custom-call(bf16[32,512]{1,0:T(8,128)(2,1)} %rows_ref.1, s32[1,32]{1,0:T(1,128)} %bitcast.14), custom_call_target="tpu_custom_call" | custom-call | bytes 155776 | tf_op jit(solution)/shard_map/pallas_call | solution.py:40
  6.5 5.0 %collective-permute-start.2 = (bf16[32,640]{1,0:T(8,128)(2,1)}, bf16[32,640]{1,0:T(8,128)(2,1)S(1)}, u32[]{:S(2)}, u32[]{:S(2)}) collective-permute-start(bf16[32,640]{1,0:T(8,128)(2,1)} %get-tuple-element.19), channel_id=1, source_target_pairs={{6,0},{7,1},{4,2},{5,3},{2,4},{3,5},{0,6},{1,7},{14,8},{15,9},{12,... | collective-permute-start | bytes 122888 | tf_op jit(solution)/shard_map/ppermute | solution.py:223
  12.1 0.8 constant_dynamic-update-slice_fusion.3
  12.9 2.8 %collective-permute-done = bf16[32,640]{1,0:T(8,128)(2,1)S(1)} collective-permute-done((bf16[32,640]{1,0:T(8,128)(2,1)}, bf16[32,640]{1,0:T(8,128)(2,1)S(1)}, u32[]{:S(2)}, u32[]{:S(2)}) %collective-permute-start) | collective-permute-done | bytes 40992 | tf_op jit(solution)/shard_map/ppermute | solution.py:223
  15.8 0.9 collective-permute-done.1
  16.7 1.6 %collective-permute-start.3 = (bf16[128,640]{1,0:T(8,128)(2,1)S(1)}, bf16[128,640]{1,0:T(8,128)(2,1)S(1)}, u32[]{:S(2)}, u32[]{:S(2)}) collective-permute-start(bf16[128,640]{1,0:T(8,128)(2,1)S(1)} %get-tuple-element.34), channel_id=1, source_target_pairs={{8,0},{0,8},{24,16},{16,24},{9,1},{1,9},{25,17},{17,25},{10,2},{2,... | collective-permute-start | bytes 491528 | tf_op jit(solution)/shard_map/ppermute | solution.py:223
  18.2 1.5 %collective-permute-start.4 = (bf16[128,640]{1,0:T(8,128)(2,1)S(1)}, bf16[128,640]{1,0:T(8,128)(2,1)S(1)}, u32[]{:S(2)}, u32[]{:S(2)}) collective-permute-start(bf16[128,640]{1,0:T(8,128)(2,1)S(1)} %get-tuple-element.34), channel_id=1, source_target_pairs={{16,0},{24,8},{0,16},{8,24},{17,1},{25,9},{1,17},{9,25},{18,2},{26... | collective-permute-start | bytes 491528 | tf_op jit(solution)/shard_map/ppermute | solution.py:223
  20.2 3.4 %collective-permute-done.3 = bf16[128,640]{1,0:T(8,128)(2,1)S(1)} collective-permute-done((bf16[128,640]{1,0:T(8,128)(2,1)S(1)}, bf16[128,640]{1,0:T(8,128)(2,1)S(1)}, u32[]{:S(2)}, u32[]{:S(2)}) %collective-permute-start.3) | collective-permute-done | bytes 163872 | tf_op jit(solution)/shard_map/ppermute | solution.py:223
  23.7 3.0 %collective-permute-done.4 = bf16[128,640]{1,0:T(8,128)(2,1)S(1)} collective-permute-done((bf16[128,640]{1,0:T(8,128)(2,1)S(1)}, bf16[128,640]{1,0:T(8,128)(2,1)S(1)}, u32[]{:S(2)}, u32[]{:S(2)}) %collective-permute-start.4) | collective-permute-done | bytes 163872 | tf_op jit(solution)/shard_map/ppermute | solution.py:223
  26.8 6.7 %shard_map.94 = (bf16[2048,512]{1,0:T(8,128)(2,1)}, bf16[512,2048]{1,0:T(8,128)(2,1)}) custom-call(bf16[2048,512]{1,0:T(8,128)(2,1)} %copy.24.memory_ref), custom_call_target="tpu_custom_call" | custom-call | bytes 6291456 | tf_op jit(solution)/shard_map/pallas_call | solution.py:40
  33.5 0.9 %copy-done.8 = bf16[512,640]{1,0:T(8,128)(2,1)} copy-done((bf16[512,640]{1,0:T(8,128)(2,1)}, bf16[512,640]{1,0:T(8,128)(2,1)S(1)}, u32[]{:S(2)}) %copy-start.8) | copy-done | bytes 655384
  34.4 7.8 %shard_map.97 = bf16[512,1152]{1,0:T(8,128)(2,1)} custom-call(bf16[512,640]{1,0:T(8,128)(2,1)} %copy-done.8, bf16[2048,512]{1,0:T(8,128)(2,1)} %get-tuple-element.20.keys_ref, bf16[512,2048]{1,0:T(8,128)(2,1)} %get-tuple-element.21.turned_ref, s32[1,2048]{1,0:T(1,128)} %bitcast.8, s32[1,2048]{1,0:T(1,128)} %bitcast.11), custom_call_target="tpu_custom_call" | custom-call | flops 3221225472 | bytes 6045696 | tf_op jit(solution)/shard_map/pallas_call | solution.py:40
  43.4 5.7 %shard_map.96.refs_1_ = f32[256,1152]{1,0:T(8,128)} custom-call(bf16[512,640]{1,0:T(8,128)(2,1)} %copy-done, bf16[2048,512]{1,0:T(8,128)(2,1)} %get-tuple-element.20.keys_ref, bf16[512,2048]{1,0:T(8,128)(2,1)} %get-tuple-element.21.turned_ref, s32[1,2048]{1,0:T(1,128)} %bitcast.9, s32[1,2048]{1,0:T(1,128)} %bitcast.12), custom_call_target="tpu_custom_call" | custom-call | flops 1610612736 | bytes 6045696 | tf_op jit(solution)/shard_map/pallas_call | solution.py:40
  49.1 5.7 %shard_map.95.refs_0_ = f32[256,1152]{1,0:T(8,128)} custom-call(bf16[512,640]{1,0:T(8,128)(2,1)} %copy-done, bf16[2048,512]{1,0:T(8,128)(2,1)} %get-tuple-element.20.keys_ref, bf16[512,2048]{1,0:T(8,128)(2,1)} %get-tuple-element.21.turned_ref, s32[1,2048]{1,0:T(1,128)} %bitcast.10, s32[1,2048]{1,0:T(1,128)} %bitcast.13), custom_call_target="tpu_custom_call" | custom-call | flops 1610612736 | bytes 6045696 | tf_op jit(solution)/shard_map/pallas_call | solution.py:40
  54.8 0.8 dynamic-slice_select_fusion
  55.7 1.0 %copy-done.1 = bf16[512,1152]{1,0:T(8,128)(2,1)} copy-done((bf16[512,1152]{1,0:T(8,128)(2,1)}, bf16[512,1152]{1,0:T(8,128)(2,1)S(1)}, u32[]{:S(2)}) %copy-start.1) | copy-done | bytes 1179672
  56.7 3.4 %shard_map.98 = (f32[128,1152]{1,0:T(8,128)}, bf16[128,1152]{1,0:T(8,128)(2,1)}, bf16[128,1152]{1,0:T(8,128)(2,1)}, bf16[128,1152]{1,0:T(8,128)(2,1)}) custom-call(f32[256,1152]{1,0:T(8,128)} %shard_map.95.refs_0_, f32[256,1152]{1,0:T(8,128)} %shard_map.96.refs_1_, bf16[512,1152]{1,0:T(8,128)(2,1)} %copy-done.1), custom_call_target="tpu_custom_call" | custom-call | bytes 5013504 | tf_op jit(solution)/shard_map/pallas_call | solution.py:40
  60.6 0.9 collective-permute-start.9
  61.5 2.1 %collective-permute-start.10 = (bf16[128,1152]{1,0:T(8,128)(2,1)}, bf16[128,1152]{1,0:T(8,128)(2,1)S(1)}, u32[]{:S(2)}, u32[]{:S(2)}) collective-permute-start(bf16[128,1152]{1,0:T(8,128)(2,1)} %get-tuple-element.25), channel_id=1, source_target_pairs={{0,24},{8,16},{16,8},{24,0},{1,25},{9,17},{17,9},{25,1},{2,26},{10... | collective-permute-start | bytes 884744 | tf_op jit(solution)/shard_map/ppermute | solution.py:227
  64.2 5.9 %collective-permute-done.8.refs_1_ = bf16[128,1152]{1,0:T(8,128)(2,1)S(1)} collective-permute-done((bf16[128,1152]{1,0:T(8,128)(2,1)}, bf16[128,1152]{1,0:T(8,128)(2,1)S(1)}, u32[]{:S(2)}, u32[]{:S(2)}) %collective-permute-start.8) | collective-permute-done | bytes 294944 | tf_op jit(solution)/shard_map/ppermute | solution.py:227
  70.2 5.9 %collective-permute-done.10.refs_3_ = bf16[128,1152]{1,0:T(8,128)(2,1)S(1)} collective-permute-done((bf16[128,1152]{1,0:T(8,128)(2,1)}, bf16[128,1152]{1,0:T(8,128)(2,1)S(1)}, u32[]{:S(2)}, u32[]{:S(2)}) %collective-permute-start.10) | collective-permute-done | bytes 294944 | tf_op jit(solution)/shard_map/ppermute | solution.py:227
  76.2 0.7 copy-done.4
  76.9 2.2 %shard_map.99 = (f32[32,1152]{1,0:T(8,128)}, bf16[32,1152]{1,0:T(8,128)(2,1)}, bf16[32,1152]{1,0:T(8,128)(2,1)}, bf16[32,1152]{1,0:T(8,128)(2,1)}) custom-call(f32[128,1152]{1,0:T(8,128)} %get-tuple-element.22.refs_0_, bf16[128,1152]{1,0:T(8,128)(2,1)} %copy-done.2, bf16[128,1152]{1,0:T(8,128)(2,1)} %copy-done.3, bf16[128,1152]{1,0:T(8,128)(2,1)} %copy-done.4), custom_call_target="tpu_custom_call" | custom-call | bytes 1843200 | tf_op jit(solution)/shard_map/pallas_call | solution.py:40
  79.5 2.0 %collective-permute-start.12 = (bf16[32,1152]{1,0:T(8,128)(2,1)}, bf16[32,1152]{1,0:T(8,128)(2,1)S(1)}, u32[]{:S(2)}, u32[]{:S(2)}) collective-permute-start(bf16[32,1152]{1,0:T(8,128)(2,1)} %get-tuple-element.28), channel_id=1, source_target_pairs={{0,4},{1,5},{2,6},{3,7},{4,0},{5,1},{6,2},{7,3},{8,12},{9,13},{10,... | collective-permute-start | bytes 221192 | tf_op jit(solution)/shard_map/ppermute | solution.py:227
  81.5 2.0 %collective-permute-start.13 = (bf16[32,1152]{1,0:T(8,128)(2,1)}, bf16[32,1152]{1,0:T(8,128)(2,1)S(1)}, u32[]{:S(2)}, u32[]{:S(2)}) collective-permute-start(bf16[32,1152]{1,0:T(8,128)(2,1)} %get-tuple-element.29), channel_id=1, source_target_pairs={{0,6},{1,7},{2,4},{3,5},{4,2},{5,3},{6,0},{7,1},{8,14},{9,15},{10,... | collective-permute-start | bytes 221192 | tf_op jit(solution)/shard_map/ppermute | solution.py:227
  83.6 1.5 %dynamic_update_slice.7 = s32[2048]{0:T(1024)} dynamic-update-slice(s32[2048]{0:T(1024)} %copy.25, s32[32]{0:T(128)S(1)} %fusion, s32[]{:T(128)S(6)} %select_n.60) | dynamic-update-slice | bytes 260 | tf_op jit(solution)/shard_map/dynamic_update_slice | solution.py:283
  85.1 3.2 %collective-permute-done.12.refs_2_ = bf16[32,1152]{1,0:T(8,128)(2,1)S(1)} collective-permute-done((bf16[32,1152]{1,0:T(8,128)(2,1)}, bf16[32,1152]{1,0:T(8,128)(2,1)S(1)}, u32[]{:S(2)}, u32[]{:S(2)}) %collective-permute-start.12) | collective-permute-done | bytes 73760 | tf_op jit(solution)/shard_map/ppermute | solution.py:227
  88.3 0.6 copy-done.6
  88.9 1.9 %shard_map.100 = (f32[32,512]{1,0:T(8,128)}, f32[32,1]{1,0:T(8,128)}) custom-call(f32[32,1152]{1,0:T(8,128)} %get-tuple-element.26.refs_0_, bf16[32,1152]{1,0:T(8,128)(2,1)} %copy-done.5, bf16[32,1152]{1,0:T(8,128)(2,1)} %copy-done.6, bf16[32,1152]{1,0:T(8,128)(2,1)} %copy-done.7, f32[32,512]{1,0:T(8,128)} %get-tuple-element.30.refs_4_, ...), custom_call_target="tpu_custom_call" | custom-call | bytes 516224 | tf_op jit(solution)/shard_map/pallas_call | solution.py:40
  90.8 1.3 %reduce = f32[32]{0:T(128)} reduce(f32[32,1]{1,0:T(8,128)} %get-tuple-element.33, f32[]{:T(128)} %constant.92), dimensions={1}, to_apply=%get-tuple-element.33.reduce_sub_computation | reduce | bytes 260 | tf_op jit(solution)/shard_map/pallas_call | solution.py:40
  (37 shorter events, 3.4 us)
Async XLA Ops:
  6.5 10.2 %collective-permute-start.2 = (bf16[32,640]{1,0:T(8,128)(2,1)}, bf16[32,640]{1,0:T(8,128)(2,1)S(1)}, u32[]{:S(2)}, u32[]{:S(2)}) collective-permute-start(bf16[32,640]{1,0:T(8,128)(2,1)} %get-tuple-element.19), channel_id=1, source_target_pairs={{6,0},{7,1},{4,2},{5,3},{2,4},{3,5},{0,6},{1,7},{14,8},{15,9},{12,... | collective-permute-start | bytes 122888 | tf_op jit(solution)/shard_map/ppermute | solution.py:223
  11.5 5.1 %collective-permute-start.1 = (bf16[32,640]{1,0:T(8,128)(2,1)}, bf16[32,640]{1,0:T(8,128)(2,1)S(1)}, u32[]{:S(2)}, u32[]{:S(2)}) collective-permute-start(bf16[32,640]{1,0:T(8,128)(2,1)} %get-tuple-element.19), channel_id=1, source_target_pairs={{4,0},{5,1},{6,2},{7,3},{0,4},{1,5},{2,6},{3,7},{12,8},{13,9},{14,... | collective-permute-start | bytes 122888 | tf_op jit(solution)/shard_map/ppermute | solution.py:223
  11.5 4.2 %collective-permute-start = (bf16[32,640]{1,0:T(8,128)(2,1)}, bf16[32,640]{1,0:T(8,128)(2,1)S(1)}, u32[]{:S(2)}, u32[]{:S(2)}) collective-permute-start(bf16[32,640]{1,0:T(8,128)(2,1)} %get-tuple-element.19), channel_id=1, source_target_pairs={{2,0},{3,1},{0,2},{1,3},{6,4},{7,5},{4,6},{5,7},{10,8},{11,9},{8,1... | collective-permute-start | bytes 122888 | tf_op jit(solution)/shard_map/ppermute | solution.py:223
  16.7 7.0 %collective-permute-start.3 = (bf16[128,640]{1,0:T(8,128)(2,1)S(1)}, bf16[128,640]{1,0:T(8,128)(2,1)S(1)}, u32[]{:S(2)}, u32[]{:S(2)}) collective-permute-start(bf16[128,640]{1,0:T(8,128)(2,1)S(1)} %get-tuple-element.34), channel_id=1, source_target_pairs={{8,0},{0,8},{24,16},{16,24},{9,1},{1,9},{25,17},{17,25},{10,2},{2,... | collective-permute-start | bytes 491528 | tf_op jit(solution)/shard_map/ppermute | solution.py:223
  18.2 8.4 %collective-permute-start.4 = (bf16[128,640]{1,0:T(8,128)(2,1)S(1)}, bf16[128,640]{1,0:T(8,128)(2,1)S(1)}, u32[]{:S(2)}, u32[]{:S(2)}) collective-permute-start(bf16[128,640]{1,0:T(8,128)(2,1)S(1)} %get-tuple-element.34), channel_id=1, source_target_pairs={{16,0},{24,8},{0,16},{8,24},{17,1},{25,9},{1,17},{9,25},{18,2},{26... | collective-permute-start | bytes 491528 | tf_op jit(solution)/shard_map/ppermute | solution.py:223
  19.8 6.9 %collective-permute-start.5 = (bf16[128,640]{1,0:T(8,128)(2,1)S(1)}, bf16[128,640]{1,0:T(8,128)(2,1)S(1)}, u32[]{:S(2)}, u32[]{:S(2)}) collective-permute-start(bf16[128,640]{1,0:T(8,128)(2,1)S(1)} %get-tuple-element.34), channel_id=1, source_target_pairs={{24,0},{16,8},{8,16},{0,24},{25,1},{17,9},{9,17},{1,25},{26,2},{18... | collective-permute-start | bytes 491528 | tf_op jit(solution)/shard_map/ppermute | solution.py:223
  26.7 15.6 %copy-start = (bf16[512,640]{1,0:T(8,128)(2,1)}, bf16[512,640]{1,0:T(8,128)(2,1)S(1)}, u32[]{:S(2)}) copy-start(bf16[512,640]{1,0:T(8,128)(2,1)S(1)} %constant_dynamic-update-slice_fusion.4.rows_ref) | copy-start | bytes 1966084
  26.7 6.8 %collective-permute-start.6 = (bf16[512,640]{1,0:T(8,128)(2,1)S(1)}, bf16[512,640]{1,0:T(8,128)(2,1)S(1)}, u32[]{:S(2)}, u32[]{:S(2)}) collective-permute-start(bf16[512,640]{1,0:T(8,128)(2,1)S(1)} %constant_dynamic-update-slice_fusion.4.rows_ref), channel_id=1, source_target_pairs={{1,0},{0,1},{3,2},{2,3},{5,4},{4,5},{7,6},{6,7},{9,8},{8,9},{11,10... | collective-permute-start | bytes 1966088 | tf_op jit(solution)/shard_map/ppermute | solution.py:223
  33.5 0.9 %copy-start.8 = (bf16[512,640]{1,0:T(8,128)(2,1)}, bf16[512,640]{1,0:T(8,128)(2,1)S(1)}, u32[]{:S(2)}) copy-start(bf16[512,640]{1,0:T(8,128)(2,1)S(1)} %collective-permute-done.6.rows_ref) | copy-start | bytes 1966084
  42.3 13.4 %collective-permute-start.7 = (bf16[512,1152]{1,0:T(8,128)(2,1)}, bf16[512,1152]{1,0:T(8,128)(2,1)S(1)}, u32[]{:S(2)}, u32[]{:S(2)}) collective-permute-start(bf16[512,1152]{1,0:T(8,128)(2,1)} %shard_map.97), channel_id=1, source_target_pairs={{0,1},{1,0},{2,3},{3,2},{4,5},{5,4},{6,7},{7,6},{8,9},{9,8},{10,11... | collective-permute-start | bytes 3538952 | tf_op jit(solution)/shard_map/ppermute | solution.py:227
  55.7 1.1 %copy-start.1 = (bf16[512,1152]{1,0:T(8,128)(2,1)}, bf16[512,1152]{1,0:T(8,128)(2,1)S(1)}, u32[]{:S(2)}) copy-start(bf16[512,1152]{1,0:T(8,128)(2,1)S(1)} %collective-permute-done.7.refs_2_) | copy-start | bytes 3538948
  60.1 10.1 %collective-permute-start.8 = (bf16[128,1152]{1,0:T(8,128)(2,1)}, bf16[128,1152]{1,0:T(8,128)(2,1)S(1)}, u32[]{:S(2)}, u32[]{:S(2)}) collective-permute-start(bf16[128,1152]{1,0:T(8,128)(2,1)} %get-tuple-element.23), channel_id=1, source_target_pairs={{0,8},{8,0},{16,24},{24,16},{1,9},{9,1},{17,25},{25,17},{2,10},{10... | collective-permute-start | bytes 884744 | tf_op jit(solution)/shard_map/ppermute | solution.py:227
  60.6 9.6 %collective-permute-start.9 = (bf16[128,1152]{1,0:T(8,128)(2,1)}, bf16[128,1152]{1,0:T(8,128)(2,1)S(1)}, u32[]{:S(2)}, u32[]{:S(2)}) collective-permute-start(bf16[128,1152]{1,0:T(8,128)(2,1)} %get-tuple-element.24), channel_id=1, source_target_pairs={{0,16},{8,24},{16,0},{24,8},{1,17},{9,25},{17,1},{25,9},{2,18},{10... | collective-permute-start | bytes 884744 | tf_op jit(solution)/shard_map/ppermute | solution.py:227
  61.5 14.6 %collective-permute-start.10 = (bf16[128,1152]{1,0:T(8,128)(2,1)}, bf16[128,1152]{1,0:T(8,128)(2,1)S(1)}, u32[]{:S(2)}, u32[]{:S(2)}) collective-permute-start(bf16[128,1152]{1,0:T(8,128)(2,1)} %get-tuple-element.25), channel_id=1, source_target_pairs={{0,24},{8,16},{16,8},{24,0},{1,25},{9,17},{17,9},{25,1},{2,26},{10... | collective-permute-start | bytes 884744 | tf_op jit(solution)/shard_map/ppermute | solution.py:227
  70.1 6.0 %copy-start.2 = (bf16[128,1152]{1,0:T(8,128)(2,1)}, bf16[128,1152]{1,0:T(8,128)(2,1)S(1)}, u32[]{:S(2)}) copy-start(bf16[128,1152]{1,0:T(8,128)(2,1)S(1)} %collective-permute-done.8.refs_1_) | copy-start | bytes 884740
  70.2 5.9 %copy-start.3 = (bf16[128,1152]{1,0:T(8,128)(2,1)}, bf16[128,1152]{1,0:T(8,128)(2,1)S(1)}, u32[]{:S(2)}) copy-start(bf16[128,1152]{1,0:T(8,128)(2,1)S(1)} %collective-permute-done.9.refs_2_) | copy-start | bytes 884740
  76.2 0.7 copy-start.4
  79.1 6.0 %collective-permute-start.11 = (bf16[32,1152]{1,0:T(8,128)(2,1)}, bf16[32,1152]{1,0:T(8,128)(2,1)S(1)}, u32[]{:S(2)}, u32[]{:S(2)}) collective-permute-start(bf16[32,1152]{1,0:T(8,128)(2,1)} %get-tuple-element.27), channel_id=1, source_target_pairs={{0,2},{1,3},{2,0},{3,1},{4,6},{5,7},{6,4},{7,5},{8,10},{9,11},{10,... | collective-permute-start | bytes 221192 | tf_op jit(solution)/shard_map/ppermute | solution.py:227
  79.5 8.8 %collective-permute-start.12 = (bf16[32,1152]{1,0:T(8,128)(2,1)}, bf16[32,1152]{1,0:T(8,128)(2,1)S(1)}, u32[]{:S(2)}, u32[]{:S(2)}) collective-permute-start(bf16[32,1152]{1,0:T(8,128)(2,1)} %get-tuple-element.28), channel_id=1, source_target_pairs={{0,4},{1,5},{2,6},{3,7},{4,0},{5,1},{6,2},{7,3},{8,12},{9,13},{10,... | collective-permute-start | bytes 221192 | tf_op jit(solution)/shard_map/ppermute | solution.py:227
  81.5 6.8 %collective-permute-start.13 = (bf16[32,1152]{1,0:T(8,128)(2,1)}, bf16[32,1152]{1,0:T(8,128)(2,1)S(1)}, u32[]{:S(2)}, u32[]{:S(2)}) collective-permute-start(bf16[32,1152]{1,0:T(8,128)(2,1)} %get-tuple-element.29), channel_id=1, source_target_pairs={{0,6},{1,7},{2,4},{3,5},{4,2},{5,3},{6,0},{7,1},{8,14},{9,15},{10,... | collective-permute-start | bytes 221192 | tf_op jit(solution)/shard_map/ppermute | solution.py:227
  85.1 3.2 %copy-start.5 = (bf16[32,1152]{1,0:T(8,128)(2,1)}, bf16[32,1152]{1,0:T(8,128)(2,1)S(1)}, u32[]{:S(2)}) copy-start(bf16[32,1152]{1,0:T(8,128)(2,1)S(1)} %collective-permute-done.11.refs_1_) | copy-start | bytes 221188
  88.3 0.6 copy-start.6
  88.3 0.7 copy-start.7

commit v2 on v0

v2 whole, which is shorter than its diff:
```python
import functools
import math

import jax
import jax.numpy as jnp
from jax import lax
from jax.experimental import pallas as pl
from jax.experimental.pallas import tpu as pltpu
from jax.sharding import PartitionSpec as P

pos_scale = 2.0
neg_scale = 50.0
margin = 0.5
lanes = 128
log2e = math.log2(math.e)
vmem_bytes = 20 * 1024 * 1024
vmem_terms = 12 * 1024 * 1024
f32 = jnp.float32
bf16 = jnp.bfloat16


def call(body, outs, *args, flops=0, limit=vmem_bytes, **kw):
    moved = sum(a.size * a.dtype.itemsize for a in args)
    moved += sum(math.prod(o.shape) * o.dtype.itemsize for o in outs)
    return pl.pallas_call(
        body,
        out_shape=outs,
        compiler_params=pltpu.CompilerParams(vmem_limit_bytes=limit),
        cost_estimate=pl.CostEstimate(flops=flops, bytes_accessed=moved, transcendentals=0),
        **kw,
    )(*args)


def shaped(shape, dtype):
    return jax.ShapeDtypeStruct(shape, dtype)


def in_vmem(value):
    return pltpu.with_memory_space_constraint(value, pltpu.VMEM)


def prepare_kernel(rows_ref, labels_ref, packed_ref, unit_ref, radius_ref):
    rows = rows_ref[...].astype(f32)
    count, width = rows.shape
    radius = jnp.sqrt(jnp.sum(rows * rows, axis=1, keepdims=True) + 1e-06)
    unit = rows / radius
    unit_ref[...] = unit
    radius_ref[...] = jnp.broadcast_to(radius, radius_ref.shape)
    packed_ref[:, :width] = unit.astype(bf16)
    column = to_column(labels_ref[...].astype(f32))
    high = jnp.floor(column * (1.0 / 256.0))
    low = column - high * 256.0
    lane = lax.broadcasted_iota(jnp.int32, (count, lanes), 1)
    digits = jnp.where(lane == 0, high, jnp.where(lane == 1, low, 0.0))
    packed_ref[:, width:] = digits.astype(bf16)


def diagonal(count):
    across = lax.broadcasted_iota(jnp.int32, (count, count), 1)
    down = lax.broadcasted_iota(jnp.int32, (count, count), 0)
    return across == down


def to_column(row):
    count = row.shape[1]
    spread = jnp.broadcast_to(row, (count, count))
    return jnp.sum(jnp.where(diagonal(count), spread, 0.0), axis=1, keepdims=True)


def to_row(column):
    count = column.shape[0]
    spread = jnp.broadcast_to(column, (count, count))
    return jnp.sum(jnp.where(diagonal(count), spread, 0.0), axis=0, keepdims=True)


def keys_kernel(memory_ref, keys_ref, *copy_refs):
    stored = memory_ref[...]
    rows = stored.astype(f32)
    radius = jnp.sqrt(jnp.sum(rows * rows, axis=1, keepdims=True) + 1e-06)
    keys_ref[...] = (rows / radius).astype(bf16)
    for copy_ref in copy_refs:
        copy_ref[...] = stored


def keys_of(memory, copied):
    slots, width = memory.shape
    block = math.gcd(512, slots)
    spec = pl.BlockSpec((block, width), lambda i: (i, 0))
    return call(
        keys_kernel,
        [shaped((slots, width), bf16)] * (2 if copied else 1),
        memory,
        grid=(slots // block,),
        in_specs=[spec],
        out_specs=[spec] * (2 if copied else 1),
    )


def score_kernel(blocks, sides, chunk, count, *refs):
    rows_refs, keys_refs = refs[:blocks], refs[blocks : blocks + sides]
    label_refs = refs[blocks + sides : blocks + 2 * sides]
    term_refs = refs[blocks + 2 * sides : 2 * blocks + 2 * sides]
    stats_ref = refs[2 * blocks + 2 * sides]
    slots, width = keys_refs[0].shape
    size = rows_refs[0].shape[0]
    anchors = jnp.concatenate([ref[:, :width] for ref in rows_refs], axis=0)
    digits = jnp.concatenate([ref[:, width:] for ref in rows_refs], axis=0).astype(f32)
    lane = lax.broadcasted_iota(jnp.int32, digits.shape, 1)
    weight = jnp.where(lane == 0, 256.0, jnp.where(lane == 1, 1.0, 0.0))
    labels = jnp.sum(digits * weight, axis=1, keepdims=True)
    pos_sum = jnp.zeros((anchors.shape[0], 1), f32)
    neg_sum = jnp.zeros((anchors.shape[0], 1), f32)
    for side in range(sides):
        slot_labels = label_refs[side][...]
        neg_shift = jnp.where(slot_labels < 0.0, -1e30, -neg_scale * margin * log2e)
        for start in range(0, slots, chunk):
            part = slice(start, start + chunk)
            scores = lax.dot_general(
                anchors, keys_refs[side][part, :], (((1,), (1,)), ((), ())), preferred_element_type=f32
            )
            same = labels == slot_labels[:, part]
            slope = jnp.where(same, -pos_scale * log2e, neg_scale * log2e)
            shift = jnp.where(same, pos_scale * margin * log2e, neg_shift[:, part])
            term = jnp.exp2(scores * slope + shift)
            pos_sum += jnp.sum(jnp.where(same, term, 0.0), axis=1, keepdims=True)
            neg_sum += jnp.sum(jnp.where(same, 0.0, term), axis=1, keepdims=True)
            signed = jnp.where(same, -term, term)
            to = slice(side * slots + start, side * slots + start + chunk)
            for block, ref in enumerate(term_refs):
                ref[:, to] = signed[block * size : (block + 1) * size, :]
    for which, total in enumerate((pos_sum, neg_sum)):
        for at in range(blocks * size // count):
            stats_ref[which, at : at + 1, :] = to_row(total[at * count : (at + 1) * count])


def score(blocks, keys, labels, count, placed):
    slots, width = keys[0].shape
    size = blocks[0].shape[0]
    shape = (size, slots * len(keys))
    outs = [placed(shape, f32) for _ in blocks]
    outs.append(shaped((2, len(blocks) * size // count, count), f32))
    return call(
        functools.partial(score_kernel, len(blocks), len(keys), math.gcd(512, slots), count),
        outs,
        *blocks, *[in_vmem(k) for k in keys], *labels,
        flops=2 * size * len(blocks) * slots * len(keys) * width,
    )


def pull_kernel(first, sides, chunk, term_ref, totals_ref, *refs):
    keys_refs, out_ref, weight_ref = refs[:sides], refs[sides], refs[sides + 1]
    slots = keys_refs[0].shape[0]
    size = term_ref.shape[0]
    count = totals_ref.shape[2]
    scales = []
    for which in range(2):
        parts = [to_column(totals_ref[which, first + at : first + at + 1, :]) for at in range(size // count)]
        scales.append(1.0 / (1.0 + jnp.concatenate(parts, axis=0)))
    for start in range(0, slots * sides, chunk):
        part = slice(start, start + chunk)
        term = term_ref[:, part]
        weight = term * jnp.where(term < 0.0, scales[0], scales[1])
        weight_ref[:, part] = weight.astype(bf16)
    total = None
    for side in range(sides):
        part = weight_ref[:, side * slots : (side + 1) * slots]
        term = jnp.dot(part, keys_refs[side][...], preferred_element_type=f32)
        total = term if total is None else total + term
    out_ref[...] = total.astype(out_ref.dtype)


def weighted(term, totals, first, keys, dtype):
    slots, width = keys[0].shape
    size = term.shape[0]
    return call(
        functools.partial(pull_kernel, first, len(keys), math.gcd(512, slots)),
        [shaped((size, width), dtype)],
        term, totals, *[in_vmem(k) for k in keys],
        flops=2 * size * slots * len(keys) * width,
        scratch_shapes=[pltpu.VMEM((size, slots * len(keys)), bf16)],
    )[0]


def finish_kernel(arrived, *refs):
    held_ref, arrived_refs = refs[0], refs[1 : 1 + arrived]
    unit_ref, radius_ref, grad_ref = refs[1 + arrived :]
    total = held_ref[...]
    for ref in arrived_refs:
        total = total + ref[...].astype(f32)
    unit = unit_ref[...]
    along = jnp.sum(unit * total, axis=1, keepdims=True)
    grad_ref[...] = (total - unit * along) / radius_ref[:, :1]


def swapped(value, axis, step):
    shape = value.shape
    cut = shape[:axis] + (shape[axis] // (2 * step), 2, step) + shape[axis + 1 :]
    return jnp.flip(value.reshape(cut), axis + 1).reshape(shape)


def per_device(batch_rows, batch_labels, memory, memory_labels, keep_bits, step_index):
    groups = lax.axis_size("grp")
    members = lax.axis_size("dev")
    cores = 2 if members % 2 == 0 else 1
    line = members // cores
    devices_all = groups * members
    my_grp = lax.axis_index("grp")
    my_dev = lax.axis_index("dev")
    count, width = batch_rows.shape
    slots = memory.shape[0]

    def exchange(value, axis, step):
        if axis == "grp":
            return lax.ppermute(value, "grp", [(i, i ^ step) for i in range(groups)])
        jump = step * cores if axis == "line" else step
        return lax.ppermute(value, "dev", [(i, i ^ jump) for i in range(members)])

    packed, unit, radius = call(
        prepare_kernel,
        [shaped((count, width + lanes), bf16), shaped((count, width), f32), shaped((count, lanes), f32)],
        batch_rows,
        batch_labels.reshape(1, count),
    )

    slot_labels = jnp.where(keep_bits > 0, memory_labels, -1)
    memories = [memory] + [exchange(memory, "core", s) for s in range(1, cores)]
    labels = [slot_labels] + [exchange(slot_labels, "core", s) for s in range(1, cores)]
    labels = [value.astype(f32).reshape(1, slots) for value in labels]
    own_keys, copied = keys_of(memory, True)
    keys = [own_keys] + [keys_of(value, False)[0] for value in memories[1:]]

    part = jnp.concatenate([packed] + [exchange(packed, "line", s) for s in range(1, line)])
    blocks = [part] + [exchange(part, "grp", s) for s in range(1, groups)]
    size = part.shape[0]

    fits = 4 * groups * size * slots * cores <= vmem_terms
    placed = pltpu.VMEM if fits else shaped
    terms, stats = [], []
    for first, last in [(0, 1)] + [(i, min(i + 3, groups)) for i in range(1, groups, 3)]:
        *more, stat = score(blocks[first:last], keys, labels, count, placed)
        terms += more
        stats.append(stat)
    totals = jnp.concatenate(stats, axis=1).reshape(2, groups, line, count)
    for axis, name, extent in ((2, "line", line), (1, "grp", groups)):
        step = 1
        while step < extent:
            totals = totals + swapped(exchange(totals, name, step), axis, step)
            step *= 2
    flat = totals.reshape(2, groups * line, count)
    loss = jnp.log(1.0 + totals[0, 0, 0]) / pos_scale + jnp.log(1.0 + totals[1, 0, 0]) / neg_scale

    arrived = []
    for s in list(range(groups - 1, 0, -1)):
        arrived.append(exchange(weighted(terms[s], flat, s * line, keys, bf16), "grp", s))
    total = weighted(terms[0], flat, 0, keys, f32)
    for value in arrived:
        total = total + value.astype(f32)
    arrived = [exchange(total[s * count : (s + 1) * count].astype(bf16), "line", s) for s in range(1, line)]
    grad_batch = call(
        functools.partial(finish_kernel, len(arrived)),
        [shaped((count, width), f32)],
        total[:count], *arrived, unit, radius,
    )[0]

    step_value = step_index[0]
    first_slot = (step_value % (slots // count)) * count
    crossing = (step_value % cores) if cores > 1 else 0
    target = my_grp * members + (my_dev ^ crossing)
    source = (target - step_value) % devices_all
    source_grp, source_line = source // members, (source % members) // cores
    at = ((my_grp ^ source_grp) * line + ((my_dev // cores) ^ source_line)) * count
    moved = lax.dynamic_slice_in_dim(jnp.concatenate(blocks), at, count, 0)
    if cores > 1:
        moved = jnp.where(crossing > 0, exchange(moved, "core", 1), moved)
    digits = moved[:, width : width + 2].astype(jnp.int32)
    moved_labels = digits[:, 0] * 256 + digits[:, 1]
    new_memory = lax.dynamic_update_slice_in_dim(copied, moved[:, :width], first_slot, 0)
    new_labels = lax.dynamic_update_slice_in_dim(memory_labels, moved_labels, first_slot, 0)
    return (grad_batch, loss, new_memory, new_labels)


def solution(mesh):
    placed = (
        P(("grp", "dev"), None),
        P(("grp", "dev")),
        P(("grp", "dev"), None),
        P(("grp", "dev")),
        P(("grp", "dev")),
        P(),
    )
    return jax.shard_map(
        per_device,
        mesh=mesh,
        in_specs=placed,
        out_specs=(
            P(("grp", "dev"), None),
            P(("grp", "dev")),
            P(("grp", "dev"), None),
            P(("grp", "dev")),
        ),
        check_vma=False,
    )
```

time: 276 us -> 83.9 us (0.30)
  waiting for transfers between devices: 143 us -> 28.7 us
  blocking collectives: 73.4 us -> 0 us
  matrix products: 27.1 us -> 0 us
  starting transfers between devices: 0.08 us -> 18.9 us
  between operations: 15.5 us -> 1.69 us
  local copies, waits for them, and re-layouts: 6.29 us -> 19.7 us
  Pallas kernels: 0 us -> 12.8 us
  other arithmetic: 9.78 us -> 1.54 us
    reduce_scatter x1 -> x0, waiting for transfers between devices: 136 us -> none  [per_device(): lax.psum_scatter(combined, ('grp', 'dev'), scatter_dimension=0, tiled=True)]
    psum x1 -> x0, blocking collectives: 39.4 us -> none  [per_device(): pos_total, neg_total = lax.psum((pos_sum, neg_sum), ('grp', 'dev'))]
    ppermute x0 -> x19, waiting for transfers between devices: none -> 28.7 us  [the longest x11 15.9 us: exchange(): return lax.ppermute(value, 'dev', [(i, i ^ jump) for i in range(members)])]
    dot_general x6 -> x0, matrix products: 27.1 us -> none  [the longest x2 13.3 us: score_block(): lax.dot_general(block_anchors, memory_keys, (((1,), (1,)), ((), ())), pre...]
    all_gather x2 -> x0, blocking collectives: 25 us -> none  [the longest x1 17 us: per_device(): lax.all_gather(local_anchors, 'dev', axis=0, tiled=True)]
    ppermute x0 -> x19, starting transfers between devices: none -> 18.9 us  [the longest x11 10.7 us: exchange(): return lax.ppermute(value, 'dev', [(i, i ^ jump) for i in range(members)])]
    unnamed x20 -> x43, local copies, waits for them, and re-layouts: 2.48 us -> 18.7 us
    pallas_call x0 -> x10, Pallas kernels: none -> 12.8 us  [call(): pl.pallas_call(body, out_shape=outs, compiler_params=pltpu.CompilerParams...]
  transfers between devices with their start and end apart: 2 -> 19, of which waited for: 2 -> 8; matrix products, arithmetic and copies ran while one was open for 2% -> 3% of each run, Pallas kernels for 0% -> 13%
where the time goes in v2:
time: 83.9 us; the launch traced here: 83.4 us
  waiting for transfers between devices  28.7 us (34%)
  local copies, waits for them, and re-layouts  19.7 us (23%)
  starting transfers between devices  18.9 us (23%)
  Pallas kernels  12.8 us (15%)
  between operations  1.69 us (2%)
  other arithmetic  1.54 us (2%)
    unnamed x43, local copies, waits for them, and re-layouts  18.7 us
    ppermute x11, waiting for transfers between devices, exchange(): return lax.ppermute(value, 'dev', [(i, i ^ jump) for i in range(members)])  15.9 us
    pallas_call x10, Pallas kernels, call(): pl.pallas_call(body, out_shape=outs, compiler_params=pltpu.CompilerParams...  12.8 us
    ppermute x8, waiting for transfers between devices, exchange(): return lax.ppermute(value, 'grp', [(i, i ^ step) for i in range(groups)])  12.8 us
    ppermute x11, starting transfers between devices, exchange(): return lax.ppermute(value, 'dev', [(i, i ^ jump) for i in range(members)])  10.7 us
    ppermute x8, starting transfers between devices, exchange(): return lax.ppermute(value, 'grp', [(i, i ^ step) for i in range(groups)])  8.23 us
  transfers between devices with their start and end apart: 19, of which 8 were waited for; matrix products, arithmetic and copies ran while one was open for 3% of the time, Pallas kernels for 13%

profile of v2, /device:TPU:0, one launch (start us, length us, event | category | flops | bytes accessed | tf_op | source)
XLA Modules:
  0.0 83.4 jit_solution(7753819563340805092)
XLA Ops:
  3.3 2.6 %collective-permute-start = (bf16[32,640]{1,0:T(8,128)(2,1)S(1)}, bf16[32,640]{1,0:T(8,128)(2,1)S(1)}, u32[]{:S(2)}, u32[]{:S(2)}) collective-permute-start(bf16[32,640]{1,0:T(8,128)(2,1)S(1)} %get-tuple-element.15), channel_id=1, source_target_pairs={{0,2},{1,3},{2,0},{3,1},{4,6},{5,7},{6,4},{7,5},{8,10},{9,11},{10,... | collective-permute-start | bytes 122888 | tf_op jit(solution)/shard_map/ppermute | solution.py:216
  5.9 2.6 %collective-permute-start.1 = (bf16[32,640]{1,0:T(8,128)(2,1)S(1)}, bf16[32,640]{1,0:T(8,128)(2,1)S(1)}, u32[]{:S(2)}, u32[]{:S(2)}) collective-permute-start(bf16[32,640]{1,0:T(8,128)(2,1)S(1)} %get-tuple-element.15), channel_id=1, source_target_pairs={{0,4},{1,5},{2,6},{3,7},{4,0},{5,1},{6,2},{7,3},{8,12},{9,13},{10,... | collective-permute-start | bytes 122888 | tf_op jit(solution)/shard_map/ppermute | solution.py:216
  8.6 3.2 %collective-permute-done.1 = bf16[32,640]{1,0:T(8,128)(2,1)S(1)} collective-permute-done((bf16[32,640]{1,0:T(8,128)(2,1)S(1)}, bf16[32,640]{1,0:T(8,128)(2,1)S(1)}, u32[]{:S(2)}, u32[]{:S(2)}) %collective-permute-start.1) | collective-permute-done | bytes 40992 | tf_op jit(solution)/shard_map/ppermute | solution.py:216
  11.8 2.5 %collective-permute-done.2 = bf16[32,640]{1,0:T(8,128)(2,1)S(1)} collective-permute-done((bf16[32,640]{1,0:T(8,128)(2,1)S(1)}, bf16[32,640]{1,0:T(8,128)(2,1)S(1)}, u32[]{:S(2)}, u32[]{:S(2)}) %collective-permute-start.2) | collective-permute-done | bytes 40992 | tf_op jit(solution)/shard_map/ppermute | solution.py:216
  14.3 1.6 %collective-permute-start.5 = (bf16[128,640]{1,0:T(8,128)(2,1)S(1)}, bf16[128,640]{1,0:T(8,128)(2,1)S(1)}, u32[]{:S(2)}, u32[]{:S(2)}) collective-permute-start(bf16[128,640]{1,0:T(8,128)(2,1)S(1)} %get-tuple-element.34.refs_0_), channel_id=1, source_target_pairs={{0,8},{8,0},{16,24},{24,16},{1,9},{9,1},{17,25},{25,17},{2,10},{10... | collective-permute-start | bytes 491528 | tf_op jit(solution)/shard_map/ppermute | solution.py:214
  15.9 1.5 %collective-permute-start.6 = (bf16[128,640]{1,0:T(8,128)(2,1)S(1)}, bf16[128,640]{1,0:T(8,128)(2,1)S(1)}, u32[]{:S(2)}, u32[]{:S(2)}) collective-permute-start(bf16[128,640]{1,0:T(8,128)(2,1)S(1)} %get-tuple-element.34.refs_0_), channel_id=1, source_target_pairs={{0,16},{8,24},{16,0},{24,8},{1,17},{9,25},{17,1},{25,9},{2,18},{10... | collective-permute-start | bytes 491528 | tf_op jit(solution)/shard_map/ppermute | solution.py:214
  18.9 1.6 %copy-done.12 = bf16[2048,512]{1,0:T(8,128)(2,1)S(1)} copy-done((bf16[2048,512]{1,0:T(8,128)(2,1)S(1)}, bf16[2048,512]{1,0:T(8,128)(2,1)}, u32[]{:S(2)}) %copy-start.12) | copy-done | bytes 2097176
  20.5 2.0 %shard_map.94 = (bf16[2048,512]{1,0:T(8,128)(2,1)S(1)}, bf16[2048,512]{1,0:T(8,128)(2,1)}) custom-call(bf16[2048,512]{1,0:T(8,128)(2,1)S(1)} %copy-done.12), custom_call_target="tpu_custom_call" | custom-call | bytes 6291456 | tf_op jit(solution)/shard_map/pallas_call | solution.py:25
  22.4 1.3 %copy-done = bf16[2048,512]{1,0:T(8,128)(2,1)} copy-done((bf16[2048,512]{1,0:T(8,128)(2,1)}, bf16[2048,512]{1,0:T(8,128)(2,1)S(1)}, u32[]{:S(2)}) %copy-start) | copy-done | bytes 2097176
  24.3 7.0 %collective-permute-done.7.refs_2_ = bf16[128,640]{1,0:T(8,128)(2,1)S(1)} collective-permute-done((bf16[128,640]{1,0:T(8,128)(2,1)S(1)}, bf16[128,640]{1,0:T(8,128)(2,1)S(1)}, u32[]{:S(2)}, u32[]{:S(2)}) %collective-permute-start.7) | collective-permute-done | bytes 163872 | tf_op jit(solution)/shard_map/ppermute | solution.py:214
  31.5 1.3 %copy-done.13 = bf16[2048,512]{1,0:T(8,128)(2,1)} copy-done((bf16[2048,512]{1,0:T(8,128)(2,1)}, bf16[2048,512]{1,0:T(8,128)(2,1)S(1)}, u32[]{:S(2)}) %copy-start.13) | copy-done | bytes 2097176
  32.8 1.6 %copy-done.14 = bf16[2048,512]{1,0:T(8,128)(2,1)S(1)} copy-done((bf16[2048,512]{1,0:T(8,128)(2,1)S(1)}, bf16[2048,512]{1,0:T(8,128)(2,1)}, u32[]{:S(2)}) %copy-start.14) | copy-done | bytes 2097176
  34.4 1.0 %shard_map.95.refs_2_.refs_4_.refs_1_ = bf16[2048,512]{1,0:T(8,128)(2,1)S(1)} custom-call(bf16[2048,512]{1,0:T(8,128)(2,1)S(1)} %copy-done.14), custom_call_target="tpu_custom_call" | custom-call | bytes 4194304 | tf_op jit(solution)/shard_map/pallas_call | solution.py:25
  35.4 1.9 %shard_map.96 = (f32[128,4096]{1,0:T(8,128)S(1)}, f32[2,4,32]{2,1,0:T(4,128)S(1)}) custom-call(bf16[128,640]{1,0:T(8,128)(2,1)S(1)} %get-tuple-element.34.refs_0_, bf16[2048,512]{1,0:T(8,128)(2,1)S(1)} %copy-done.1, bf16[2048,512]{1,0:T(8,128)(2,1)S(1)} %shard_map.95.refs_2_.refs_4_.refs_1_, f32[1,2048]{1,0:T(1,128)S(1)} %bitcast.25, f32[1,2048]{1,0:T(1,128)S(1)} %bitcast.23), custom_call_target="tpu_custom_call" | custom-call | flops 536870912 | bytes 6472704 | tf_op jit(solution)/shard_map/pallas_call | solution.py:25
  37.2 3.8 %shard_map.97 = (f32[128,4096]{1,0:T(8,128)S(1)}, f32[128,4096]{1,0:T(8,128)S(1)}, f32[128,4096]{1,0:T(8,128)S(1)}, f32[2,12,32]{2,1,0:T(8,128)S(1)}) custom-call(bf16[128,640]{1,0:T(8,128)(2,1)S(1)} %collective-permute-done.5.refs_0_, bf16[128,640]{1,0:T(8,128)(2,1)S(1)} %collective-permute-done.6.refs_1_, ...), custom_call_target="tpu_custom_call" | custom-call | flops 1610612736 | bytes 10996736 | tf_op jit(solution)/shard_map/pallas_call | solution.py:25
  41.0 1.4 %copy-done.6 = f32[128,4096]{1,0:T(8,128)} copy-done((f32[128,4096]{1,0:T(8,128)}, f32[128,4096]{1,0:T(8,128)S(1)}, u32[]{:S(2)}) %copy-start.6) | copy-done | bytes 2097176
  42.4 1.4 %copy-done.8 = f32[128,4096]{1,0:T(8,128)} copy-done((f32[128,4096]{1,0:T(8,128)}, f32[128,4096]{1,0:T(8,128)S(1)}, u32[]{:S(2)}) %copy-start.8) | copy-done | bytes 2097176
  43.8 1.3 %copy-done.10 = f32[128,4096]{1,0:T(8,128)} copy-done((f32[128,4096]{1,0:T(8,128)}, f32[128,4096]{1,0:T(8,128)S(1)}, u32[]{:S(2)}) %copy-start.10) | copy-done | bytes 2097176
  45.2 3.7 %collective-permute-done.8 = f32[2,4,4,32]{3,2,1,0:T(4,128)S(1)} collective-permute-done((f32[2,4,4,32]{3,2,1,0:T(4,128)S(1)}, f32[2,4,4,32]{3,2,1,0:T(4,128)S(1)}, u32[]{:S(2)}, u32[]{:S(2)}) %collective-permute-start.8) | collective-permute-done | bytes 4128 | tf_op jit(solution)/shard_map/ppermute | solution.py:216
  49.5 4.2 %collective-permute-done.9 = f32[2,4,4,32]{3,2,1,0:T(4,128)S(1)} collective-permute-done((f32[2,4,4,32]{3,2,1,0:T(4,128)S(1)}, f32[2,4,4,32]{3,2,1,0:T(4,128)S(1)}, u32[]{:S(2)}, u32[]{:S(2)}) %collective-permute-start.9) | collective-permute-done | bytes 4128 | tf_op jit(solution)/shard_map/ppermute | solution.py:216
  54.9 2.6 %collective-permute-done.10 = f32[2,4,4,32]{3,2,1,0:T(4,128)S(1)} collective-permute-done((f32[2,4,4,32]{3,2,1,0:T(4,128)S(1)}, f32[2,4,4,32]{3,2,1,0:T(4,128)S(1)}, u32[]{:S(2)}, u32[]{:S(2)}) %collective-permute-start.10) | collective-permute-done | bytes 4128 | tf_op jit(solution)/shard_map/ppermute | solution.py:214
  58.1 3.2 %collective-permute-done.11 = f32[2,4,4,32]{3,2,1,0:T(4,128)S(1)} collective-permute-done((f32[2,4,4,32]{3,2,1,0:T(4,128)S(1)}, f32[2,4,4,32]{3,2,1,0:T(4,128)S(1)}, u32[]{:S(2)}, u32[]{:S(2)}) %collective-permute-start.11) | collective-permute-done | bytes 4128 | tf_op jit(solution)/shard_map/ppermute | solution.py:214
  61.3 1.6 %copy-done.2 = bf16[2048,512]{1,0:T(8,128)(2,1)S(1)} copy-done((bf16[2048,512]{1,0:T(8,128)(2,1)S(1)}, bf16[2048,512]{1,0:T(8,128)(2,1)}, u32[]{:S(2)}) %copy-start.2) | copy-done | bytes 2097176
  62.9 1.6 %copy-done.11 = f32[128,4096]{1,0:T(8,128)S(1)} copy-done((f32[128,4096]{1,0:T(8,128)S(1)}, f32[128,4096]{1,0:T(8,128)}, u32[]{:S(2)}) %copy-start.11) | copy-done | bytes 2097176
  64.5 0.9 %shard_map.99 = bf16[128,512]{1,0:T(8,128)(2,1)S(1)} custom-call(f32[128,4096]{1,0:T(8,128)S(1)} %copy-done.11, f32[2,16,32]{2,1,0:T(8,128)S(1)} %add_add_fusion.totals_ref, bf16[2048,512]{1,0:T(8,128)(2,1)S(1)} %copy-done.2, bf16[2048,512]{1,0:T(8,128)(2,1)S(1)} %shard_map.95.refs_2_.refs_4_.refs_1_), custom_call_target="tpu_custom_call" | custom-call | flops 536870912 | bytes 6426624 | tf_op jit(solution)/shard_map/pallas_call | solution.py:25
  66.9 1.4 %collective-permute-start.13 = (bf16[128,512]{1,0:T(8,128)(2,1)S(1)}, bf16[128,512]{1,0:T(8,128)(2,1)S(1)}, u32[]{:S(2)}, u32[]{:S(2)}) collective-permute-start(bf16[128,512]{1,0:T(8,128)(2,1)S(1)} %shard_map.100), channel_id=1, source_target_pairs={{0,16},{8,24},{16,0},{24,8},{1,17},{9,25},{17,1},{25,9},{2,18},{10... | collective-permute-start | bytes 393224 | tf_op jit(solution)/shard_map/ppermute | solution.py:214
  69.2 1.6 %collective-permute-start.14 = (bf16[128,512]{1,0:T(8,128)(2,1)S(1)}, bf16[128,512]{1,0:T(8,128)(2,1)S(1)}, u32[]{:S(2)}, u32[]{:S(2)}) collective-permute-start(bf16[128,512]{1,0:T(8,128)(2,1)S(1)} %shard_map.101), channel_id=1, source_target_pairs={{0,8},{8,0},{16,24},{24,16},{1,9},{9,1},{17,25},{25,17},{2,10},{10... | collective-permute-start | bytes 393224 | tf_op jit(solution)/shard_map/ppermute | solution.py:214
  71.2 1.6 %copy-done.3 = bf16[2048,512]{1,0:T(8,128)(2,1)S(1)} copy-done((bf16[2048,512]{1,0:T(8,128)(2,1)S(1)}, bf16[2048,512]{1,0:T(8,128)(2,1)}, u32[]{:S(2)}) %copy-start.3) | copy-done | bytes 2097176
  72.8 1.6 %copy-done.5 = f32[128,4096]{1,0:T(8,128)S(1)} copy-done((f32[128,4096]{1,0:T(8,128)S(1)}, f32[128,4096]{1,0:T(8,128)}, u32[]{:S(2)}) %copy-start.5) | copy-done | bytes 2097176
  75.5 1.5 %collective-permute-start.16 = (bf16[32,512]{1,0:T(8,128)(2,1)S(1)}, bf16[32,512]{1,0:T(8,128)(2,1)S(1)}, u32[]{:S(2)}, u32[]{:S(2)}) collective-permute-start(bf16[32,512]{1,0:T(8,128)(2,1)S(1)} %get-tuple-element.31), channel_id=1, source_target_pairs={{0,4},{1,5},{2,6},{3,7},{4,0},{5,1},{6,2},{7,3},{8,12},{9,13},{10,... | collective-permute-start | bytes 98312 | tf_op jit(solution)/shard_map/ppermute | solution.py:216
  76.9 2.9 %collective-permute-start.17 = (bf16[32,512]{1,0:T(8,128)(2,1)S(1)}, bf16[32,512]{1,0:T(8,128)(2,1)S(1)}, u32[]{:S(2)}, u32[]{:S(2)}) collective-permute-start(bf16[32,512]{1,0:T(8,128)(2,1)S(1)} %get-tuple-element.30), channel_id=1, source_target_pairs={{0,6},{1,7},{2,4},{3,5},{4,2},{5,3},{6,0},{7,1},{8,14},{9,15},{10,... | collective-permute-start | bytes 98312 | tf_op jit(solution)/shard_map/ppermute | solution.py:216
  80.4 2.2 %collective-permute-done.17.refs_3_ = bf16[32,512]{1,0:T(8,128)(2,1)S(1)} collective-permute-done((bf16[32,512]{1,0:T(8,128)(2,1)S(1)}, bf16[32,512]{1,0:T(8,128)(2,1)S(1)}, u32[]{:S(2)}, u32[]{:S(2)}) %collective-permute-start.17) | collective-permute-done | bytes 32800 | tf_op jit(solution)/shard_map/ppermute | solution.py:216
  (82 shorter events, 11.7 us)
Async XLA Ops:
  1.3 30.1 %collective-permute-start.3 = (bf16[2048,512]{1,0:T(8,128)(2,1)}, bf16[2048,512]{1,0:T(8,128)(2,1)S(1)}, u32[]{:S(2)}, u32[]{:S(2)}) collective-permute-start(bf16[2048,512]{1,0:T(8,128)(2,1)} %memory_ref.1), channel_id=1, source_target_pairs={{0,1},{1,0},{2,3},{3,2},{4,5},{5,4},{6,7},{7,6},{8,9},{9,8},{10,11... | collective-permute-start | bytes 6291464 | tf_op jit(solution)/shard_map/ppermute | solution.py:216
  3.3 5.2 %collective-permute-start = (bf16[32,640]{1,0:T(8,128)(2,1)S(1)}, bf16[32,640]{1,0:T(8,128)(2,1)S(1)}, u32[]{:S(2)}, u32[]{:S(2)}) collective-permute-start(bf16[32,640]{1,0:T(8,128)(2,1)S(1)} %get-tuple-element.15), channel_id=1, source_target_pairs={{0,2},{1,3},{2,0},{3,1},{4,6},{5,7},{6,4},{7,5},{8,10},{9,11},{10,... | collective-permute-start | bytes 122888 | tf_op jit(solution)/shard_map/ppermute | solution.py:216
  5.9 5.8 %collective-permute-start.1 = (bf16[32,640]{1,0:T(8,128)(2,1)S(1)}, bf16[32,640]{1,0:T(8,128)(2,1)S(1)}, u32[]{:S(2)}, u32[]{:S(2)}) collective-permute-start(bf16[32,640]{1,0:T(8,128)(2,1)S(1)} %get-tuple-element.15), channel_id=1, source_target_pairs={{0,4},{1,5},{2,6},{3,7},{4,0},{5,1},{6,2},{7,3},{8,12},{9,13},{10,... | collective-permute-start | bytes 122888 | tf_op jit(solution)/shard_map/ppermute | solution.py:216
  8.5 5.8 %collective-permute-start.2 = (bf16[32,640]{1,0:T(8,128)(2,1)S(1)}, bf16[32,640]{1,0:T(8,128)(2,1)S(1)}, u32[]{:S(2)}, u32[]{:S(2)}) collective-permute-start(bf16[32,640]{1,0:T(8,128)(2,1)S(1)} %get-tuple-element.15), channel_id=1, source_target_pairs={{0,6},{1,7},{2,4},{3,5},{4,2},{5,3},{6,0},{7,1},{8,14},{9,15},{10,... | collective-permute-start | bytes 122888 | tf_op jit(solution)/shard_map/ppermute | solution.py:216
  14.3 9.9 %collective-permute-start.5 = (bf16[128,640]{1,0:T(8,128)(2,1)S(1)}, bf16[128,640]{1,0:T(8,128)(2,1)S(1)}, u32[]{:S(2)}, u32[]{:S(2)}) collective-permute-start(bf16[128,640]{1,0:T(8,128)(2,1)S(1)} %get-tuple-element.34.refs_0_), channel_id=1, source_target_pairs={{0,8},{8,0},{16,24},{24,16},{1,9},{9,1},{17,25},{25,17},{2,10},{10... | collective-permute-start | bytes 491528 | tf_op jit(solution)/shard_map/ppermute | solution.py:214
  15.9 8.4 %collective-permute-start.6 = (bf16[128,640]{1,0:T(8,128)(2,1)S(1)}, bf16[128,640]{1,0:T(8,128)(2,1)S(1)}, u32[]{:S(2)}, u32[]{:S(2)}) collective-permute-start(bf16[128,640]{1,0:T(8,128)(2,1)S(1)} %get-tuple-element.34.refs_0_), channel_id=1, source_target_pairs={{0,16},{8,24},{16,0},{24,8},{1,17},{9,25},{17,1},{25,9},{2,18},{10... | collective-permute-start | bytes 491528 | tf_op jit(solution)/shard_map/ppermute | solution.py:214
  18.1 5.7 %collective-permute-start.4 = (s32[2048]{0:T(1024)S(1)}, s32[2048]{0:T(1024)S(1)}, u32[]{:S(2)}, u32[]{:S(2)}) collective-permute-start(s32[2048]{0:T(1024)S(1)} %get-tuple-element.29), channel_id=1, source_target_pairs={{0,1},{1,0},{2,3},{3,2},{4,5},{5,4},{6,7},{7,6},{8,9},{9,8},{10,11... | collective-permute-start | bytes 24584 | tf_op jit(solution)/shard_map/ppermute | solution.py:216
  18.9 1.6 %copy-start.12 = (bf16[2048,512]{1,0:T(8,128)(2,1)S(1)}, bf16[2048,512]{1,0:T(8,128)(2,1)}, u32[]{:S(2)}) copy-start(bf16[2048,512]{1,0:T(8,128)(2,1)} %memory_ref.1) | copy-start | bytes 6291460
  23.8 7.5 %collective-permute-start.7 = (bf16[128,640]{1,0:T(8,128)(2,1)S(1)}, bf16[128,640]{1,0:T(8,128)(2,1)S(1)}, u32[]{:S(2)}, u32[]{:S(2)}) collective-permute-start(bf16[128,640]{1,0:T(8,128)(2,1)S(1)} %get-tuple-element.34.refs_0_), channel_id=1, source_target_pairs={{0,24},{8,16},{16,8},{24,0},{1,25},{9,17},{17,9},{25,1},{2,26},{10... | collective-permute-start | bytes 491528 | tf_op jit(solution)/shard_map/ppermute | solution.py:214
  31.4 4.0 %copy-start.1 = (bf16[2048,512]{1,0:T(8,128)(2,1)S(1)}, bf16[2048,512]{1,0:T(8,128)(2,1)}, u32[]{:S(2)}) copy-start(bf16[2048,512]{1,0:T(8,128)(2,1)} %copy-done) | copy-start | bytes 6291460
  31.4 18.1 %collective-permute-start.18 = (bf16[32,640]{1,0:T(8,128)(2,1)S(1)}, bf16[32,640]{1,0:T(8,128)(2,1)S(1)}, u32[]{:S(2)}, u32[]{:S(2)}) collective-permute-start(bf16[32,640]{1,0:T(8,128)(2,1)S(1)} %constant_dynamic-slice_fusion), channel_id=1, source_target_pairs={{0,1},{1,0},{2,3},{3,2},{4,5},{5,4},{6,7},{7,6},{8,9},{9,8},{10,11... | collective-permute-start | bytes 122888 | tf_op jit(solution)/shard_map/ppermute | solution.py:216
  32.8 1.6 %copy-start.14 = (bf16[2048,512]{1,0:T(8,128)(2,1)S(1)}, bf16[2048,512]{1,0:T(8,128)(2,1)}, u32[]{:S(2)}) copy-start(bf16[2048,512]{1,0:T(8,128)(2,1)} %copy-done.13) | copy-start | bytes 6291460
  37.2 3.8 %copy-start.4 = (f32[128,4096]{1,0:T(8,128)}, f32[128,4096]{1,0:T(8,128)S(1)}, u32[]{:S(2)}) copy-start(f32[128,4096]{1,0:T(8,128)S(1)} %get-tuple-element.17.term_ref) | copy-start | bytes 6291460
  41.0 1.4 %copy-start.6 = (f32[128,4096]{1,0:T(8,128)}, f32[128,4096]{1,0:T(8,128)S(1)}, u32[]{:S(2)}) copy-start(f32[128,4096]{1,0:T(8,128)S(1)} %get-tuple-element.22.term_ref) | copy-start | bytes 6291460
  42.4 1.4 %copy-start.8 = (f32[128,4096]{1,0:T(8,128)}, f32[128,4096]{1,0:T(8,128)S(1)}, u32[]{:S(2)}) copy-start(f32[128,4096]{1,0:T(8,128)S(1)} %get-tuple-element.21.term_ref) | copy-start | bytes 6291460
  45.1 3.7 %collective-permute-start.8 = (f32[2,4,4,32]{3,2,1,0:T(4,128)S(1)}, f32[2,4,4,32]{3,2,1,0:T(4,128)S(1)}, u32[]{:S(2)}, u32[]{:S(2)}) collective-permute-start(f32[2,4,4,32]{3,2,1,0:T(4,128)S(1)} %bitcast.36), channel_id=1, source_target_pairs={{0,2},{1,3},{2,0},{3,1},{4,6},{5,7},{6,4},{7,5},{8,10},{9,11},{10,... | collective-permute-start | bytes 12296 | tf_op jit(solution)/shard_map/ppermute | solution.py:216
  48.9 4.7 %collective-permute-start.9 = (f32[2,4,4,32]{3,2,1,0:T(4,128)S(1)}, f32[2,4,4,32]{3,2,1,0:T(4,128)S(1)}, u32[]{:S(2)}, u32[]{:S(2)}) collective-permute-start(f32[2,4,4,32]{3,2,1,0:T(4,128)S(1)} %add.83), channel_id=1, source_target_pairs={{0,4},{1,5},{2,6},{3,7},{4,0},{5,1},{6,2},{7,3},{8,12},{9,13},{10,... | collective-permute-start | bytes 12296 | tf_op jit(solution)/shard_map/ppermute | solution.py:216
  53.7 3.8 %collective-permute-start.10 = (f32[2,4,4,32]{3,2,1,0:T(4,128)S(1)}, f32[2,4,4,32]{3,2,1,0:T(4,128)S(1)}, u32[]{:S(2)}, u32[]{:S(2)}) collective-permute-start(f32[2,4,4,32]{3,2,1,0:T(4,128)S(1)} %add.85), channel_id=1, source_target_pairs={{0,8},{8,0},{16,24},{24,16},{1,9},{9,1},{17,25},{25,17},{2,10},{10... | collective-permute-start | bytes 12296 | tf_op jit(solution)/shard_map/ppermute | solution.py:214
  57.5 3.8 %collective-permute-start.11 = (f32[2,4,4,32]{3,2,1,0:T(4,128)S(1)}, f32[2,4,4,32]{3,2,1,0:T(4,128)S(1)}, u32[]{:S(2)}, u32[]{:S(2)}) collective-permute-start(f32[2,4,4,32]{3,2,1,0:T(4,128)S(1)} %add.87), channel_id=1, source_target_pairs={{0,16},{8,24},{16,0},{24,8},{1,17},{9,25},{17,1},{25,9},{2,18},{10... | collective-permute-start | bytes 12296 | tf_op jit(solution)/shard_map/ppermute | solution.py:214
  61.3 1.6 %copy-start.2 = (bf16[2048,512]{1,0:T(8,128)(2,1)S(1)}, bf16[2048,512]{1,0:T(8,128)(2,1)}, u32[]{:S(2)}) copy-start(bf16[2048,512]{1,0:T(8,128)(2,1)} %copy-done) | copy-start | bytes 6291460
  62.9 1.6 %copy-start.11 = (f32[128,4096]{1,0:T(8,128)S(1)}, f32[128,4096]{1,0:T(8,128)}, u32[]{:S(2)}) copy-start(f32[128,4096]{1,0:T(8,128)} %copy-done.10) | copy-start | bytes 6291460
  64.5 1.6 %copy-start.9 = (f32[128,4096]{1,0:T(8,128)S(1)}, f32[128,4096]{1,0:T(8,128)}, u32[]{:S(2)}) copy-start(f32[128,4096]{1,0:T(8,128)} %copy-done.8) | copy-start | bytes 6291460
  65.3 9.9 %collective-permute-start.12 = (bf16[128,512]{1,0:T(8,128)(2,1)S(1)}, bf16[128,512]{1,0:T(8,128)(2,1)S(1)}, u32[]{:S(2)}, u32[]{:S(2)}) collective-permute-start(bf16[128,512]{1,0:T(8,128)(2,1)S(1)} %shard_map.99), channel_id=1, source_target_pairs={{0,24},{8,16},{16,8},{24,0},{1,25},{9,17},{17,9},{25,1},{2,26},{10... | collective-permute-start | bytes 393224 | tf_op jit(solution)/shard_map/ppermute | solution.py:214
  66.1 2.3 %copy-start.7 = (f32[128,4096]{1,0:T(8,128)S(1)}, f32[128,4096]{1,0:T(8,128)}, u32[]{:S(2)}) copy-start(f32[128,4096]{1,0:T(8,128)} %copy-done.6) | copy-start | bytes 6291460
  66.9 8.3 %collective-permute-start.13 = (bf16[128,512]{1,0:T(8,128)(2,1)S(1)}, bf16[128,512]{1,0:T(8,128)(2,1)S(1)}, u32[]{:S(2)}, u32[]{:S(2)}) collective-permute-start(bf16[128,512]{1,0:T(8,128)(2,1)S(1)} %shard_map.100), channel_id=1, source_target_pairs={{0,16},{8,24},{16,0},{24,8},{1,17},{9,25},{17,1},{25,9},{2,18},{10... | collective-permute-start | bytes 393224 | tf_op jit(solution)/shard_map/ppermute | solution.py:214
  69.2 6.1 %collective-permute-start.14 = (bf16[128,512]{1,0:T(8,128)(2,1)S(1)}, bf16[128,512]{1,0:T(8,128)(2,1)S(1)}, u32[]{:S(2)}, u32[]{:S(2)}) collective-permute-start(bf16[128,512]{1,0:T(8,128)(2,1)S(1)} %shard_map.101), channel_id=1, source_target_pairs={{0,8},{8,0},{16,24},{24,16},{1,9},{9,1},{17,25},{25,17},{2,10},{10... | collective-permute-start | bytes 393224 | tf_op jit(solution)/shard_map/ppermute | solution.py:214
  71.2 4.0 %copy-start.17 = (s32[2048]{0:T(1024)}, s32[2048]{0:T(1024)S(1)}, u32[]{:S(2)}) copy-start(s32[2048]{0:T(1024)S(1)} %dynamic_update_slice.7) | copy-start | bytes 24580
  71.2 1.6 %copy-start.3 = (bf16[2048,512]{1,0:T(8,128)(2,1)S(1)}, bf16[2048,512]{1,0:T(8,128)(2,1)}, u32[]{:S(2)}) copy-start(bf16[2048,512]{1,0:T(8,128)(2,1)} %copy-done) | copy-start | bytes 6291460
  72.8 1.6 %copy-start.5 = (f32[128,4096]{1,0:T(8,128)S(1)}, f32[128,4096]{1,0:T(8,128)}, u32[]{:S(2)}) copy-start(f32[128,4096]{1,0:T(8,128)} %copy-done.4) | copy-start | bytes 6291460
  75.4 5.0 %collective-permute-start.15 = (bf16[32,512]{1,0:T(8,128)(2,1)S(1)}, bf16[32,512]{1,0:T(8,128)(2,1)S(1)}, u32[]{:S(2)}, u32[]{:S(2)}) collective-permute-start(bf16[32,512]{1,0:T(8,128)(2,1)S(1)} %get-tuple-element.32), channel_id=1, source_target_pairs={{0,2},{1,3},{2,0},{3,1},{4,6},{5,7},{6,4},{7,5},{8,10},{9,11},{10,... | collective-permute-start | bytes 98312 | tf_op jit(solution)/shard_map/ppermute | solution.py:216
  75.5 4.9 %collective-permute-start.16 = (bf16[32,512]{1,0:T(8,128)(2,1)S(1)}, bf16[32,512]{1,0:T(8,128)(2,1)S(1)}, u32[]{:S(2)}, u32[]{:S(2)}) collective-permute-start(bf16[32,512]{1,0:T(8,128)(2,1)S(1)} %get-tuple-element.31), channel_id=1, source_target_pairs={{0,4},{1,5},{2,6},{3,7},{4,0},{5,1},{6,2},{7,3},{8,12},{9,13},{10,... | collective-permute-start | bytes 98312 | tf_op jit(solution)/shard_map/ppermute | solution.py:216
  76.9 5.7 %collective-permute-start.17 = (bf16[32,512]{1,0:T(8,128)(2,1)S(1)}, bf16[32,512]{1,0:T(8,128)(2,1)S(1)}, u32[]{:S(2)}, u32[]{:S(2)}) collective-permute-start(bf16[32,512]{1,0:T(8,128)(2,1)S(1)} %get-tuple-element.30), channel_id=1, source_target_pairs={{0,6},{1,7},{2,4},{3,5},{4,2},{5,3},{6,0},{7,1},{8,14},{9,15},{10,... | collective-permute-start | bytes 98312 | tf_op jit(solution)/shard_map/ppermute | solution.py:216
  (5 other events, 5.4 us)

commit v3 on v2

v3 whole, which is shorter than its diff:
```python
import functools
import math

import jax
import jax.numpy as jnp
from jax import lax
from jax.experimental import pallas as pl
from jax.experimental.pallas import tpu as pltpu
from jax.sharding import PartitionSpec as P

pos_scale = 2.0
neg_scale = 50.0
margin = 0.5
lanes = 128
log2e = math.log2(math.e)
vmem_bytes = 20 * 1024 * 1024
vmem_most = 56 * 1024 * 1024
f32 = jnp.float32
bf16 = jnp.bfloat16


def call(body, outs, *args, flops=0, limit=vmem_bytes, **kw):
    moved = sum(a.size * a.dtype.itemsize for a in args)
    moved += sum(math.prod(o.shape) * o.dtype.itemsize for o in outs)
    return pl.pallas_call(
        body,
        out_shape=outs,
        compiler_params=pltpu.CompilerParams(vmem_limit_bytes=limit),
        cost_estimate=pl.CostEstimate(flops=flops, bytes_accessed=moved, transcendentals=0),
        **kw,
    )(*args)


def shaped(shape, dtype):
    return jax.ShapeDtypeStruct(shape, dtype)


def in_vmem(value):
    return pltpu.with_memory_space_constraint(value, pltpu.VMEM)


def prepare_kernel(rows_ref, labels_ref, stored_ref, keep_ref, packed_ref, unit_ref, radius_ref, slot_ref, copy_ref):
    stored = stored_ref[...]
    slot_ref[...] = jnp.where(keep_ref[...] > 0, stored, -1)
    copy_ref[...] = stored
    rows = rows_ref[...].astype(f32)
    count, width = rows.shape
    radius = jnp.sqrt(jnp.sum(rows * rows, axis=1, keepdims=True) + 1e-06)
    unit = rows / radius
    unit_ref[...] = unit
    radius_ref[...] = jnp.broadcast_to(radius, radius_ref.shape)
    packed_ref[:, :width] = unit.astype(bf16)
    column = to_column(labels_ref[...].astype(f32))
    high = jnp.floor(column * (1.0 / 256.0))
    low = column - high * 256.0
    lane = lax.broadcasted_iota(jnp.int32, (count, lanes), 1)
    digits = jnp.where(lane == 0, high, jnp.where(lane == 1, low, 0.0))
    packed_ref[:, width:] = digits.astype(bf16)


def diagonal(count):
    across = lax.broadcasted_iota(jnp.int32, (count, count), 1)
    down = lax.broadcasted_iota(jnp.int32, (count, count), 0)
    return across == down


def to_column(row):
    count = row.shape[1]
    spread = jnp.broadcast_to(row, (count, count))
    return jnp.sum(jnp.where(diagonal(count), spread, 0.0), axis=1, keepdims=True)


def keys_kernel(memory_ref, keys_ref, *copy_refs):
    stored = memory_ref[...]
    rows = stored.astype(f32)
    radius = jnp.sqrt(jnp.sum(rows * rows, axis=1, keepdims=True) + 1e-06)
    keys_ref[...] = (rows / radius).astype(bf16)
    for copy_ref in copy_refs:
        copy_ref[...] = stored


def keys_of(memory, copied):
    slots, width = memory.shape
    block = math.gcd(512, slots)
    spec = pl.BlockSpec((block, width), lambda i: (i, 0))
    return call(
        keys_kernel,
        [shaped((slots, width), bf16)] * (2 if copied else 1),
        memory,
        grid=(slots // block,),
        in_specs=[spec],
        out_specs=[spec] * (2 if copied else 1),
    )


def pack_sums(values):
    rows = values[0].shape[0]
    lane = lax.broadcasted_iota(jnp.int32, (rows, lanes), 1)
    packed = jnp.zeros((rows, lanes), f32)
    for at, value in enumerate(values):
        high = value.astype(bf16).astype(f32)
        packed = jnp.where(lane == 2 * at, high, packed)
        packed = jnp.where(lane == 2 * at + 1, value - high, packed)
    return packed


def unpack_sums(packed):
    lane = lax.broadcasted_iota(jnp.int32, packed.shape, 1)
    return [
        jnp.sum(jnp.where((lane >= 2 * at) & (lane < 2 * at + 2), packed, 0.0), axis=1, keepdims=True)
        for at in range(4)
    ]


def block_kernel(sides, chunk, rows_ref, *refs):
    keys_refs, label_refs = refs[:sides], refs[sides : 2 * sides]
    out_ref, weight_ref = refs[2 * sides :]
    slots, width = keys_refs[0].shape
    size = rows_ref.shape[0]
    anchors = rows_ref[:, :width]
    digits = rows_ref[:, width:].astype(f32)
    lane = lax.broadcasted_iota(jnp.int32, digits.shape, 1)
    digit = jnp.where(lane == 0, 256.0, jnp.where(lane == 1, 1.0, 0.0))
    labels = jnp.sum(digits * digit, axis=1, keepdims=True)
    pos_sum = jnp.zeros((size, 1), f32)
    neg_sum = jnp.zeros((size, 1), f32)
    for side in range(sides):
        slot_labels = label_refs[side][...].astype(f32)
        neg_shift = jnp.where(slot_labels < 0.0, -1e30, -neg_scale * margin * log2e)
        for start in range(0, slots, chunk):
            part = slice(start, start + chunk)
            scores = lax.dot_general(
                anchors, keys_refs[side][part, :], (((1,), (1,)), ((), ())), preferred_element_type=f32
            )
            same = labels == slot_labels[:, part]
            slope = jnp.where(same, -pos_scale * log2e, neg_scale * log2e)
            shift = jnp.where(same, pos_scale * margin * log2e, neg_shift[:, part])
            term = jnp.exp2(scores * slope + shift)
            pos = jnp.where(same, term, 0.0)
            neg = jnp.where(same, 0.0, term)
            pos_sum += jnp.sum(pos, axis=1, keepdims=True)
            neg_sum += jnp.sum(neg, axis=1, keepdims=True)
            to = slice(side * slots + start, side * slots + start + chunk)
            weight_ref[:size, to] = neg.astype(bf16)
            weight_ref[size:, to] = pos.astype(bf16)
    total = None
    for side in range(sides):
        part = weight_ref[:, side * slots : (side + 1) * slots]
        term = jnp.dot(part, keys_refs[side][...], preferred_element_type=f32)
        total = term if total is None else total + term
    floats = anchors.astype(f32)
    sums = [pos_sum, neg_sum]
    for which in range(2):
        value = total[which * size : (which + 1) * size, :]
        along = jnp.sum(value * floats, axis=1, keepdims=True)
        out_ref[:, which * width : (which + 1) * width] = (value - along * floats).astype(out_ref.dtype)
        sums.append(along)
    out_ref[:, 2 * width :] = pack_sums(sums).astype(out_ref.dtype)


def block_sums(rows, keys, labels, dtype):
    slots, width = keys[0].shape
    size = rows.shape[0]
    return call(
        functools.partial(block_kernel, len(keys), math.gcd(512, slots)),
        [shaped((size, 2 * width + lanes), dtype)],
        rows, *[in_vmem(k) for k in keys], *labels,
        flops=6 * size * slots * len(keys) * width,
        scratch_shapes=[pltpu.VMEM((2 * size, slots * len(keys)), bf16)],
    )[0]


def add_kernel(arrived, *refs):
    in_refs, out_refs = refs[: 1 + arrived], refs[1 + arrived :]
    rows, columns = out_refs[0].shape
    for block, out_ref in enumerate(out_refs):
        part = slice(block * rows, (block + 1) * rows)
        total = in_refs[0][part, :]
        for ref in in_refs[1:]:
            total = total + ref[part, :].astype(f32)
        out_ref[:, : columns - lanes] = total[:, : columns - lanes].astype(out_ref.dtype)
        sums = pack_sums(unpack_sums(total[:, columns - lanes :]))
        out_ref[:, columns - lanes :] = sums.astype(out_ref.dtype)


def add(held, arrived, blocks):
    rows, columns = held.shape
    outs = [shaped((rows // blocks, columns), f32 if b == 0 else bf16) for b in range(blocks)]
    return call(functools.partial(add_kernel, len(arrived)), outs, held, *arrived)


def finish_kernel(arrived, *refs):
    held_ref, arrived_refs = refs[0], refs[1 : 1 + arrived]
    unit_ref, radius_ref, grad_ref, loss_ref = refs[1 + arrived :]
    count, width = unit_ref.shape
    total = held_ref[...]
    for ref in arrived_refs:
        total = total + ref[...].astype(f32)
    pos, neg, push_along, pull_along = unpack_sums(total[:, 2 * width :])
    unit = unit_ref[...]
    anchors = unit.astype(bf16).astype(f32)
    push = total[:, :width] + push_along * anchors
    pull = total[:, width : 2 * width] + pull_along * anchors
    grad_unit = push / (1.0 + neg) - pull / (1.0 + pos)
    along = jnp.sum(unit * grad_unit, axis=1, keepdims=True)
    grad_ref[...] = (grad_unit - unit * along) / radius_ref[:, :1]
    loss = jnp.log(1.0 + pos) / pos_scale + jnp.log(1.0 + neg) / neg_scale
    spread = jnp.broadcast_to(loss, (count, count))
    loss_ref[...] = jnp.sum(jnp.where(diagonal(count), spread, 0.0), axis=0, keepdims=True)


def per_device(batch_rows, batch_labels, memory, memory_labels, keep_bits, step_index):
    groups = lax.axis_size("grp")
    members = lax.axis_size("dev")
    cores = 2 if members % 2 == 0 else 1
    line = members // cores
    devices_all = groups * members
    my_grp = lax.axis_index("grp")
    my_dev = lax.axis_index("dev")
    count, width = batch_rows.shape
    slots = memory.shape[0]

    def exchange(value, axis, step):
        if axis == "grp":
            return lax.ppermute(value, "grp", [(i, i ^ step) for i in range(groups)])
        jump = step * cores if axis == "line" else step
        return lax.ppermute(value, "dev", [(i, i ^ jump) for i in range(members)])

    folded = (slots // lanes, lanes)
    packed, unit, radius, slot_labels, copied_labels = call(
        prepare_kernel,
        [
            shaped((count, width + lanes), bf16),
            shaped((count, width), f32),
            shaped((count, lanes), f32),
            shaped(folded, jnp.int32),
            shaped(folded, jnp.int32),
        ],
        batch_rows, batch_labels.reshape(1, count), memory_labels.reshape(folded), keep_bits.reshape(folded),
        limit=vmem_most,
    )

    labels = [slot_labels] + [exchange(slot_labels, "core", s) for s in range(1, cores)]
    labels = [value.reshape(1, slots) for value in labels]
    memories = [memory] + [exchange(memory, "core", s) for s in range(1, cores)]
    own_keys, copied = keys_of(memory, True)
    keys = [own_keys] + [keys_of(value, False)[0] for value in memories[1:]]

    part = jnp.concatenate([packed] + [exchange(packed, "line", s) for s in range(1, line)])
    blocks = [part] + [exchange(part, "grp", s) for s in range(1, groups)]

    arrived = []
    for s in range(groups - 1, 0, -1):
        sums = block_sums(blocks[s], keys, labels, bf16)
        arrived.append(exchange(sums, "grp", s))
    if groups > 1:
        part, sums = lax.optimization_barrier((part, sums))
    held = block_sums(part, keys, labels, f32)
    held, *parts = add(held, arrived, line)
    arrived = [exchange(value, "line", s) for s, value in enumerate(parts, 1)]
    grad_batch, loss = call(
        functools.partial(finish_kernel, len(arrived)),
        [shaped((count, width), f32), shaped((1, count), f32)],
        held, *arrived, unit, radius,
    )

    step_value = step_index[0]
    first_slot = (step_value % (slots // count)) * count
    crossing = (step_value % cores) if cores > 1 else 0
    target = my_grp * members + (my_dev ^ crossing)
    source = (target - step_value) % devices_all
    source_grp, source_line = source // members, (source % members) // cores
    at = ((my_grp ^ source_grp) * line + ((my_dev // cores) ^ source_line)) * count
    moved = lax.dynamic_slice_in_dim(jnp.concatenate(blocks), at, count, 0)
    if cores > 1:
        moved = jnp.where(crossing > 0, exchange(moved, "core", 1), moved)
    digits = moved[:, width : width + 2].astype(jnp.int32)
    moved_labels = digits[:, 0] * 256 + digits[:, 1]
    new_memory = lax.dynamic_update_slice_in_dim(copied, moved[:, :width], first_slot, 0)
    new_labels = lax.dynamic_update_slice_in_dim(copied_labels.reshape(slots), moved_labels, first_slot, 0)
    return (grad_batch, loss.reshape(count), new_memory, new_labels)


def solution(mesh):
    placed = (
        P(("grp", "dev"), None),
        P(("grp", "dev")),
        P(("grp", "dev"), None),
        P(("grp", "dev")),
        P(("grp", "dev")),
        P(),
    )
    return jax.shard_map(
        per_device,
        mesh=mesh,
        in_specs=placed,
        out_specs=(
            P(("grp", "dev"), None),
            P(("grp", "dev")),
            P(("grp", "dev"), None),
            P(("grp", "dev")),
        ),
        check_vma=False,
    )
```

time: 83.9 us -> 68 us (0.81)
  local copies, waits for them, and re-layouts: 19.7 us -> 6.57 us
  waiting for transfers between devices: 28.7 us -> 24.3 us
  Pallas kernels: 12.8 us -> 17 us
  other arithmetic: 1.54 us -> 0.2 us
  starting transfers between devices: 18.9 us -> 18 us
    unnamed x43 -> x18, local copies, waits for them, and re-layouts: 18.7 us -> 4.46 us
    ppermute x11 -> x9, waiting for transfers between devices: 15.9 us -> 8.22 us  [exchange(): return lax.ppermute(value, 'dev', [(i, i ^ jump) for i in range(members)])]
    pallas_call x10 -> x9, Pallas kernels: 12.8 us -> 17 us  [call(): pl.pallas_call(body, out_shape=outs, compiler_params=pltpu.CompilerParams...]
    ppermute x8 -> x6, waiting for transfers between devices: 12.8 us -> 16.1 us  [exchange(): return lax.ppermute(value, 'grp', [(i, i ^ step) for i in range(groups)])]
    dynamic_update_slice x1, local copies, waits for them, and re-layouts: 0.28 us -> 1.45 us  [per_device(): lax.dynamic_update_slice_in_dim(copied_labels.reshape(slots), moved_label...]
    ppermute x8 -> x6, starting transfers between devices: 8.23 us -> 7.3 us  [exchange(): return lax.ppermute(value, 'grp', [(i, i ^ step) for i in range(groups)])]
    ppermute x11 -> x9, starting transfers between devices: 10.7 us -> 10.7 us  [exchange(): return lax.ppermute(value, 'dev', [(i, i ^ jump) for i in range(members)])]
  transfers between devices with their start and end apart: 19 -> 15, of which waited for: 8 -> 7; matrix products, arithmetic and copies ran while one was open for 3% -> 5% of each run, Pallas kernels for 13% -> 19%
where the time goes in v3:
time: 68 us; the launch traced here: 67.7 us
  waiting for transfers between devices  24.3 us (36%)
  starting transfers between devices  18 us (26%)
  Pallas kernels  17 us (25%)
  local copies, waits for them, and re-layouts  6.57 us (10%)
  between operations  1.52 us (2%)
    pallas_call x9, Pallas kernels, call(): pl.pallas_call(body, out_shape=outs, compiler_params=pltpu.CompilerParams...  17 us
    ppermute x6, waiting for transfers between devices, exchange(): return lax.ppermute(value, 'grp', [(i, i ^ step) for i in range(groups)])  16.1 us
    ppermute x9, starting transfers between devices, exchange(): return lax.ppermute(value, 'dev', [(i, i ^ jump) for i in range(members)])  10.7 us
    ppermute x9, waiting for transfers between devices, exchange(): return lax.ppermute(value, 'dev', [(i, i ^ jump) for i in range(members)])  8.22 us
    ppermute x6, starting transfers between devices, exchange(): return lax.ppermute(value, 'grp', [(i, i ^ step) for i in range(groups)])  7.3 us
    unnamed x18, local copies, waits for them, and re-layouts  4.46 us
    dynamic_update_slice x1, local copies, waits for them, and re-layouts, per_device(): lax.dynamic_update_slice_in_dim(copied_labels.reshape(slots), moved_label...  1.45 us
  transfers between devices with their start and end apart: 15, of which 7 were waited for; matrix products, arithmetic and copies ran while one was open for 5% of the time, Pallas kernels for 19%

profile of v3, /device:TPU:0, one launch (start us, length us, event | category | flops | bytes accessed | tf_op | source)
XLA Modules:
  0.0 67.7 jit_solution(976969299165550674)
XLA Ops:
  0.6 0.5 collective-permute-start.4
  1.1 1.5 %shard_map.93 = (bf16[32,640]{1,0:T(8,128)(2,1)}, f32[32,512]{1,0:T(8,128)}, f32[32,128]{1,0:T(8,128)}, s32[16,128]{1,0:T(8,128)}, s32[16,128]{1,0:T(8,128)}) custom-call(bf16[32,512]{1,0:T(8,128)(2,1)} %rows_ref.1, s32[1,32]{1,0:T(1,128)} %bitcast.22, s32[16,128]{1,0:T(8,128)} %bitcast.20, s32[16,128]{1,0:T(8,128)} %bitcast.21), custom_call_target="tpu_custom_call" | custom-call | bytes 188544 | tf_op jit(solution)/shard_map/pallas_call | solution.py:25
  2.7 2.6 %collective-permute-start = (bf16[32,640]{1,0:T(8,128)(2,1)}, bf16[32,640]{1,0:T(8,128)(2,1)S(1)}, u32[]{:S(2)}, u32[]{:S(2)}) collective-permute-start(bf16[32,640]{1,0:T(8,128)(2,1)} %get-tuple-element.18), channel_id=1, source_target_pairs={{0,2},{1,3},{2,0},{3,1},{4,6},{5,7},{6,4},{7,5},{8,10},{9,11},{10,... | collective-permute-start | bytes 122888 | tf_op jit(solution)/shard_map/ppermute | solution.py:227
  5.3 2.6 %collective-permute-start.1 = (bf16[32,640]{1,0:T(8,128)(2,1)}, bf16[32,640]{1,0:T(8,128)(2,1)S(1)}, u32[]{:S(2)}, u32[]{:S(2)}) collective-permute-start(bf16[32,640]{1,0:T(8,128)(2,1)} %get-tuple-element.18), channel_id=1, source_target_pairs={{0,4},{1,5},{2,6},{3,7},{4,0},{5,1},{6,2},{7,3},{8,12},{9,13},{10,... | collective-permute-start | bytes 122888 | tf_op jit(solution)/shard_map/ppermute | solution.py:227
  7.9 0.9 %constant_dynamic-update-slice_fusion.10 = (bf16[512,640]{1,0:T(8,128)(2,1)S(1)}, bf16[128,640]{1,0:T(8,128)(2,1)S(1)}) fusion(bf16[32,640]{1,0:T(8,128)(2,1)} %get-tuple-element.18), kind=kLoop, calls=%fused_computation.12 | loop fusion | bytes 122880
  8.7 2.6 %collective-permute-done.1 = bf16[32,640]{1,0:T(8,128)(2,1)S(1)} collective-permute-done((bf16[32,640]{1,0:T(8,128)(2,1)}, bf16[32,640]{1,0:T(8,128)(2,1)S(1)}, u32[]{:S(2)}, u32[]{:S(2)}) %collective-permute-start.1) | collective-permute-done | bytes 40992 | tf_op jit(solution)/shard_map/ppermute | solution.py:227
  11.3 2.6 %collective-permute-done.2 = bf16[32,640]{1,0:T(8,128)(2,1)S(1)} collective-permute-done((bf16[32,640]{1,0:T(8,128)(2,1)}, bf16[32,640]{1,0:T(8,128)(2,1)S(1)}, u32[]{:S(2)}, u32[]{:S(2)}) %collective-permute-start.2) | collective-permute-done | bytes 40992 | tf_op jit(solution)/shard_map/ppermute | solution.py:227
  13.9 1.6 %collective-permute-start.3 = (bf16[128,640]{1,0:T(8,128)(2,1)S(1)}, bf16[128,640]{1,0:T(8,128)(2,1)S(1)}, u32[]{:S(2)}, u32[]{:S(2)}) collective-permute-start(bf16[128,640]{1,0:T(8,128)(2,1)S(1)} %get-tuple-element.21.rows_ref), channel_id=1, source_target_pairs={{0,8},{8,0},{16,24},{24,16},{1,9},{9,1},{17,25},{25,17},{2,10},{10... | collective-permute-start | bytes 491528 | tf_op jit(solution)/shard_map/ppermute | solution.py:225
  15.4 1.5 %collective-permute-start.8 = (bf16[128,640]{1,0:T(8,128)(2,1)S(1)}, bf16[128,640]{1,0:T(8,128)(2,1)S(1)}, u32[]{:S(2)}, u32[]{:S(2)}) collective-permute-start(bf16[128,640]{1,0:T(8,128)(2,1)S(1)} %get-tuple-element.21.rows_ref), channel_id=1, source_target_pairs={{0,16},{8,24},{16,0},{24,8},{1,17},{9,25},{17,1},{25,9},{2,18},{10... | collective-permute-start | bytes 491528 | tf_op jit(solution)/shard_map/ppermute | solution.py:225
  17.7 0.5 collective-permute-start.6
  18.3 1.7 %collective-permute-done.3.rows_ref = bf16[128,640]{1,0:T(8,128)(2,1)S(1)} collective-permute-done((bf16[128,640]{1,0:T(8,128)(2,1)S(1)}, bf16[128,640]{1,0:T(8,128)(2,1)S(1)}, u32[]{:S(2)}, u32[]{:S(2)}) %collective-permute-start.3) | collective-permute-done | bytes 163872 | tf_op jit(solution)/shard_map/ppermute | solution.py:225
  20.0 4.2 %collective-permute-done.8.rows_ref = bf16[128,640]{1,0:T(8,128)(2,1)S(1)} collective-permute-done((bf16[128,640]{1,0:T(8,128)(2,1)S(1)}, bf16[128,640]{1,0:T(8,128)(2,1)S(1)}, u32[]{:S(2)}, u32[]{:S(2)}) %collective-permute-start.8) | collective-permute-done | bytes 163872 | tf_op jit(solution)/shard_map/ppermute | solution.py:225
  24.9 1.6 %copy-done = bf16[2048,512]{1,0:T(8,128)(2,1)S(1)} copy-done((bf16[2048,512]{1,0:T(8,128)(2,1)S(1)}, bf16[2048,512]{1,0:T(8,128)(2,1)}, u32[]{:S(2)}) %copy-start) | copy-done | bytes 2097176
  26.5 2.0 %shard_map.94 = (bf16[2048,512]{1,0:T(8,128)(2,1)S(1)}, bf16[2048,512]{1,0:T(8,128)(2,1)}) custom-call(bf16[2048,512]{1,0:T(8,128)(2,1)S(1)} %copy-done), custom_call_target="tpu_custom_call" | custom-call | bytes 6291456 | tf_op jit(solution)/shard_map/pallas_call | solution.py:25
  28.5 1.3 %copy-done.3 = bf16[2048,512]{1,0:T(8,128)(2,1)} copy-done((bf16[2048,512]{1,0:T(8,128)(2,1)}, bf16[2048,512]{1,0:T(8,128)(2,1)S(1)}, u32[]{:S(2)}) %copy-start.3) | copy-done | bytes 2097176
  29.9 0.6 slice_dynamic-update-slice_fusion
  30.5 1.0 %shard_map.95.refs_1_ = bf16[2048,512]{1,0:T(8,128)(2,1)S(1)} custom-call(bf16[2048,512]{1,0:T(8,128)(2,1)S(1)} %collective-permute-done.4.memory_ref), custom_call_target="tpu_custom_call" | custom-call | bytes 4194304 | tf_op jit(solution)/shard_map/pallas_call | solution.py:25
  31.5 0.6 copy-done.4
  32.1 2.9 %shard_map.96 = bf16[128,1152]{1,0:T(8,128)(2,1)S(1)} custom-call(bf16[128,640]{1,0:T(8,128)(2,1)S(1)} %collective-permute-done.3.rows_ref, bf16[2048,512]{1,0:T(8,128)(2,1)S(1)} %copy-done.4, bf16[2048,512]{1,0:T(8,128)(2,1)S(1)} %shard_map.95.refs_1_, s32[1,2048]{1,0:T(1,128)S(1)} %bitcast.12, s32[1,2048]{1,0:T(1,128)S(1)} %bitcast.16), custom_call_target="tpu_custom_call" | custom-call | flops 1610612736 | bytes 4669440 | tf_op jit(solution)/shard_map/pallas_call | solution.py:25
  34.9 1.0 %collective-permute-start.10 = (bf16[128,1152]{1,0:T(8,128)(2,1)S(1)}, bf16[128,1152]{1,0:T(8,128)(2,1)S(1)}, u32[]{:S(2)}, u32[]{:S(2)}) collective-permute-start(bf16[128,1152]{1,0:T(8,128)(2,1)S(1)} %shard_map.96), channel_id=1, source_target_pairs={{0,8},{8,0},{16,24},{24,16},{1,9},{9,1},{17,25},{25,17},{2,10},{10... | collective-permute-start | bytes 884744 | tf_op jit(solution)/shard_map/ppermute | solution.py:225
  35.9 2.9 %shard_map.98 = bf16[128,1152]{1,0:T(8,128)(2,1)S(1)} custom-call(bf16[128,640]{1,0:T(8,128)(2,1)S(1)} %collective-permute-done.6.rows_ref, bf16[2048,512]{1,0:T(8,128)(2,1)S(1)} %copy-done.4, bf16[2048,512]{1,0:T(8,128)(2,1)S(1)} %shard_map.95.refs_1_, s32[1,2048]{1,0:T(1,128)S(1)} %bitcast.13, s32[1,2048]{1,0:T(1,128)S(1)} %bitcast.17), custom_call_target="tpu_custom_call" | custom-call | flops 1610612736 | bytes 4669440 | tf_op jit(solution)/shard_map/pallas_call | solution.py:25
  38.8 1.9 %collective-permute-start.7 = (bf16[128,1152]{1,0:T(8,128)(2,1)S(1)}, bf16[128,1152]{1,0:T(8,128)(2,1)S(1)}, u32[]{:S(2)}, u32[]{:S(2)}) collective-permute-start(bf16[128,1152]{1,0:T(8,128)(2,1)S(1)} %shard_map.98), channel_id=1, source_target_pairs={{0,24},{8,16},{16,8},{24,0},{1,25},{9,17},{17,9},{25,1},{2,26},{10... | collective-permute-start | bytes 884744 | tf_op jit(solution)/shard_map/ppermute | solution.py:225
  40.7 2.9 %shard_map.99 = bf16[128,1152]{1,0:T(8,128)(2,1)S(1)} custom-call(bf16[128,640]{1,0:T(8,128)(2,1)S(1)} %collective-permute-done.8.rows_ref, bf16[2048,512]{1,0:T(8,128)(2,1)S(1)} %copy-done.4, bf16[2048,512]{1,0:T(8,128)(2,1)S(1)} %shard_map.95.refs_1_, s32[1,2048]{1,0:T(1,128)S(1)} %bitcast.14, s32[1,2048]{1,0:T(1,128)S(1)} %bitcast.18), custom_call_target="tpu_custom_call" | custom-call | flops 1610612736 | bytes 4669440 | tf_op jit(solution)/shard_map/pallas_call | solution.py:25
  43.5 0.8 %collective-permute-start.9 = (bf16[128,1152]{1,0:T(8,128)(2,1)S(1)}, bf16[128,1152]{1,0:T(8,128)(2,1)S(1)}, u32[]{:S(2)}, u32[]{:S(2)}) collective-permute-start(bf16[128,1152]{1,0:T(8,128)(2,1)S(1)} %shard_map.99), channel_id=1, source_target_pairs={{0,16},{8,24},{16,0},{24,8},{1,17},{9,25},{17,1},{25,9},{2,18},{10... | collective-permute-start | bytes 884744 | tf_op jit(solution)/shard_map/ppermute | solution.py:225
  44.4 2.9 %shard_map.97.refs_0_ = f32[128,1152]{1,0:T(8,128)S(1)} custom-call(bf16[128,640]{1,0:T(8,128)(2,1)S(1)} %get-tuple-element.21.rows_ref, bf16[2048,512]{1,0:T(8,128)(2,1)S(1)} %copy-done.4, bf16[2048,512]{1,0:T(8,128)(2,1)S(1)} %shard_map.95.refs_1_, s32[1,2048]{1,0:T(1,128)S(1)} %bitcast.15, s32[1,2048]{1,0:T(1,128)S(1)} %bitcast.19), custom_call_target="tpu_custom_call" | custom-call | flops 1610612736 | bytes 4964352 | tf_op jit(solution)/shard_map/pallas_call | solution.py:25
  47.2 3.9 %collective-permute-done.7.refs_1_ = bf16[128,1152]{1,0:T(8,128)(2,1)S(1)} collective-permute-done((bf16[128,1152]{1,0:T(8,128)(2,1)S(1)}, bf16[128,1152]{1,0:T(8,128)(2,1)S(1)}, u32[]{:S(2)}, u32[]{:S(2)}) %collective-permute-start.7) | collective-permute-done | bytes 294944 | tf_op jit(solution)/shard_map/ppermute | solution.py:225
  51.1 6.2 %collective-permute-done.9.refs_2_ = bf16[128,1152]{1,0:T(8,128)(2,1)S(1)} collective-permute-done((bf16[128,1152]{1,0:T(8,128)(2,1)S(1)}, bf16[128,1152]{1,0:T(8,128)(2,1)S(1)}, u32[]{:S(2)}, u32[]{:S(2)}) %collective-permute-start.9) | collective-permute-done | bytes 294944 | tf_op jit(solution)/shard_map/ppermute | solution.py:225
  57.7 1.5 %collective-permute-start.12 = (bf16[32,1152]{1,0:T(8,128)(2,1)S(1)}, bf16[32,1152]{1,0:T(8,128)(2,1)S(1)}, u32[]{:S(2)}, u32[]{:S(2)}) collective-permute-start(bf16[32,1152]{1,0:T(8,128)(2,1)S(1)} %get-tuple-element.24), channel_id=1, source_target_pairs={{0,4},{1,5},{2,6},{3,7},{4,0},{5,1},{6,2},{7,3},{8,12},{9,13},{10,... | collective-permute-start | bytes 221192 | tf_op jit(solution)/shard_map/ppermute | solution.py:227
  59.1 2.9 %collective-permute-start.13 = (bf16[32,1152]{1,0:T(8,128)(2,1)S(1)}, bf16[32,1152]{1,0:T(8,128)(2,1)S(1)}, u32[]{:S(2)}, u32[]{:S(2)}) collective-permute-start(bf16[32,1152]{1,0:T(8,128)(2,1)S(1)} %get-tuple-element.25), channel_id=1, source_target_pairs={{0,6},{1,7},{2,4},{3,5},{4,2},{5,3},{6,0},{7,1},{8,14},{9,15},{10,... | collective-permute-start | bytes 221192 | tf_op jit(solution)/shard_map/ppermute | solution.py:227
  62.2 1.5 %dynamic_update_slice.7 = s32[2048]{0:T(1024)} dynamic-update-slice(s32[2048]{0:T(1024)} %bitcast.23, s32[32]{0:T(128)S(1)} %fusion, s32[]{:T(128)S(6)} %select_n.54) | dynamic-update-slice | bytes 260 | tf_op jit(solution)/shard_map/dynamic_update_slice | solution.py:280
  63.7 3.1 %collective-permute-done.12.refs_2_ = bf16[32,1152]{1,0:T(8,128)(2,1)S(1)} collective-permute-done((bf16[32,1152]{1,0:T(8,128)(2,1)S(1)}, bf16[32,1152]{1,0:T(8,128)(2,1)S(1)}, u32[]{:S(2)}, u32[]{:S(2)}) %collective-permute-start.12) | collective-permute-done | bytes 73760 | tf_op jit(solution)/shard_map/ppermute | solution.py:227
  66.8 0.9 %shard_map.101 = (f32[32,512]{1,0:T(8,128)}, f32[1,32]{1,0:T(1,128)}) custom-call(f32[32,1152]{1,0:T(8,128)S(1)} %get-tuple-element.22.refs_0_, bf16[32,1152]{1,0:T(8,128)(2,1)S(1)} %collective-permute-done.11.refs_1_, bf16[32,1152]{1,0:T(8,128)(2,1)S(1)} %collective-permute-done.12.refs_2_, bf16[32,1152]{1,0:T(8,128)(2,1)S(1)} %collective-permute-done.13.refs_3_, ...), custom_call_target="tpu_custom_call" | custom-call | bytes 516224 | tf_op jit(solution)/shard_map/pallas_call | solution.py:25
  (32 shorter events, 1.2 us)
Async XLA Ops:
  0.6 29.9 %collective-permute-start.4 = (bf16[2048,512]{1,0:T(8,128)(2,1)}, bf16[2048,512]{1,0:T(8,128)(2,1)S(1)}, u32[]{:S(2)}, u32[]{:S(2)}) collective-permute-start(bf16[2048,512]{1,0:T(8,128)(2,1)} %memory_ref.1), channel_id=1, source_target_pairs={{0,1},{1,0},{2,3},{3,2},{4,5},{5,4},{6,7},{7,6},{8,9},{9,8},{10,11... | collective-permute-start | bytes 6291464 | tf_op jit(solution)/shard_map/ppermute | solution.py:227
  2.7 6.0 %collective-permute-start = (bf16[32,640]{1,0:T(8,128)(2,1)}, bf16[32,640]{1,0:T(8,128)(2,1)S(1)}, u32[]{:S(2)}, u32[]{:S(2)}) collective-permute-start(bf16[32,640]{1,0:T(8,128)(2,1)} %get-tuple-element.18), channel_id=1, source_target_pairs={{0,2},{1,3},{2,0},{3,1},{4,6},{5,7},{6,4},{7,5},{8,10},{9,11},{10,... | collective-permute-start | bytes 122888 | tf_op jit(solution)/shard_map/ppermute | solution.py:227
  5.3 6.0 %collective-permute-start.1 = (bf16[32,640]{1,0:T(8,128)(2,1)}, bf16[32,640]{1,0:T(8,128)(2,1)S(1)}, u32[]{:S(2)}, u32[]{:S(2)}) collective-permute-start(bf16[32,640]{1,0:T(8,128)(2,1)} %get-tuple-element.18), channel_id=1, source_target_pairs={{0,4},{1,5},{2,6},{3,7},{4,0},{5,1},{6,2},{7,3},{8,12},{9,13},{10,... | collective-permute-start | bytes 122888 | tf_op jit(solution)/shard_map/ppermute | solution.py:227
  7.9 6.0 %collective-permute-start.2 = (bf16[32,640]{1,0:T(8,128)(2,1)}, bf16[32,640]{1,0:T(8,128)(2,1)S(1)}, u32[]{:S(2)}, u32[]{:S(2)}) collective-permute-start(bf16[32,640]{1,0:T(8,128)(2,1)} %get-tuple-element.18), channel_id=1, source_target_pairs={{0,6},{1,7},{2,4},{3,5},{4,2},{5,3},{6,0},{7,1},{8,14},{9,15},{10,... | collective-permute-start | bytes 122888 | tf_op jit(solution)/shard_map/ppermute | solution.py:227
  13.9 6.1 %collective-permute-start.3 = (bf16[128,640]{1,0:T(8,128)(2,1)S(1)}, bf16[128,640]{1,0:T(8,128)(2,1)S(1)}, u32[]{:S(2)}, u32[]{:S(2)}) collective-permute-start(bf16[128,640]{1,0:T(8,128)(2,1)S(1)} %get-tuple-element.21.rows_ref), channel_id=1, source_target_pairs={{0,8},{8,0},{16,24},{24,16},{1,9},{9,1},{17,25},{25,17},{2,10},{10... | collective-permute-start | bytes 491528 | tf_op jit(solution)/shard_map/ppermute | solution.py:225
  15.4 8.8 %collective-permute-start.8 = (bf16[128,640]{1,0:T(8,128)(2,1)S(1)}, bf16[128,640]{1,0:T(8,128)(2,1)S(1)}, u32[]{:S(2)}, u32[]{:S(2)}) collective-permute-start(bf16[128,640]{1,0:T(8,128)(2,1)S(1)} %get-tuple-element.21.rows_ref), channel_id=1, source_target_pairs={{0,16},{8,24},{16,0},{24,8},{1,17},{9,25},{17,1},{25,9},{2,18},{10... | collective-permute-start | bytes 491528 | tf_op jit(solution)/shard_map/ppermute | solution.py:225
  17.7 6.6 %collective-permute-start.6 = (bf16[128,640]{1,0:T(8,128)(2,1)S(1)}, bf16[128,640]{1,0:T(8,128)(2,1)S(1)}, u32[]{:S(2)}, u32[]{:S(2)}) collective-permute-start(bf16[128,640]{1,0:T(8,128)(2,1)S(1)} %get-tuple-element.21.rows_ref), channel_id=1, source_target_pairs={{0,24},{8,16},{16,8},{24,0},{1,25},{9,17},{17,9},{25,1},{2,26},{10... | collective-permute-start | bytes 491528 | tf_op jit(solution)/shard_map/ppermute | solution.py:225
  24.4 5.5 %collective-permute-start.14 = (bf16[32,640]{1,0:T(8,128)(2,1)S(1)}, bf16[32,640]{1,0:T(8,128)(2,1)S(1)}, u32[]{:S(2)}, u32[]{:S(2)}) collective-permute-start(bf16[32,640]{1,0:T(8,128)(2,1)S(1)} %constant_dynamic-slice_fusion), channel_id=1, source_target_pairs={{0,1},{1,0},{2,3},{3,2},{4,5},{5,4},{6,7},{7,6},{8,9},{9,8},{10,11... | collective-permute-start | bytes 122888 | tf_op jit(solution)/shard_map/ppermute | solution.py:227
  24.4 7.0 %collective-permute-start.5 = (s32[16,128]{1,0:T(8,128)}, s32[16,128]{1,0:T(8,128)S(1)}, u32[]{:S(2)}, u32[]{:S(2)}) collective-permute-start(s32[16,128]{1,0:T(8,128)} %get-tuple-element.20), channel_id=1, source_target_pairs={{0,1},{1,0},{2,3},{3,2},{4,5},{5,4},{6,7},{7,6},{8,9},{9,8},{10,11... | collective-permute-start | bytes 24584 | tf_op jit(solution)/shard_map/ppermute | solution.py:227
  24.9 1.6 %copy-start = (bf16[2048,512]{1,0:T(8,128)(2,1)S(1)}, bf16[2048,512]{1,0:T(8,128)(2,1)}, u32[]{:S(2)}) copy-start(bf16[2048,512]{1,0:T(8,128)(2,1)} %memory_ref.1) | copy-start | bytes 6291460
  28.5 1.3 %copy-start.3 = (bf16[2048,512]{1,0:T(8,128)(2,1)}, bf16[2048,512]{1,0:T(8,128)(2,1)S(1)}, u32[]{:S(2)}) copy-start(bf16[2048,512]{1,0:T(8,128)(2,1)S(1)} %get-tuple-element.19.refs_0_) | copy-start | bytes 6291460
  30.5 1.6 %copy-start.4 = (bf16[2048,512]{1,0:T(8,128)(2,1)S(1)}, bf16[2048,512]{1,0:T(8,128)(2,1)}, u32[]{:S(2)}) copy-start(bf16[2048,512]{1,0:T(8,128)(2,1)} %copy-done.3) | copy-start | bytes 6291460
  30.5 1.6 %copy-start.5 = (s32[16,128]{1,0:T(8,128)S(1)}, s32[16,128]{1,0:T(8,128)}, u32[]{:S(2)}) copy-start(s32[16,128]{1,0:T(8,128)} %get-tuple-element.20) | copy-start | bytes 24580
  34.9 12.3 %collective-permute-start.10 = (bf16[128,1152]{1,0:T(8,128)(2,1)S(1)}, bf16[128,1152]{1,0:T(8,128)(2,1)S(1)}, u32[]{:S(2)}, u32[]{:S(2)}) collective-permute-start(bf16[128,1152]{1,0:T(8,128)(2,1)S(1)} %shard_map.96), channel_id=1, source_target_pairs={{0,8},{8,0},{16,24},{24,16},{1,9},{9,1},{17,25},{25,17},{2,10},{10... | collective-permute-start | bytes 884744 | tf_op jit(solution)/shard_map/ppermute | solution.py:225
  38.8 12.3 %collective-permute-start.7 = (bf16[128,1152]{1,0:T(8,128)(2,1)S(1)}, bf16[128,1152]{1,0:T(8,128)(2,1)S(1)}, u32[]{:S(2)}, u32[]{:S(2)}) collective-permute-start(bf16[128,1152]{1,0:T(8,128)(2,1)S(1)} %shard_map.98), channel_id=1, source_target_pairs={{0,24},{8,16},{16,8},{24,0},{1,25},{9,17},{17,9},{25,1},{2,26},{10... | collective-permute-start | bytes 884744 | tf_op jit(solution)/shard_map/ppermute | solution.py:225
  43.5 13.8 %collective-permute-start.9 = (bf16[128,1152]{1,0:T(8,128)(2,1)S(1)}, bf16[128,1152]{1,0:T(8,128)(2,1)S(1)}, u32[]{:S(2)}, u32[]{:S(2)}) collective-permute-start(bf16[128,1152]{1,0:T(8,128)(2,1)S(1)} %shard_map.99), channel_id=1, source_target_pairs={{0,16},{8,24},{16,0},{24,8},{1,17},{9,25},{17,1},{25,9},{2,18},{10... | collective-permute-start | bytes 884744 | tf_op jit(solution)/shard_map/ppermute | solution.py:225
  44.4 22.4 %copy-start.1 = (f32[32,512]{1,0:T(8,128)S(1)}, f32[32,512]{1,0:T(8,128)}, u32[]{:S(2)}) copy-start(f32[32,512]{1,0:T(8,128)} %get-tuple-element.26.refs_4_) | copy-start | bytes 196612
  44.4 22.4 %copy-start.2 = (f32[32,128]{1,0:T(8,128)S(1)}, f32[32,128]{1,0:T(8,128)}, u32[]{:S(2)}) copy-start(f32[32,128]{1,0:T(8,128)} %get-tuple-element.27.refs_5_) | copy-start | bytes 49156
  57.6 6.1 %collective-permute-start.11 = (bf16[32,1152]{1,0:T(8,128)(2,1)S(1)}, bf16[32,1152]{1,0:T(8,128)(2,1)S(1)}, u32[]{:S(2)}, u32[]{:S(2)}) collective-permute-start(bf16[32,1152]{1,0:T(8,128)(2,1)S(1)} %get-tuple-element.23), channel_id=1, source_target_pairs={{0,2},{1,3},{2,0},{3,1},{4,6},{5,7},{6,4},{7,5},{8,10},{9,11},{10,... | collective-permute-start | bytes 221192 | tf_op jit(solution)/shard_map/ppermute | solution.py:227
  57.7 9.1 %collective-permute-start.12 = (bf16[32,1152]{1,0:T(8,128)(2,1)S(1)}, bf16[32,1152]{1,0:T(8,128)(2,1)S(1)}, u32[]{:S(2)}, u32[]{:S(2)}) collective-permute-start(bf16[32,1152]{1,0:T(8,128)(2,1)S(1)} %get-tuple-element.24), channel_id=1, source_target_pairs={{0,4},{1,5},{2,6},{3,7},{4,0},{5,1},{6,2},{7,3},{8,12},{9,13},{10,... | collective-permute-start | bytes 221192 | tf_op jit(solution)/shard_map/ppermute | solution.py:227
  59.1 7.6 %collective-permute-start.13 = (bf16[32,1152]{1,0:T(8,128)(2,1)S(1)}, bf16[32,1152]{1,0:T(8,128)(2,1)S(1)}, u32[]{:S(2)}, u32[]{:S(2)}) collective-permute-start(bf16[32,1152]{1,0:T(8,128)(2,1)S(1)} %get-tuple-element.25), channel_id=1, source_target_pairs={{0,6},{1,7},{2,4},{3,5},{4,2},{5,3},{6,0},{7,1},{8,14},{9,15},{10,... | collective-permute-start | bytes 221192 | tf_op jit(solution)/shard_map/ppermute | solution.py:227

commit v4 on v3

--- a/solution.py
+++ b/solution.py
@@ -19,14 +19,12 @@
 bf16 = jnp.bfloat16
 
 
-def call(body, outs, *args, flops=0, limit=vmem_bytes, **kw):
-    moved = sum(a.size * a.dtype.itemsize for a in args)
-    moved += sum(math.prod(o.shape) * o.dtype.itemsize for o in outs)
+def call(body, outs, *args, work=0, limit=vmem_bytes, **kw):
     return pl.pallas_call(
         body,
         out_shape=outs,
         compiler_params=pltpu.CompilerParams(vmem_limit_bytes=limit),
-        cost_estimate=pl.CostEstimate(flops=flops, bytes_accessed=moved, transcendentals=0),
+        cost_estimate=pl.CostEstimate(flops=work, bytes_accessed=0, transcendentals=0),
         **kw,
     )(*args)
 
@@ -70,26 +68,122 @@
     return jnp.sum(jnp.where(diagonal(count), spread, 0.0), axis=1, keepdims=True)
 
 
-def keys_kernel(memory_ref, keys_ref, *copy_refs):
+def keys_kernel(memory_ref, keys_ref, copy_ref):
     stored = memory_ref[...]
+    keys_ref[...] = normalized(stored)
+    copy_ref[...] = stored
+
+
+def normalized(stored):
     rows = stored.astype(f32)
     radius = jnp.sqrt(jnp.sum(rows * rows, axis=1, keepdims=True) + 1e-06)
-    keys_ref[...] = (rows / radius).astype(bf16)
-    for copy_ref in copy_refs:
-        copy_ref[...] = stored
-
-
-def keys_of(memory, copied):
+    return (rows / radius).astype(bf16)
+
+
+def keys_of(memory):
     slots, width = memory.shape
     block = math.gcd(512, slots)
     spec = pl.BlockSpec((block, width), lambda i: (i, 0))
     return call(
         keys_kernel,
-        [shaped((slots, width), bf16)] * (2 if copied else 1),
+        [shaped((slots, width), bf16)] * 2,
         memory,
         grid=(slots // block,),
         in_specs=[spec],
-        out_specs=[spec] * (2 if copied else 1),
+        out_specs=[spec] * 2,
+    )
+
+
+def join_kernel(blocks, *refs):
+    block_refs, out_ref = refs[:blocks], refs[-1]
+    size = block_refs[0].shape[0]
+    for place, ref in enumerate(block_refs):
+        out_ref[place * size : (place + 1) * size, :] = ref[...]
+
+
+def join(blocks, after):
+    size, width = blocks[0].shape
+    return call(
+        functools.partial(join_kernel, len(blocks)),
+        [shaped((size * len(blocks), width), blocks[0].dtype)],
+        *blocks, *after,
+        in_specs=[pl.BlockSpec(memory_space=pltpu.VMEM)] * len(blocks)
+        + [pl.BlockSpec(memory_space=pl.ANY)] * len(after),
+    )[0]
+
+
+def other_keys_kernel(block, memory_ref, rows_ref, keys_ref, same_ref):
+    same_ref[...] = rows_ref[...]
+
+    @pl.loop(0, memory_ref.shape[0] // block)
+    def _(i):
+        part = pl.ds(pl.multiple_of(i * block, block), block)
+        keys_ref[part, :] = normalized(memory_ref[part, :])
+
+
+def other_keys(memory, rows):
+    return call(
+        functools.partial(other_keys_kernel, math.gcd(256, memory.shape[0])),
+        [shaped(memory.shape, bf16), shaped(rows.shape, bf16)],
+        memory, rows,
+    )
+
+
+def pick_kernel(groups, count, at_ref, *refs):
+    blocks_refs, out_ref = refs[:groups], refs[-1]
+    size = blocks_refs[0].shape[0]
+    for place, ref in enumerate(blocks_refs):
+        inside = at_ref[0] - place * size
+
+        @pl.when((inside >= 0) & (inside < size))
+        def _():
+            out_ref[...] = ref[pl.ds(pl.multiple_of(inside, count), count), :]
+
+
+def pick(blocks, at, count, after):
+    return call(
+        functools.partial(pick_kernel, len(blocks), count),
+        [shaped((count, blocks[0].shape[1]), bf16)],
+        at.reshape(1), *blocks, *after,
+        in_specs=[pl.BlockSpec(memory_space=pltpu.SMEM)]
+        + [pl.BlockSpec(memory_space=pltpu.VMEM)] * len(blocks)
+        + [pl.BlockSpec(memory_space=pl.ANY)] * len(after),
+    )[0]
+
+
+def patch_kernel(choices, where_ref, stored_ref, labels_ref, *refs):
+    moved_refs, (memory_ref, new_labels_ref, rows_ref, sem) = refs[:choices], refs[choices:]
+    first = where_ref[0]
+    count, width = rows_ref.shape
+    moved = moved_refs[0][...]
+    for choice in range(1, choices):
+        moved = jnp.where(where_ref[1] == choice, moved_refs[choice][...], moved)
+    rows_ref[...] = moved[:, :width]
+    target = memory_ref.at[pl.ds(pl.multiple_of(first, count), count), :]
+    copy = pltpu.make_async_copy(rows_ref, target, sem)
+    copy.start()
+    digits = moved[:, width:].astype(f32)
+    labels = (digits[:, 0:1] * 256.0 + digits[:, 1:2]).astype(jnp.int32)
+    new = labels_ref[...]
+    slot = lax.broadcasted_iota(jnp.int32, new.shape, 0) * lanes + lax.broadcasted_iota(jnp.int32, new.shape, 1)
+    for row in range(count):
+        new = jnp.where(slot == first + row, labels[row : row + 1, :], new)
+    new_labels_ref[...] = new
+    copy.wait()
+
+
+def patch(stored, labels, choices, where):
+    count = choices[0].shape[0]
+    width = stored.shape[1]
+    return call(
+        functools.partial(patch_kernel, len(choices)),
+        [shaped(stored.shape, bf16), shaped(labels.shape, jnp.int32)],
+        where, stored, labels, *choices,
+        in_specs=[pl.BlockSpec(memory_space=pltpu.SMEM), pl.BlockSpec(memory_space=pl.ANY)]
+        + [pl.BlockSpec(memory_space=pltpu.VMEM)] * (1 + len(choices)),
+        out_specs=[pl.BlockSpec(memory_space=pl.ANY), pl.BlockSpec(memory_space=pltpu.VMEM)],
+        scratch_shapes=[pltpu.VMEM((count, width), bf16), pltpu.SemaphoreType.DMA],
+        input_output_aliases={1: 0},
     )
 
 
@@ -114,7 +208,7 @@
 
 def block_kernel(sides, chunk, rows_ref, *refs):
     keys_refs, label_refs = refs[:sides], refs[sides : 2 * sides]
-    out_ref, weight_ref = refs[2 * sides :]
+    out_ref, weight_ref = refs[-2:]
     slots, width = keys_refs[0].shape
     size = rows_ref.shape[0]
     anchors = rows_ref[:, :width]
@@ -158,14 +252,16 @@
     out_ref[:, 2 * width :] = pack_sums(sums).astype(out_ref.dtype)
 
 
-def block_sums(rows, keys, labels, dtype):
+def block_sums(rows, keys, labels, dtype, after):
     slots, width = keys[0].shape
     size = rows.shape[0]
     return call(
         functools.partial(block_kernel, len(keys), math.gcd(512, slots)),
         [shaped((size, 2 * width + lanes), dtype)],
-        rows, *[in_vmem(k) for k in keys], *labels,
-        flops=6 * size * slots * len(keys) * width,
+        rows, *[in_vmem(k) for k in keys], *labels, *after,
+        work=12 * size * slots * len(keys) * width,
+        in_specs=[pl.BlockSpec(memory_space=pltpu.VMEM)] * (1 + 2 * len(keys))
+        + [pl.BlockSpec(memory_space=pl.ANY)] * len(after),
         scratch_shapes=[pltpu.VMEM((2 * size, slots * len(keys)), bf16)],
     )[0]
 
@@ -241,44 +337,48 @@
     )
 
     labels = [slot_labels] + [exchange(slot_labels, "core", s) for s in range(1, cores)]
+    memories = [memory] + [exchange(memory, "core", s) for s in range(1, cores)]
+    own_keys, copied = keys_of(memory)
+    keys = [own_keys]
+
+    near = [packed] + [None] * (line - 1)
+    for s in range(line - 1, 0, -1):
+        near[s] = exchange(packed, "line", s)
+    part = join(near, [own_keys, *labels])
     labels = [value.reshape(1, slots) for value in labels]
-    memories = [memory] + [exchange(memory, "core", s) for s in range(1, cores)]
-    own_keys, copied = keys_of(memory, True)
-    keys = [own_keys] + [keys_of(value, False)[0] for value in memories[1:]]
-
-    part = jnp.concatenate([packed] + [exchange(packed, "line", s) for s in range(1, line)])
-    blocks = [part] + [exchange(part, "grp", s) for s in range(1, groups)]
-
-    arrived = []
+    blocks = [part] + [None] * (groups - 1)
+    for s in range(groups - 1, 1, -1):
+        blocks[s] = exchange(part, "grp", s)
+    for value in memories[1:]:
+        other, part = other_keys(value, part)
+        keys.append(other)
+    if groups > 1:
+        blocks[1] = exchange(part, "grp", 1)
+
+    arrived, after = [], []
     for s in range(groups - 1, 0, -1):
-        sums = block_sums(blocks[s], keys, labels, bf16)
-        arrived.append(exchange(sums, "grp", s))
-    if groups > 1:
-        part, sums = lax.optimization_barrier((part, sums))
-    held = block_sums(part, keys, labels, f32)
-    held, *parts = add(held, arrived, line)
-    arrived = [exchange(value, "line", s) for s, value in enumerate(parts, 1)]
+        after = [block_sums(blocks[s], keys, labels, bf16, after)]
+        arrived.append(exchange(after[0], "grp", s))
+    held = block_sums(part, keys, labels, f32, after)
+    sums, *parts = add(held, arrived, line)
+    arrived = [exchange(parts[s - 1], "line", s) for s in range(line - 1, 0, -1)]
     grad_batch, loss = call(
         functools.partial(finish_kernel, len(arrived)),
         [shaped((count, width), f32), shaped((1, count), f32)],
-        held, *arrived, unit, radius,
+        sums, *arrived, unit, radius,
     )
 
     step_value = step_index[0]
     first_slot = (step_value % (slots // count)) * count
-    crossing = (step_value % cores) if cores > 1 else 0
+    crossing = step_value % cores
     target = my_grp * members + (my_dev ^ crossing)
     source = (target - step_value) % devices_all
     source_grp, source_line = source // members, (source % members) // cores
     at = ((my_grp ^ source_grp) * line + ((my_dev // cores) ^ source_line)) * count
-    moved = lax.dynamic_slice_in_dim(jnp.concatenate(blocks), at, count, 0)
-    if cores > 1:
-        moved = jnp.where(crossing > 0, exchange(moved, "core", 1), moved)
-    digits = moved[:, width : width + 2].astype(jnp.int32)
-    moved_labels = digits[:, 0] * 256 + digits[:, 1]
-    new_memory = lax.dynamic_update_slice_in_dim(copied, moved[:, :width], first_slot, 0)
-    new_labels = lax.dynamic_update_slice_in_dim(copied_labels.reshape(slots), moved_labels, first_slot, 0)
-    return (grad_batch, loss.reshape(count), new_memory, new_labels)
+    moved = pick(blocks, at, count, after)
+    choices = [moved] + [exchange(moved, "core", s) for s in range(1, cores)]
+    new_memory, new_labels = patch(copied, copied_labels, choices, jnp.stack([first_slot, crossing]))
+    return (grad_batch, loss.reshape(count), new_memory, new_labels.reshape(slots))
 
 
 def solution(mesh):

time: 68 us -> 50.2 us (0.74)
  waiting for transfers between devices: 24.3 us -> 8.5 us
  local copies, waits for them, and re-layouts: 6.57 us -> 1.61 us
  Pallas kernels: 17 us -> 20.7 us
    ppermute x6, waiting for transfers between devices: 16.1 us -> 3.28 us  [exchange(): return lax.ppermute(value, 'grp', [(i, i ^ step) for i in range(groups)])]
    pallas_call x9 -> x12, Pallas kernels: 17 us -> 20.7 us  [call(): pl.pallas_call(body, out_shape=outs, compiler_params=pltpu.CompilerParams...]
    ppermute x9, waiting for transfers between devices: 8.22 us -> 5.22 us  [exchange(): return lax.ppermute(value, 'dev', [(i, i ^ jump) for i in range(members)])]
    unnamed x18 -> x12, local copies, waits for them, and re-layouts: 4.46 us -> 1.61 us
    dynamic_update_slice x2 -> x0, local copies, waits for them, and re-layouts: 2.08 us -> none  [the longest x1 1.45 us: per_device(): lax.dynamic_update_slice_in_dim(copied_labels.reshape(slots), moved_label...]
  transfers between devices with their start and end apart: 15 -> 15, of which waited for: 7 -> 5; matrix products, arithmetic and copies ran while one was open for 5% -> 0% of each run, Pallas kernels for 19% -> 40%
where the time goes in v4:
time: 50.2 us; the launch traced here: 49.9 us
  Pallas kernels  20.7 us (41%)
  starting transfers between devices  17.5 us (35%)
  waiting for transfers between devices  8.5 us (17%)
  local copies, waits for them, and re-layouts  1.61 us (3%)
  between operations  1.5 us (3%)
    pallas_call x12, Pallas kernels, call(): pl.pallas_call(body, out_shape=outs, compiler_params=pltpu.CompilerParams...  20.7 us
    ppermute x9, starting transfers between devices, exchange(): return lax.ppermute(value, 'dev', [(i, i ^ jump) for i in range(members)])  10.2 us
    ppermute x6, starting transfers between devices, exchange(): return lax.ppermute(value, 'grp', [(i, i ^ step) for i in range(groups)])  7.37 us
    ppermute x9, waiting for transfers between devices, exchange(): return lax.ppermute(value, 'dev', [(i, i ^ jump) for i in range(members)])  5.22 us
    ppermute x6, waiting for transfers between devices, exchange(): return lax.ppermute(value, 'grp', [(i, i ^ step) for i in range(groups)])  3.28 us
    unnamed x12, local copies, waits for them, and re-layouts  1.61 us
  transfers between devices with their start and end apart: 15, of which 5 were waited for; matrix products, arithmetic and copies ran while one was open for 0% of the time, Pallas kernels for 40%

profile of v4, /device:TPU:0, one launch (start us, length us, event | category | flops | bytes accessed | tf_op | source)
XLA Modules:
  0.0 49.9 jit_solution(13989369128380997398)
XLA Ops:
  0.6 0.5 %collective-permute-start = (bf16[2048,512]{1,0:T(8,128)(2,1)}, bf16[2048,512]{1,0:T(8,128)(2,1)}, u32[]{:S(2)}, u32[]{:S(2)}) collective-permute-start(bf16[2048,512]{1,0:T(8,128)(2,1)} %memory_ref.1), channel_id=1, source_target_pairs={{0,1},{1,0},{2,3},{3,2},{4,5},{5,4},{6,7},{7,6},{8,9},{9,8},{10,11... | collective-permute-start | bytes 6291464 | tf_op jit(solution)/shard_map/ppermute | solution.py:323
  1.1 1.5 %shard_map.93 = (bf16[32,640]{1,0:T(8,128)(2,1)}, f32[32,512]{1,0:T(8,128)}, f32[32,128]{1,0:T(8,128)}, s32[16,128]{1,0:T(8,128)}, s32[16,128]{1,0:T(8,128)}) custom-call(bf16[32,512]{1,0:T(8,128)(2,1)} %rows_ref.1, s32[1,32]{1,0:T(1,128)} %bitcast.25, s32[16,128]{1,0:T(8,128)} %bitcast.23, s32[16,128]{1,0:T(8,128)} %bitcast.24), custom_call_target="tpu_custom_call" | custom-call | tf_op jit(solution)/shard_map/pallas_call | solution.py:23
  2.7 2.6 %collective-permute-start.1 = (bf16[32,640]{1,0:T(8,128)(2,1)}, bf16[32,640]{1,0:T(8,128)(2,1)S(1)}, u32[]{:S(2)}, u32[]{:S(2)}) collective-permute-start(bf16[32,640]{1,0:T(8,128)(2,1)} %get-tuple-element.21.refs_0_), channel_id=1, source_target_pairs={{0,2},{1,3},{2,0},{3,1},{4,6},{5,7},{6,4},{7,5},{8,10},{9,11},{10,... | collective-permute-start | bytes 122888 | tf_op jit(solution)/shard_map/ppermute | solution.py:323
  5.3 2.6 %collective-permute-start.2 = (bf16[32,640]{1,0:T(8,128)(2,1)}, bf16[32,640]{1,0:T(8,128)(2,1)S(1)}, u32[]{:S(2)}, u32[]{:S(2)}) collective-permute-start(bf16[32,640]{1,0:T(8,128)(2,1)} %get-tuple-element.21.refs_0_), channel_id=1, source_target_pairs={{0,4},{1,5},{2,6},{3,7},{4,0},{5,1},{6,2},{7,3},{8,12},{9,13},{10,... | collective-permute-start | bytes 122888 | tf_op jit(solution)/shard_map/ppermute | solution.py:323
  7.9 0.0 collective-permute-start.3
  7.9 0.0 collective-permute-start.4
  7.9 1.6 %copy-done = bf16[2048,512]{1,0:T(8,128)(2,1)S(1)} copy-done((bf16[2048,512]{1,0:T(8,128)(2,1)S(1)}, bf16[2048,512]{1,0:T(8,128)(2,1)}, u32[]{:S(2)}) %copy-start) | copy-done | bytes 2097176
  9.5 2.0 %shard_map.94 = (bf16[2048,512]{1,0:T(8,128)(2,1)S(1)}, bf16[2048,512]{1,0:T(8,128)(2,1)}) custom-call(bf16[2048,512]{1,0:T(8,128)(2,1)S(1)} %copy-done), custom_call_target="tpu_custom_call" | custom-call | tf_op jit(solution)/shard_map/pallas_call | solution.py:23
  11.4 0.0 collective-permute-done.4.refs_6_
  11.5 2.4 %collective-permute-done.3.refs_3_ = bf16[32,640]{1,0:T(8,128)(2,1)S(1)} collective-permute-done((bf16[32,640]{1,0:T(8,128)(2,1)}, bf16[32,640]{1,0:T(8,128)(2,1)S(1)}, u32[]{:S(2)}, u32[]{:S(2)}) %collective-permute-start.3) | collective-permute-done | bytes 40992 | tf_op jit(solution)/shard_map/ppermute | solution.py:323
  13.9 2.5 %collective-permute-start.7 = (bf16[128,640]{1,0:T(8,128)(2,1)S(1)}, bf16[128,640]{1,0:T(8,128)(2,1)S(1)}, u32[]{:S(2)}, u32[]{:S(2)}) collective-permute-start(bf16[128,640]{1,0:T(8,128)(2,1)S(1)} %shard_map.95.rows_ref.refs_0_), channel_id=1, source_target_pairs={{0,24},{8,16},{16,8},{24,0},{1,25},{9,17},{17,9},{25,1},{2,26},{10... | collective-permute-start | bytes 491528 | tf_op jit(solution)/shard_map/ppermute | solution.py:321
  17.2 0.6 %collective-permute-start.6 = (bf16[128,640]{1,0:T(8,128)(2,1)S(1)}, bf16[128,640]{1,0:T(8,128)(2,1)S(1)}, u32[]{:S(2)}, u32[]{:S(2)}) collective-permute-start(bf16[128,640]{1,0:T(8,128)(2,1)S(1)} %shard_map.95.rows_ref.refs_0_), channel_id=1, source_target_pairs={{0,16},{8,24},{16,0},{24,8},{1,17},{9,25},{17,1},{25,9},{2,18},{10... | collective-permute-start | bytes 491528 | tf_op jit(solution)/shard_map/ppermute | solution.py:321
  17.7 2.9 %shard_map.96 = (bf16[2048,512]{1,0:T(8,128)(2,1)S(1)}, bf16[128,640]{1,0:T(8,128)(2,1)S(1)}) custom-call(bf16[2048,512]{1,0:T(8,128)(2,1)} %collective-permute-done.memory_ref, bf16[128,640]{1,0:T(8,128)(2,1)S(1)} %shard_map.95.rows_ref.refs_0_), custom_call_target="tpu_custom_call" | custom-call | tf_op jit(solution)/shard_map/pallas_call | solution.py:23
  20.6 0.6 %collective-permute-start.5 = (bf16[128,640]{1,0:T(8,128)(2,1)S(1)}, bf16[128,640]{1,0:T(8,128)(2,1)S(1)}, u32[]{:S(2)}, u32[]{:S(2)}) collective-permute-start(bf16[128,640]{1,0:T(8,128)(2,1)S(1)} %get-tuple-element.24.rows_ref), channel_id=1, source_target_pairs={{0,8},{8,0},{16,24},{24,16},{1,9},{9,1},{17,25},{25,17},{2,10},{10... | collective-permute-start | bytes 491528 | tf_op jit(solution)/shard_map/ppermute | solution.py:321
  21.2 2.9 %shard_map.97.refs_4_ = bf16[128,1152]{1,0:T(8,128)(2,1)S(1)} custom-call(bf16[128,640]{1,0:T(8,128)(2,1)S(1)} %collective-permute-done.7.rows_ref.refs_3_, bf16[2048,512]{1,0:T(8,128)(2,1)S(1)} %get-tuple-element.22.refs_4_.refs_0_, bf16[2048,512]{1,0:T(8,128)(2,1)S(1)} %get-tuple-element.25.refs_1_, s32[1,2048]{1,0:T(1,128)S(1)} %bitcast.15, ...), custom_call_target="tpu_custom_call" | custom-call | flops 3221225472 | tf_op jit(solution)/shard_map/pallas_call | solution.py:23
  24.1 2.5 %collective-permute-start.8 = (bf16[128,1152]{1,0:T(8,128)(2,1)S(1)}, bf16[128,1152]{1,0:T(8,128)(2,1)S(1)}, u32[]{:S(2)}, u32[]{:S(2)}) collective-permute-start(bf16[128,1152]{1,0:T(8,128)(2,1)S(1)} %shard_map.97.refs_4_), channel_id=1, source_target_pairs={{0,24},{8,16},{16,8},{24,0},{1,25},{9,17},{17,9},{25,1},{2,26},{10... | collective-permute-start | bytes 884744 | tf_op jit(solution)/shard_map/ppermute | solution.py:321
  26.6 2.9 %shard_map.98.refs_4_ = bf16[128,1152]{1,0:T(8,128)(2,1)S(1)} custom-call(bf16[128,640]{1,0:T(8,128)(2,1)S(1)} %collective-permute-done.6.rows_ref.refs_2_, bf16[2048,512]{1,0:T(8,128)(2,1)S(1)} %get-tuple-element.22.refs_4_.refs_0_, bf16[2048,512]{1,0:T(8,128)(2,1)S(1)} %get-tuple-element.25.refs_1_, s32[1,2048]{1,0:T(1,128)S(1)} %bitcast.16, ...), custom_call_target="tpu_custom_call" | custom-call | flops 3221225472 | tf_op jit(solution)/shard_map/pallas_call | solution.py:23
  29.5 0.6 %collective-permute-start.9 = (bf16[128,1152]{1,0:T(8,128)(2,1)S(1)}, bf16[128,1152]{1,0:T(8,128)(2,1)S(1)}, u32[]{:S(2)}, u32[]{:S(2)}) collective-permute-start(bf16[128,1152]{1,0:T(8,128)(2,1)S(1)} %shard_map.98.refs_4_), channel_id=1, source_target_pairs={{0,16},{8,24},{16,0},{24,8},{1,17},{9,25},{17,1},{25,9},{2,18},{10... | collective-permute-start | bytes 884744 | tf_op jit(solution)/shard_map/ppermute | solution.py:321
  30.0 2.9 %shard_map.99.refs_4_ = bf16[128,1152]{1,0:T(8,128)(2,1)S(1)} custom-call(bf16[128,640]{1,0:T(8,128)(2,1)S(1)} %collective-permute-done.5.rows_ref.refs_1_, bf16[2048,512]{1,0:T(8,128)(2,1)S(1)} %get-tuple-element.22.refs_4_.refs_0_, bf16[2048,512]{1,0:T(8,128)(2,1)S(1)} %get-tuple-element.25.refs_1_, s32[1,2048]{1,0:T(1,128)S(1)} %bitcast.17, ...), custom_call_target="tpu_custom_call" | custom-call | flops 3221225472 | tf_op jit(solution)/shard_map/pallas_call | solution.py:23
  32.9 0.6 %collective-permute-start.10 = (bf16[128,1152]{1,0:T(8,128)(2,1)S(1)}, bf16[128,1152]{1,0:T(8,128)(2,1)S(1)}, u32[]{:S(2)}, u32[]{:S(2)}) collective-permute-start(bf16[128,1152]{1,0:T(8,128)(2,1)S(1)} %shard_map.99.refs_4_), channel_id=1, source_target_pairs={{0,8},{8,0},{16,24},{24,16},{1,9},{9,1},{17,25},{25,17},{2,10},{10... | collective-permute-start | bytes 884744 | tf_op jit(solution)/shard_map/ppermute | solution.py:321
  33.5 2.9 %shard_map.100.refs_0_ = f32[128,1152]{1,0:T(8,128)S(1)} custom-call(bf16[128,640]{1,0:T(8,128)(2,1)S(1)} %get-tuple-element.24.rows_ref, bf16[2048,512]{1,0:T(8,128)(2,1)S(1)} %get-tuple-element.22.refs_4_.refs_0_, bf16[2048,512]{1,0:T(8,128)(2,1)S(1)} %get-tuple-element.25.refs_1_, s32[1,2048]{1,0:T(1,128)S(1)} %bitcast.18, s32[1,2048]{1,0:T(1,128)S(1)} %bitcast.22, ...), custom_call_target="tpu_custom_call" | custom-call | flops 3221225472 | tf_op jit(solution)/shard_map/pallas_call | solution.py:23
  36.4 0.0 copy-start.1
  36.4 3.2 %collective-permute-done.9.refs_2_ = bf16[128,1152]{1,0:T(8,128)(2,1)S(1)} collective-permute-done((bf16[128,1152]{1,0:T(8,128)(2,1)S(1)}, bf16[128,1152]{1,0:T(8,128)(2,1)S(1)}, u32[]{:S(2)}, u32[]{:S(2)}) %collective-permute-start.9) | collective-permute-done | bytes 294944 | tf_op jit(solution)/shard_map/ppermute | solution.py:321
  39.6 0.1 collective-permute-done.10.refs_3_
  39.7 0.2 shard_map.101
  39.9 3.2 %collective-permute-start.11 = (bf16[32,1152]{1,0:T(8,128)(2,1)S(1)}, bf16[32,1152]{1,0:T(8,128)(2,1)S(1)}, u32[]{:S(2)}, u32[]{:S(2)}) collective-permute-start(bf16[32,1152]{1,0:T(8,128)(2,1)S(1)} %get-tuple-element.27), channel_id=1, source_target_pairs={{0,6},{1,7},{2,4},{3,5},{4,2},{5,3},{6,0},{7,1},{8,14},{9,15},{10,... | collective-permute-start | bytes 221192 | tf_op jit(solution)/shard_map/ppermute | solution.py:323
  43.1 1.3 %collective-permute-start.13 = (bf16[32,1152]{1,0:T(8,128)(2,1)S(1)}, bf16[32,1152]{1,0:T(8,128)(2,1)S(1)}, u32[]{:S(2)}, u32[]{:S(2)}) collective-permute-start(bf16[32,1152]{1,0:T(8,128)(2,1)S(1)} %get-tuple-element.29), channel_id=1, source_target_pairs={{0,2},{1,3},{2,0},{3,1},{4,6},{5,7},{6,4},{7,5},{8,10},{9,11},{10,... | collective-permute-start | bytes 221192 | tf_op jit(solution)/shard_map/ppermute | solution.py:323
  44.4 0.1 pad_add_fusion.where_ref
  44.4 1.8 %shard_map.104 = (bf16[2048,512]{1,0:T(8,128)(2,1)}, s32[16,128]{1,0:T(8,128)}) custom-call(s32[2]{0:T(128)S(1)} %pad_add_fusion.where_ref, bf16[2048,512]{1,0:T(8,128)(2,1)} %get-tuple-element.34.stored_ref, s32[16,128]{1,0:T(8,128)S(1)} %copy-done.4, bf16[32,640]{1,0:T(8,128)(2,1)S(1)} %shard_map.103.refs_0_, ...), custom_call_target="tpu_custom_call", output_to_operand_aliasing={{0}: (1, {})} | custom-call | tf_op jit(solution)/shard_map/pallas_call | solution.py:23
  46.2 0.6 %collective-permute-done.11.refs_1_ = bf16[32,1152]{1,0:T(8,128)(2,1)S(1)} collective-permute-done((bf16[32,1152]{1,0:T(8,128)(2,1)S(1)}, bf16[32,1152]{1,0:T(8,128)(2,1)S(1)}, u32[]{:S(2)}, u32[]{:S(2)}) %collective-permute-start.11) | collective-permute-done | bytes 73760 | tf_op jit(solution)/shard_map/ppermute | solution.py:323
  46.8 2.2 %collective-permute-done.12.refs_2_ = bf16[32,1152]{1,0:T(8,128)(2,1)S(1)} collective-permute-done((bf16[32,1152]{1,0:T(8,128)(2,1)S(1)}, bf16[32,1152]{1,0:T(8,128)(2,1)S(1)}, u32[]{:S(2)}, u32[]{:S(2)}) %collective-permute-start.12) | collective-permute-done | bytes 73760 | tf_op jit(solution)/shard_map/ppermute | solution.py:323
  49.0 0.9 %shard_map.102 = (f32[32,512]{1,0:T(8,128)}, f32[1,32]{1,0:T(1,128)}) custom-call(f32[32,1152]{1,0:T(8,128)S(1)} %get-tuple-element.26.refs_0_, bf16[32,1152]{1,0:T(8,128)(2,1)S(1)} %collective-permute-done.11.refs_1_, bf16[32,1152]{1,0:T(8,128)(2,1)S(1)} %collective-permute-done.12.refs_2_, bf16[32,1152]{1,0:T(8,128)(2,1)S(1)} %collective-permute-done.13.refs_3_, ...), custom_call_target="tpu_custom_call" | custom-call | tf_op jit(solution)/shard_map/pallas_call | solution.py:23
  (23 shorter events, 0.1 us)
Async XLA Ops:
  0.6 17.1 %collective-permute-start = (bf16[2048,512]{1,0:T(8,128)(2,1)}, bf16[2048,512]{1,0:T(8,128)(2,1)}, u32[]{:S(2)}, u32[]{:S(2)}) collective-permute-start(bf16[2048,512]{1,0:T(8,128)(2,1)} %memory_ref.1), channel_id=1, source_target_pairs={{0,1},{1,0},{2,3},{3,2},{4,5},{5,4},{6,7},{7,6},{8,9},{9,8},{10,11... | collective-permute-start | bytes 6291464 | tf_op jit(solution)/shard_map/ppermute | solution.py:323
  2.7 8.8 %collective-permute-start.1 = (bf16[32,640]{1,0:T(8,128)(2,1)}, bf16[32,640]{1,0:T(8,128)(2,1)S(1)}, u32[]{:S(2)}, u32[]{:S(2)}) collective-permute-start(bf16[32,640]{1,0:T(8,128)(2,1)} %get-tuple-element.21.refs_0_), channel_id=1, source_target_pairs={{0,2},{1,3},{2,0},{3,1},{4,6},{5,7},{6,4},{7,5},{8,10},{9,11},{10,... | collective-permute-start | bytes 122888 | tf_op jit(solution)/shard_map/ppermute | solution.py:323
  5.3 6.2 %collective-permute-start.2 = (bf16[32,640]{1,0:T(8,128)(2,1)}, bf16[32,640]{1,0:T(8,128)(2,1)S(1)}, u32[]{:S(2)}, u32[]{:S(2)}) collective-permute-start(bf16[32,640]{1,0:T(8,128)(2,1)} %get-tuple-element.21.refs_0_), channel_id=1, source_target_pairs={{0,4},{1,5},{2,6},{3,7},{4,0},{5,1},{6,2},{7,3},{8,12},{9,13},{10,... | collective-permute-start | bytes 122888 | tf_op jit(solution)/shard_map/ppermute | solution.py:323
  7.9 6.0 %collective-permute-start.3 = (bf16[32,640]{1,0:T(8,128)(2,1)}, bf16[32,640]{1,0:T(8,128)(2,1)S(1)}, u32[]{:S(2)}, u32[]{:S(2)}) collective-permute-start(bf16[32,640]{1,0:T(8,128)(2,1)} %get-tuple-element.21.refs_0_), channel_id=1, source_target_pairs={{0,6},{1,7},{2,4},{3,5},{4,2},{5,3},{6,0},{7,1},{8,14},{9,15},{10,... | collective-permute-start | bytes 122888 | tf_op jit(solution)/shard_map/ppermute | solution.py:323
  7.9 3.6 %collective-permute-start.4 = (s32[16,128]{1,0:T(8,128)}, s32[16,128]{1,0:T(8,128)S(1)}, u32[]{:S(2)}, u32[]{:S(2)}) collective-permute-start(s32[16,128]{1,0:T(8,128)} %get-tuple-element.23.refs_5_), channel_id=1, source_target_pairs={{0,1},{1,0},{2,3},{3,2},{4,5},{5,4},{6,7},{7,6},{8,9},{9,8},{10,11... | collective-permute-start | bytes 24584 | tf_op jit(solution)/shard_map/ppermute | solution.py:323
  7.9 1.6 %copy-start = (bf16[2048,512]{1,0:T(8,128)(2,1)S(1)}, bf16[2048,512]{1,0:T(8,128)(2,1)}, u32[]{:S(2)}) copy-start(bf16[2048,512]{1,0:T(8,128)(2,1)} %memory_ref.1) | copy-start | bytes 6291460
  9.5 4.4 %copy-start.2 = (bf16[32,640]{1,0:T(8,128)(2,1)S(1)}, bf16[32,640]{1,0:T(8,128)(2,1)}, u32[]{:S(2)}) copy-start(bf16[32,640]{1,0:T(8,128)(2,1)} %get-tuple-element.21.refs_0_) | copy-start | bytes 122884
  9.5 4.4 %copy-start.5 = (s32[16,128]{1,0:T(8,128)S(1)}, s32[16,128]{1,0:T(8,128)}, u32[]{:S(2)}) copy-start(s32[16,128]{1,0:T(8,128)} %get-tuple-element.23.refs_5_) | copy-start | bytes 24580
  13.9 7.3 %collective-permute-start.7 = (bf16[128,640]{1,0:T(8,128)(2,1)S(1)}, bf16[128,640]{1,0:T(8,128)(2,1)S(1)}, u32[]{:S(2)}, u32[]{:S(2)}) collective-permute-start(bf16[128,640]{1,0:T(8,128)(2,1)S(1)} %shard_map.95.rows_ref.refs_0_), channel_id=1, source_target_pairs={{0,24},{8,16},{16,8},{24,0},{1,25},{9,17},{17,9},{25,1},{2,26},{10... | collective-permute-start | bytes 491528 | tf_op jit(solution)/shard_map/ppermute | solution.py:321
  17.2 9.4 %collective-permute-start.6 = (bf16[128,640]{1,0:T(8,128)(2,1)S(1)}, bf16[128,640]{1,0:T(8,128)(2,1)S(1)}, u32[]{:S(2)}, u32[]{:S(2)}) collective-permute-start(bf16[128,640]{1,0:T(8,128)(2,1)S(1)} %shard_map.95.rows_ref.refs_0_), channel_id=1, source_target_pairs={{0,16},{8,24},{16,0},{24,8},{1,17},{9,25},{17,1},{25,9},{2,18},{10... | collective-permute-start | bytes 491528 | tf_op jit(solution)/shard_map/ppermute | solution.py:321
  20.6 9.4 %collective-permute-start.5 = (bf16[128,640]{1,0:T(8,128)(2,1)S(1)}, bf16[128,640]{1,0:T(8,128)(2,1)S(1)}, u32[]{:S(2)}, u32[]{:S(2)}) collective-permute-start(bf16[128,640]{1,0:T(8,128)(2,1)S(1)} %get-tuple-element.24.rows_ref), channel_id=1, source_target_pairs={{0,8},{8,0},{16,24},{24,16},{1,9},{9,1},{17,25},{25,17},{2,10},{10... | collective-permute-start | bytes 491528 | tf_op jit(solution)/shard_map/ppermute | solution.py:321
  24.1 12.3 %collective-permute-start.8 = (bf16[128,1152]{1,0:T(8,128)(2,1)S(1)}, bf16[128,1152]{1,0:T(8,128)(2,1)S(1)}, u32[]{:S(2)}, u32[]{:S(2)}) collective-permute-start(bf16[128,1152]{1,0:T(8,128)(2,1)S(1)} %shard_map.97.refs_4_), channel_id=1, source_target_pairs={{0,24},{8,16},{16,8},{24,0},{1,25},{9,17},{17,9},{25,1},{2,26},{10... | collective-permute-start | bytes 884744 | tf_op jit(solution)/shard_map/ppermute | solution.py:321
  29.5 10.1 %collective-permute-start.9 = (bf16[128,1152]{1,0:T(8,128)(2,1)S(1)}, bf16[128,1152]{1,0:T(8,128)(2,1)S(1)}, u32[]{:S(2)}, u32[]{:S(2)}) collective-permute-start(bf16[128,1152]{1,0:T(8,128)(2,1)S(1)} %shard_map.98.refs_4_), channel_id=1, source_target_pairs={{0,16},{8,24},{16,0},{24,8},{1,17},{9,25},{17,1},{25,9},{2,18},{10... | collective-permute-start | bytes 884744 | tf_op jit(solution)/shard_map/ppermute | solution.py:321
  32.9 6.8 %collective-permute-start.10 = (bf16[128,1152]{1,0:T(8,128)(2,1)S(1)}, bf16[128,1152]{1,0:T(8,128)(2,1)S(1)}, u32[]{:S(2)}, u32[]{:S(2)}) collective-permute-start(bf16[128,1152]{1,0:T(8,128)(2,1)S(1)} %shard_map.99.refs_4_), channel_id=1, source_target_pairs={{0,8},{8,0},{16,24},{24,16},{1,9},{9,1},{17,25},{25,17},{2,10},{10... | collective-permute-start | bytes 884744 | tf_op jit(solution)/shard_map/ppermute | solution.py:321
  33.5 10.9 %copy-start.4 = (s32[16,128]{1,0:T(8,128)S(1)}, s32[16,128]{1,0:T(8,128)}, u32[]{:S(2)}) copy-start(s32[16,128]{1,0:T(8,128)} %get-tuple-element.35.labels_ref) | copy-start | bytes 24580
  33.5 10.9 %collective-permute-start.14 = (bf16[32,640]{1,0:T(8,128)(2,1)S(1)}, bf16[32,640]{1,0:T(8,128)(2,1)S(1)}, u32[]{:S(2)}, u32[]{:S(2)}) collective-permute-start(bf16[32,640]{1,0:T(8,128)(2,1)S(1)} %shard_map.103.refs_0_), channel_id=1, source_target_pairs={{0,1},{1,0},{2,3},{3,2},{4,5},{5,4},{6,7},{7,6},{8,9},{9,8},{10,11... | collective-permute-start | bytes 122888 | tf_op jit(solution)/shard_map/ppermute | solution.py:323
  36.4 12.6 %copy-start.1 = (f32[32,512]{1,0:T(8,128)S(1)}, f32[32,512]{1,0:T(8,128)}, u32[]{:S(2)}) copy-start(f32[32,512]{1,0:T(8,128)} %get-tuple-element.30.refs_4_) | copy-start | bytes 196612
  36.4 12.6 %copy-start.3 = (f32[32,128]{1,0:T(8,128)S(1)}, f32[32,128]{1,0:T(8,128)}, u32[]{:S(2)}) copy-start(f32[32,128]{1,0:T(8,128)} %get-tuple-element.31.refs_5_) | copy-start | bytes 49156
  39.9 6.9 %collective-permute-start.11 = (bf16[32,1152]{1,0:T(8,128)(2,1)S(1)}, bf16[32,1152]{1,0:T(8,128)(2,1)S(1)}, u32[]{:S(2)}, u32[]{:S(2)}) collective-permute-start(bf16[32,1152]{1,0:T(8,128)(2,1)S(1)} %get-tuple-element.27), channel_id=1, source_target_pairs={{0,6},{1,7},{2,4},{3,5},{4,2},{5,3},{6,0},{7,1},{8,14},{9,15},{10,... | collective-permute-start | bytes 221192 | tf_op jit(solution)/shard_map/ppermute | solution.py:323
  43.1 6.0 %collective-permute-start.12 = (bf16[32,1152]{1,0:T(8,128)(2,1)S(1)}, bf16[32,1152]{1,0:T(8,128)(2,1)S(1)}, u32[]{:S(2)}, u32[]{:S(2)}) collective-permute-start(bf16[32,1152]{1,0:T(8,128)(2,1)S(1)} %get-tuple-element.28), channel_id=1, source_target_pairs={{0,4},{1,5},{2,6},{3,7},{4,0},{5,1},{6,2},{7,3},{8,12},{9,13},{10,... | collective-permute-start | bytes 221192 | tf_op jit(solution)/shard_map/ppermute | solution.py:323
  43.1 6.0 %collective-permute-start.13 = (bf16[32,1152]{1,0:T(8,128)(2,1)S(1)}, bf16[32,1152]{1,0:T(8,128)(2,1)S(1)}, u32[]{:S(2)}, u32[]{:S(2)}) collective-permute-start(bf16[32,1152]{1,0:T(8,128)(2,1)S(1)} %get-tuple-element.29), channel_id=1, source_target_pairs={{0,2},{1,3},{2,0},{3,1},{4,6},{5,7},{6,4},{7,5},{8,10},{9,11},{10,... | collective-permute-start | bytes 221192 | tf_op jit(solution)/shard_map/ppermute | solution.py:323

commit v5 on v4

--- a/solution.py
+++ b/solution.py
@@ -68,29 +68,26 @@
     return jnp.sum(jnp.where(diagonal(count), spread, 0.0), axis=1, keepdims=True)
 
 
-def keys_kernel(memory_ref, keys_ref, copy_ref):
+def keys_kernel(memory_ref, keys_ref, *copy_refs):
     stored = memory_ref[...]
-    keys_ref[...] = normalized(stored)
-    copy_ref[...] = stored
-
-
-def normalized(stored):
     rows = stored.astype(f32)
     radius = jnp.sqrt(jnp.sum(rows * rows, axis=1, keepdims=True) + 1e-06)
-    return (rows / radius).astype(bf16)
-
-
-def keys_of(memory):
+    keys_ref[...] = (rows / radius).astype(bf16)
+    for copy_ref in copy_refs:
+        copy_ref[...] = stored
+
+
+def keys_of(memory, copies):
     slots, width = memory.shape
     block = math.gcd(512, slots)
     spec = pl.BlockSpec((block, width), lambda i: (i, 0))
     return call(
         keys_kernel,
-        [shaped((slots, width), bf16)] * 2,
+        [shaped((slots, width), bf16)] * (1 + copies),
         memory,
         grid=(slots // block,),
         in_specs=[spec],
-        out_specs=[spec] * 2,
+        out_specs=[spec] * (1 + copies),
     )
 
 
@@ -208,7 +205,7 @@
 
 def block_kernel(sides, chunk, rows_ref, *refs):
     keys_refs, label_refs = refs[:sides], refs[sides : 2 * sides]
-    out_ref, weight_ref = refs[-2:]
+    out_ref = refs[-1]
     slots, width = keys_refs[0].shape
     size = rows_ref.shape[0]
     anchors = rows_ref[:, :width]
@@ -218,30 +215,30 @@
     labels = jnp.sum(digits * digit, axis=1, keepdims=True)
     pos_sum = jnp.zeros((size, 1), f32)
     neg_sum = jnp.zeros((size, 1), f32)
-    for side in range(sides):
-        slot_labels = label_refs[side][...].astype(f32)
+    total = jnp.zeros((2 * size, width), f32)
+    chunks = [(side, slice(at, at + chunk)) for side in range(sides) for at in range(0, slots, chunk)]
+
+    def scores_of(side, part):
+        return lax.dot_general(
+            anchors, keys_refs[side][part, :], (((1,), (1,)), ((), ())), preferred_element_type=f32
+        )
+
+    scores = scores_of(*chunks[0])
+    for at, (side, part) in enumerate(chunks):
+        following = scores_of(*chunks[at + 1]) if at + 1 < len(chunks) else None
+        slot_labels = label_refs[side][:, part].astype(f32)
         neg_shift = jnp.where(slot_labels < 0.0, -1e30, -neg_scale * margin * log2e)
-        for start in range(0, slots, chunk):
-            part = slice(start, start + chunk)
-            scores = lax.dot_general(
-                anchors, keys_refs[side][part, :], (((1,), (1,)), ((), ())), preferred_element_type=f32
-            )
-            same = labels == slot_labels[:, part]
-            slope = jnp.where(same, -pos_scale * log2e, neg_scale * log2e)
-            shift = jnp.where(same, pos_scale * margin * log2e, neg_shift[:, part])
-            term = jnp.exp2(scores * slope + shift)
-            pos = jnp.where(same, term, 0.0)
-            neg = jnp.where(same, 0.0, term)
-            pos_sum += jnp.sum(pos, axis=1, keepdims=True)
-            neg_sum += jnp.sum(neg, axis=1, keepdims=True)
-            to = slice(side * slots + start, side * slots + start + chunk)
-            weight_ref[:size, to] = neg.astype(bf16)
-            weight_ref[size:, to] = pos.astype(bf16)
-    total = None
-    for side in range(sides):
-        part = weight_ref[:, side * slots : (side + 1) * slots]
-        term = jnp.dot(part, keys_refs[side][...], preferred_element_type=f32)
-        total = term if total is None else total + term
+        same = labels == slot_labels
+        slope = jnp.where(same, -pos_scale * log2e, neg_scale * log2e)
+        shift = jnp.where(same, pos_scale * margin * log2e, neg_shift)
+        term = jnp.exp2(scores * slope + shift)
+        pos = jnp.where(same, term, 0.0)
+        neg = jnp.where(same, 0.0, term)
+        pos_sum += jnp.sum(pos, axis=1, keepdims=True)
+        neg_sum += jnp.sum(neg, axis=1, keepdims=True)
+        weights = jnp.concatenate([neg.astype(bf16), pos.astype(bf16)], axis=0)
+        total += jnp.dot(weights, keys_refs[side][part, :], preferred_element_type=f32)
+        scores = following
     floats = anchors.astype(f32)
     sums = [pos_sum, neg_sum]
     for which in range(2):
@@ -262,7 +259,6 @@
         work=12 * size * slots * len(keys) * width,
         in_specs=[pl.BlockSpec(memory_space=pltpu.VMEM)] * (1 + 2 * len(keys))
         + [pl.BlockSpec(memory_space=pl.ANY)] * len(after),
-        scratch_shapes=[pltpu.VMEM((2 * size, slots * len(keys)), bf16)],
     )[0]
 
 
@@ -338,22 +334,17 @@
 
     labels = [slot_labels] + [exchange(slot_labels, "core", s) for s in range(1, cores)]
     memories = [memory] + [exchange(memory, "core", s) for s in range(1, cores)]
-    own_keys, copied = keys_of(memory)
-    keys = [own_keys]
+    own_keys, copied = keys_of(memory, 1)
+    keys = [own_keys] + [keys_of(value, 0)[0] for value in memories[1:]]
 
     near = [packed] + [None] * (line - 1)
     for s in range(line - 1, 0, -1):
         near[s] = exchange(packed, "line", s)
-    part = join(near, [own_keys, *labels])
+    part = join(near, [*keys, *labels])
     labels = [value.reshape(1, slots) for value in labels]
     blocks = [part] + [None] * (groups - 1)
-    for s in range(groups - 1, 1, -1):
+    for s in range(groups - 1, 0, -1):
         blocks[s] = exchange(part, "grp", s)
-    for value in memories[1:]:
-        other, part = other_keys(value, part)
-        keys.append(other)
-    if groups > 1:
-        blocks[1] = exchange(part, "grp", 1)
 
     arrived, after = [], []
     for s in range(groups - 1, 0, -1):

time: 50.2 us -> 52.6 us (1.048)
  waiting for transfers between devices: 8.5 us -> 11.1 us
  Pallas kernels: 20.7 us -> 18.5 us
  local copies, waits for them, and re-layouts: 1.61 us -> 3.5 us
    ppermute x6, waiting for transfers between devices: 3.28 us -> 8.03 us  [exchange(): return lax.ppermute(value, 'grp', [(i, i ^ step) for i in range(groups)])]
    pallas_call x12, Pallas kernels: 20.7 us -> 18.5 us  [call(): pl.pallas_call(body, out_shape=outs, compiler_params=pltpu.CompilerParams...]
    ppermute x9, waiting for transfers between devices: 5.22 us -> 3.06 us  [exchange(): return lax.ppermute(value, 'dev', [(i, i ^ jump) for i in range(members)])]
    unnamed x12 -> x18, local copies, waits for them, and re-layouts: 1.61 us -> 3.5 us
  transfers between devices with their start and end apart: 15 -> 15, of which waited for: 5 -> 4; matrix products, arithmetic and copies ran while one was open for 0% -> 0% of each run, Pallas kernels for 40% -> 34%
where the time goes in v5:
time: 52.6 us; the launch traced here: 52.3 us
  Pallas kernels  18.5 us (35%)
  starting transfers between devices  17.6 us (33%)
  waiting for transfers between devices  11.1 us (21%)
  local copies, waits for them, and re-layouts  3.5 us (7%)
  between operations  1.54 us (3%)
    pallas_call x12, Pallas kernels, call(): pl.pallas_call(body, out_shape=outs, compiler_params=pltpu.CompilerParams...  18.5 us
    ppermute x9, starting transfers between devices, exchange(): return lax.ppermute(value, 'dev', [(i, i ^ jump) for i in range(members)])  10.3 us
    ppermute x6, waiting for transfers between devices, exchange(): return lax.ppermute(value, 'grp', [(i, i ^ step) for i in range(groups)])  8.03 us
    ppermute x6, starting transfers between devices, exchange(): return lax.ppermute(value, 'grp', [(i, i ^ step) for i in range(groups)])  7.34 us
    unnamed x18, local copies, waits for them, and re-layouts  3.5 us
    ppermute x9, waiting for transfers between devices, exchange(): return lax.ppermute(value, 'dev', [(i, i ^ jump) for i in range(members)])  3.06 us
  transfers between devices with their start and end apart: 15, of which 4 were waited for; matrix products, arithmetic and copies ran while one was open for 0% of the time, Pallas kernels for 34%

profile of v5, /device:TPU:0, one launch (start us, length us, event | category | flops | bytes accessed | tf_op | source)
XLA Modules:
  0.0 52.3 jit_solution(5054457207483278108)
XLA Ops:
  0.6 0.5 collective-permute-start.3
  1.1 1.5 %shard_map.93 = (bf16[32,640]{1,0:T(8,128)(2,1)}, f32[32,512]{1,0:T(8,128)}, f32[32,128]{1,0:T(8,128)}, s32[16,128]{1,0:T(8,128)}, s32[16,128]{1,0:T(8,128)}) custom-call(bf16[32,512]{1,0:T(8,128)(2,1)} %rows_ref.1, s32[1,32]{1,0:T(1,128)} %bitcast.25, s32[16,128]{1,0:T(8,128)} %bitcast.23, s32[16,128]{1,0:T(8,128)} %bitcast.24), custom_call_target="tpu_custom_call" | custom-call | tf_op jit(solution)/shard_map/pallas_call | solution.py:23
  2.7 4.6 %collective-permute-start.2 = (bf16[32,640]{1,0:T(8,128)(2,1)}, bf16[32,640]{1,0:T(8,128)(2,1)S(1)}, u32[]{:S(2)}, u32[]{:S(2)}) collective-permute-start(bf16[32,640]{1,0:T(8,128)(2,1)} %get-tuple-element.19.refs_0_), channel_id=1, source_target_pairs={{0,6},{1,7},{2,4},{3,5},{4,2},{5,3},{6,0},{7,1},{8,14},{9,15},{10,... | collective-permute-start | bytes 122888 | tf_op jit(solution)/shard_map/ppermute | solution.py:319
  7.3 0.6 %collective-permute-start = (bf16[32,640]{1,0:T(8,128)(2,1)}, bf16[32,640]{1,0:T(8,128)(2,1)S(1)}, u32[]{:S(2)}, u32[]{:S(2)}) collective-permute-start(bf16[32,640]{1,0:T(8,128)(2,1)} %get-tuple-element.19.refs_0_), channel_id=1, source_target_pairs={{0,2},{1,3},{2,0},{3,1},{4,6},{5,7},{6,4},{7,5},{8,10},{9,11},{10,... | collective-permute-start | bytes 122888 | tf_op jit(solution)/shard_map/ppermute | solution.py:319
  7.9 1.6 %copy-done = bf16[2048,512]{1,0:T(8,128)(2,1)S(1)} copy-done((bf16[2048,512]{1,0:T(8,128)(2,1)S(1)}, bf16[2048,512]{1,0:T(8,128)(2,1)}, u32[]{:S(2)}) %copy-start) | copy-done | bytes 2097176
  9.5 2.0 %shard_map.94 = (bf16[2048,512]{1,0:T(8,128)(2,1)S(1)}, bf16[2048,512]{1,0:T(8,128)(2,1)}) custom-call(bf16[2048,512]{1,0:T(8,128)(2,1)S(1)} %copy-done), custom_call_target="tpu_custom_call" | custom-call | tf_op jit(solution)/shard_map/pallas_call | solution.py:23
  11.5 1.0 %shard_map.95.refs_5_.refs_1_ = bf16[2048,512]{1,0:T(8,128)(2,1)S(1)} custom-call(bf16[2048,512]{1,0:T(8,128)(2,1)S(1)} %collective-permute-done.3.memory_ref), custom_call_target="tpu_custom_call" | custom-call | tf_op jit(solution)/shard_map/pallas_call | solution.py:23
  12.6 0.3 copy-done.1
  12.9 2.7 %collective-permute-start.7 = (bf16[128,640]{1,0:T(8,128)(2,1)S(1)}, bf16[128,640]{1,0:T(8,128)(2,1)S(1)}, u32[]{:S(2)}, u32[]{:S(2)}) collective-permute-start(bf16[128,640]{1,0:T(8,128)(2,1)S(1)} %shard_map.96.rows_ref.refs_0_), channel_id=1, source_target_pairs={{0,24},{8,16},{16,8},{24,0},{1,25},{9,17},{17,9},{25,1},{2,26},{10... | collective-permute-start | bytes 491528 | tf_op jit(solution)/shard_map/ppermute | solution.py:317
  16.3 0.6 %collective-permute-start.6 = (bf16[128,640]{1,0:T(8,128)(2,1)S(1)}, bf16[128,640]{1,0:T(8,128)(2,1)S(1)}, u32[]{:S(2)}, u32[]{:S(2)}) collective-permute-start(bf16[128,640]{1,0:T(8,128)(2,1)S(1)} %shard_map.96.rows_ref.refs_0_), channel_id=1, source_target_pairs={{0,16},{8,24},{16,0},{24,8},{1,17},{9,25},{17,1},{25,9},{2,18},{10... | collective-permute-start | bytes 491528 | tf_op jit(solution)/shard_map/ppermute | solution.py:317
  16.9 0.4 collective-permute-start.5
  17.2 3.3 %collective-permute-done.7.rows_ref.refs_3_ = bf16[128,640]{1,0:T(8,128)(2,1)S(1)} collective-permute-done((bf16[128,640]{1,0:T(8,128)(2,1)S(1)}, bf16[128,640]{1,0:T(8,128)(2,1)S(1)}, u32[]{:S(2)}, u32[]{:S(2)}) %collective-permute-start.7) | collective-permute-done | bytes 163872 | tf_op jit(solution)/shard_map/ppermute | solution.py:317
  20.5 1.6 %copy-done.2 = bf16[2048,512]{1,0:T(8,128)(2,1)S(1)} copy-done((bf16[2048,512]{1,0:T(8,128)(2,1)S(1)}, bf16[2048,512]{1,0:T(8,128)(2,1)}, u32[]{:S(2)}) %copy-start.2) | copy-done | bytes 2097176
  22.1 2.8 %shard_map.97.refs_4_ = bf16[128,1152]{1,0:T(8,128)(2,1)S(1)} custom-call(bf16[128,640]{1,0:T(8,128)(2,1)S(1)} %collective-permute-done.7.rows_ref.refs_3_, bf16[2048,512]{1,0:T(8,128)(2,1)S(1)} %copy-done.2, bf16[2048,512]{1,0:T(8,128)(2,1)S(1)} %shard_map.95.refs_5_.refs_1_, s32[1,2048]{1,0:T(1,128)S(1)} %bitcast.15, s32[1,2048]{1,0:T(1,128)S(1)} %bitcast.19), custom_call_target="tpu_custom_call" | custom-call | flops 3221225472 | tf_op jit(solution)/shard_map/pallas_call | solution.py:23
  24.9 3.0 %collective-permute-start.8 = (bf16[128,1152]{1,0:T(8,128)(2,1)S(1)}, bf16[128,1152]{1,0:T(8,128)(2,1)S(1)}, u32[]{:S(2)}, u32[]{:S(2)}) collective-permute-start(bf16[128,1152]{1,0:T(8,128)(2,1)S(1)} %shard_map.97.refs_4_), channel_id=1, source_target_pairs={{0,24},{8,16},{16,8},{24,0},{1,25},{9,17},{17,9},{25,1},{2,26},{10... | collective-permute-start | bytes 884744 | tf_op jit(solution)/shard_map/ppermute | solution.py:317
  27.9 2.8 %shard_map.98.refs_4_ = bf16[128,1152]{1,0:T(8,128)(2,1)S(1)} custom-call(bf16[128,640]{1,0:T(8,128)(2,1)S(1)} %collective-permute-done.6.rows_ref.refs_2_, bf16[2048,512]{1,0:T(8,128)(2,1)S(1)} %copy-done.2, bf16[2048,512]{1,0:T(8,128)(2,1)S(1)} %shard_map.95.refs_5_.refs_1_, s32[1,2048]{1,0:T(1,128)S(1)} %bitcast.16, s32[1,2048]{1,0:T(1,128)S(1)} %bitcast.20, ...), custom_call_target="tpu_custom_call" | custom-call | flops 3221225472 | tf_op jit(solution)/shard_map/pallas_call | solution.py:23
  30.7 0.6 %collective-permute-start.9 = (bf16[128,1152]{1,0:T(8,128)(2,1)S(1)}, bf16[128,1152]{1,0:T(8,128)(2,1)S(1)}, u32[]{:S(2)}, u32[]{:S(2)}) collective-permute-start(bf16[128,1152]{1,0:T(8,128)(2,1)S(1)} %shard_map.98.refs_4_), channel_id=1, source_target_pairs={{0,16},{8,24},{16,0},{24,8},{1,17},{9,25},{17,1},{25,9},{2,18},{10... | collective-permute-start | bytes 884744 | tf_op jit(solution)/shard_map/ppermute | solution.py:317
  31.3 2.8 %shard_map.99.refs_4_ = bf16[128,1152]{1,0:T(8,128)(2,1)S(1)} custom-call(bf16[128,640]{1,0:T(8,128)(2,1)S(1)} %collective-permute-done.5.rows_ref.refs_1_, bf16[2048,512]{1,0:T(8,128)(2,1)S(1)} %copy-done.2, bf16[2048,512]{1,0:T(8,128)(2,1)S(1)} %shard_map.95.refs_5_.refs_1_, s32[1,2048]{1,0:T(1,128)S(1)} %bitcast.17, s32[1,2048]{1,0:T(1,128)S(1)} %bitcast.21, ...), custom_call_target="tpu_custom_call" | custom-call | flops 3221225472 | tf_op jit(solution)/shard_map/pallas_call | solution.py:23
  34.1 0.1 collective-permute-start.10
  34.2 0.1 collective-permute-start.14
  34.3 2.8 %shard_map.100.refs_0_ = f32[128,1152]{1,0:T(8,128)S(1)} custom-call(bf16[128,640]{1,0:T(8,128)(2,1)S(1)} %shard_map.96.rows_ref.refs_0_, bf16[2048,512]{1,0:T(8,128)(2,1)S(1)} %copy-done.3, bf16[2048,512]{1,0:T(8,128)(2,1)S(1)} %shard_map.95.refs_5_.refs_1_, s32[1,2048]{1,0:T(1,128)S(1)} %bitcast.18, s32[1,2048]{1,0:T(1,128)S(1)} %bitcast.22, ...), custom_call_target="tpu_custom_call" | custom-call | flops 3221225472 | tf_op jit(solution)/shard_map/pallas_call | solution.py:23
  37.1 0.0 copy-start.4
  37.1 4.7 %collective-permute-done.10.refs_3_ = bf16[128,1152]{1,0:T(8,128)(2,1)S(1)} collective-permute-done((bf16[128,1152]{1,0:T(8,128)(2,1)S(1)}, bf16[128,1152]{1,0:T(8,128)(2,1)S(1)}, u32[]{:S(2)}, u32[]{:S(2)}) %collective-permute-start.10) | collective-permute-done | bytes 294944 | tf_op jit(solution)/shard_map/ppermute | solution.py:317
  41.9 0.2 shard_map.101
  42.1 3.7 %collective-permute-start.11 = (bf16[32,1152]{1,0:T(8,128)(2,1)S(1)}, bf16[32,1152]{1,0:T(8,128)(2,1)S(1)}, u32[]{:S(2)}, u32[]{:S(2)}) collective-permute-start(bf16[32,1152]{1,0:T(8,128)(2,1)S(1)} %get-tuple-element.23), channel_id=1, source_target_pairs={{0,6},{1,7},{2,4},{3,5},{4,2},{5,3},{6,0},{7,1},{8,14},{9,15},{10,... | collective-permute-start | bytes 221192 | tf_op jit(solution)/shard_map/ppermute | solution.py:319
  45.7 0.8 %collective-permute-start.13 = (bf16[32,1152]{1,0:T(8,128)(2,1)S(1)}, bf16[32,1152]{1,0:T(8,128)(2,1)S(1)}, u32[]{:S(2)}, u32[]{:S(2)}) collective-permute-start(bf16[32,1152]{1,0:T(8,128)(2,1)S(1)} %get-tuple-element.25), channel_id=1, source_target_pairs={{0,2},{1,3},{2,0},{3,1},{4,6},{5,7},{6,4},{7,5},{8,10},{9,11},{10,... | collective-permute-start | bytes 221192 | tf_op jit(solution)/shard_map/ppermute | solution.py:319
  46.5 0.1 pad_add_fusion.where_ref
  46.6 1.8 %shard_map.104 = (bf16[2048,512]{1,0:T(8,128)(2,1)}, s32[16,128]{1,0:T(8,128)}) custom-call(s32[2]{0:T(128)S(1)} %pad_add_fusion.where_ref, bf16[2048,512]{1,0:T(8,128)(2,1)} %get-tuple-element.30.stored_ref, s32[16,128]{1,0:T(8,128)S(1)} %copy-done.7, bf16[32,640]{1,0:T(8,128)(2,1)S(1)} %shard_map.103.refs_0_, ...), custom_call_target="tpu_custom_call", output_to_operand_aliasing={{0}: (1, {})} | custom-call | tf_op jit(solution)/shard_map/pallas_call | solution.py:23
  48.4 0.0 collective-permute-done.11.refs_1_
  48.4 2.9 %collective-permute-done.12.refs_2_ = bf16[32,1152]{1,0:T(8,128)(2,1)S(1)} collective-permute-done((bf16[32,1152]{1,0:T(8,128)(2,1)S(1)}, bf16[32,1152]{1,0:T(8,128)(2,1)S(1)}, u32[]{:S(2)}, u32[]{:S(2)}) %collective-permute-start.12) | collective-permute-done | bytes 73760 | tf_op jit(solution)/shard_map/ppermute | solution.py:319
  51.3 0.1 collective-permute-done.13.refs_3_
  51.4 0.9 %shard_map.102 = (f32[32,512]{1,0:T(8,128)}, f32[1,32]{1,0:T(1,128)}) custom-call(f32[32,1152]{1,0:T(8,128)S(1)} %get-tuple-element.22.refs_0_, bf16[32,1152]{1,0:T(8,128)(2,1)S(1)} %collective-permute-done.11.refs_1_, bf16[32,1152]{1,0:T(8,128)(2,1)S(1)} %collective-permute-done.12.refs_2_, bf16[32,1152]{1,0:T(8,128)(2,1)S(1)} %collective-permute-done.13.refs_3_, ...), custom_call_target="tpu_custom_call" | custom-call | tf_op jit(solution)/shard_map/pallas_call | solution.py:23
  (29 shorter events, 0.1 us)
Async XLA Ops:
  0.6 10.9 %collective-permute-start.3 = (bf16[2048,512]{1,0:T(8,128)(2,1)}, bf16[2048,512]{1,0:T(8,128)(2,1)S(1)}, u32[]{:S(2)}, u32[]{:S(2)}) collective-permute-start(bf16[2048,512]{1,0:T(8,128)(2,1)} %memory_ref.1), channel_id=1, source_target_pairs={{0,1},{1,0},{2,3},{3,2},{4,5},{5,4},{6,7},{7,6},{8,9},{9,8},{10,11... | collective-permute-start | bytes 6291464 | tf_op jit(solution)/shard_map/ppermute | solution.py:319
  2.7 9.8 %collective-permute-start.2 = (bf16[32,640]{1,0:T(8,128)(2,1)}, bf16[32,640]{1,0:T(8,128)(2,1)S(1)}, u32[]{:S(2)}, u32[]{:S(2)}) collective-permute-start(bf16[32,640]{1,0:T(8,128)(2,1)} %get-tuple-element.19.refs_0_), channel_id=1, source_target_pairs={{0,6},{1,7},{2,4},{3,5},{4,2},{5,3},{6,0},{7,1},{8,14},{9,15},{10,... | collective-permute-start | bytes 122888 | tf_op jit(solution)/shard_map/ppermute | solution.py:319
  7.3 5.2 %collective-permute-start.1 = (bf16[32,640]{1,0:T(8,128)(2,1)}, bf16[32,640]{1,0:T(8,128)(2,1)S(1)}, u32[]{:S(2)}, u32[]{:S(2)}) collective-permute-start(bf16[32,640]{1,0:T(8,128)(2,1)} %get-tuple-element.19.refs_0_), channel_id=1, source_target_pairs={{0,4},{1,5},{2,6},{3,7},{4,0},{5,1},{6,2},{7,3},{8,12},{9,13},{10,... | collective-permute-start | bytes 122888 | tf_op jit(solution)/shard_map/ppermute | solution.py:319
  7.3 5.3 %collective-permute-start = (bf16[32,640]{1,0:T(8,128)(2,1)}, bf16[32,640]{1,0:T(8,128)(2,1)S(1)}, u32[]{:S(2)}, u32[]{:S(2)}) collective-permute-start(bf16[32,640]{1,0:T(8,128)(2,1)} %get-tuple-element.19.refs_0_), channel_id=1, source_target_pairs={{0,2},{1,3},{2,0},{3,1},{4,6},{5,7},{6,4},{7,5},{8,10},{9,11},{10,... | collective-permute-start | bytes 122888 | tf_op jit(solution)/shard_map/ppermute | solution.py:319
  7.9 4.6 %collective-permute-start.4 = (s32[16,128]{1,0:T(8,128)}, s32[16,128]{1,0:T(8,128)S(1)}, u32[]{:S(2)}, u32[]{:S(2)}) collective-permute-start(s32[16,128]{1,0:T(8,128)} %get-tuple-element.21.refs_6_), channel_id=1, source_target_pairs={{0,1},{1,0},{2,3},{3,2},{4,5},{5,4},{6,7},{7,6},{8,9},{9,8},{10,11... | collective-permute-start | bytes 24584 | tf_op jit(solution)/shard_map/ppermute | solution.py:319
  7.9 1.6 %copy-start = (bf16[2048,512]{1,0:T(8,128)(2,1)S(1)}, bf16[2048,512]{1,0:T(8,128)(2,1)}, u32[]{:S(2)}) copy-start(bf16[2048,512]{1,0:T(8,128)(2,1)} %memory_ref.1) | copy-start | bytes 6291460
  11.5 1.3 %copy-start.1 = (bf16[2048,512]{1,0:T(8,128)(2,1)}, bf16[2048,512]{1,0:T(8,128)(2,1)S(1)}, u32[]{:S(2)}) copy-start(bf16[2048,512]{1,0:T(8,128)(2,1)S(1)} %get-tuple-element.20.refs_4_.refs_0_) | copy-start | bytes 6291460
  11.5 1.3 %copy-start.5 = (bf16[32,640]{1,0:T(8,128)(2,1)S(1)}, bf16[32,640]{1,0:T(8,128)(2,1)}, u32[]{:S(2)}) copy-start(bf16[32,640]{1,0:T(8,128)(2,1)} %get-tuple-element.19.refs_0_) | copy-start | bytes 122884
  11.5 1.3 %copy-start.8 = (s32[16,128]{1,0:T(8,128)S(1)}, s32[16,128]{1,0:T(8,128)}, u32[]{:S(2)}) copy-start(s32[16,128]{1,0:T(8,128)} %get-tuple-element.21.refs_6_) | copy-start | bytes 24580
  12.9 7.7 %collective-permute-start.7 = (bf16[128,640]{1,0:T(8,128)(2,1)S(1)}, bf16[128,640]{1,0:T(8,128)(2,1)S(1)}, u32[]{:S(2)}, u32[]{:S(2)}) collective-permute-start(bf16[128,640]{1,0:T(8,128)(2,1)S(1)} %shard_map.96.rows_ref.refs_0_), channel_id=1, source_target_pairs={{0,24},{8,16},{16,8},{24,0},{1,25},{9,17},{17,9},{25,1},{2,26},{10... | collective-permute-start | bytes 491528 | tf_op jit(solution)/shard_map/ppermute | solution.py:317
  16.3 11.6 %collective-permute-start.6 = (bf16[128,640]{1,0:T(8,128)(2,1)S(1)}, bf16[128,640]{1,0:T(8,128)(2,1)S(1)}, u32[]{:S(2)}, u32[]{:S(2)}) collective-permute-start(bf16[128,640]{1,0:T(8,128)(2,1)S(1)} %shard_map.96.rows_ref.refs_0_), channel_id=1, source_target_pairs={{0,16},{8,24},{16,0},{24,8},{1,17},{9,25},{17,1},{25,9},{2,18},{10... | collective-permute-start | bytes 491528 | tf_op jit(solution)/shard_map/ppermute | solution.py:317
  16.9 14.4 %collective-permute-start.5 = (bf16[128,640]{1,0:T(8,128)(2,1)S(1)}, bf16[128,640]{1,0:T(8,128)(2,1)S(1)}, u32[]{:S(2)}, u32[]{:S(2)}) collective-permute-start(bf16[128,640]{1,0:T(8,128)(2,1)S(1)} %shard_map.96.rows_ref.refs_0_), channel_id=1, source_target_pairs={{0,8},{8,0},{16,24},{24,16},{1,9},{9,1},{17,25},{25,17},{2,10},{10... | collective-permute-start | bytes 491528 | tf_op jit(solution)/shard_map/ppermute | solution.py:317
  20.5 1.6 %copy-start.2 = (bf16[2048,512]{1,0:T(8,128)(2,1)S(1)}, bf16[2048,512]{1,0:T(8,128)(2,1)}, u32[]{:S(2)}) copy-start(bf16[2048,512]{1,0:T(8,128)(2,1)} %copy-done.1) | copy-start | bytes 6291460
  24.9 16.9 %collective-permute-start.8 = (bf16[128,1152]{1,0:T(8,128)(2,1)S(1)}, bf16[128,1152]{1,0:T(8,128)(2,1)S(1)}, u32[]{:S(2)}, u32[]{:S(2)}) collective-permute-start(bf16[128,1152]{1,0:T(8,128)(2,1)S(1)} %shard_map.97.refs_4_), channel_id=1, source_target_pairs={{0,24},{8,16},{16,8},{24,0},{1,25},{9,17},{17,9},{25,1},{2,26},{10... | collective-permute-start | bytes 884744 | tf_op jit(solution)/shard_map/ppermute | solution.py:317
  30.7 3.6 %copy-start.3 = (bf16[2048,512]{1,0:T(8,128)(2,1)S(1)}, bf16[2048,512]{1,0:T(8,128)(2,1)}, u32[]{:S(2)}) copy-start(bf16[2048,512]{1,0:T(8,128)(2,1)} %copy-done.1) | copy-start | bytes 6291460
  30.7 11.1 %collective-permute-start.9 = (bf16[128,1152]{1,0:T(8,128)(2,1)S(1)}, bf16[128,1152]{1,0:T(8,128)(2,1)S(1)}, u32[]{:S(2)}, u32[]{:S(2)}) collective-permute-start(bf16[128,1152]{1,0:T(8,128)(2,1)S(1)} %shard_map.98.refs_4_), channel_id=1, source_target_pairs={{0,16},{8,24},{16,0},{24,8},{1,17},{9,25},{17,1},{25,9},{2,18},{10... | collective-permute-start | bytes 884744 | tf_op jit(solution)/shard_map/ppermute | solution.py:317
  34.1 7.8 %collective-permute-start.10 = (bf16[128,1152]{1,0:T(8,128)(2,1)S(1)}, bf16[128,1152]{1,0:T(8,128)(2,1)S(1)}, u32[]{:S(2)}, u32[]{:S(2)}) collective-permute-start(bf16[128,1152]{1,0:T(8,128)(2,1)S(1)} %shard_map.99.refs_4_), channel_id=1, source_target_pairs={{0,8},{8,0},{16,24},{24,16},{1,9},{9,1},{17,25},{25,17},{2,10},{10... | collective-permute-start | bytes 884744 | tf_op jit(solution)/shard_map/ppermute | solution.py:317
  34.2 12.4 %copy-start.7 = (s32[16,128]{1,0:T(8,128)S(1)}, s32[16,128]{1,0:T(8,128)}, u32[]{:S(2)}) copy-start(s32[16,128]{1,0:T(8,128)} %get-tuple-element.31.labels_ref) | copy-start | bytes 24580
  34.2 12.4 %collective-permute-start.14 = (bf16[32,640]{1,0:T(8,128)(2,1)S(1)}, bf16[32,640]{1,0:T(8,128)(2,1)S(1)}, u32[]{:S(2)}, u32[]{:S(2)}) collective-permute-start(bf16[32,640]{1,0:T(8,128)(2,1)S(1)} %shard_map.103.refs_0_), channel_id=1, source_target_pairs={{0,1},{1,0},{2,3},{3,2},{4,5},{5,4},{6,7},{7,6},{8,9},{9,8},{10,11... | collective-permute-start | bytes 122888 | tf_op jit(solution)/shard_map/ppermute | solution.py:319
  37.1 14.3 %copy-start.4 = (f32[32,512]{1,0:T(8,128)S(1)}, f32[32,512]{1,0:T(8,128)}, u32[]{:S(2)}) copy-start(f32[32,512]{1,0:T(8,128)} %get-tuple-element.26.refs_4_) | copy-start | bytes 196612
  37.1 14.3 %copy-start.6 = (f32[32,128]{1,0:T(8,128)S(1)}, f32[32,128]{1,0:T(8,128)}, u32[]{:S(2)}) copy-start(f32[32,128]{1,0:T(8,128)} %get-tuple-element.27.refs_5_) | copy-start | bytes 49156
  42.1 6.3 %collective-permute-start.11 = (bf16[32,1152]{1,0:T(8,128)(2,1)S(1)}, bf16[32,1152]{1,0:T(8,128)(2,1)S(1)}, u32[]{:S(2)}, u32[]{:S(2)}) collective-permute-start(bf16[32,1152]{1,0:T(8,128)(2,1)S(1)} %get-tuple-element.23), channel_id=1, source_target_pairs={{0,6},{1,7},{2,4},{3,5},{4,2},{5,3},{6,0},{7,1},{8,14},{9,15},{10,... | collective-permute-start | bytes 221192 | tf_op jit(solution)/shard_map/ppermute | solution.py:319
  45.7 5.6 %collective-permute-start.12 = (bf16[32,1152]{1,0:T(8,128)(2,1)S(1)}, bf16[32,1152]{1,0:T(8,128)(2,1)S(1)}, u32[]{:S(2)}, u32[]{:S(2)}) collective-permute-start(bf16[32,1152]{1,0:T(8,128)(2,1)S(1)} %get-tuple-element.24), channel_id=1, source_target_pairs={{0,4},{1,5},{2,6},{3,7},{4,0},{5,1},{6,2},{7,3},{8,12},{9,13},{10,... | collective-permute-start | bytes 221192 | tf_op jit(solution)/shard_map/ppermute | solution.py:319
  45.7 5.7 %collective-permute-start.13 = (bf16[32,1152]{1,0:T(8,128)(2,1)S(1)}, bf16[32,1152]{1,0:T(8,128)(2,1)S(1)}, u32[]{:S(2)}, u32[]{:S(2)}) collective-permute-start(bf16[32,1152]{1,0:T(8,128)(2,1)S(1)} %get-tuple-element.25), channel_id=1, source_target_pairs={{0,2},{1,3},{2,0},{3,1},{4,6},{5,7},{6,4},{7,5},{8,10},{9,11},{10,... | collective-permute-start | bytes 221192 | tf_op jit(solution)/shard_map/ppermute | solution.py:319

commit v6 on v5

v6 whole, which is shorter than its diff:
```python
import functools
import math

import jax
import jax.numpy as jnp
from jax import lax
from jax.experimental import pallas as pl
from jax.experimental.pallas import tpu as pltpu
from jax.sharding import PartitionSpec as P

pos_scale = 2.0
neg_scale = 50.0
margin = 0.5
lanes = 128
log2e = math.log2(math.e)
vmem_bytes = 20 * 1024 * 1024
vmem_most = 56 * 1024 * 1024
f32 = jnp.float32
bf16 = jnp.bfloat16


def call(body, outs, *args, work=0, limit=vmem_bytes, **kw):
    return pl.pallas_call(
        body,
        out_shape=outs,
        compiler_params=pltpu.CompilerParams(vmem_limit_bytes=limit),
        cost_estimate=pl.CostEstimate(flops=work, bytes_accessed=0, transcendentals=0),
        **kw,
    )(*args)


def shaped(shape, dtype):
    return jax.ShapeDtypeStruct(shape, dtype)


def in_vmem(value):
    return pltpu.with_memory_space_constraint(value, pltpu.VMEM)


def rounded_up(value, unit):
    return (value + unit - 1) // unit * unit


def blocks_of(width):
    return width // lanes


def rows_as_lanes(parts, rows):
    row = lax.broadcasted_iota(jnp.int32, (rows, lanes), 0)
    out = jnp.zeros((rows, lanes), f32)
    for at, part in enumerate(parts):
        out = jnp.where(row == at, part, out)
    return out


def prepare_kernel(rows_ref, labels_ref, stored_ref, keep_ref, packed_ref, unit_ref, radius_ref, slot_ref, copy_ref):
    stored = stored_ref[...]
    slot_ref[...] = jnp.where(keep_ref[...] > 0, stored, -1)
    copy_ref[...] = stored
    rows = rows_ref[...].astype(f32)
    count, width = rows.shape
    radius = jnp.sqrt(jnp.sum(rows * rows, axis=1, keepdims=True) + 1e-06)
    unit = rows / radius
    unit_ref[...] = unit
    radius_ref[...] = jnp.broadcast_to(radius, radius_ref.shape)
    anchors = unit.astype(bf16)
    for at in range(blocks_of(width)):
        packed_ref[at * count : (at + 1) * count, :] = anchors[:, at * lanes : (at + 1) * lanes]
    row = jnp.concatenate([labels_ref[...].astype(f32), jnp.zeros((1, lanes - count), f32)], axis=1)
    high = jnp.floor(row * (1.0 / 256.0))
    tail = packed_ref.shape[0] - blocks_of(width) * count
    packed_ref[blocks_of(width) * count :, :] = rows_as_lanes([high, row - high * 256.0], tail).astype(bf16)


def diagonal(count):
    across = lax.broadcasted_iota(jnp.int32, (count, count), 1)
    down = lax.broadcasted_iota(jnp.int32, (count, count), 0)
    return across == down


def to_column(row):
    count = row.shape[1]
    spread = jnp.broadcast_to(row, (count, count))
    return jnp.sum(jnp.where(diagonal(count), spread, 0.0), axis=1, keepdims=True)


def to_row(column):
    count = column.shape[0]
    spread = jnp.broadcast_to(column, (count, count))
    return jnp.sum(jnp.where(diagonal(count), spread, 0.0), axis=0, keepdims=True)


def keys_kernel(memory_ref, keys_ref, *copy_refs):
    stored = memory_ref[...]
    rows = stored.astype(f32)
    radius = jnp.sqrt(jnp.sum(rows * rows, axis=1, keepdims=True) + 1e-06)
    keys_ref[...] = (rows / radius).astype(bf16)
    for copy_ref in copy_refs:
        copy_ref[...] = stored


def keys_of(memory, copies):
    slots, width = memory.shape
    block = math.gcd(512, slots)
    spec = pl.BlockSpec((block, width), lambda i: (i, 0))
    return call(
        keys_kernel,
        [shaped((slots, width), bf16)] * (1 + copies),
        memory,
        grid=(slots // block,),
        in_specs=[spec],
        out_specs=[spec] * (1 + copies),
    )


def join_kernel(blocks, *refs):
    block_refs, out_ref = refs[:blocks], refs[-1]
    size = block_refs[0].shape[0]
    for place, ref in enumerate(block_refs):
        out_ref[place * size : (place + 1) * size, :] = ref[...]


def join(blocks, after):
    size, width = blocks[0].shape
    return call(
        functools.partial(join_kernel, len(blocks)),
        [shaped((size * len(blocks), width), blocks[0].dtype)],
        *blocks, *after,
        in_specs=[pl.BlockSpec(memory_space=pltpu.VMEM)] * len(blocks)
        + [pl.BlockSpec(memory_space=pl.ANY)] * len(after),
    )[0]


def other_keys_kernel(block, memory_ref, rows_ref, keys_ref, same_ref):
    same_ref[...] = rows_ref[...]

    @pl.loop(0, memory_ref.shape[0] // block)
    def _(i):
        part = pl.ds(pl.multiple_of(i * block, block), block)
        keys_ref[part, :] = normalized(memory_ref[part, :])


def other_keys(memory, rows):
    return call(
        functools.partial(other_keys_kernel, math.gcd(256, memory.shape[0])),
        [shaped(memory.shape, bf16), shaped(rows.shape, bf16)],
        memory, rows,
    )


def positions(step, count, slots, groups, line, cores):
    first = lax.rem(step, slots // count) * count
    crossing = lax.rem(step, cores)
    members = line * cores
    devices_all = groups * members
    grp = lax.axis_index("grp")
    dev = lax.axis_index("dev")
    target = grp * members + (dev ^ crossing)
    source = lax.rem(target + devices_all - lax.rem(step, devices_all), devices_all)
    source_grp = lax.div(source, members)
    source_line = lax.div(lax.rem(source, members), cores)
    return first, crossing, grp ^ source_grp, lax.div(dev, cores) ^ source_line


def pick_kernel(groups, sizes, step_ref, *refs):
    blocks_refs, out_ref = refs[:groups], refs[-1]
    rows = out_ref.shape[0]
    _, _, grp_place, line_place = positions(step_ref[0], *sizes)
    for place, ref in enumerate(blocks_refs):

        @pl.when(grp_place == place)
        def _():
            out_ref[...] = ref[pl.ds(pl.multiple_of(line_place * rows, 16), rows), :]


def pick(blocks, step, sizes, after):
    line = sizes[3]
    return call(
        functools.partial(pick_kernel, len(blocks), sizes),
        [shaped((blocks[0].shape[0] // line, lanes), bf16)],
        step, *blocks, *after,
        in_specs=[pl.BlockSpec(memory_space=pltpu.SMEM)]
        + [pl.BlockSpec(memory_space=pltpu.VMEM)] * len(blocks)
        + [pl.BlockSpec(memory_space=pl.ANY)] * len(after),
    )[0]


def patch_kernel(choices, sizes, step_ref, stored_ref, labels_ref, *refs):
    moved_refs, (memory_ref, new_labels_ref, rows_ref, sem) = refs[:choices], refs[choices:]
    count, width = rows_ref.shape
    first, crossing, _, _ = positions(step_ref[0], *sizes)
    moved = moved_refs[0][...]
    for choice in range(1, choices):
        moved = jnp.where(crossing == choice, moved_refs[choice][...], moved)
    for at in range(blocks_of(width)):
        rows_ref[:, at * lanes : (at + 1) * lanes] = moved[at * count : (at + 1) * count, :]
    target = memory_ref.at[pl.ds(pl.multiple_of(first, count), count), :]
    copy = pltpu.make_async_copy(rows_ref, target, sem)
    copy.start()
    digits = moved[blocks_of(width) * count :, :].astype(f32)
    row = (digits[0:1, :] * 256.0 + digits[1:2, :]).astype(jnp.int32)
    old = labels_ref[...]
    turned = pltpu.roll(jnp.broadcast_to(row, old.shape), lax.rem(first, lanes), 1)
    slot = lax.broadcasted_iota(jnp.int32, old.shape, 0) * lanes + lax.broadcasted_iota(jnp.int32, old.shape, 1)
    new_labels_ref[...] = jnp.where((slot >= first) & (slot < first + count), turned, old)
    copy.wait()


def patch(stored, labels, choices, step, sizes):
    count, width = sizes[0], stored.shape[1]
    return call(
        functools.partial(patch_kernel, len(choices), sizes),
        [shaped(stored.shape, bf16), shaped(labels.shape, jnp.int32)],
        step, stored, labels, *choices,
        in_specs=[pl.BlockSpec(memory_space=pltpu.SMEM), pl.BlockSpec(memory_space=pl.ANY)]
        + [pl.BlockSpec(memory_space=pltpu.VMEM)] * (1 + len(choices)),
        out_specs=[pl.BlockSpec(memory_space=pl.ANY), pl.BlockSpec(memory_space=pltpu.VMEM)],
        scratch_shapes=[pltpu.VMEM((count, width), bf16), pltpu.SemaphoreType.DMA],
        input_output_aliases={1: 0},
    )


def split_digits(row):
    high = row.astype(bf16).astype(f32)
    return [high, row - high]


def sum_rows(size):
    return rounded_up(8 * (rounded_up(size, lanes) // lanes), 16)


def block_kernel(blocks, sides, chunk, count, *refs):
    rows_refs, keys_refs = refs[:blocks], refs[blocks : blocks + sides]
    label_refs = refs[blocks + sides : blocks + 2 * sides]
    out_refs = refs[-1 - blocks : -1]
    anchors_ref = refs[-1]
    slots, width = keys_refs[0].shape
    parts = blocks_of(width)
    packed = rows_refs[0].shape[0]
    members = packed // (parts * count + 16)
    size = members * count
    columns = []
    for block, ref in enumerate(rows_refs):
        for member in range(members):
            first = member * (parts * count + 16)
            to = block * size + member * count
            for at in range(parts):
                anchors_ref[to : to + count, at * lanes : (at + 1) * lanes] = ref[
                    first + at * count : first + (at + 1) * count, :
                ]
            digits = ref[first + parts * count : first + parts * count + 16, :].astype(f32)
            columns.append(to_column((digits[0:1, :] * 256.0 + digits[1:2, :])[:, :count]))
    labels = jnp.concatenate(columns, axis=0)
    anchors = anchors_ref[...]
    rows = blocks * size
    pos_sum = jnp.zeros((rows, 1), f32)
    neg_sum = jnp.zeros((rows, 1), f32)
    total = None
    chunks = [(side, slice(at, at + chunk)) for side in range(sides) for at in range(0, slots, chunk)]

    def scores_of(side, part):
        return lax.dot_general(
            anchors, keys_refs[side][part, :], (((1,), (1,)), ((), ())), preferred_element_type=f32
        )

    scores = scores_of(*chunks[0])
    for at, (side, part) in enumerate(chunks):
        following = scores_of(*chunks[at + 1]) if at + 1 < len(chunks) else None
        slot_labels = label_refs[side][:, part].astype(f32)
        neg_shift = jnp.where(slot_labels < 0.0, -1e30, -neg_scale * margin * log2e)
        same = labels == slot_labels
        slope = jnp.where(same, -pos_scale * log2e, neg_scale * log2e)
        shift = jnp.where(same, pos_scale * margin * log2e, neg_shift)
        term = jnp.exp2(scores * slope + shift)
        pos = jnp.where(same, term, 0.0)
        neg = jnp.where(same, 0.0, term)
        pos_sum += jnp.sum(pos, axis=1, keepdims=True)
        neg_sum += jnp.sum(neg, axis=1, keepdims=True)
        weights = jnp.concatenate([neg.astype(bf16), pos.astype(bf16)], axis=0)
        more = jnp.dot(weights, keys_refs[side][part, :], preferred_element_type=f32)
        total = more if total is None else total + more
        scores = following
    floats = anchors.astype(f32)
    sums = [pos_sum, neg_sum]
    for which in range(2):
        value = total[which * rows : (which + 1) * rows, :]
        along = jnp.sum(value * floats, axis=1, keepdims=True)
        sums.append(along)
        rest = value - along * floats
        for block, ref in enumerate(out_refs):
            for at in range(parts):
                first = (which * parts + at) * size
                ref[first : first + size, :] = rest[
                    block * size : (block + 1) * size, at * lanes : (at + 1) * lanes
                ].astype(ref.dtype)
    for block, ref in enumerate(out_refs):
        lines = []
        for first in range(0, size, lanes):
            last = min(first + lanes, size)
            for value in sums:
                row = to_row(value[block * size + first : block * size + last])
                if last - first < lanes:
                    row = jnp.concatenate([row, jnp.zeros((1, lanes - last + first), f32)], axis=1)
                lines += split_digits(row)
        first = 2 * parts * size
        ref[first:, :] = rows_as_lanes(lines, ref.shape[0] - first).astype(ref.dtype)


def block_sums(blocks, keys, labels, count, dtype, after):
    slots, width = keys[0].shape
    parts = blocks_of(width)
    size = blocks[0].shape[0] // (parts * count + 16) * count
    return call(
        functools.partial(block_kernel, len(blocks), len(keys), math.gcd(1024, slots), count),
        [shaped((2 * parts * size + sum_rows(size), lanes), dtype)] * len(blocks),
        *blocks, *[in_vmem(k) for k in keys], *labels, *after,
        work=12 * size * len(blocks) * slots * len(keys) * width,
        in_specs=[pl.BlockSpec(memory_space=pltpu.VMEM)] * (len(blocks) + 2 * len(keys))
        + [pl.BlockSpec(memory_space=pl.ANY)] * len(after),
        scratch_shapes=[pltpu.VMEM((len(blocks) * size, width), bf16)],
    )


def add_kernel(arrived, size, count, *refs):
    in_refs, out_refs = refs[: 1 + arrived], refs[-(size // count) :]
    columns = (in_refs[0].shape[0] - sum_rows(size)) // size

    def total(first, rows):
        value = in_refs[0][first : first + rows, :]
        for ref in in_refs[1:]:
            value = value + ref[first : first + rows, :].astype(f32)
        return value

    sums = total(columns * size, sum_rows(size))
    for block, ref in enumerate(out_refs):
        for at in range(columns):
            part = total(at * size + block * count, count)
            ref[at * count : (at + 1) * count, :] = part.astype(ref.dtype)
        group, lane = divmod(block * count, lanes)
        lines = []
        for which in range(4):
            row = 8 * group + 2 * which
            lines += split_digits(sums[row : row + 1, :] + sums[row + 1 : row + 2, :])
        packed = rows_as_lanes(lines, ref.shape[0] - columns * count)
        if lane:
            packed = pltpu.roll(packed, lanes - lane, 1)
        ref[columns * count :, :] = packed.astype(ref.dtype)


def add(held, arrived, size, count, columns, after):
    shape = (columns * count + sum_rows(count), lanes)
    outs = [shaped(shape, f32 if b == 0 else bf16) for b in range(size // count)]
    return call(
        functools.partial(add_kernel, len(arrived), size, count),
        outs,
        held, *arrived, *after,
        in_specs=[pl.BlockSpec(memory_space=pltpu.VMEM)] * (1 + len(arrived))
        + [pl.BlockSpec(memory_space=pl.ANY)] * len(after),
    )


def finish_kernel(arrived, *refs):
    held_ref, arrived_refs = refs[0], refs[1 : 1 + arrived]
    unit_ref, radius_ref, grad_ref, loss_ref = refs[1 + arrived :]
    count, width = unit_ref.shape
    parts = blocks_of(width)
    total = held_ref[...]
    for ref in arrived_refs:
        total = total + ref[...].astype(f32)
    sums = []
    for which in range(4):
        row = 2 * parts * count + 2 * which
        sums.append((total[row : row + 1, :] + total[row + 1 : row + 2, :])[:, :count])
    pos, neg = sums[:2]
    loss_ref[...] = jnp.log(1.0 + pos) / pos_scale + jnp.log(1.0 + neg) / neg_scale
    pos, neg, push_along, pull_along = [to_column(row) for row in sums]
    unit = unit_ref[...]
    anchors = unit.astype(bf16).astype(f32)
    push, pull = [
        jnp.concatenate([total[(first + at) * count : (first + at + 1) * count, :] for at in range(parts)], axis=1)
        for first in (0, parts)
    ]
    push = push + push_along * anchors
    pull = pull + pull_along * anchors
    grad_unit = push / (1.0 + neg) - pull / (1.0 + pos)
    along = jnp.sum(unit * grad_unit, axis=1, keepdims=True)
    grad_ref[...] = (grad_unit - unit * along) / radius_ref[:, :1]


def per_device(batch_rows, batch_labels, memory, memory_labels, keep_bits, step_index):
    groups = lax.axis_size("grp")
    members = lax.axis_size("dev")
    cores = 2 if members % 2 == 0 else 1
    line = members // cores
    count, width = batch_rows.shape
    slots = memory.shape[0]

    def exchange(value, axis, step):
        if axis == "grp":
            return lax.ppermute(value, "grp", [(i, i ^ step) for i in range(groups)])
        jump = step * cores if axis == "line" else step
        return lax.ppermute(value, "dev", [(i, i ^ jump) for i in range(members)])

    folded = (slots // lanes, lanes)
    parts = blocks_of(width)
    packed, unit, radius, slot_labels, copied_labels = call(
        prepare_kernel,
        [
            pltpu.VMEM((parts * count + 16, lanes), bf16),
            pltpu.VMEM((count, width), f32),
            pltpu.VMEM((count, lanes), f32),
            pltpu.VMEM(folded, jnp.int32),
            pltpu.VMEM(folded, jnp.int32),
        ],
        batch_rows, batch_labels.reshape(1, count), memory_labels.reshape(folded), keep_bits.reshape(folded),
        limit=vmem_most,
    )

    labels = [slot_labels] + [exchange(slot_labels, "core", s) for s in range(1, cores)]
    memories = [memory] + [exchange(memory, "core", s) for s in range(1, cores)]
    own_keys, copied = keys_of(memory, 1)
    keys = [own_keys] + [keys_of(value, 0)[0] for value in memories[1:]]

    near = [packed] + [None] * (line - 1)
    for s in range(line - 1, 0, -1):
        near[s] = exchange(packed, "line", s)
    part = join(near, [*keys, *labels])
    labels = [value.reshape(1, slots) for value in labels]
    blocks = [part] + [None] * (groups - 1)
    for s in range(groups - 1, 0, -1):
        blocks[s] = exchange(part, "grp", s)

    size = count * line
    arrived, after = [], []
    places = list(range(groups - 1, 0, -1))
    while places:
        now = places[:1] if not after else places[:2]
        places = places[len(now) :]
        after = block_sums([blocks[s] for s in now], keys, labels, count, bf16, after)
        arrived += [exchange(value, "grp", s) for s, value in zip(now, after)]
    held = block_sums([part], keys, labels, count, f32, after)[0]
    sizes = (count, slots, groups, line, cores)
    moved = pick(blocks, step_index, sizes, after)
    choices = [moved] + [exchange(moved, "core", s) for s in range(1, cores)]

    sums, *others = add(held, arrived, size, count, 2 * parts, choices)
    arrived = [exchange(others[s - 1], "line", s) for s in range(line - 1, 0, -1)]
    grad_batch, loss = call(
        functools.partial(finish_kernel, len(arrived)),
        [shaped((count, width), f32), shaped((1, count), f32)],
        sums, *arrived, unit, radius,
    )

    new_memory, new_labels = patch(copied, copied_labels, choices, step_index, sizes)
    return (grad_batch, loss.reshape(count), new_memory, new_labels.reshape(slots))


def solution(mesh):
    placed = (
        P(("grp", "dev"), None),
        P(("grp", "dev")),
        P(("grp", "dev"), None),
        P(("grp", "dev")),
        P(("grp", "dev")),
        P(),
    )
    return jax.shard_map(
        per_device,
        mesh=mesh,
        in_specs=placed,
        out_specs=(
            P(("grp", "dev"), None),
            P(("grp", "dev")),
            P(("grp", "dev"), None),
            P(("grp", "dev")),
        ),
        check_vma=False,
    )
```

time: 52.6 us -> 47.6 us (0.905)
  local copies, waits for them, and re-layouts: 3.5 us -> 1.59 us
  Pallas kernels: 18.5 us -> 16.6 us
  waiting for transfers between devices: 11.1 us -> 10.3 us
    unnamed x18 -> x2, local copies, waits for them, and re-layouts: 3.5 us -> 1.59 us
    pallas_call x12 -> x11, Pallas kernels: 18.5 us -> 16.6 us  [call(): pl.pallas_call(body, out_shape=outs, compiler_params=pltpu.CompilerParams...]
    ppermute x6, waiting for transfers between devices: 8.03 us -> 7.09 us  [exchange(): return lax.ppermute(value, 'grp', [(i, i ^ step) for i in range(groups)])]
  transfers between devices with their start and end apart: 15 -> 15, of which waited for: 4 -> 5; matrix products, arithmetic and copies ran while one was open for 0% -> 0% of each run, Pallas kernels for 34% -> 33%
where the time goes in v6:
time: 47.6 us; the launch traced here: 47.4 us
  starting transfers between devices  17.5 us (37%)
  Pallas kernels  16.6 us (35%)
  waiting for transfers between devices  10.3 us (22%)
  local copies, waits for them, and re-layouts  1.59 us (3%)
  between operations  1.39 us (3%)
    pallas_call x11, Pallas kernels, call(): pl.pallas_call(body, out_shape=outs, compiler_params=pltpu.CompilerParams...  16.6 us
    ppermute x9, starting transfers between devices, exchange(): return lax.ppermute(value, 'dev', [(i, i ^ jump) for i in range(members)])  10.3 us
    ppermute x6, starting transfers between devices, exchange(): return lax.ppermute(value, 'grp', [(i, i ^ step) for i in range(groups)])  7.24 us
    ppermute x6, waiting for transfers between devices, exchange(): return lax.ppermute(value, 'grp', [(i, i ^ step) for i in range(groups)])  7.09 us
    ppermute x9, waiting for transfers between devices, exchange(): return lax.ppermute(value, 'dev', [(i, i ^ jump) for i in range(members)])  3.2 us
    unnamed x2, local copies, waits for them, and re-layouts  1.59 us
  transfers between devices with their start and end apart: 15, of which 5 were waited for; matrix products, arithmetic and copies ran while one was open for 0% of the time, Pallas kernels for 33%

profile of v6, /device:TPU:0, one launch (start us, length us, event | category | flops | bytes accessed | tf_op | source)
XLA Modules:
  0.0 47.4 jit_solution(10753537897263570061)
XLA Ops:
  0.6 0.5 %collective-permute-start.3 = (bf16[2048,512]{1,0:T(8,128)(2,1)}, bf16[2048,512]{1,0:T(8,128)(2,1)S(1)}, u32[]{:S(2)}, u32[]{:S(2)}) collective-permute-start(bf16[2048,512]{1,0:T(8,128)(2,1)} %memory_ref.1), channel_id=1, source_target_pairs={{0,1},{1,0},{2,3},{3,2},{4,5},{5,4},{6,7},{7,6},{8,9},{9,8},{10,11... | collective-permute-start | bytes 6291464 | tf_op jit(solution)/shard_map/ppermute | solution.py:402
  1.1 0.9 %shard_map.93 = (bf16[144,128]{1,0:T(8,128)(2,1)S(1)}, f32[32,512]{1,0:T(8,128)S(1)}, f32[32,128]{1,0:T(8,128)S(1)}, s32[16,128]{1,0:T(8,128)S(1)}, s32[16,128]{1,0:T(8,128)S(1)}) custom-call(bf16[32,512]{1,0:T(8,128)(2,1)} %rows_ref.1, s32[1,32]{1,0:T(1,128)} %bitcast.15, s32[16,128]{1,0:T(8,128)} %bitcast.13, s32[16,128]{1,0:T(8,128)} %bitcast.14), custom_call_target="tpu_custom_call" | custom-call | tf_op jit(solution)/shard_map/pallas_call | solution.py:23
  2.0 4.7 %collective-permute-start.2 = (bf16[144,128]{1,0:T(8,128)(2,1)S(1)}, bf16[144,128]{1,0:T(8,128)(2,1)S(1)}, u32[]{:S(2)}, u32[]{:S(2)}) collective-permute-start(bf16[144,128]{1,0:T(8,128)(2,1)S(1)} %get-tuple-element.21.refs_0_), channel_id=1, source_target_pairs={{0,6},{1,7},{2,4},{3,5},{4,2},{5,3},{6,0},{7,1},{8,14},{9,15},{10,... | collective-permute-start | bytes 110600 | tf_op jit(solution)/shard_map/ppermute | solution.py:402
  6.7 0.0 collective-permute-start.1
  6.7 0.6 %collective-permute-start = (bf16[144,128]{1,0:T(8,128)(2,1)S(1)}, bf16[144,128]{1,0:T(8,128)(2,1)S(1)}, u32[]{:S(2)}, u32[]{:S(2)}) collective-permute-start(bf16[144,128]{1,0:T(8,128)(2,1)S(1)} %get-tuple-element.21.refs_0_), channel_id=1, source_target_pairs={{0,2},{1,3},{2,0},{3,1},{4,6},{5,7},{6,4},{7,5},{8,10},{9,11},{10,... | collective-permute-start | bytes 110600 | tf_op jit(solution)/shard_map/ppermute | solution.py:402
  7.4 0.0 collective-permute-start.4
  7.4 1.6 %copy-done = bf16[2048,512]{1,0:T(8,128)(2,1)S(1)} copy-done((bf16[2048,512]{1,0:T(8,128)(2,1)S(1)}, bf16[2048,512]{1,0:T(8,128)(2,1)}, u32[]{:S(2)}) %copy-start) | copy-done | bytes 2097176
  9.0 2.0 %shard_map.94 = (bf16[2048,512]{1,0:T(8,128)(2,1)S(1)}, bf16[2048,512]{1,0:T(8,128)(2,1)}) custom-call(bf16[2048,512]{1,0:T(8,128)(2,1)S(1)} %copy-done), custom_call_target="tpu_custom_call" | custom-call | tf_op jit(solution)/shard_map/pallas_call | solution.py:23
  10.9 1.0 %shard_map.95.refs_5_.refs_2_.refs_3_ = bf16[2048,512]{1,0:T(8,128)(2,1)S(1)} custom-call(bf16[2048,512]{1,0:T(8,128)(2,1)S(1)} %collective-permute-done.3.memory_ref), custom_call_target="tpu_custom_call" | custom-call | tf_op jit(solution)/shard_map/pallas_call | solution.py:23
  11.9 0.0 collective-permute-done.2.refs_3_
  11.9 0.0 collective-permute-done.1.refs_2_
  12.0 2.7 %collective-permute-start.7 = (bf16[576,128]{1,0:T(8,128)(2,1)S(1)}, bf16[576,128]{1,0:T(8,128)(2,1)S(1)}, u32[]{:S(2)}, u32[]{:S(2)}) collective-permute-start(bf16[576,128]{1,0:T(8,128)(2,1)S(1)} %shard_map.96.refs_0_), channel_id=1, source_target_pairs={{0,24},{8,16},{16,8},{24,0},{1,25},{9,17},{17,9},{25,1},{2,26},{10... | collective-permute-start | bytes 442376 | tf_op jit(solution)/shard_map/ppermute | solution.py:400
  15.3 0.6 %collective-permute-start.6 = (bf16[576,128]{1,0:T(8,128)(2,1)S(1)}, bf16[576,128]{1,0:T(8,128)(2,1)S(1)}, u32[]{:S(2)}, u32[]{:S(2)}) collective-permute-start(bf16[576,128]{1,0:T(8,128)(2,1)S(1)} %shard_map.96.refs_0_), channel_id=1, source_target_pairs={{0,8},{8,0},{16,24},{24,16},{1,9},{9,1},{17,25},{25,17},{2,10},{10... | collective-permute-start | bytes 442376 | tf_op jit(solution)/shard_map/ppermute | solution.py:400
  15.9 0.4 collective-permute-start.5
  16.3 3.3 %collective-permute-done.7.refs_0_.refs_3_ = bf16[576,128]{1,0:T(8,128)(2,1)S(1)} collective-permute-done((bf16[576,128]{1,0:T(8,128)(2,1)S(1)}, bf16[576,128]{1,0:T(8,128)(2,1)S(1)}, u32[]{:S(2)}, u32[]{:S(2)}) %collective-permute-start.7) | collective-permute-done | bytes 147488 | tf_op jit(solution)/shard_map/ppermute | solution.py:400
  19.6 2.9 %shard_map.97.refs_6_ = bf16[1040,128]{1,0:T(8,128)(2,1)S(1)} custom-call(bf16[576,128]{1,0:T(8,128)(2,1)S(1)} %collective-permute-done.7.refs_0_.refs_3_, bf16[2048,512]{1,0:T(8,128)(2,1)S(1)} %get-tuple-element.22.refs_4_.refs_1_.refs_2_, bf16[2048,512]{1,0:T(8,128)(2,1)S(1)} %shard_map.95.refs_5_.refs_2_.refs_3_, s32[1,2048]{1,0:T(1,128)S(1)} %bitcast.7, ...), custom_call_target="tpu_custom_call" | custom-call | flops 3221225472 | tf_op jit(solution)/shard_map/pallas_call | solution.py:23
  22.5 2.7 %collective-permute-start.8 = (bf16[1040,128]{1,0:T(8,128)(2,1)S(1)}, bf16[1040,128]{1,0:T(8,128)(2,1)S(1)}, u32[]{:S(2)}, u32[]{:S(2)}) collective-permute-start(bf16[1040,128]{1,0:T(8,128)(2,1)S(1)} %shard_map.97.refs_6_), channel_id=1, source_target_pairs={{0,24},{8,16},{16,8},{24,0},{1,25},{9,17},{17,9},{25,1},{2,26},{10... | collective-permute-start | bytes 798728 | tf_op jit(solution)/shard_map/ppermute | solution.py:400
  25.2 4.6 %shard_map.98 = (bf16[1040,128]{1,0:T(8,128)(2,1)S(1)}, bf16[1040,128]{1,0:T(8,128)(2,1)S(1)}) custom-call(bf16[576,128]{1,0:T(8,128)(2,1)S(1)} %collective-permute-done.5.refs_0_.refs_2_, bf16[576,128]{1,0:T(8,128)(2,1)S(1)} %collective-permute-done.6.refs_1_, bf16[2048,512]{1,0:T(8,128)(2,1)S(1)} %get-tuple-element.22.refs_4_.refs_1_.refs_2_, ...), custom_call_target="tpu_custom_call" | custom-call | flops 6442450944 | tf_op jit(solution)/shard_map/pallas_call | solution.py:23
  29.9 0.6 %collective-permute-start.9 = (bf16[1040,128]{1,0:T(8,128)(2,1)S(1)}, bf16[1040,128]{1,0:T(8,128)(2,1)S(1)}, u32[]{:S(2)}, u32[]{:S(2)}) collective-permute-start(bf16[1040,128]{1,0:T(8,128)(2,1)S(1)} %get-tuple-element.24.refs_5_.refs_4_), channel_id=1, source_target_pairs={{0,16},{8,24},{16,0},{24,8},{1,17},{9,25},{17,1},{25,9},{2,18},{10... | collective-permute-start | bytes 798728 | tf_op jit(solution)/shard_map/ppermute | solution.py:400
  30.4 0.4 collective-permute-start.10
  30.8 0.0 collective-permute-start.11
  30.8 2.9 %shard_map.99.refs_0_ = f32[1040,128]{1,0:T(8,128)S(1)} custom-call(bf16[576,128]{1,0:T(8,128)(2,1)S(1)} %shard_map.96.refs_0_, bf16[2048,512]{1,0:T(8,128)(2,1)S(1)} %get-tuple-element.22.refs_4_.refs_1_.refs_2_, bf16[2048,512]{1,0:T(8,128)(2,1)S(1)} %shard_map.95.refs_5_.refs_2_.refs_3_, s32[1,2048]{1,0:T(1,128)S(1)} %bitcast.9, s32[1,2048]{1,0:T(1,128)S(1)} %bitcast.12, ...), custom_call_target="tpu_custom_call" | custom-call | flops 3221225472 | tf_op jit(solution)/shard_map/pallas_call | solution.py:23
  33.8 0.0 collective-permute-done.11.refs_5_.refs_1_
  33.8 3.5 %collective-permute-done.9.refs_2_ = bf16[1040,128]{1,0:T(8,128)(2,1)S(1)} collective-permute-done((bf16[1040,128]{1,0:T(8,128)(2,1)S(1)}, bf16[1040,128]{1,0:T(8,128)(2,1)S(1)}, u32[]{:S(2)}, u32[]{:S(2)}) %collective-permute-start.9) | collective-permute-done | bytes 266272 | tf_op jit(solution)/shard_map/ppermute | solution.py:400
  37.3 0.3 collective-permute-done.10.refs_3_
  37.5 0.1 shard_map.101
  37.7 3.7 %collective-permute-start.12 = (bf16[272,128]{1,0:T(8,128)(2,1)S(1)}, bf16[272,128]{1,0:T(8,128)(2,1)S(1)}, u32[]{:S(2)}, u32[]{:S(2)}) collective-permute-start(bf16[272,128]{1,0:T(8,128)(2,1)S(1)} %get-tuple-element.27), channel_id=1, source_target_pairs={{0,6},{1,7},{2,4},{3,5},{4,2},{5,3},{6,0},{7,1},{8,14},{9,15},{10,... | collective-permute-start | bytes 208904 | tf_op jit(solution)/shard_map/ppermute | solution.py:402
  41.3 0.8 %collective-permute-start.14 = (bf16[272,128]{1,0:T(8,128)(2,1)S(1)}, bf16[272,128]{1,0:T(8,128)(2,1)S(1)}, u32[]{:S(2)}, u32[]{:S(2)}) collective-permute-start(bf16[272,128]{1,0:T(8,128)(2,1)S(1)} %get-tuple-element.29), channel_id=1, source_target_pairs={{0,2},{1,3},{2,0},{3,1},{4,6},{5,7},{6,4},{7,5},{8,10},{9,11},{10,... | collective-permute-start | bytes 208904 | tf_op jit(solution)/shard_map/ppermute | solution.py:402
  42.1 1.2 %shard_map.103 = (bf16[2048,512]{1,0:T(8,128)(2,1)}, s32[16,128]{1,0:T(8,128)}) custom-call(s32[1]{0:T(128)S(6)} %copy.12.step_ref, bf16[2048,512]{1,0:T(8,128)(2,1)} %get-tuple-element.34.stored_ref, s32[16,128]{1,0:T(8,128)S(1)} %get-tuple-element.35.labels_ref, bf16[144,128]{1,0:T(8,128)(2,1)S(1)} %shard_map.100.refs_4_.refs_0_, ...), custom_call_target="tpu_custom_call", output_to_operand_aliasing={{0}: (1, {})} | custom-call | tf_op jit(solution)/shard_map/pallas_call | solution.py:23
  43.4 0.8 %collective-permute-done.12.refs_1_ = bf16[272,128]{1,0:T(8,128)(2,1)S(1)} collective-permute-done((bf16[272,128]{1,0:T(8,128)(2,1)S(1)}, bf16[272,128]{1,0:T(8,128)(2,1)S(1)}, u32[]{:S(2)}, u32[]{:S(2)}) %collective-permute-start.12) | collective-permute-done | bytes 69664 | tf_op jit(solution)/shard_map/ppermute | solution.py:402
  44.1 2.4 %collective-permute-done.13.refs_2_ = bf16[272,128]{1,0:T(8,128)(2,1)S(1)} collective-permute-done((bf16[272,128]{1,0:T(8,128)(2,1)S(1)}, bf16[272,128]{1,0:T(8,128)(2,1)S(1)}, u32[]{:S(2)}, u32[]{:S(2)}) %collective-permute-start.13) | collective-permute-done | bytes 69664 | tf_op jit(solution)/shard_map/ppermute | solution.py:402
  46.6 0.9 %shard_map.102 = (f32[32,512]{1,0:T(8,128)}, f32[1,32]{1,0:T(1,128)}) custom-call(f32[272,128]{1,0:T(8,128)S(1)} %get-tuple-element.26.refs_0_, bf16[272,128]{1,0:T(8,128)(2,1)S(1)} %collective-permute-done.12.refs_1_, bf16[272,128]{1,0:T(8,128)(2,1)S(1)} %collective-permute-done.13.refs_2_, bf16[272,128]{1,0:T(8,128)(2,1)S(1)} %collective-permute-done.14.refs_3_, ...), custom_call_target="tpu_custom_call" | custom-call | tf_op jit(solution)/shard_map/pallas_call | solution.py:23
  (11 shorter events, 0.0 us)
Async XLA Ops:
  0.6 10.3 %collective-permute-start.3 = (bf16[2048,512]{1,0:T(8,128)(2,1)}, bf16[2048,512]{1,0:T(8,128)(2,1)S(1)}, u32[]{:S(2)}, u32[]{:S(2)}) collective-permute-start(bf16[2048,512]{1,0:T(8,128)(2,1)} %memory_ref.1), channel_id=1, source_target_pairs={{0,1},{1,0},{2,3},{3,2},{4,5},{5,4},{6,7},{7,6},{8,9},{9,8},{10,11... | collective-permute-start | bytes 6291464 | tf_op jit(solution)/shard_map/ppermute | solution.py:402
  2.0 9.9 %collective-permute-start.2 = (bf16[144,128]{1,0:T(8,128)(2,1)S(1)}, bf16[144,128]{1,0:T(8,128)(2,1)S(1)}, u32[]{:S(2)}, u32[]{:S(2)}) collective-permute-start(bf16[144,128]{1,0:T(8,128)(2,1)S(1)} %get-tuple-element.21.refs_0_), channel_id=1, source_target_pairs={{0,6},{1,7},{2,4},{3,5},{4,2},{5,3},{6,0},{7,1},{8,14},{9,15},{10,... | collective-permute-start | bytes 110600 | tf_op jit(solution)/shard_map/ppermute | solution.py:402
  6.7 5.2 %collective-permute-start.1 = (bf16[144,128]{1,0:T(8,128)(2,1)S(1)}, bf16[144,128]{1,0:T(8,128)(2,1)S(1)}, u32[]{:S(2)}, u32[]{:S(2)}) collective-permute-start(bf16[144,128]{1,0:T(8,128)(2,1)S(1)} %get-tuple-element.21.refs_0_), channel_id=1, source_target_pairs={{0,4},{1,5},{2,6},{3,7},{4,0},{5,1},{6,2},{7,3},{8,12},{9,13},{10,... | collective-permute-start | bytes 110600 | tf_op jit(solution)/shard_map/ppermute | solution.py:402
  6.7 5.2 %collective-permute-start = (bf16[144,128]{1,0:T(8,128)(2,1)S(1)}, bf16[144,128]{1,0:T(8,128)(2,1)S(1)}, u32[]{:S(2)}, u32[]{:S(2)}) collective-permute-start(bf16[144,128]{1,0:T(8,128)(2,1)S(1)} %get-tuple-element.21.refs_0_), channel_id=1, source_target_pairs={{0,2},{1,3},{2,0},{3,1},{4,6},{5,7},{6,4},{7,5},{8,10},{9,11},{10,... | collective-permute-start | bytes 110600 | tf_op jit(solution)/shard_map/ppermute | solution.py:402
  7.4 4.6 %collective-permute-start.4 = (s32[16,128]{1,0:T(8,128)S(1)}, s32[16,128]{1,0:T(8,128)S(1)}, u32[]{:S(2)}, u32[]{:S(2)}) collective-permute-start(s32[16,128]{1,0:T(8,128)S(1)} %get-tuple-element.23.refs_6_), channel_id=1, source_target_pairs={{0,1},{1,0},{2,3},{3,2},{4,5},{5,4},{6,7},{7,6},{8,9},{9,8},{10,11... | collective-permute-start | bytes 24584 | tf_op jit(solution)/shard_map/ppermute | solution.py:402
  7.4 1.6 %copy-start = (bf16[2048,512]{1,0:T(8,128)(2,1)S(1)}, bf16[2048,512]{1,0:T(8,128)(2,1)}, u32[]{:S(2)}) copy-start(bf16[2048,512]{1,0:T(8,128)(2,1)} %memory_ref.1) | copy-start | bytes 6291460
  12.0 7.6 %collective-permute-start.7 = (bf16[576,128]{1,0:T(8,128)(2,1)S(1)}, bf16[576,128]{1,0:T(8,128)(2,1)S(1)}, u32[]{:S(2)}, u32[]{:S(2)}) collective-permute-start(bf16[576,128]{1,0:T(8,128)(2,1)S(1)} %shard_map.96.refs_0_), channel_id=1, source_target_pairs={{0,24},{8,16},{16,8},{24,0},{1,25},{9,17},{17,9},{25,1},{2,26},{10... | collective-permute-start | bytes 442376 | tf_op jit(solution)/shard_map/ppermute | solution.py:400
  15.3 9.9 %collective-permute-start.6 = (bf16[576,128]{1,0:T(8,128)(2,1)S(1)}, bf16[576,128]{1,0:T(8,128)(2,1)S(1)}, u32[]{:S(2)}, u32[]{:S(2)}) collective-permute-start(bf16[576,128]{1,0:T(8,128)(2,1)S(1)} %shard_map.96.refs_0_), channel_id=1, source_target_pairs={{0,8},{8,0},{16,24},{24,16},{1,9},{9,1},{17,25},{25,17},{2,10},{10... | collective-permute-start | bytes 442376 | tf_op jit(solution)/shard_map/ppermute | solution.py:400
  15.9 9.3 %collective-permute-start.5 = (bf16[576,128]{1,0:T(8,128)(2,1)S(1)}, bf16[576,128]{1,0:T(8,128)(2,1)S(1)}, u32[]{:S(2)}, u32[]{:S(2)}) collective-permute-start(bf16[576,128]{1,0:T(8,128)(2,1)S(1)} %shard_map.96.refs_0_), channel_id=1, source_target_pairs={{0,16},{8,24},{16,0},{24,8},{1,17},{9,25},{17,1},{25,9},{2,18},{10... | collective-permute-start | bytes 442376 | tf_op jit(solution)/shard_map/ppermute | solution.py:400
  22.5 11.2 %collective-permute-start.8 = (bf16[1040,128]{1,0:T(8,128)(2,1)S(1)}, bf16[1040,128]{1,0:T(8,128)(2,1)S(1)}, u32[]{:S(2)}, u32[]{:S(2)}) collective-permute-start(bf16[1040,128]{1,0:T(8,128)(2,1)S(1)} %shard_map.97.refs_6_), channel_id=1, source_target_pairs={{0,24},{8,16},{16,8},{24,0},{1,25},{9,17},{17,9},{25,1},{2,26},{10... | collective-permute-start | bytes 798728 | tf_op jit(solution)/shard_map/ppermute | solution.py:400
  29.9 7.4 %collective-permute-start.9 = (bf16[1040,128]{1,0:T(8,128)(2,1)S(1)}, bf16[1040,128]{1,0:T(8,128)(2,1)S(1)}, u32[]{:S(2)}, u32[]{:S(2)}) collective-permute-start(bf16[1040,128]{1,0:T(8,128)(2,1)S(1)} %get-tuple-element.24.refs_5_.refs_4_), channel_id=1, source_target_pairs={{0,16},{8,24},{16,0},{24,8},{1,17},{9,25},{17,1},{25,9},{2,18},{10... | collective-permute-start | bytes 798728 | tf_op jit(solution)/shard_map/ppermute | solution.py:400
  30.4 7.1 %collective-permute-start.10 = (bf16[1040,128]{1,0:T(8,128)(2,1)S(1)}, bf16[1040,128]{1,0:T(8,128)(2,1)S(1)}, u32[]{:S(2)}, u32[]{:S(2)}) collective-permute-start(bf16[1040,128]{1,0:T(8,128)(2,1)S(1)} %get-tuple-element.25.refs_6_.refs_5_), channel_id=1, source_target_pairs={{0,8},{8,0},{16,24},{24,16},{1,9},{9,1},{17,25},{25,17},{2,10},{10... | collective-permute-start | bytes 798728 | tf_op jit(solution)/shard_map/ppermute | solution.py:400
  30.8 2.9 %collective-permute-start.11 = (bf16[144,128]{1,0:T(8,128)(2,1)S(1)}, bf16[144,128]{1,0:T(8,128)(2,1)S(1)}, u32[]{:S(2)}, u32[]{:S(2)}) collective-permute-start(bf16[144,128]{1,0:T(8,128)(2,1)S(1)} %shard_map.100.refs_4_.refs_0_), channel_id=1, source_target_pairs={{0,1},{1,0},{2,3},{3,2},{4,5},{5,4},{6,7},{7,6},{8,9},{9,8},{10,11... | collective-permute-start | bytes 110600 | tf_op jit(solution)/shard_map/ppermute | solution.py:402
  37.7 6.5 %collective-permute-start.12 = (bf16[272,128]{1,0:T(8,128)(2,1)S(1)}, bf16[272,128]{1,0:T(8,128)(2,1)S(1)}, u32[]{:S(2)}, u32[]{:S(2)}) collective-permute-start(bf16[272,128]{1,0:T(8,128)(2,1)S(1)} %get-tuple-element.27), channel_id=1, source_target_pairs={{0,6},{1,7},{2,4},{3,5},{4,2},{5,3},{6,0},{7,1},{8,14},{9,15},{10,... | collective-permute-start | bytes 208904 | tf_op jit(solution)/shard_map/ppermute | solution.py:402
  41.3 5.2 %collective-permute-start.13 = (bf16[272,128]{1,0:T(8,128)(2,1)S(1)}, bf16[272,128]{1,0:T(8,128)(2,1)S(1)}, u32[]{:S(2)}, u32[]{:S(2)}) collective-permute-start(bf16[272,128]{1,0:T(8,128)(2,1)S(1)} %get-tuple-element.28), channel_id=1, source_target_pairs={{0,4},{1,5},{2,6},{3,7},{4,0},{5,1},{6,2},{7,3},{8,12},{9,13},{10,... | collective-permute-start | bytes 208904 | tf_op jit(solution)/shard_map/ppermute | solution.py:402
  41.3 5.2 %collective-permute-start.14 = (bf16[272,128]{1,0:T(8,128)(2,1)S(1)}, bf16[272,128]{1,0:T(8,128)(2,1)S(1)}, u32[]{:S(2)}, u32[]{:S(2)}) collective-permute-start(bf16[272,128]{1,0:T(8,128)(2,1)S(1)} %get-tuple-element.29), channel_id=1, source_target_pairs={{0,2},{1,3},{2,0},{3,1},{4,6},{5,7},{6,4},{7,5},{8,10},{9,11},{10,... | collective-permute-start | bytes 208904 | tf_op jit(solution)/shard_map/ppermute | solution.py:402

commit v7 on v6

--- a/solution.py
+++ b/solution.py
@@ -53,7 +53,9 @@
     return out
 
 
-def prepare_kernel(rows_ref, labels_ref, stored_ref, keep_ref, packed_ref, unit_ref, radius_ref, slot_ref, copy_ref):
+def prepare_kernel(rows_ref, labels_ref, stored_ref, keep_ref, step_ref, *refs):
+    packed_ref, unit_ref, radius_ref, slot_ref, copy_ref, step_out_ref = refs
+    step_out_ref[...] = jnp.broadcast_to(step_ref[...], step_out_ref.shape)
     stored = stored_ref[...]
     slot_ref[...] = jnp.where(keep_ref[...] > 0, stored, -1)
     copy_ref[...] = stored
@@ -99,14 +101,14 @@
         copy_ref[...] = stored
 
 
-def keys_of(memory, copies):
+def keys_of(memory, copies, place):
     slots, width = memory.shape
     block = math.gcd(512, slots)
     spec = pl.BlockSpec((block, width), lambda i: (i, 0))
     return call(
         keys_kernel,
         [shaped((slots, width), bf16)] * (1 + copies),
-        memory,
+        pltpu.with_memory_space_constraint(memory, place),
         grid=(slots // block,),
         in_specs=[spec],
         out_specs=[spec] * (1 + copies),
@@ -162,10 +164,17 @@
     return first, crossing, grp ^ source_grp, lax.div(dev, cores) ^ source_line
 
 
+def read_step(step_ref, scalar_ref, sem):
+    copy = pltpu.make_async_copy(step_ref, scalar_ref, sem)
+    copy.start()
+    copy.wait()
+    return scalar_ref[0, 0]
+
+
 def pick_kernel(groups, sizes, step_ref, *refs):
-    blocks_refs, out_ref = refs[:groups], refs[-1]
+    blocks_refs, (out_ref, scalar_ref, sem) = refs[:groups], refs[-3:]
     rows = out_ref.shape[0]
-    _, _, grp_place, line_place = positions(step_ref[0], *sizes)
+    _, _, grp_place, line_place = positions(read_step(step_ref, scalar_ref, sem), *sizes)
     for place, ref in enumerate(blocks_refs):
 
         @pl.when(grp_place == place)
@@ -179,16 +188,17 @@
         functools.partial(pick_kernel, len(blocks), sizes),
         [shaped((blocks[0].shape[0] // line, lanes), bf16)],
         step, *blocks, *after,
-        in_specs=[pl.BlockSpec(memory_space=pltpu.SMEM)]
+        in_specs=[pl.BlockSpec(memory_space=pl.ANY)]
         + [pl.BlockSpec(memory_space=pltpu.VMEM)] * len(blocks)
         + [pl.BlockSpec(memory_space=pl.ANY)] * len(after),
+        scratch_shapes=[pltpu.SMEM((8, lanes), jnp.int32), pltpu.SemaphoreType.DMA],
     )[0]
 
 
 def patch_kernel(choices, sizes, step_ref, stored_ref, labels_ref, *refs):
-    moved_refs, (memory_ref, new_labels_ref, rows_ref, sem) = refs[:choices], refs[choices:]
+    moved_refs, (memory_ref, new_labels_ref, rows_ref, scalar_ref, sem) = refs[:choices], refs[choices:]
     count, width = rows_ref.shape
-    first, crossing, _, _ = positions(step_ref[0], *sizes)
+    first, crossing, _, _ = positions(read_step(step_ref, scalar_ref, sem), *sizes)
     moved = moved_refs[0][...]
     for choice in range(1, choices):
         moved = jnp.where(crossing == choice, moved_refs[choice][...], moved)
@@ -212,10 +222,14 @@
         functools.partial(patch_kernel, len(choices), sizes),
         [shaped(stored.shape, bf16), shaped(labels.shape, jnp.int32)],
         step, stored, labels, *choices,
-        in_specs=[pl.BlockSpec(memory_space=pltpu.SMEM), pl.BlockSpec(memory_space=pl.ANY)]
+        in_specs=[pl.BlockSpec(memory_space=pl.ANY)] * 2
         + [pl.BlockSpec(memory_space=pltpu.VMEM)] * (1 + len(choices)),
         out_specs=[pl.BlockSpec(memory_space=pl.ANY), pl.BlockSpec(memory_space=pltpu.VMEM)],
-        scratch_shapes=[pltpu.VMEM((count, width), bf16), pltpu.SemaphoreType.DMA],
+        scratch_shapes=[
+            pltpu.VMEM((count, width), bf16),
+            pltpu.SMEM((8, lanes), jnp.int32),
+            pltpu.SemaphoreType.DMA,
+        ],
         input_output_aliases={1: 0},
     )
 
@@ -403,7 +417,7 @@
 
     folded = (slots // lanes, lanes)
     parts = blocks_of(width)
-    packed, unit, radius, slot_labels, copied_labels = call(
+    packed, unit, radius, slot_labels, copied_labels, step = call(
         prepare_kernel,
         [
             pltpu.VMEM((parts * count + 16, lanes), bf16),
@@ -411,24 +425,28 @@
             pltpu.VMEM((count, lanes), f32),
             pltpu.VMEM(folded, jnp.int32),
             pltpu.VMEM(folded, jnp.int32),
+            pltpu.VMEM((8, lanes), jnp.int32),
         ],
         batch_rows, batch_labels.reshape(1, count), memory_labels.reshape(folded), keep_bits.reshape(folded),
+        step_index.reshape(1, 1),
         limit=vmem_most,
     )
 
     labels = [slot_labels] + [exchange(slot_labels, "core", s) for s in range(1, cores)]
     memories = [memory] + [exchange(memory, "core", s) for s in range(1, cores)]
-    own_keys, copied = keys_of(memory, 1)
-    keys = [own_keys] + [keys_of(value, 0)[0] for value in memories[1:]]
+    own_keys, copied = keys_of(memory, 1, pltpu.HBM)
+    keys = [own_keys] + [keys_of(value, 0, pltpu.VMEM)[0] for value in memories[1:]]
 
     near = [packed] + [None] * (line - 1)
     for s in range(line - 1, 0, -1):
         near[s] = exchange(packed, "line", s)
-    part = join(near, [*keys, *labels])
+    part = join(near, [own_keys, *labels])
     labels = [value.reshape(1, slots) for value in labels]
     blocks = [part] + [None] * (groups - 1)
     for s in range(groups - 1, 0, -1):
-        blocks[s] = exchange(part, "grp", s)
+        blocks[s] = exchange(part if s == groups - 1 else later, "grp", s)
+        if s == groups - 1:
+            later = join([part], keys[1:])
 
     size = count * line
     arrived, after = [], []
@@ -440,7 +458,7 @@
         arrived += [exchange(value, "grp", s) for s, value in zip(now, after)]
     held = block_sums([part], keys, labels, count, f32, after)[0]
     sizes = (count, slots, groups, line, cores)
-    moved = pick(blocks, step_index, sizes, after)
+    moved = pick(blocks, step, sizes, after)
     choices = [moved] + [exchange(moved, "core", s) for s in range(1, cores)]
 
     sums, *others = add(held, arrived, size, count, 2 * parts, choices)
@@ -451,7 +469,7 @@
         sums, *arrived, unit, radius,
     )
 
-    new_memory, new_labels = patch(copied, copied_labels, choices, step_index, sizes)
+    new_memory, new_labels = patch(copied, copied_labels, choices, step, sizes)
     return (grad_batch, loss.reshape(count), new_memory, new_labels.reshape(slots))
 
 

time: 47.6 us -> 47.6 us (level)
  Pallas kernels: 16.6 us -> 19.7 us
  waiting for transfers between devices: 10.3 us -> 8.55 us
  local copies, waits for them, and re-layouts: 1.59 us -> 0 us
    pallas_call x11 -> x12, Pallas kernels: 16.6 us -> 19.7 us  [call(): pl.pallas_call(body, out_shape=outs, compiler_params=pltpu.CompilerParams...]
    ppermute x6, waiting for transfers between devices: 7.09 us -> 5.44 us  [exchange(): return lax.ppermute(value, 'grp', [(i, i ^ step) for i in range(groups)])]
    unnamed x2 -> x0, local copies, waits for them, and re-layouts: 1.59 us -> none
  transfers between devices with their start and end apart: 15 -> 15, of which waited for: 5 -> 5; matrix products, arithmetic and copies ran while one was open for 0% -> 0% of each run, Pallas kernels for 33% -> 40%
where the time goes in v7:
time: 47.6 us; the launch traced here: 47.3 us
  Pallas kernels  19.7 us (41%)
  starting transfers between devices  17.7 us (37%)
  waiting for transfers between devices  8.55 us (18%)
  between operations  1.39 us (3%)
    pallas_call x12, Pallas kernels, call(): pl.pallas_call(body, out_shape=outs, compiler_params=pltpu.CompilerParams...  19.7 us
    ppermute x9, starting transfers between devices, exchange(): return lax.ppermute(value, 'dev', [(i, i ^ jump) for i in range(members)])  10.4 us
    ppermute x6, starting transfers between devices, exchange(): return lax.ppermute(value, 'grp', [(i, i ^ step) for i in range(groups)])  7.22 us
    ppermute x6, waiting for transfers between devices, exchange(): return lax.ppermute(value, 'grp', [(i, i ^ step) for i in range(groups)])  5.44 us
    ppermute x9, waiting for transfers between devices, exchange(): return lax.ppermute(value, 'dev', [(i, i ^ jump) for i in range(members)])  3.12 us
  transfers between devices with their start and end apart: 15, of which 5 were waited for; matrix products, arithmetic and copies ran while one was open for 0% of the time, Pallas kernels for 40%

profile of v7, /device:TPU:0, one launch (start us, length us, event | category | flops | bytes accessed | tf_op | source)
XLA Modules:
  0.0 47.3 jit_solution(8122886013760328266)
XLA Ops:
  0.6 0.5 %collective-permute-start.4 = (bf16[2048,512]{1,0:T(8,128)(2,1)}, bf16[2048,512]{1,0:T(8,128)(2,1)S(1)}, u32[]{:S(2)}, u32[]{:S(2)}) collective-permute-start(bf16[2048,512]{1,0:T(8,128)(2,1)} %memory_ref.1), channel_id=1, source_target_pairs={{0,1},{1,0},{2,3},{3,2},{4,5},{5,4},{6,7},{7,6},{8,9},{9,8},{10,11... | collective-permute-start | bytes 6291464 | tf_op jit(solution)/shard_map/ppermute | solution.py:416
  1.8 0.9 %shard_map.93 = (bf16[144,128]{1,0:T(8,128)(2,1)S(1)}, f32[32,512]{1,0:T(8,128)S(1)}, f32[32,128]{1,0:T(8,128)S(1)}, s32[16,128]{1,0:T(8,128)S(1)}, s32[16,128]{1,0:T(8,128)S(1)}, /*index=5*/s32[8,128]{1,0:T(8,128)S(1)}) custom-call(bf16[32,512]{1,0:T(8,128)(2,1)} %rows_ref.1, s32[1,32]{1,0:T(1,128)} %bitcast.17, s32[16,128]{1,0:T(8,128)} %bitcast.15, ...), custom_call_target="tpu_custom_call" | custom-call | tf_op jit(solution)/shard_map/pallas_call | solution.py:23
  2.7 4.7 %collective-permute-start.2 = (bf16[144,128]{1,0:T(8,128)(2,1)S(1)}, bf16[144,128]{1,0:T(8,128)(2,1)S(1)}, u32[]{:S(2)}, u32[]{:S(2)}) collective-permute-start(bf16[144,128]{1,0:T(8,128)(2,1)S(1)} %get-tuple-element.22.refs_0_), channel_id=1, source_target_pairs={{0,6},{1,7},{2,4},{3,5},{4,2},{5,3},{6,0},{7,1},{8,14},{9,15},{10,... | collective-permute-start | bytes 110600 | tf_op jit(solution)/shard_map/ppermute | solution.py:416
  7.4 0.0 collective-permute-start.1
  7.4 0.6 %collective-permute-start = (bf16[144,128]{1,0:T(8,128)(2,1)S(1)}, bf16[144,128]{1,0:T(8,128)(2,1)S(1)}, u32[]{:S(2)}, u32[]{:S(2)}) collective-permute-start(bf16[144,128]{1,0:T(8,128)(2,1)S(1)} %get-tuple-element.22.refs_0_), channel_id=1, source_target_pairs={{0,2},{1,3},{2,0},{3,1},{4,6},{5,7},{6,4},{7,5},{8,10},{9,11},{10,... | collective-permute-start | bytes 110600 | tf_op jit(solution)/shard_map/ppermute | solution.py:416
  8.0 0.0 collective-permute-start.3
  8.0 3.8 %shard_map.94 = (bf16[2048,512]{1,0:T(8,128)(2,1)S(1)}, bf16[2048,512]{1,0:T(8,128)(2,1)}) custom-call(bf16[2048,512]{1,0:T(8,128)(2,1)} %memory_ref.1), custom_call_target="tpu_custom_call" | custom-call | tf_op jit(solution)/shard_map/pallas_call | solution.py:23
  11.8 0.0 collective-permute-done.3.refs_6_
  11.8 0.0 collective-permute-done.2.refs_3_
  11.8 0.4 collective-permute-done.1.refs_2_
  12.2 0.0 collective-permute-done.refs_1_
  12.2 2.5 %collective-permute-start.7 = (bf16[576,128]{1,0:T(8,128)(2,1)S(1)}, bf16[576,128]{1,0:T(8,128)(2,1)S(1)}, u32[]{:S(2)}, u32[]{:S(2)}) collective-permute-start(bf16[576,128]{1,0:T(8,128)(2,1)S(1)} %shard_map.95.refs_0_), channel_id=1, source_target_pairs={{0,24},{8,16},{16,8},{24,0},{1,25},{9,17},{17,9},{25,1},{2,26},{10... | collective-permute-start | bytes 442376 | tf_op jit(solution)/shard_map/ppermute | solution.py:414
  14.8 1.0 %shard_map.96.refs_1_.refs_2_.refs_3_ = bf16[2048,512]{1,0:T(8,128)(2,1)S(1)} custom-call(bf16[2048,512]{1,0:T(8,128)(2,1)S(1)} %collective-permute-done.4.memory_ref), custom_call_target="tpu_custom_call" | custom-call | tf_op jit(solution)/shard_map/pallas_call | solution.py:23
  15.8 0.6 %collective-permute-start.6 = (bf16[576,128]{1,0:T(8,128)(2,1)S(1)}, bf16[576,128]{1,0:T(8,128)(2,1)S(1)}, u32[]{:S(2)}, u32[]{:S(2)}) collective-permute-start(bf16[576,128]{1,0:T(8,128)(2,1)S(1)} %shard_map.97), channel_id=1, source_target_pairs={{0,8},{8,0},{16,24},{24,16},{1,9},{9,1},{17,25},{25,17},{2,10},{10... | collective-permute-start | bytes 442376 | tf_op jit(solution)/shard_map/ppermute | solution.py:414
  16.4 0.5 %collective-permute-start.5 = (bf16[576,128]{1,0:T(8,128)(2,1)S(1)}, bf16[576,128]{1,0:T(8,128)(2,1)S(1)}, u32[]{:S(2)}, u32[]{:S(2)}) collective-permute-start(bf16[576,128]{1,0:T(8,128)(2,1)S(1)} %shard_map.97), channel_id=1, source_target_pairs={{0,16},{8,24},{16,0},{24,8},{1,17},{9,25},{17,1},{25,9},{2,18},{10... | collective-permute-start | bytes 442376 | tf_op jit(solution)/shard_map/ppermute | solution.py:414
  16.9 2.9 %collective-permute-done.7.refs_0_.refs_3_ = bf16[576,128]{1,0:T(8,128)(2,1)S(1)} collective-permute-done((bf16[576,128]{1,0:T(8,128)(2,1)S(1)}, bf16[576,128]{1,0:T(8,128)(2,1)S(1)}, u32[]{:S(2)}, u32[]{:S(2)}) %collective-permute-start.7) | collective-permute-done | bytes 147488 | tf_op jit(solution)/shard_map/ppermute | solution.py:414
  19.8 2.9 %shard_map.98.refs_6_ = bf16[1040,128]{1,0:T(8,128)(2,1)S(1)} custom-call(bf16[576,128]{1,0:T(8,128)(2,1)S(1)} %collective-permute-done.7.refs_0_.refs_3_, bf16[2048,512]{1,0:T(8,128)(2,1)S(1)} %get-tuple-element.23.refs_4_.refs_1_.refs_2_, bf16[2048,512]{1,0:T(8,128)(2,1)S(1)} %shard_map.96.refs_1_.refs_2_.refs_3_, s32[1,2048]{1,0:T(1,128)S(1)} %bitcast.9, ...), custom_call_target="tpu_custom_call" | custom-call | flops 3221225472 | tf_op jit(solution)/shard_map/pallas_call | solution.py:23
  22.7 2.6 %collective-permute-start.8 = (bf16[1040,128]{1,0:T(8,128)(2,1)S(1)}, bf16[1040,128]{1,0:T(8,128)(2,1)S(1)}, u32[]{:S(2)}, u32[]{:S(2)}) collective-permute-start(bf16[1040,128]{1,0:T(8,128)(2,1)S(1)} %shard_map.98.refs_6_), channel_id=1, source_target_pairs={{0,24},{8,16},{16,8},{24,0},{1,25},{9,17},{17,9},{25,1},{2,26},{10... | collective-permute-start | bytes 798728 | tf_op jit(solution)/shard_map/ppermute | solution.py:414
  25.3 4.7 %shard_map.99 = (bf16[1040,128]{1,0:T(8,128)(2,1)S(1)}, bf16[1040,128]{1,0:T(8,128)(2,1)S(1)}) custom-call(bf16[576,128]{1,0:T(8,128)(2,1)S(1)} %collective-permute-done.5.refs_0_.refs_2_, bf16[576,128]{1,0:T(8,128)(2,1)S(1)} %collective-permute-done.6.refs_1_, bf16[2048,512]{1,0:T(8,128)(2,1)S(1)} %get-tuple-element.23.refs_4_.refs_1_.refs_2_, ...), custom_call_target="tpu_custom_call" | custom-call | flops 6442450944 | tf_op jit(solution)/shard_map/pallas_call | solution.py:23
  30.0 0.6 %collective-permute-start.9 = (bf16[1040,128]{1,0:T(8,128)(2,1)S(1)}, bf16[1040,128]{1,0:T(8,128)(2,1)S(1)}, u32[]{:S(2)}, u32[]{:S(2)}) collective-permute-start(bf16[1040,128]{1,0:T(8,128)(2,1)S(1)} %get-tuple-element.25.refs_5_.refs_4_), channel_id=1, source_target_pairs={{0,16},{8,24},{16,0},{24,8},{1,17},{9,25},{17,1},{25,9},{2,18},{10... | collective-permute-start | bytes 798728 | tf_op jit(solution)/shard_map/ppermute | solution.py:414
  30.6 0.4 collective-permute-start.10
  31.0 0.6 %shard_map.101.refs_4_.refs_0_ = bf16[144,128]{1,0:T(8,128)(2,1)S(1)} custom-call(s32[8,128]{1,0:T(8,128)S(1)} %get-tuple-element.27.step_ref, bf16[576,128]{1,0:T(8,128)(2,1)S(1)} %shard_map.95.refs_0_, bf16[576,128]{1,0:T(8,128)(2,1)S(1)} %collective-permute-done.6.refs_1_, bf16[576,128]{1,0:T(8,128)(2,1)S(1)} %collective-permute-done.5.refs_0_.refs_2_, ...), custom_call_target="tpu_custom_call" | custom-call | tf_op jit(solution)/shard_map/pallas_call | solution.py:23
  31.6 0.1 collective-permute-start.11
  31.7 2.9 %shard_map.100.refs_0_ = f32[1040,128]{1,0:T(8,128)S(1)} custom-call(bf16[576,128]{1,0:T(8,128)(2,1)S(1)} %shard_map.95.refs_0_, bf16[2048,512]{1,0:T(8,128)(2,1)S(1)} %get-tuple-element.23.refs_4_.refs_1_.refs_2_, bf16[2048,512]{1,0:T(8,128)(2,1)S(1)} %shard_map.96.refs_1_.refs_2_.refs_3_, s32[1,2048]{1,0:T(1,128)S(1)} %bitcast.11, s32[1,2048]{1,0:T(1,128)S(1)} %bitcast.14, ...), custom_call_target="tpu_custom_call" | custom-call | flops 3221225472 | tf_op jit(solution)/shard_map/pallas_call | solution.py:23
  34.7 2.3 %collective-permute-done.9.refs_2_ = bf16[1040,128]{1,0:T(8,128)(2,1)S(1)} collective-permute-done((bf16[1040,128]{1,0:T(8,128)(2,1)S(1)}, bf16[1040,128]{1,0:T(8,128)(2,1)S(1)}, u32[]{:S(2)}, u32[]{:S(2)}) %collective-permute-start.9) | collective-permute-done | bytes 266272 | tf_op jit(solution)/shard_map/ppermute | solution.py:414
  37.0 0.2 collective-permute-done.10.refs_3_
  37.2 0.1 shard_map.102
  37.4 3.9 %collective-permute-start.12 = (bf16[272,128]{1,0:T(8,128)(2,1)S(1)}, bf16[272,128]{1,0:T(8,128)(2,1)S(1)}, u32[]{:S(2)}, u32[]{:S(2)}) collective-permute-start(bf16[272,128]{1,0:T(8,128)(2,1)S(1)} %get-tuple-element.29), channel_id=1, source_target_pairs={{0,6},{1,7},{2,4},{3,5},{4,2},{5,3},{6,0},{7,1},{8,14},{9,15},{10,... | collective-permute-start | bytes 208904 | tf_op jit(solution)/shard_map/ppermute | solution.py:416
  41.2 0.6 %collective-permute-start.14 = (bf16[272,128]{1,0:T(8,128)(2,1)S(1)}, bf16[272,128]{1,0:T(8,128)(2,1)S(1)}, u32[]{:S(2)}, u32[]{:S(2)}) collective-permute-start(bf16[272,128]{1,0:T(8,128)(2,1)S(1)} %get-tuple-element.31), channel_id=1, source_target_pairs={{0,2},{1,3},{2,0},{3,1},{4,6},{5,7},{6,4},{7,5},{8,10},{9,11},{10,... | collective-permute-start | bytes 208904 | tf_op jit(solution)/shard_map/ppermute | solution.py:416
  41.9 1.8 %shard_map.104 = (bf16[2048,512]{1,0:T(8,128)(2,1)}, s32[16,128]{1,0:T(8,128)}) custom-call(s32[8,128]{1,0:T(8,128)S(1)} %get-tuple-element.27.step_ref, bf16[2048,512]{1,0:T(8,128)(2,1)} %get-tuple-element.36.stored_ref, s32[16,128]{1,0:T(8,128)S(1)} %get-tuple-element.37.labels_ref, ...), custom_call_target="tpu_custom_call", output_to_operand_aliasing={{0}: (1, {})} | custom-call | tf_op jit(solution)/shard_map/pallas_call | solution.py:23
  43.7 2.7 %collective-permute-done.13.refs_2_ = bf16[272,128]{1,0:T(8,128)(2,1)S(1)} collective-permute-done((bf16[272,128]{1,0:T(8,128)(2,1)S(1)}, bf16[272,128]{1,0:T(8,128)(2,1)S(1)}, u32[]{:S(2)}, u32[]{:S(2)}) %collective-permute-start.13) | collective-permute-done | bytes 69664 | tf_op jit(solution)/shard_map/ppermute | solution.py:416
  46.5 0.9 %shard_map.103 = (f32[32,512]{1,0:T(8,128)}, f32[1,32]{1,0:T(1,128)}) custom-call(f32[272,128]{1,0:T(8,128)S(1)} %get-tuple-element.28.refs_0_, bf16[272,128]{1,0:T(8,128)(2,1)S(1)} %collective-permute-done.12.refs_1_, bf16[272,128]{1,0:T(8,128)(2,1)S(1)} %collective-permute-done.13.refs_2_, bf16[272,128]{1,0:T(8,128)(2,1)S(1)} %collective-permute-done.14.refs_3_, ...), custom_call_target="tpu_custom_call" | custom-call | tf_op jit(solution)/shard_map/pallas_call | solution.py:23
  (10 shorter events, 0.0 us)
Async XLA Ops:
  0.6 14.1 %collective-permute-start.4 = (bf16[2048,512]{1,0:T(8,128)(2,1)}, bf16[2048,512]{1,0:T(8,128)(2,1)S(1)}, u32[]{:S(2)}, u32[]{:S(2)}) collective-permute-start(bf16[2048,512]{1,0:T(8,128)(2,1)} %memory_ref.1), channel_id=1, source_target_pairs={{0,1},{1,0},{2,3},{3,2},{4,5},{5,4},{6,7},{7,6},{8,9},{9,8},{10,11... | collective-permute-start | bytes 6291464 | tf_op jit(solution)/shard_map/ppermute | solution.py:416
  2.7 9.1 %collective-permute-start.2 = (bf16[144,128]{1,0:T(8,128)(2,1)S(1)}, bf16[144,128]{1,0:T(8,128)(2,1)S(1)}, u32[]{:S(2)}, u32[]{:S(2)}) collective-permute-start(bf16[144,128]{1,0:T(8,128)(2,1)S(1)} %get-tuple-element.22.refs_0_), channel_id=1, source_target_pairs={{0,6},{1,7},{2,4},{3,5},{4,2},{5,3},{6,0},{7,1},{8,14},{9,15},{10,... | collective-permute-start | bytes 110600 | tf_op jit(solution)/shard_map/ppermute | solution.py:416
  7.4 4.9 %collective-permute-start.1 = (bf16[144,128]{1,0:T(8,128)(2,1)S(1)}, bf16[144,128]{1,0:T(8,128)(2,1)S(1)}, u32[]{:S(2)}, u32[]{:S(2)}) collective-permute-start(bf16[144,128]{1,0:T(8,128)(2,1)S(1)} %get-tuple-element.22.refs_0_), channel_id=1, source_target_pairs={{0,4},{1,5},{2,6},{3,7},{4,0},{5,1},{6,2},{7,3},{8,12},{9,13},{10,... | collective-permute-start | bytes 110600 | tf_op jit(solution)/shard_map/ppermute | solution.py:416
  7.4 4.9 %collective-permute-start = (bf16[144,128]{1,0:T(8,128)(2,1)S(1)}, bf16[144,128]{1,0:T(8,128)(2,1)S(1)}, u32[]{:S(2)}, u32[]{:S(2)}) collective-permute-start(bf16[144,128]{1,0:T(8,128)(2,1)S(1)} %get-tuple-element.22.refs_0_), channel_id=1, source_target_pairs={{0,2},{1,3},{2,0},{3,1},{4,6},{5,7},{6,4},{7,5},{8,10},{9,11},{10,... | collective-permute-start | bytes 110600 | tf_op jit(solution)/shard_map/ppermute | solution.py:416
  8.0 3.8 %collective-permute-start.3 = (s32[16,128]{1,0:T(8,128)S(1)}, s32[16,128]{1,0:T(8,128)S(1)}, u32[]{:S(2)}, u32[]{:S(2)}) collective-permute-start(s32[16,128]{1,0:T(8,128)S(1)} %get-tuple-element.24.refs_5_), channel_id=1, source_target_pairs={{0,1},{1,0},{2,3},{3,2},{4,5},{5,4},{6,7},{7,6},{8,9},{9,8},{10,11... | collective-permute-start | bytes 24584 | tf_op jit(solution)/shard_map/ppermute | solution.py:416
  12.2 7.5 %collective-permute-start.7 = (bf16[576,128]{1,0:T(8,128)(2,1)S(1)}, bf16[576,128]{1,0:T(8,128)(2,1)S(1)}, u32[]{:S(2)}, u32[]{:S(2)}) collective-permute-start(bf16[576,128]{1,0:T(8,128)(2,1)S(1)} %shard_map.95.refs_0_), channel_id=1, source_target_pairs={{0,24},{8,16},{16,8},{24,0},{1,25},{9,17},{17,9},{25,1},{2,26},{10... | collective-permute-start | bytes 442376 | tf_op jit(solution)/shard_map/ppermute | solution.py:414
  15.8 9.6 %collective-permute-start.6 = (bf16[576,128]{1,0:T(8,128)(2,1)S(1)}, bf16[576,128]{1,0:T(8,128)(2,1)S(1)}, u32[]{:S(2)}, u32[]{:S(2)}) collective-permute-start(bf16[576,128]{1,0:T(8,128)(2,1)S(1)} %shard_map.97), channel_id=1, source_target_pairs={{0,8},{8,0},{16,24},{24,16},{1,9},{9,1},{17,25},{25,17},{2,10},{10... | collective-permute-start | bytes 442376 | tf_op jit(solution)/shard_map/ppermute | solution.py:414
  16.4 9.0 %collective-permute-start.5 = (bf16[576,128]{1,0:T(8,128)(2,1)S(1)}, bf16[576,128]{1,0:T(8,128)(2,1)S(1)}, u32[]{:S(2)}, u32[]{:S(2)}) collective-permute-start(bf16[576,128]{1,0:T(8,128)(2,1)S(1)} %shard_map.97), channel_id=1, source_target_pairs={{0,16},{8,24},{16,0},{24,8},{1,17},{9,25},{17,1},{25,9},{2,18},{10... | collective-permute-start | bytes 442376 | tf_op jit(solution)/shard_map/ppermute | solution.py:414
  22.7 12.0 %collective-permute-start.8 = (bf16[1040,128]{1,0:T(8,128)(2,1)S(1)}, bf16[1040,128]{1,0:T(8,128)(2,1)S(1)}, u32[]{:S(2)}, u32[]{:S(2)}) collective-permute-start(bf16[1040,128]{1,0:T(8,128)(2,1)S(1)} %shard_map.98.refs_6_), channel_id=1, source_target_pairs={{0,24},{8,16},{16,8},{24,0},{1,25},{9,17},{17,9},{25,1},{2,26},{10... | collective-permute-start | bytes 798728 | tf_op jit(solution)/shard_map/ppermute | solution.py:414
  30.0 7.0 %collective-permute-start.9 = (bf16[1040,128]{1,0:T(8,128)(2,1)S(1)}, bf16[1040,128]{1,0:T(8,128)(2,1)S(1)}, u32[]{:S(2)}, u32[]{:S(2)}) collective-permute-start(bf16[1040,128]{1,0:T(8,128)(2,1)S(1)} %get-tuple-element.25.refs_5_.refs_4_), channel_id=1, source_target_pairs={{0,16},{8,24},{16,0},{24,8},{1,17},{9,25},{17,1},{25,9},{2,18},{10... | collective-permute-start | bytes 798728 | tf_op jit(solution)/shard_map/ppermute | solution.py:414
  30.6 6.6 %collective-permute-start.10 = (bf16[1040,128]{1,0:T(8,128)(2,1)S(1)}, bf16[1040,128]{1,0:T(8,128)(2,1)S(1)}, u32[]{:S(2)}, u32[]{:S(2)}) collective-permute-start(bf16[1040,128]{1,0:T(8,128)(2,1)S(1)} %get-tuple-element.26.refs_6_.refs_5_), channel_id=1, source_target_pairs={{0,8},{8,0},{16,24},{24,16},{1,9},{9,1},{17,25},{25,17},{2,10},{10... | collective-permute-start | bytes 798728 | tf_op jit(solution)/shard_map/ppermute | solution.py:414
  31.6 3.0 %collective-permute-start.11 = (bf16[144,128]{1,0:T(8,128)(2,1)S(1)}, bf16[144,128]{1,0:T(8,128)(2,1)S(1)}, u32[]{:S(2)}, u32[]{:S(2)}) collective-permute-start(bf16[144,128]{1,0:T(8,128)(2,1)S(1)} %shard_map.101.refs_4_.refs_0_), channel_id=1, source_target_pairs={{0,1},{1,0},{2,3},{3,2},{4,5},{5,4},{6,7},{7,6},{8,9},{9,8},{10,11... | collective-permute-start | bytes 110600 | tf_op jit(solution)/shard_map/ppermute | solution.py:416
  37.4 6.4 %collective-permute-start.12 = (bf16[272,128]{1,0:T(8,128)(2,1)S(1)}, bf16[272,128]{1,0:T(8,128)(2,1)S(1)}, u32[]{:S(2)}, u32[]{:S(2)}) collective-permute-start(bf16[272,128]{1,0:T(8,128)(2,1)S(1)} %get-tuple-element.29), channel_id=1, source_target_pairs={{0,6},{1,7},{2,4},{3,5},{4,2},{5,3},{6,0},{7,1},{8,14},{9,15},{10,... | collective-permute-start | bytes 208904 | tf_op jit(solution)/shard_map/ppermute | solution.py:416
  41.2 5.2 %collective-permute-start.13 = (bf16[272,128]{1,0:T(8,128)(2,1)S(1)}, bf16[272,128]{1,0:T(8,128)(2,1)S(1)}, u32[]{:S(2)}, u32[]{:S(2)}) collective-permute-start(bf16[272,128]{1,0:T(8,128)(2,1)S(1)} %get-tuple-element.30), channel_id=1, source_target_pairs={{0,4},{1,5},{2,6},{3,7},{4,0},{5,1},{6,2},{7,3},{8,12},{9,13},{10,... | collective-permute-start | bytes 208904 | tf_op jit(solution)/shard_map/ppermute | solution.py:416
  41.2 5.2 %collective-permute-start.14 = (bf16[272,128]{1,0:T(8,128)(2,1)S(1)}, bf16[272,128]{1,0:T(8,128)(2,1)S(1)}, u32[]{:S(2)}, u32[]{:S(2)}) collective-permute-start(bf16[272,128]{1,0:T(8,128)(2,1)S(1)} %get-tuple-element.31), channel_id=1, source_target_pairs={{0,2},{1,3},{2,0},{3,1},{4,6},{5,7},{6,4},{7,5},{8,10},{9,11},{10,... | collective-permute-start | bytes 208904 | tf_op jit(solution)/shard_map/ppermute | solution.py:416

commit v8 on v6

--- a/solution.py
+++ b/solution.py
@@ -90,27 +90,24 @@
     return jnp.sum(jnp.where(diagonal(count), spread, 0.0), axis=0, keepdims=True)
 
 
-def keys_kernel(memory_ref, keys_ref, *copy_refs):
-    stored = memory_ref[...]
-    rows = stored.astype(f32)
+def keys_kernel(memory_ref, keys_ref):
+    rows = memory_ref[...].astype(f32)
     radius = jnp.sqrt(jnp.sum(rows * rows, axis=1, keepdims=True) + 1e-06)
     keys_ref[...] = (rows / radius).astype(bf16)
-    for copy_ref in copy_refs:
-        copy_ref[...] = stored
-
-
-def keys_of(memory, copies):
+
+
+def keys_of(memory, place):
     slots, width = memory.shape
     block = math.gcd(512, slots)
     spec = pl.BlockSpec((block, width), lambda i: (i, 0))
     return call(
         keys_kernel,
-        [shaped((slots, width), bf16)] * (1 + copies),
-        memory,
+        [shaped((slots, width), bf16)],
+        pltpu.with_memory_space_constraint(memory, place),
         grid=(slots // block,),
         in_specs=[spec],
-        out_specs=[spec] * (1 + copies),
-    )
+        out_specs=[spec],
+    )[0]
 
 
 def join_kernel(blocks, *refs):
@@ -229,7 +226,12 @@
     return rounded_up(8 * (rounded_up(size, lanes) // lanes), 16)
 
 
-def block_kernel(blocks, sides, chunk, count, *refs):
+def block_kernel(blocks, sides, chunk, count, copies, *refs):
+    if copies:
+        source_ref, target_ref, sem = refs[blocks + 2 * sides], refs[-3], refs[-1]
+        copy = pltpu.make_async_copy(source_ref, target_ref, sem)
+        copy.start()
+        refs = refs[:-3] + refs[-2:-1]
     rows_refs, keys_refs = refs[:blocks], refs[blocks : blocks + sides]
     label_refs = refs[blocks + sides : blocks + 2 * sides]
     out_refs = refs[-1 - blocks : -1]
@@ -304,20 +306,26 @@
                 lines += split_digits(row)
         first = 2 * parts * size
         ref[first:, :] = rows_as_lanes(lines, ref.shape[0] - first).astype(ref.dtype)
-
-
-def block_sums(blocks, keys, labels, count, dtype, after):
+    if copies:
+        copy.wait()
+
+
+def block_sums(blocks, keys, labels, count, dtype, after, copied=()):
     slots, width = keys[0].shape
     parts = blocks_of(width)
     size = blocks[0].shape[0] // (parts * count + 16) * count
-    return call(
-        functools.partial(block_kernel, len(blocks), len(keys), math.gcd(1024, slots), count),
-        [shaped((2 * parts * size + sum_rows(size), lanes), dtype)] * len(blocks),
-        *blocks, *[in_vmem(k) for k in keys], *labels, *after,
+    anywhere = pl.BlockSpec(memory_space=pl.ANY)
+    vmem = pl.BlockSpec(memory_space=pltpu.VMEM)
+    return call(
+        functools.partial(block_kernel, len(blocks), len(keys), math.gcd(1024, slots), count, len(copied)),
+        [shaped((2 * parts * size + sum_rows(size), lanes), dtype)] * len(blocks)
+        + [shaped(value.shape, value.dtype) for value in copied],
+        *blocks, *[in_vmem(k) for k in keys], *labels, *copied, *after,
         work=12 * size * len(blocks) * slots * len(keys) * width,
-        in_specs=[pl.BlockSpec(memory_space=pltpu.VMEM)] * (len(blocks) + 2 * len(keys))
-        + [pl.BlockSpec(memory_space=pl.ANY)] * len(after),
-        scratch_shapes=[pltpu.VMEM((len(blocks) * size, width), bf16)],
+        in_specs=[vmem] * (len(blocks) + 2 * len(keys)) + [anywhere] * (len(copied) + len(after)),
+        out_specs=[vmem] * len(blocks) + [anywhere] * len(copied),
+        scratch_shapes=[pltpu.VMEM((len(blocks) * size, width), bf16)]
+        + [pltpu.SemaphoreType.DMA] * len(copied),
     )
 
 
@@ -418,17 +426,18 @@
 
     labels = [slot_labels] + [exchange(slot_labels, "core", s) for s in range(1, cores)]
     memories = [memory] + [exchange(memory, "core", s) for s in range(1, cores)]
-    own_keys, copied = keys_of(memory, 1)
-    keys = [own_keys] + [keys_of(value, 0)[0] for value in memories[1:]]
+    keys = [keys_of(memory, pltpu.HBM)] + [keys_of(value, pltpu.VMEM) for value in memories[1:]]
 
     near = [packed] + [None] * (line - 1)
     for s in range(line - 1, 0, -1):
         near[s] = exchange(packed, "line", s)
-    part = join(near, [*keys, *labels])
+    part = join(near, [keys[0], *labels])
     labels = [value.reshape(1, slots) for value in labels]
     blocks = [part] + [None] * (groups - 1)
     for s in range(groups - 1, 0, -1):
-        blocks[s] = exchange(part, "grp", s)
+        blocks[s] = exchange(part if s == groups - 1 else later, "grp", s)
+        if s == groups - 1:
+            later = join([part], keys[1:])
 
     size = count * line
     arrived, after = [], []
@@ -438,7 +447,7 @@
         places = places[len(now) :]
         after = block_sums([blocks[s] for s in now], keys, labels, count, bf16, after)
         arrived += [exchange(value, "grp", s) for s, value in zip(now, after)]
-    held = block_sums([part], keys, labels, count, f32, after)[0]
+    held, copied = block_sums([part], keys, labels, count, f32, after, [memory])
     sizes = (count, slots, groups, line, cores)
     moved = pick(blocks, step_index, sizes, after)
     choices = [moved] + [exchange(moved, "core", s) for s in range(1, cores)]

time: 47.6 us -> 46.3 us (0.973)
  local copies, waits for them, and re-layouts: 1.59 us -> 0.01 us
  waiting for transfers between devices: 10.3 us -> 9.17 us
  Pallas kernels: 16.6 us -> 17.5 us
  starting transfers between devices: 17.5 us -> 18 us
    ppermute x6, waiting for transfers between devices: 7.09 us -> 4.28 us  [exchange(): return lax.ppermute(value, 'grp', [(i, i ^ step) for i in range(groups)])]
    ppermute x9, waiting for transfers between devices: 3.2 us -> 4.89 us  [exchange(): return lax.ppermute(value, 'dev', [(i, i ^ jump) for i in range(members)])]
    unnamed x2, local copies, waits for them, and re-layouts: 1.59 us -> 0.01 us
    pallas_call x11 -> x12, Pallas kernels: 16.6 us -> 17.5 us  [call(): pl.pallas_call(body, out_shape=outs, compiler_params=pltpu.CompilerParams...]
    ppermute x6, starting transfers between devices: 7.24 us -> 7.75 us  [exchange(): return lax.ppermute(value, 'grp', [(i, i ^ step) for i in range(groups)])]
  transfers between devices with their start and end apart: 15 -> 15, of which waited for: 5 -> 7; matrix products, arithmetic and copies ran while one was open for 0% -> 0% of each run, Pallas kernels for 33% -> 36%
where the time goes in v8:
time: 46.3 us; the launch traced here: 46.1 us
  starting transfers between devices  18 us (39%)
  Pallas kernels  17.5 us (38%)
  waiting for transfers between devices  9.17 us (20%)
  between operations  1.42 us (3%)
    pallas_call x12, Pallas kernels, call(): pl.pallas_call(body, out_shape=outs, compiler_params=pltpu.CompilerParams...  17.5 us
    ppermute x9, starting transfers between devices, exchange(): return lax.ppermute(value, 'dev', [(i, i ^ jump) for i in range(members)])  10.2 us
    ppermute x6, starting transfers between devices, exchange(): return lax.ppermute(value, 'grp', [(i, i ^ step) for i in range(groups)])  7.75 us
    ppermute x9, waiting for transfers between devices, exchange(): return lax.ppermute(value, 'dev', [(i, i ^ jump) for i in range(members)])  4.89 us
    ppermute x6, waiting for transfers between devices, exchange(): return lax.ppermute(value, 'grp', [(i, i ^ step) for i in range(groups)])  4.28 us
  transfers between devices with their start and end apart: 15, of which 7 were waited for; matrix products, arithmetic and copies ran while one was open for 0% of the time, Pallas kernels for 36%

profile of v8, /device:TPU:0, one launch (start us, length us, event | category | flops | bytes accessed | tf_op | source)
XLA Modules:
  0.0 46.1 jit_solution(12579362864479327304)
XLA Ops:
  0.6 0.5 %collective-permute-start.4 = (bf16[2048,512]{1,0:T(8,128)(2,1)}, bf16[2048,512]{1,0:T(8,128)(2,1)S(1)}, u32[]{:S(2)}, u32[]{:S(2)}) collective-permute-start(bf16[2048,512]{1,0:T(8,128)(2,1)} %refs_5_.1), channel_id=1, source_target_pairs={{0,1},{1,0},{2,3},{3,2},{4,5},{5,4},{6,7},{7,6},{8,9},{9,8},{10,11... | collective-permute-start | bytes 6291464 | tf_op jit(solution)/shard_map/ppermute | solution.py:410
  1.1 0.9 %shard_map.93 = (bf16[144,128]{1,0:T(8,128)(2,1)S(1)}, f32[32,512]{1,0:T(8,128)S(1)}, f32[32,128]{1,0:T(8,128)S(1)}, s32[16,128]{1,0:T(8,128)S(1)}, s32[16,128]{1,0:T(8,128)S(1)}) custom-call(bf16[32,512]{1,0:T(8,128)(2,1)} %rows_ref.1, s32[1,32]{1,0:T(1,128)} %bitcast.15, s32[16,128]{1,0:T(8,128)} %bitcast.13, s32[16,128]{1,0:T(8,128)} %bitcast.14), custom_call_target="tpu_custom_call" | custom-call | tf_op jit(solution)/shard_map/pallas_call | solution.py:23
  2.0 2.7 %collective-permute-start = (bf16[144,128]{1,0:T(8,128)(2,1)S(1)}, bf16[144,128]{1,0:T(8,128)(2,1)S(1)}, u32[]{:S(2)}, u32[]{:S(2)}) collective-permute-start(bf16[144,128]{1,0:T(8,128)(2,1)S(1)} %get-tuple-element.21.refs_0_), channel_id=1, source_target_pairs={{0,2},{1,3},{2,0},{3,1},{4,6},{5,7},{6,4},{7,5},{8,10},{9,11},{10,... | collective-permute-start | bytes 110600 | tf_op jit(solution)/shard_map/ppermute | solution.py:410
  4.7 2.6 %collective-permute-start.1 = (bf16[144,128]{1,0:T(8,128)(2,1)S(1)}, bf16[144,128]{1,0:T(8,128)(2,1)S(1)}, u32[]{:S(2)}, u32[]{:S(2)}) collective-permute-start(bf16[144,128]{1,0:T(8,128)(2,1)S(1)} %get-tuple-element.21.refs_0_), channel_id=1, source_target_pairs={{0,4},{1,5},{2,6},{3,7},{4,0},{5,1},{6,2},{7,3},{8,12},{9,13},{10,... | collective-permute-start | bytes 110600 | tf_op jit(solution)/shard_map/ppermute | solution.py:410
  7.3 2.9 %shard_map.94.refs_4_.refs_1_.refs_2_ = bf16[2048,512]{1,0:T(8,128)(2,1)S(1)} custom-call(bf16[2048,512]{1,0:T(8,128)(2,1)} %refs_5_.1), custom_call_target="tpu_custom_call" | custom-call | tf_op jit(solution)/shard_map/pallas_call | solution.py:23
  10.1 0.0 collective-permute-done.3.refs_6_
  10.2 0.2 collective-permute-done.1.refs_2_
  10.3 2.7 %collective-permute-done.2.refs_3_ = bf16[144,128]{1,0:T(8,128)(2,1)S(1)} collective-permute-done((bf16[144,128]{1,0:T(8,128)(2,1)S(1)}, bf16[144,128]{1,0:T(8,128)(2,1)S(1)}, u32[]{:S(2)}, u32[]{:S(2)}) %collective-permute-start.2) | collective-permute-done | bytes 36896 | tf_op jit(solution)/shard_map/ppermute | solution.py:410
  13.1 2.5 %collective-permute-start.7 = (bf16[576,128]{1,0:T(8,128)(2,1)S(1)}, bf16[576,128]{1,0:T(8,128)(2,1)S(1)}, u32[]{:S(2)}, u32[]{:S(2)}) collective-permute-start(bf16[576,128]{1,0:T(8,128)(2,1)S(1)} %shard_map.95.refs_0_), channel_id=1, source_target_pairs={{0,24},{8,16},{16,8},{24,0},{1,25},{9,17},{17,9},{25,1},{2,26},{10... | collective-permute-start | bytes 442376 | tf_op jit(solution)/shard_map/ppermute | solution.py:408
  16.2 1.0 %shard_map.96.refs_1_.refs_2_.refs_3_ = bf16[2048,512]{1,0:T(8,128)(2,1)S(1)} custom-call(bf16[2048,512]{1,0:T(8,128)(2,1)S(1)} %collective-permute-done.4.memory_ref), custom_call_target="tpu_custom_call" | custom-call | tf_op jit(solution)/shard_map/pallas_call | solution.py:23
  17.2 0.6 %collective-permute-start.5 = (bf16[576,128]{1,0:T(8,128)(2,1)S(1)}, bf16[576,128]{1,0:T(8,128)(2,1)S(1)}, u32[]{:S(2)}, u32[]{:S(2)}) collective-permute-start(bf16[576,128]{1,0:T(8,128)(2,1)S(1)} %shard_map.97), channel_id=1, source_target_pairs={{0,16},{8,24},{16,0},{24,8},{1,17},{9,25},{17,1},{25,9},{2,18},{10... | collective-permute-start | bytes 442376 | tf_op jit(solution)/shard_map/ppermute | solution.py:408
  17.8 0.5 %collective-permute-start.6 = (bf16[576,128]{1,0:T(8,128)(2,1)S(1)}, bf16[576,128]{1,0:T(8,128)(2,1)S(1)}, u32[]{:S(2)}, u32[]{:S(2)}) collective-permute-start(bf16[576,128]{1,0:T(8,128)(2,1)S(1)} %shard_map.97), channel_id=1, source_target_pairs={{0,8},{8,0},{16,24},{24,16},{1,9},{9,1},{17,25},{25,17},{2,10},{10... | collective-permute-start | bytes 442376 | tf_op jit(solution)/shard_map/ppermute | solution.py:408
  18.4 1.4 %collective-permute-done.7.refs_0_.refs_3_ = bf16[576,128]{1,0:T(8,128)(2,1)S(1)} collective-permute-done((bf16[576,128]{1,0:T(8,128)(2,1)S(1)}, bf16[576,128]{1,0:T(8,128)(2,1)S(1)}, u32[]{:S(2)}, u32[]{:S(2)}) %collective-permute-start.7) | collective-permute-done | bytes 147488 | tf_op jit(solution)/shard_map/ppermute | solution.py:408
  19.8 2.9 %shard_map.98.refs_6_ = bf16[1040,128]{1,0:T(8,128)(2,1)S(1)} custom-call(bf16[576,128]{1,0:T(8,128)(2,1)S(1)} %collective-permute-done.7.refs_0_.refs_3_, bf16[2048,512]{1,0:T(8,128)(2,1)S(1)} %shard_map.94.refs_4_.refs_1_.refs_2_, bf16[2048,512]{1,0:T(8,128)(2,1)S(1)} %shard_map.96.refs_1_.refs_2_.refs_3_, s32[1,2048]{1,0:T(1,128)S(1)} %bitcast.7, ...), custom_call_target="tpu_custom_call" | custom-call | flops 3221225472 | tf_op jit(solution)/shard_map/pallas_call | solution.py:23
  22.7 0.0 copy-start
  22.7 3.5 %collective-permute-start.8 = (bf16[1040,128]{1,0:T(8,128)(2,1)S(1)}, bf16[1040,128]{1,0:T(8,128)(2,1)S(1)}, u32[]{:S(2)}, u32[]{:S(2)}) collective-permute-start(bf16[1040,128]{1,0:T(8,128)(2,1)S(1)} %shard_map.98.refs_6_), channel_id=1, source_target_pairs={{0,24},{8,16},{16,8},{24,0},{1,25},{9,17},{17,9},{25,1},{2,26},{10... | collective-permute-start | bytes 798728 | tf_op jit(solution)/shard_map/ppermute | solution.py:408
  26.2 0.0 collective-permute-done.5.refs_0_.refs_2_
  26.2 4.7 %shard_map.99 = (bf16[1040,128]{1,0:T(8,128)(2,1)S(1)}, bf16[1040,128]{1,0:T(8,128)(2,1)S(1)}) custom-call(bf16[576,128]{1,0:T(8,128)(2,1)S(1)} %collective-permute-done.5.refs_0_.refs_2_, bf16[576,128]{1,0:T(8,128)(2,1)S(1)} %collective-permute-done.6.refs_1_, bf16[2048,512]{1,0:T(8,128)(2,1)S(1)} %shard_map.94.refs_4_.refs_1_.refs_2_, ...), custom_call_target="tpu_custom_call" | custom-call | flops 6442450944 | tf_op jit(solution)/shard_map/pallas_call | solution.py:23
  30.8 0.1 collective-permute-start.10
  30.9 0.6 %collective-permute-start.9 = (bf16[1040,128]{1,0:T(8,128)(2,1)S(1)}, bf16[1040,128]{1,0:T(8,128)(2,1)S(1)}, u32[]{:S(2)}, u32[]{:S(2)}) collective-permute-start(bf16[1040,128]{1,0:T(8,128)(2,1)S(1)} %get-tuple-element.23.refs_6_.refs_4_), channel_id=1, source_target_pairs={{0,16},{8,24},{16,0},{24,8},{1,17},{9,25},{17,1},{25,9},{2,18},{10... | collective-permute-start | bytes 798728 | tf_op jit(solution)/shard_map/ppermute | solution.py:408
  31.5 3.0 %shard_map.100 = (f32[1040,128]{1,0:T(8,128)S(1)}, bf16[2048,512]{1,0:T(8,128)(2,1)}) custom-call(bf16[576,128]{1,0:T(8,128)(2,1)S(1)} %shard_map.95.refs_0_, bf16[2048,512]{1,0:T(8,128)(2,1)S(1)} %shard_map.94.refs_4_.refs_1_.refs_2_, bf16[2048,512]{1,0:T(8,128)(2,1)S(1)} %shard_map.96.refs_1_.refs_2_.refs_3_, s32[1,2048]{1,0:T(1,128)S(1)} %bitcast.9, ...), custom_call_target="tpu_custom_call" | custom-call | flops 3221225472 | tf_op jit(solution)/shard_map/pallas_call | solution.py:23
  34.5 0.0 collective-permute-done.11.refs_5_.refs_1_
  34.5 0.0 collective-permute-done.8.refs_1_
  34.5 2.8 %collective-permute-done.10.refs_3_ = bf16[1040,128]{1,0:T(8,128)(2,1)S(1)} collective-permute-done((bf16[1040,128]{1,0:T(8,128)(2,1)S(1)}, bf16[1040,128]{1,0:T(8,128)(2,1)S(1)}, u32[]{:S(2)}, u32[]{:S(2)}) %collective-permute-start.10) | collective-permute-done | bytes 266272 | tf_op jit(solution)/shard_map/ppermute | solution.py:408
  37.3 0.1 collective-permute-done.9.refs_2_
  37.4 0.1 shard_map.102
  37.5 2.2 %collective-permute-start.12 = (bf16[272,128]{1,0:T(8,128)(2,1)S(1)}, bf16[272,128]{1,0:T(8,128)(2,1)S(1)}, u32[]{:S(2)}, u32[]{:S(2)}) collective-permute-start(bf16[272,128]{1,0:T(8,128)(2,1)S(1)} %get-tuple-element.27), channel_id=1, source_target_pairs={{0,6},{1,7},{2,4},{3,5},{4,2},{5,3},{6,0},{7,1},{8,14},{9,15},{10,... | collective-permute-start | bytes 208904 | tf_op jit(solution)/shard_map/ppermute | solution.py:410
  39.7 2.3 %collective-permute-start.14 = (bf16[272,128]{1,0:T(8,128)(2,1)S(1)}, bf16[272,128]{1,0:T(8,128)(2,1)S(1)}, u32[]{:S(2)}, u32[]{:S(2)}) collective-permute-start(bf16[272,128]{1,0:T(8,128)(2,1)S(1)} %get-tuple-element.29), channel_id=1, source_target_pairs={{0,2},{1,3},{2,0},{3,1},{4,6},{5,7},{6,4},{7,5},{8,10},{9,11},{10,... | collective-permute-start | bytes 208904 | tf_op jit(solution)/shard_map/ppermute | solution.py:410
  42.0 1.2 %shard_map.104 = (bf16[2048,512]{1,0:T(8,128)(2,1)}, s32[16,128]{1,0:T(8,128)}) custom-call(s32[1]{0:T(128)S(6)} %copy.12.step_ref, bf16[2048,512]{1,0:T(8,128)(2,1)} %get-tuple-element.34.stored_ref, s32[16,128]{1,0:T(8,128)S(1)} %get-tuple-element.35.labels_ref, bf16[144,128]{1,0:T(8,128)(2,1)S(1)} %shard_map.101.refs_4_.refs_0_, ...), custom_call_target="tpu_custom_call", output_to_operand_aliasing={{0}: (1, {})} | custom-call | tf_op jit(solution)/shard_map/pallas_call | solution.py:23
  43.2 0.5 %collective-permute-done.12.refs_1_ = bf16[272,128]{1,0:T(8,128)(2,1)S(1)} collective-permute-done((bf16[272,128]{1,0:T(8,128)(2,1)S(1)}, bf16[272,128]{1,0:T(8,128)(2,1)S(1)}, u32[]{:S(2)}, u32[]{:S(2)}) %collective-permute-start.12) | collective-permute-done | bytes 69664 | tf_op jit(solution)/shard_map/ppermute | solution.py:410
  43.8 1.5 %collective-permute-done.13.refs_2_ = bf16[272,128]{1,0:T(8,128)(2,1)S(1)} collective-permute-done((bf16[272,128]{1,0:T(8,128)(2,1)S(1)}, bf16[272,128]{1,0:T(8,128)(2,1)S(1)}, u32[]{:S(2)}, u32[]{:S(2)}) %collective-permute-start.13) | collective-permute-done | bytes 69664 | tf_op jit(solution)/shard_map/ppermute | solution.py:410
  45.2 0.9 %shard_map.103 = (f32[32,512]{1,0:T(8,128)}, f32[1,32]{1,0:T(1,128)}) custom-call(f32[272,128]{1,0:T(8,128)S(1)} %get-tuple-element.26.refs_0_, bf16[272,128]{1,0:T(8,128)(2,1)S(1)} %collective-permute-done.12.refs_1_, bf16[272,128]{1,0:T(8,128)(2,1)S(1)} %collective-permute-done.13.refs_2_, bf16[272,128]{1,0:T(8,128)(2,1)S(1)} %collective-permute-done.14.refs_3_, ...), custom_call_target="tpu_custom_call" | custom-call | tf_op jit(solution)/shard_map/pallas_call | solution.py:23
  (12 shorter events, 0.0 us)
Async XLA Ops:
  0.6 15.6 %collective-permute-start.4 = (bf16[2048,512]{1,0:T(8,128)(2,1)}, bf16[2048,512]{1,0:T(8,128)(2,1)S(1)}, u32[]{:S(2)}, u32[]{:S(2)}) collective-permute-start(bf16[2048,512]{1,0:T(8,128)(2,1)} %refs_5_.1), channel_id=1, source_target_pairs={{0,1},{1,0},{2,3},{3,2},{4,5},{5,4},{6,7},{7,6},{8,9},{9,8},{10,11... | collective-permute-start | bytes 6291464 | tf_op jit(solution)/shard_map/ppermute | solution.py:410
  2.0 8.1 %collective-permute-start = (bf16[144,128]{1,0:T(8,128)(2,1)S(1)}, bf16[144,128]{1,0:T(8,128)(2,1)S(1)}, u32[]{:S(2)}, u32[]{:S(2)}) collective-permute-start(bf16[144,128]{1,0:T(8,128)(2,1)S(1)} %get-tuple-element.21.refs_0_), channel_id=1, source_target_pairs={{0,2},{1,3},{2,0},{3,1},{4,6},{5,7},{6,4},{7,5},{8,10},{9,11},{10,... | collective-permute-start | bytes 110600 | tf_op jit(solution)/shard_map/ppermute | solution.py:410
  4.7 5.6 %collective-permute-start.1 = (bf16[144,128]{1,0:T(8,128)(2,1)S(1)}, bf16[144,128]{1,0:T(8,128)(2,1)S(1)}, u32[]{:S(2)}, u32[]{:S(2)}) collective-permute-start(bf16[144,128]{1,0:T(8,128)(2,1)S(1)} %get-tuple-element.21.refs_0_), channel_id=1, source_target_pairs={{0,4},{1,5},{2,6},{3,7},{4,0},{5,1},{6,2},{7,3},{8,12},{9,13},{10,... | collective-permute-start | bytes 110600 | tf_op jit(solution)/shard_map/ppermute | solution.py:410
  7.3 5.8 %collective-permute-start.2 = (bf16[144,128]{1,0:T(8,128)(2,1)S(1)}, bf16[144,128]{1,0:T(8,128)(2,1)S(1)}, u32[]{:S(2)}, u32[]{:S(2)}) collective-permute-start(bf16[144,128]{1,0:T(8,128)(2,1)S(1)} %get-tuple-element.21.refs_0_), channel_id=1, source_target_pairs={{0,6},{1,7},{2,4},{3,5},{4,2},{5,3},{6,0},{7,1},{8,14},{9,15},{10,... | collective-permute-start | bytes 110600 | tf_op jit(solution)/shard_map/ppermute | solution.py:410
  7.3 2.9 %collective-permute-start.3 = (s32[16,128]{1,0:T(8,128)S(1)}, s32[16,128]{1,0:T(8,128)S(1)}, u32[]{:S(2)}, u32[]{:S(2)}) collective-permute-start(s32[16,128]{1,0:T(8,128)S(1)} %get-tuple-element.22.refs_5_), channel_id=1, source_target_pairs={{0,1},{1,0},{2,3},{3,2},{4,5},{5,4},{6,7},{7,6},{8,9},{9,8},{10,11... | collective-permute-start | bytes 24584 | tf_op jit(solution)/shard_map/ppermute | solution.py:410
  13.1 6.7 %collective-permute-start.7 = (bf16[576,128]{1,0:T(8,128)(2,1)S(1)}, bf16[576,128]{1,0:T(8,128)(2,1)S(1)}, u32[]{:S(2)}, u32[]{:S(2)}) collective-permute-start(bf16[576,128]{1,0:T(8,128)(2,1)S(1)} %shard_map.95.refs_0_), channel_id=1, source_target_pairs={{0,24},{8,16},{16,8},{24,0},{1,25},{9,17},{17,9},{25,1},{2,26},{10... | collective-permute-start | bytes 442376 | tf_op jit(solution)/shard_map/ppermute | solution.py:408
  17.2 8.9 %collective-permute-start.5 = (bf16[576,128]{1,0:T(8,128)(2,1)S(1)}, bf16[576,128]{1,0:T(8,128)(2,1)S(1)}, u32[]{:S(2)}, u32[]{:S(2)}) collective-permute-start(bf16[576,128]{1,0:T(8,128)(2,1)S(1)} %shard_map.97), channel_id=1, source_target_pairs={{0,16},{8,24},{16,0},{24,8},{1,17},{9,25},{17,1},{25,9},{2,18},{10... | collective-permute-start | bytes 442376 | tf_op jit(solution)/shard_map/ppermute | solution.py:408
  17.8 8.3 %collective-permute-start.6 = (bf16[576,128]{1,0:T(8,128)(2,1)S(1)}, bf16[576,128]{1,0:T(8,128)(2,1)S(1)}, u32[]{:S(2)}, u32[]{:S(2)}) collective-permute-start(bf16[576,128]{1,0:T(8,128)(2,1)S(1)} %shard_map.97), channel_id=1, source_target_pairs={{0,8},{8,0},{16,24},{24,16},{1,9},{9,1},{17,25},{25,17},{2,10},{10... | collective-permute-start | bytes 442376 | tf_op jit(solution)/shard_map/ppermute | solution.py:408
  22.7 8.8 %copy-start = (bf16[2048,512]{1,0:T(8,128)(2,1)S(1)}, bf16[2048,512]{1,0:T(8,128)(2,1)}, u32[]{:S(2)}) copy-start(bf16[2048,512]{1,0:T(8,128)(2,1)} %refs_5_.1) | copy-start | bytes 6291460
  22.7 11.8 %collective-permute-start.8 = (bf16[1040,128]{1,0:T(8,128)(2,1)S(1)}, bf16[1040,128]{1,0:T(8,128)(2,1)S(1)}, u32[]{:S(2)}, u32[]{:S(2)}) collective-permute-start(bf16[1040,128]{1,0:T(8,128)(2,1)S(1)} %shard_map.98.refs_6_), channel_id=1, source_target_pairs={{0,24},{8,16},{16,8},{24,0},{1,25},{9,17},{17,9},{25,1},{2,26},{10... | collective-permute-start | bytes 798728 | tf_op jit(solution)/shard_map/ppermute | solution.py:408
  30.8 6.5 %collective-permute-start.10 = (bf16[1040,128]{1,0:T(8,128)(2,1)S(1)}, bf16[1040,128]{1,0:T(8,128)(2,1)S(1)}, u32[]{:S(2)}, u32[]{:S(2)}) collective-permute-start(bf16[1040,128]{1,0:T(8,128)(2,1)S(1)} %get-tuple-element.24.refs_7_.refs_5_), channel_id=1, source_target_pairs={{0,8},{8,0},{16,24},{24,16},{1,9},{9,1},{17,25},{25,17},{2,10},{10... | collective-permute-start | bytes 798728 | tf_op jit(solution)/shard_map/ppermute | solution.py:408
  30.9 6.5 %collective-permute-start.9 = (bf16[1040,128]{1,0:T(8,128)(2,1)S(1)}, bf16[1040,128]{1,0:T(8,128)(2,1)S(1)}, u32[]{:S(2)}, u32[]{:S(2)}) collective-permute-start(bf16[1040,128]{1,0:T(8,128)(2,1)S(1)} %get-tuple-element.23.refs_6_.refs_4_), channel_id=1, source_target_pairs={{0,16},{8,24},{16,0},{24,8},{1,17},{9,25},{17,1},{25,9},{2,18},{10... | collective-permute-start | bytes 798728 | tf_op jit(solution)/shard_map/ppermute | solution.py:408
  31.5 3.0 %collective-permute-start.11 = (bf16[144,128]{1,0:T(8,128)(2,1)S(1)}, bf16[144,128]{1,0:T(8,128)(2,1)S(1)}, u32[]{:S(2)}, u32[]{:S(2)}) collective-permute-start(bf16[144,128]{1,0:T(8,128)(2,1)S(1)} %shard_map.101.refs_4_.refs_0_), channel_id=1, source_target_pairs={{0,1},{1,0},{2,3},{3,2},{4,5},{5,4},{6,7},{7,6},{8,9},{9,8},{10,11... | collective-permute-start | bytes 110600 | tf_op jit(solution)/shard_map/ppermute | solution.py:410
  37.5 6.2 %collective-permute-start.12 = (bf16[272,128]{1,0:T(8,128)(2,1)S(1)}, bf16[272,128]{1,0:T(8,128)(2,1)S(1)}, u32[]{:S(2)}, u32[]{:S(2)}) collective-permute-start(bf16[272,128]{1,0:T(8,128)(2,1)S(1)} %get-tuple-element.27), channel_id=1, source_target_pairs={{0,6},{1,7},{2,4},{3,5},{4,2},{5,3},{6,0},{7,1},{8,14},{9,15},{10,... | collective-permute-start | bytes 208904 | tf_op jit(solution)/shard_map/ppermute | solution.py:410
  39.7 5.5 %collective-permute-start.13 = (bf16[272,128]{1,0:T(8,128)(2,1)S(1)}, bf16[272,128]{1,0:T(8,128)(2,1)S(1)}, u32[]{:S(2)}, u32[]{:S(2)}) collective-permute-start(bf16[272,128]{1,0:T(8,128)(2,1)S(1)} %get-tuple-element.28), channel_id=1, source_target_pairs={{0,4},{1,5},{2,6},{3,7},{4,0},{5,1},{6,2},{7,3},{8,12},{9,13},{10,... | collective-permute-start | bytes 208904 | tf_op jit(solution)/shard_map/ppermute | solution.py:410
  39.7 5.5 %collective-permute-start.14 = (bf16[272,128]{1,0:T(8,128)(2,1)S(1)}, bf16[272,128]{1,0:T(8,128)(2,1)S(1)}, u32[]{:S(2)}, u32[]{:S(2)}) collective-permute-start(bf16[272,128]{1,0:T(8,128)(2,1)S(1)} %get-tuple-element.29), channel_id=1, source_target_pairs={{0,2},{1,3},{2,0},{3,1},{4,6},{5,7},{6,4},{7,5},{8,10},{9,11},{10,... | collective-permute-start | bytes 208904 | tf_op jit(solution)/shard_map/ppermute | solution.py:410

commit v9 on v8

--- a/solution.py
+++ b/solution.py
@@ -64,12 +64,15 @@
     unit_ref[...] = unit
     radius_ref[...] = jnp.broadcast_to(radius, radius_ref.shape)
     anchors = unit.astype(bf16)
-    for at in range(blocks_of(width)):
-        packed_ref[at * count : (at + 1) * count, :] = anchors[:, at * lanes : (at + 1) * lanes]
     row = jnp.concatenate([labels_ref[...].astype(f32), jnp.zeros((1, lanes - count), f32)], axis=1)
     high = jnp.floor(row * (1.0 / 256.0))
-    tail = packed_ref.shape[0] - blocks_of(width) * count
-    packed_ref[blocks_of(width) * count :, :] = rows_as_lanes([high, row - high * 256.0], tail).astype(bf16)
+    digits = rows_as_lanes([high, row - high * 256.0], 16).astype(bf16)
+    size = blocks_of(width) * count
+    for first in range(0, packed_ref.shape[0], size + 16):
+        for at in range(blocks_of(width)):
+            part = slice(first + at * count, first + (at + 1) * count)
+            packed_ref[part, :] = anchors[:, at * lanes : (at + 1) * lanes]
+        packed_ref[first + size : first + size + 16, :] = digits
 
 
 def diagonal(count):
@@ -156,7 +159,7 @@
     source = lax.rem(target + devices_all - lax.rem(step, devices_all), devices_all)
     source_grp = lax.div(source, members)
     source_line = lax.div(lax.rem(source, members), cores)
-    return first, crossing, grp ^ source_grp, lax.div(dev, cores) ^ source_line
+    return first, crossing, grp ^ source_grp, source_line
 
 
 def pick_kernel(groups, sizes, step_ref, *refs):
@@ -330,7 +333,7 @@
 
 
 def add_kernel(arrived, size, count, *refs):
-    in_refs, out_refs = refs[: 1 + arrived], refs[-(size // count) :]
+    in_refs, out_ref = refs[: 1 + arrived], refs[-1]
     columns = (in_refs[0].shape[0] - sum_rows(size)) // size
 
     def total(first, rows):
@@ -340,41 +343,42 @@
         return value
 
     sums = total(columns * size, sum_rows(size))
-    for block, ref in enumerate(out_refs):
+    tail = sum_rows(count)
+    for block in range(size // count):
+        base = block * (columns * count + tail)
         for at in range(columns):
             part = total(at * size + block * count, count)
-            ref[at * count : (at + 1) * count, :] = part.astype(ref.dtype)
+            out_ref[base + at * count : base + (at + 1) * count, :] = part.astype(bf16)
         group, lane = divmod(block * count, lanes)
         lines = []
         for which in range(4):
             row = 8 * group + 2 * which
             lines += split_digits(sums[row : row + 1, :] + sums[row + 1 : row + 2, :])
-        packed = rows_as_lanes(lines, ref.shape[0] - columns * count)
+        packed = rows_as_lanes(lines, tail)
         if lane:
             packed = pltpu.roll(packed, lanes - lane, 1)
-        ref[columns * count :, :] = packed.astype(ref.dtype)
+        base += columns * count
+        out_ref[base : base + tail, :] = packed.astype(bf16)
 
 
 def add(held, arrived, size, count, columns, after):
-    shape = (columns * count + sum_rows(count), lanes)
-    outs = [shaped(shape, f32 if b == 0 else bf16) for b in range(size // count)]
+    blocks = size // count
     return call(
         functools.partial(add_kernel, len(arrived), size, count),
-        outs,
+        [shaped((blocks * (columns * count + sum_rows(count)), lanes), bf16)],
         held, *arrived, *after,
         in_specs=[pl.BlockSpec(memory_space=pltpu.VMEM)] * (1 + len(arrived))
         + [pl.BlockSpec(memory_space=pl.ANY)] * len(after),
-    )
-
-
-def finish_kernel(arrived, *refs):
-    held_ref, arrived_refs = refs[0], refs[1 : 1 + arrived]
-    unit_ref, radius_ref, grad_ref, loss_ref = refs[1 + arrived :]
+    )[0]
+
+
+def finish_kernel(sums_ref, unit_ref, radius_ref, grad_ref, loss_ref):
     count, width = unit_ref.shape
     parts = blocks_of(width)
-    total = held_ref[...]
-    for ref in arrived_refs:
-        total = total + ref[...].astype(f32)
+    rows = 2 * parts * count + sum_rows(count)
+    total = sums_ref[:rows, :].astype(f32)
+    for first in range(rows, sums_ref.shape[0], rows):
+        total = total + sums_ref[first : first + rows, :].astype(f32)
     sums = []
     for which in range(4):
         row = 2 * parts * count + 2 * which
@@ -403,18 +407,21 @@
     count, width = batch_rows.shape
     slots = memory.shape[0]
 
+    def along_line(value):
+        members_of = [[at * cores + core for at in range(line)] for core in range(cores)]
+        return lax.all_to_all(value, "dev", 0, 0, axis_index_groups=members_of, tiled=True)
+
     def exchange(value, axis, step):
         if axis == "grp":
             return lax.ppermute(value, "grp", [(i, i ^ step) for i in range(groups)])
-        jump = step * cores if axis == "line" else step
-        return lax.ppermute(value, "dev", [(i, i ^ jump) for i in range(members)])
+        return lax.ppermute(value, "dev", [(i, i ^ step) for i in range(members)])
 
     folded = (slots // lanes, lanes)
     parts = blocks_of(width)
     packed, unit, radius, slot_labels, copied_labels = call(
         prepare_kernel,
         [
-            pltpu.VMEM((parts * count + 16, lanes), bf16),
+            pltpu.VMEM((line * (parts * count + 16), lanes), bf16),
             pltpu.VMEM((count, width), f32),
             pltpu.VMEM((count, lanes), f32),
             pltpu.VMEM(folded, jnp.int32),
@@ -428,16 +435,13 @@
     memories = [memory] + [exchange(memory, "core", s) for s in range(1, cores)]
     keys = [keys_of(memory, pltpu.HBM)] + [keys_of(value, pltpu.VMEM) for value in memories[1:]]
 
-    near = [packed] + [None] * (line - 1)
-    for s in range(line - 1, 0, -1):
-        near[s] = exchange(packed, "line", s)
-    part = join(near, [keys[0], *labels])
+    part = join([along_line(packed)], labels)
     labels = [value.reshape(1, slots) for value in labels]
     blocks = [part] + [None] * (groups - 1)
     for s in range(groups - 1, 0, -1):
         blocks[s] = exchange(part if s == groups - 1 else later, "grp", s)
         if s == groups - 1:
-            later = join([part], keys[1:])
+            later = join([part], keys)
 
     size = count * line
     arrived, after = [], []
@@ -452,12 +456,11 @@
     moved = pick(blocks, step_index, sizes, after)
     choices = [moved] + [exchange(moved, "core", s) for s in range(1, cores)]
 
-    sums, *others = add(held, arrived, size, count, 2 * parts, choices)
-    arrived = [exchange(others[s - 1], "line", s) for s in range(line - 1, 0, -1)]
+    sums = along_line(add(held, arrived, size, count, 2 * parts, choices))
     grad_batch, loss = call(
-        functools.partial(finish_kernel, len(arrived)),
+        finish_kernel,
         [shaped((count, width), f32), shaped((1, count), f32)],
-        sums, *arrived, unit, radius,
+        sums, unit, radius,
     )
 
     new_memory, new_labels = patch(copied, copied_labels, choices, step_index, sizes)

time: 46.3 us -> 54.6 us (1.18)
  waiting for transfers between devices: 9.17 us -> 15.5 us
  Pallas kernels: 17.5 us -> 18.9 us
    all_to_all x0 -> x2, waiting for transfers between devices: none -> 11.1 us  [along_line(): lax.all_to_all(value, 'dev', 0, 0, axis_index_groups=members_of, tiled=True)]
    ppermute x9 -> x3, starting transfers between devices: 10.2 us -> 0.73 us  [exchange(): return lax.ppermute(value, 'dev', [(i, i ^ step) for i in range(members)])]
    all_to_all x0 -> x2, starting transfers between devices: none -> 9.33 us  [along_line(): lax.all_to_all(value, 'dev', 0, 0, axis_index_groups=members_of, tiled=True)]
    ppermute x9 -> x3, waiting for transfers between devices: 4.89 us -> 0.97 us  [exchange(): return lax.ppermute(value, 'dev', [(i, i ^ step) for i in range(members)])]
    pallas_call x12, Pallas kernels: 17.5 us -> 18.9 us  [call(): pl.pallas_call(body, out_shape=outs, compiler_params=pltpu.CompilerParams...]
    ppermute x6, waiting for transfers between devices: 4.28 us -> 3.42 us  [exchange(): return lax.ppermute(value, 'grp', [(i, i ^ step) for i in range(groups)])]
  transfers between devices with their start and end apart: 15 -> 11, of which waited for: 7 -> 5; matrix products, arithmetic and copies ran while one was open for 0% -> 0% of each run, Pallas kernels for 36% -> 32%
where the time goes in v9:
time: 54.6 us; the launch traced here: 54.2 us
  Pallas kernels  18.9 us (35%)
  starting transfers between devices  18.4 us (34%)
  waiting for transfers between devices  15.5 us (28%)
  between operations  1.4 us (3%)
    pallas_call x12, Pallas kernels, call(): pl.pallas_call(body, out_shape=outs, compiler_params=pltpu.CompilerParams...  18.9 us
    all_to_all x2, waiting for transfers between devices, along_line(): lax.all_to_all(value, 'dev', 0, 0, axis_index_groups=members_of, tiled=True)  11.1 us
    all_to_all x2, starting transfers between devices, along_line(): lax.all_to_all(value, 'dev', 0, 0, axis_index_groups=members_of, tiled=True)  9.33 us
    ppermute x6, starting transfers between devices, exchange(): return lax.ppermute(value, 'grp', [(i, i ^ step) for i in range(groups)])  8.29 us
    ppermute x6, waiting for transfers between devices, exchange(): return lax.ppermute(value, 'grp', [(i, i ^ step) for i in range(groups)])  3.42 us
  transfers between devices with their start and end apart: 11, of which 5 were waited for; matrix products, arithmetic and copies ran while one was open for 0% of the time, Pallas kernels for 32%

profile of v9, /device:TPU:0, one launch (start us, length us, event | category | flops | bytes accessed | tf_op | source)
XLA Modules:
  0.0 54.2 jit_solution(4190201455391697467)
XLA Ops:
  0.6 0.5 collective-permute-start.1
  1.1 1.5 %shard_map.93 = (bf16[576,128]{1,0:T(8,128)(2,1)}, f32[32,512]{1,0:T(8,128)S(1)}, f32[32,128]{1,0:T(8,128)S(1)}, s32[16,128]{1,0:T(8,128)S(1)}, s32[16,128]{1,0:T(8,128)S(1)}) custom-call(bf16[32,512]{1,0:T(8,128)(2,1)} %rows_ref.1, s32[1,32]{1,0:T(1,128)} %bitcast.21, s32[16,128]{1,0:T(8,128)} %bitcast.19, s32[16,128]{1,0:T(8,128)} %bitcast.20), custom_call_target="tpu_custom_call" | custom-call | tf_op jit(solution)/shard_map/pallas_call | solution.py:23
  2.7 5.9 %all-to-all-start = ((bf16[4,144,128]{2,1,0:T(8,128)(2,1)}), bf16[4,144,128]{2,1,0:T(8,128)(2,1)S(1)}, u32[]{:S(2)}, u32[]{:S(2)}) async-start(bf16[4,144,128]{2,1,0:T(8,128)(2,1)} %bitcast.3), calls=%async_computation | async-start | bytes 294912 | tf_op jit(solution)/shard_map/all_to_all | solution.py:412
  8.6 0.2 collective-permute-start
  8.8 1.0 %collective-permute-done.refs_2_ = s32[16,128]{1,0:T(8,128)S(1)} collective-permute-done((s32[16,128]{1,0:T(8,128)S(1)}, s32[16,128]{1,0:T(8,128)S(1)}, u32[]{:S(2)}, u32[]{:S(2)}) %collective-permute-start) | collective-permute-done | bytes 8224 | tf_op jit(solution)/shard_map/ppermute | solution.py:417
  9.8 5.5 %all-to-all-done = bf16[4,144,128]{2,1,0:T(8,128)(2,1)S(1)} async-done(((bf16[4,144,128]{2,1,0:T(8,128)(2,1)}), bf16[4,144,128]{2,1,0:T(8,128)(2,1)S(1)}, u32[]{:S(2)}, u32[]{:S(2)}) %all-to-all-start) | async-done | bytes 147488 | tf_op jit(solution)/shard_map/all_to_all | solution.py:412
  15.3 2.5 %collective-permute-start.4 = (bf16[576,128]{1,0:T(8,128)(2,1)S(1)}, bf16[576,128]{1,0:T(8,128)(2,1)S(1)}, u32[]{:S(2)}, u32[]{:S(2)}) collective-permute-start(bf16[576,128]{1,0:T(8,128)(2,1)S(1)} %shard_map.94.refs_0_), channel_id=1, source_target_pairs={{0,24},{8,16},{16,8},{24,0},{1,25},{9,17},{17,9},{25,1},{2,26},{10... | collective-permute-start | bytes 442376 | tf_op jit(solution)/shard_map/ppermute | solution.py:416
  17.8 2.9 %shard_map.95.refs_1_.refs_2_ = bf16[2048,512]{1,0:T(8,128)(2,1)S(1)} custom-call(bf16[2048,512]{1,0:T(8,128)(2,1)} %refs_5_.1), custom_call_target="tpu_custom_call" | custom-call | tf_op jit(solution)/shard_map/pallas_call | solution.py:23
  21.3 0.0 collective-permute-done.1.memory_ref
  21.3 1.0 %shard_map.96.refs_2_.refs_3_ = bf16[2048,512]{1,0:T(8,128)(2,1)S(1)} custom-call(bf16[2048,512]{1,0:T(8,128)(2,1)S(1)} %collective-permute-done.1.memory_ref), custom_call_target="tpu_custom_call" | custom-call | tf_op jit(solution)/shard_map/pallas_call | solution.py:23
  22.3 0.6 %collective-permute-start.2 = (bf16[576,128]{1,0:T(8,128)(2,1)S(1)}, bf16[576,128]{1,0:T(8,128)(2,1)S(1)}, u32[]{:S(2)}, u32[]{:S(2)}) collective-permute-start(bf16[576,128]{1,0:T(8,128)(2,1)S(1)} %shard_map.97), channel_id=1, source_target_pairs={{0,16},{8,24},{16,0},{24,8},{1,17},{9,25},{17,1},{25,9},{2,18},{10... | collective-permute-start | bytes 442376 | tf_op jit(solution)/shard_map/ppermute | solution.py:416
  22.9 0.5 collective-permute-start.3
  23.4 0.0 collective-permute-done.4.refs_0_.refs_3_
  23.4 2.9 %shard_map.98.refs_6_ = bf16[1040,128]{1,0:T(8,128)(2,1)S(1)} custom-call(bf16[576,128]{1,0:T(8,128)(2,1)S(1)} %collective-permute-done.4.refs_0_.refs_3_, bf16[2048,512]{1,0:T(8,128)(2,1)S(1)} %shard_map.95.refs_1_.refs_2_, bf16[2048,512]{1,0:T(8,128)(2,1)S(1)} %shard_map.96.refs_2_.refs_3_, s32[1,2048]{1,0:T(1,128)S(1)} %bitcast.13, s32[1,2048]{1,0:T(1,128)S(1)} %bitcast.16), custom_call_target="tpu_custom_call" | custom-call | flops 3221225472 | tf_op jit(solution)/shard_map/pallas_call | solution.py:23
  26.4 0.0 copy-start
  26.4 2.5 %collective-permute-start.5 = (bf16[1040,128]{1,0:T(8,128)(2,1)S(1)}, bf16[1040,128]{1,0:T(8,128)(2,1)S(1)}, u32[]{:S(2)}, u32[]{:S(2)}) collective-permute-start(bf16[1040,128]{1,0:T(8,128)(2,1)S(1)} %shard_map.98.refs_6_), channel_id=1, source_target_pairs={{0,24},{8,16},{16,8},{24,0},{1,25},{9,17},{17,9},{25,1},{2,26},{10... | collective-permute-start | bytes 798728 | tf_op jit(solution)/shard_map/ppermute | solution.py:416
  28.9 0.0 collective-permute-done.2.refs_0_.refs_2_
  28.9 0.0 collective-permute-done.3.refs_1_
  28.9 4.7 %shard_map.99 = (bf16[1040,128]{1,0:T(8,128)(2,1)S(1)}, bf16[1040,128]{1,0:T(8,128)(2,1)S(1)}) custom-call(bf16[576,128]{1,0:T(8,128)(2,1)S(1)} %collective-permute-done.2.refs_0_.refs_2_, bf16[576,128]{1,0:T(8,128)(2,1)S(1)} %collective-permute-done.3.refs_1_, bf16[2048,512]{1,0:T(8,128)(2,1)S(1)} %shard_map.95.refs_1_.refs_2_, ...), custom_call_target="tpu_custom_call" | custom-call | flops 6442450944 | tf_op jit(solution)/shard_map/pallas_call | solution.py:23
  33.6 2.1 %collective-permute-start.6 = (bf16[1040,128]{1,0:T(8,128)(2,1)S(1)}, bf16[1040,128]{1,0:T(8,128)(2,1)S(1)}, u32[]{:S(2)}, u32[]{:S(2)}) collective-permute-start(bf16[1040,128]{1,0:T(8,128)(2,1)S(1)} %get-tuple-element.19.refs_6_.refs_4_), channel_id=1, source_target_pairs={{0,16},{8,24},{16,0},{24,8},{1,17},{9,25},{17,1},{25,9},{2,18},{10... | collective-permute-start | bytes 798728 | tf_op jit(solution)/shard_map/ppermute | solution.py:416
  35.7 0.0 collective-permute-start.7
  35.7 0.0 collective-permute-start.8
  35.7 2.9 %shard_map.100 = (f32[1040,128]{1,0:T(8,128)S(1)}, bf16[2048,512]{1,0:T(8,128)(2,1)}) custom-call(bf16[576,128]{1,0:T(8,128)(2,1)S(1)} %shard_map.94.refs_0_, bf16[2048,512]{1,0:T(8,128)(2,1)S(1)} %shard_map.95.refs_1_.refs_2_, bf16[2048,512]{1,0:T(8,128)(2,1)S(1)} %shard_map.96.refs_2_.refs_3_, s32[1,2048]{1,0:T(1,128)S(1)} %bitcast.15, ...), custom_call_target="tpu_custom_call" | custom-call | flops 3221225472 | tf_op jit(solution)/shard_map/pallas_call | solution.py:23
  38.7 0.0 collective-permute-done.8.refs_5_.refs_1_
  38.7 0.0 collective-permute-done.5.refs_1_
  38.7 1.7 %collective-permute-done.6.refs_2_ = bf16[1040,128]{1,0:T(8,128)(2,1)S(1)} collective-permute-done((bf16[1040,128]{1,0:T(8,128)(2,1)S(1)}, bf16[1040,128]{1,0:T(8,128)(2,1)S(1)}, u32[]{:S(2)}, u32[]{:S(2)}) %collective-permute-start.6) | collective-permute-done | bytes 266272 | tf_op jit(solution)/shard_map/ppermute | solution.py:416
  40.4 1.7 %collective-permute-done.7.refs_3_ = bf16[1040,128]{1,0:T(8,128)(2,1)S(1)} collective-permute-done((bf16[1040,128]{1,0:T(8,128)(2,1)S(1)}, bf16[1040,128]{1,0:T(8,128)(2,1)S(1)}, u32[]{:S(2)}, u32[]{:S(2)}) %collective-permute-start.7) | collective-permute-done | bytes 266272 | tf_op jit(solution)/shard_map/ppermute | solution.py:416
  42.1 0.8 %shard_map.102 = bf16[1088,128]{1,0:T(8,128)(2,1)} custom-call(f32[1040,128]{1,0:T(8,128)S(1)} %get-tuple-element.21.refs_0_, bf16[1040,128]{1,0:T(8,128)(2,1)S(1)} %collective-permute-done.5.refs_1_, bf16[1040,128]{1,0:T(8,128)(2,1)S(1)} %collective-permute-done.6.refs_2_, bf16[1040,128]{1,0:T(8,128)(2,1)S(1)} %collective-permute-done.7.refs_3_, ...), custom_call_target="tpu_custom_call" | custom-call | tf_op jit(solution)/shard_map/pallas_call | solution.py:23
  43.0 3.4 %all-to-all-start.1 = ((bf16[4,272,128]{2,1,0:T(8,128)(2,1)}), bf16[4,272,128]{2,1,0:T(8,128)(2,1)S(1)}, u32[]{:S(2)}, u32[]{:S(2)}) async-start(bf16[4,272,128]{2,1,0:T(8,128)(2,1)} %bitcast.7), calls=%async_computation.1 | async-start | bytes 557056 | tf_op jit(solution)/shard_map/all_to_all | solution.py:412
  46.4 1.2 %shard_map.104 = (bf16[2048,512]{1,0:T(8,128)(2,1)}, s32[16,128]{1,0:T(8,128)}) custom-call(s32[1]{0:T(128)S(6)} %copy.12.step_ref, bf16[2048,512]{1,0:T(8,128)(2,1)} %get-tuple-element.26.stored_ref, s32[16,128]{1,0:T(8,128)S(1)} %get-tuple-element.27.labels_ref, bf16[144,128]{1,0:T(8,128)(2,1)S(1)} %shard_map.101.refs_4_.refs_0_, ...), custom_call_target="tpu_custom_call", output_to_operand_aliasing={{0}: (1, {})} | custom-call | tf_op jit(solution)/shard_map/pallas_call | solution.py:23
  47.7 5.6 %all-to-all-done.1 = bf16[4,272,128]{2,1,0:T(8,128)(2,1)S(1)} async-done(((bf16[4,272,128]{2,1,0:T(8,128)(2,1)}), bf16[4,272,128]{2,1,0:T(8,128)(2,1)S(1)}, u32[]{:S(2)}, u32[]{:S(2)}) %all-to-all-start.1) | async-done | bytes 278560 | tf_op jit(solution)/shard_map/all_to_all | solution.py:412
  53.3 0.9 %shard_map.103 = (f32[32,512]{1,0:T(8,128)}, f32[1,32]{1,0:T(1,128)}) custom-call(bf16[1088,128]{1,0:T(8,128)(2,1)S(1)} %bitcast.11, f32[32,512]{1,0:T(8,128)S(1)} %get-tuple-element.22.unit_ref, f32[32,128]{1,0:T(8,128)S(1)} %get-tuple-element.23.radius_ref), custom_call_target="tpu_custom_call" | custom-call | tf_op jit(solution)/shard_map/pallas_call | solution.py:23
  (4 shorter events, 0.0 us)
Async XLA Ops:
  0.6 20.7 %collective-permute-start.1 = (bf16[2048,512]{1,0:T(8,128)(2,1)}, bf16[2048,512]{1,0:T(8,128)(2,1)S(1)}, u32[]{:S(2)}, u32[]{:S(2)}) collective-permute-start(bf16[2048,512]{1,0:T(8,128)(2,1)} %refs_5_.1), channel_id=1, source_target_pairs={{0,1},{1,0},{2,3},{3,2},{4,5},{5,4},{6,7},{7,6},{8,9},{9,8},{10,11... | collective-permute-start | bytes 6291464 | tf_op jit(solution)/shard_map/ppermute | solution.py:417
  2.7 12.6 %all-to-all-start = ((bf16[4,144,128]{2,1,0:T(8,128)(2,1)}), bf16[4,144,128]{2,1,0:T(8,128)(2,1)S(1)}, u32[]{:S(2)}, u32[]{:S(2)}) async-start(bf16[4,144,128]{2,1,0:T(8,128)(2,1)} %bitcast.3), calls=%async_computation | async-start | bytes 294912 | tf_op jit(solution)/shard_map/all_to_all | solution.py:412
  8.6 1.2 %collective-permute-start = (s32[16,128]{1,0:T(8,128)S(1)}, s32[16,128]{1,0:T(8,128)S(1)}, u32[]{:S(2)}, u32[]{:S(2)}) collective-permute-start(s32[16,128]{1,0:T(8,128)S(1)} %get-tuple-element.18.refs_1_), channel_id=1, source_target_pairs={{0,1},{1,0},{2,3},{3,2},{4,5},{5,4},{6,7},{7,6},{8,9},{9,8},{10,11... | collective-permute-start | bytes 24584 | tf_op jit(solution)/shard_map/ppermute | solution.py:417
  15.3 8.2 %collective-permute-start.4 = (bf16[576,128]{1,0:T(8,128)(2,1)S(1)}, bf16[576,128]{1,0:T(8,128)(2,1)S(1)}, u32[]{:S(2)}, u32[]{:S(2)}) collective-permute-start(bf16[576,128]{1,0:T(8,128)(2,1)S(1)} %shard_map.94.refs_0_), channel_id=1, source_target_pairs={{0,24},{8,16},{16,8},{24,0},{1,25},{9,17},{17,9},{25,1},{2,26},{10... | collective-permute-start | bytes 442376 | tf_op jit(solution)/shard_map/ppermute | solution.py:416
  22.3 6.6 %collective-permute-start.2 = (bf16[576,128]{1,0:T(8,128)(2,1)S(1)}, bf16[576,128]{1,0:T(8,128)(2,1)S(1)}, u32[]{:S(2)}, u32[]{:S(2)}) collective-permute-start(bf16[576,128]{1,0:T(8,128)(2,1)S(1)} %shard_map.97), channel_id=1, source_target_pairs={{0,16},{8,24},{16,0},{24,8},{1,17},{9,25},{17,1},{25,9},{2,18},{10... | collective-permute-start | bytes 442376 | tf_op jit(solution)/shard_map/ppermute | solution.py:416
  22.9 6.0 %collective-permute-start.3 = (bf16[576,128]{1,0:T(8,128)(2,1)S(1)}, bf16[576,128]{1,0:T(8,128)(2,1)S(1)}, u32[]{:S(2)}, u32[]{:S(2)}) collective-permute-start(bf16[576,128]{1,0:T(8,128)(2,1)S(1)} %shard_map.97), channel_id=1, source_target_pairs={{0,8},{8,0},{16,24},{24,16},{1,9},{9,1},{17,25},{25,17},{2,10},{10... | collective-permute-start | bytes 442376 | tf_op jit(solution)/shard_map/ppermute | solution.py:416
  26.4 9.4 %copy-start = (bf16[2048,512]{1,0:T(8,128)(2,1)S(1)}, bf16[2048,512]{1,0:T(8,128)(2,1)}, u32[]{:S(2)}) copy-start(bf16[2048,512]{1,0:T(8,128)(2,1)} %refs_5_.1) | copy-start | bytes 6291460
  26.4 12.3 %collective-permute-start.5 = (bf16[1040,128]{1,0:T(8,128)(2,1)S(1)}, bf16[1040,128]{1,0:T(8,128)(2,1)S(1)}, u32[]{:S(2)}, u32[]{:S(2)}) collective-permute-start(bf16[1040,128]{1,0:T(8,128)(2,1)S(1)} %shard_map.98.refs_6_), channel_id=1, source_target_pairs={{0,24},{8,16},{16,8},{24,0},{1,25},{9,17},{17,9},{25,1},{2,26},{10... | collective-permute-start | bytes 798728 | tf_op jit(solution)/shard_map/ppermute | solution.py:416
  33.6 6.8 %collective-permute-start.6 = (bf16[1040,128]{1,0:T(8,128)(2,1)S(1)}, bf16[1040,128]{1,0:T(8,128)(2,1)S(1)}, u32[]{:S(2)}, u32[]{:S(2)}) collective-permute-start(bf16[1040,128]{1,0:T(8,128)(2,1)S(1)} %get-tuple-element.19.refs_6_.refs_4_), channel_id=1, source_target_pairs={{0,16},{8,24},{16,0},{24,8},{1,17},{9,25},{17,1},{25,9},{2,18},{10... | collective-permute-start | bytes 798728 | tf_op jit(solution)/shard_map/ppermute | solution.py:416
  35.7 6.4 %collective-permute-start.7 = (bf16[1040,128]{1,0:T(8,128)(2,1)S(1)}, bf16[1040,128]{1,0:T(8,128)(2,1)S(1)}, u32[]{:S(2)}, u32[]{:S(2)}) collective-permute-start(bf16[1040,128]{1,0:T(8,128)(2,1)S(1)} %get-tuple-element.20.refs_7_.refs_5_), channel_id=1, source_target_pairs={{0,8},{8,0},{16,24},{24,16},{1,9},{9,1},{17,25},{25,17},{2,10},{10... | collective-permute-start | bytes 798728 | tf_op jit(solution)/shard_map/ppermute | solution.py:416
  35.7 3.0 %collective-permute-start.8 = (bf16[144,128]{1,0:T(8,128)(2,1)S(1)}, bf16[144,128]{1,0:T(8,128)(2,1)S(1)}, u32[]{:S(2)}, u32[]{:S(2)}) collective-permute-start(bf16[144,128]{1,0:T(8,128)(2,1)S(1)} %shard_map.101.refs_4_.refs_0_), channel_id=1, source_target_pairs={{0,1},{1,0},{2,3},{3,2},{4,5},{5,4},{6,7},{7,6},{8,9},{9,8},{10,11... | collective-permute-start | bytes 110600 | tf_op jit(solution)/shard_map/ppermute | solution.py:417
  43.0 10.3 %all-to-all-start.1 = ((bf16[4,272,128]{2,1,0:T(8,128)(2,1)}), bf16[4,272,128]{2,1,0:T(8,128)(2,1)S(1)}, u32[]{:S(2)}, u32[]{:S(2)}) async-start(bf16[4,272,128]{2,1,0:T(8,128)(2,1)} %bitcast.7), calls=%async_computation.1 | async-start | bytes 557056 | tf_op jit(solution)/shard_map/all_to_all | solution.py:412

commit v10 on v8

--- a/solution.py
+++ b/solution.py
@@ -90,22 +90,24 @@
     return jnp.sum(jnp.where(diagonal(count), spread, 0.0), axis=0, keepdims=True)
 
 
-def keys_kernel(memory_ref, keys_ref):
+def keys_kernel(memory_ref, *refs):
+    keys_ref = refs[-1]
     rows = memory_ref[...].astype(f32)
     radius = jnp.sqrt(jnp.sum(rows * rows, axis=1, keepdims=True) + 1e-06)
     keys_ref[...] = (rows / radius).astype(bf16)
 
 
-def keys_of(memory, place):
+def keys_of(memory, place, after):
     slots, width = memory.shape
     block = math.gcd(512, slots)
     spec = pl.BlockSpec((block, width), lambda i: (i, 0))
     return call(
         keys_kernel,
         [shaped((slots, width), bf16)],
-        pltpu.with_memory_space_constraint(memory, place),
+        pltpu.with_memory_space_constraint(memory, place), *after,
+        work=64 * slots * width * width,
         grid=(slots // block,),
-        in_specs=[spec],
+        in_specs=[spec] + [pl.BlockSpec(memory_space=pl.ANY)] * len(after),
         out_specs=[spec],
     )[0]
 
@@ -317,7 +319,7 @@
     anywhere = pl.BlockSpec(memory_space=pl.ANY)
     vmem = pl.BlockSpec(memory_space=pltpu.VMEM)
     return call(
-        functools.partial(block_kernel, len(blocks), len(keys), math.gcd(1024, slots), count, len(copied)),
+        functools.partial(block_kernel, len(blocks), len(keys), math.gcd(512, slots), count, len(copied)),
         [shaped((2 * parts * size + sum_rows(size), lanes), dtype)] * len(blocks)
         + [shaped(value.shape, value.dtype) for value in copied],
         *blocks, *[in_vmem(k) for k in keys], *labels, *copied, *after,
@@ -426,18 +428,16 @@
 
     labels = [slot_labels] + [exchange(slot_labels, "core", s) for s in range(1, cores)]
     memories = [memory] + [exchange(memory, "core", s) for s in range(1, cores)]
-    keys = [keys_of(memory, pltpu.HBM)] + [keys_of(value, pltpu.VMEM) for value in memories[1:]]
 
     near = [packed] + [None] * (line - 1)
     for s in range(line - 1, 0, -1):
         near[s] = exchange(packed, "line", s)
-    part = join(near, [keys[0], *labels])
+    part = join(near, labels)
     labels = [value.reshape(1, slots) for value in labels]
     blocks = [part] + [None] * (groups - 1)
     for s in range(groups - 1, 0, -1):
-        blocks[s] = exchange(part if s == groups - 1 else later, "grp", s)
-        if s == groups - 1:
-            later = join([part], keys[1:])
+        blocks[s] = exchange(part, "grp", s)
+    keys = [keys_of(memory, pltpu.HBM, [part])] + [keys_of(value, pltpu.VMEM, [part]) for value in memories[1:]]
 
     size = count * line
     arrived, after = [], []

time: 46.3 us -> 46.3 us (level)
    ppermute x6, waiting for transfers between devices: 4.28 us -> 2.94 us  [exchange(): return lax.ppermute(value, 'grp', [(i, i ^ step) for i in range(groups)])]
    ppermute x9, waiting for transfers between devices: 4.89 us -> 6.16 us  [exchange(): return lax.ppermute(value, 'dev', [(i, i ^ jump) for i in range(members)])]
    ppermute x6, starting transfers between devices: 7.75 us -> 7.17 us  [exchange(): return lax.ppermute(value, 'grp', [(i, i ^ step) for i in range(groups)])]
    pallas_call x12 -> x11, Pallas kernels: 17.5 us -> 17.7 us  [call(): pl.pallas_call(body, out_shape=outs, compiler_params=pltpu.CompilerParams...]
  transfers between devices with their start and end apart: 15 -> 15, of which waited for: 7 -> 7; matrix products, arithmetic and copies ran while one was open for 0% -> 0% of each run, Pallas kernels for 36% -> 34%
where the time goes in v10:
time: 46.3 us; the launch traced here: 46 us
  starting transfers between devices  17.8 us (38%)
  Pallas kernels  17.7 us (38%)
  waiting for transfers between devices  9.1 us (20%)
  between operations  1.39 us (3%)
    pallas_call x11, Pallas kernels, call(): pl.pallas_call(body, out_shape=outs, compiler_params=pltpu.CompilerParams...  17.7 us
    ppermute x9, starting transfers between devices, exchange(): return lax.ppermute(value, 'dev', [(i, i ^ jump) for i in range(members)])  10.6 us
    ppermute x6, starting transfers between devices, exchange(): return lax.ppermute(value, 'grp', [(i, i ^ step) for i in range(groups)])  7.17 us
    ppermute x9, waiting for transfers between devices, exchange(): return lax.ppermute(value, 'dev', [(i, i ^ jump) for i in range(members)])  6.16 us
    ppermute x6, waiting for transfers between devices, exchange(): return lax.ppermute(value, 'grp', [(i, i ^ step) for i in range(groups)])  2.94 us
  transfers between devices with their start and end apart: 15, of which 7 were waited for; matrix products, arithmetic and copies ran while one was open for 0% of the time, Pallas kernels for 34%

profile of v10, /device:TPU:0, one launch (start us, length us, event | category | flops | bytes accessed | tf_op | source)
XLA Modules:
  0.0 46.0 jit_solution(15426836444897697964)
XLA Ops:
  0.6 0.9 %shard_map.93 = (bf16[144,128]{1,0:T(8,128)(2,1)S(1)}, f32[32,512]{1,0:T(8,128)S(1)}, f32[32,128]{1,0:T(8,128)S(1)}, s32[16,128]{1,0:T(8,128)S(1)}, s32[16,128]{1,0:T(8,128)S(1)}) custom-call(bf16[32,512]{1,0:T(8,128)(2,1)} %rows_ref.1, s32[1,32]{1,0:T(1,128)} %bitcast.15, s32[16,128]{1,0:T(8,128)} %bitcast.13, s32[16,128]{1,0:T(8,128)} %bitcast.14), custom_call_target="tpu_custom_call" | custom-call | tf_op jit(solution)/shard_map/pallas_call | solution.py:23
  1.5 3.1 %collective-permute-start = (bf16[144,128]{1,0:T(8,128)(2,1)S(1)}, bf16[144,128]{1,0:T(8,128)(2,1)S(1)}, u32[]{:S(2)}, u32[]{:S(2)}) collective-permute-start(bf16[144,128]{1,0:T(8,128)(2,1)S(1)} %get-tuple-element.21.refs_0_), channel_id=1, source_target_pairs={{0,2},{1,3},{2,0},{3,1},{4,6},{5,7},{6,4},{7,5},{8,10},{9,11},{10,... | collective-permute-start | bytes 110600 | tf_op jit(solution)/shard_map/ppermute | solution.py:412
  4.6 2.6 %collective-permute-start.1 = (bf16[144,128]{1,0:T(8,128)(2,1)S(1)}, bf16[144,128]{1,0:T(8,128)(2,1)S(1)}, u32[]{:S(2)}, u32[]{:S(2)}) collective-permute-start(bf16[144,128]{1,0:T(8,128)(2,1)S(1)} %get-tuple-element.21.refs_0_), channel_id=1, source_target_pairs={{0,4},{1,5},{2,6},{3,7},{4,0},{5,1},{6,2},{7,3},{8,12},{9,13},{10,... | collective-permute-start | bytes 110600 | tf_op jit(solution)/shard_map/ppermute | solution.py:412
  7.2 0.0 collective-permute-start.2
  7.2 0.0 collective-permute-start.3
  7.2 0.5 %collective-permute-start.4 = (bf16[2048,512]{1,0:T(8,128)(2,1)}, bf16[2048,512]{1,0:T(8,128)(2,1)S(1)}, u32[]{:S(2)}, u32[]{:S(2)}) collective-permute-start(bf16[2048,512]{1,0:T(8,128)(2,1)} %refs_5_.1), channel_id=1, source_target_pairs={{0,1},{1,0},{2,3},{3,2},{4,5},{5,4},{6,7},{7,6},{8,9},{9,8},{10,11... | collective-permute-start | bytes 6291464 | tf_op jit(solution)/shard_map/ppermute | solution.py:412
  8.4 0.0 collective-permute-done.3.refs_5_
  8.4 1.8 %collective-permute-done.1.refs_2_ = bf16[144,128]{1,0:T(8,128)(2,1)S(1)} collective-permute-done((bf16[144,128]{1,0:T(8,128)(2,1)S(1)}, bf16[144,128]{1,0:T(8,128)(2,1)S(1)}, u32[]{:S(2)}, u32[]{:S(2)}) %collective-permute-start.1) | collective-permute-done | bytes 36896 | tf_op jit(solution)/shard_map/ppermute | solution.py:412
  10.1 2.8 %collective-permute-done.2.refs_3_ = bf16[144,128]{1,0:T(8,128)(2,1)S(1)} collective-permute-done((bf16[144,128]{1,0:T(8,128)(2,1)S(1)}, bf16[144,128]{1,0:T(8,128)(2,1)S(1)}, u32[]{:S(2)}, u32[]{:S(2)}) %collective-permute-start.2) | collective-permute-done | bytes 36896 | tf_op jit(solution)/shard_map/ppermute | solution.py:412
  13.0 2.5 %collective-permute-start.7 = (bf16[576,128]{1,0:T(8,128)(2,1)S(1)}, bf16[576,128]{1,0:T(8,128)(2,1)S(1)}, u32[]{:S(2)}, u32[]{:S(2)}) collective-permute-start(bf16[576,128]{1,0:T(8,128)(2,1)S(1)} %shard_map.94.refs_0_), channel_id=1, source_target_pairs={{0,24},{8,16},{16,8},{24,0},{1,25},{9,17},{17,9},{25,1},{2,26},{10... | collective-permute-start | bytes 442376 | tf_op jit(solution)/shard_map/ppermute | solution.py:410
  15.5 0.5 %collective-permute-start.5 = (bf16[576,128]{1,0:T(8,128)(2,1)S(1)}, bf16[576,128]{1,0:T(8,128)(2,1)S(1)}, u32[]{:S(2)}, u32[]{:S(2)}) collective-permute-start(bf16[576,128]{1,0:T(8,128)(2,1)S(1)} %shard_map.94.refs_0_), channel_id=1, source_target_pairs={{0,16},{8,24},{16,0},{24,8},{1,17},{9,25},{17,1},{25,9},{2,18},{10... | collective-permute-start | bytes 442376 | tf_op jit(solution)/shard_map/ppermute | solution.py:410
  16.0 0.5 %collective-permute-start.6 = (bf16[576,128]{1,0:T(8,128)(2,1)S(1)}, bf16[576,128]{1,0:T(8,128)(2,1)S(1)}, u32[]{:S(2)}, u32[]{:S(2)}) collective-permute-start(bf16[576,128]{1,0:T(8,128)(2,1)S(1)} %shard_map.94.refs_0_), channel_id=1, source_target_pairs={{0,8},{8,0},{16,24},{24,16},{1,9},{9,1},{17,25},{25,17},{2,10},{10... | collective-permute-start | bytes 442376 | tf_op jit(solution)/shard_map/ppermute | solution.py:410
  16.5 2.9 %shard_map.95.refs_1_.refs_2_ = bf16[2048,512]{1,0:T(8,128)(2,1)S(1)} custom-call(bf16[2048,512]{1,0:T(8,128)(2,1)} %refs_5_.1, bf16[576,128]{1,0:T(8,128)(2,1)S(1)} %shard_map.94.refs_0_), custom_call_target="tpu_custom_call" | custom-call | flops 34359738368 | tf_op jit(solution)/shard_map/pallas_call | solution.py:23
  19.4 1.0 %shard_map.96.refs_2_.refs_3_ = bf16[2048,512]{1,0:T(8,128)(2,1)S(1)} custom-call(bf16[2048,512]{1,0:T(8,128)(2,1)S(1)} %collective-permute-done.4.memory_ref, bf16[576,128]{1,0:T(8,128)(2,1)S(1)} %shard_map.94.refs_0_), custom_call_target="tpu_custom_call" | custom-call | flops 34359738368 | tf_op jit(solution)/shard_map/pallas_call | solution.py:23
  20.4 0.1 collective-permute-done.7.refs_0_.refs_3_
  20.5 2.9 %shard_map.97.refs_6_ = bf16[1040,128]{1,0:T(8,128)(2,1)S(1)} custom-call(bf16[576,128]{1,0:T(8,128)(2,1)S(1)} %collective-permute-done.7.refs_0_.refs_3_, bf16[2048,512]{1,0:T(8,128)(2,1)S(1)} %shard_map.95.refs_1_.refs_2_, bf16[2048,512]{1,0:T(8,128)(2,1)S(1)} %shard_map.96.refs_2_.refs_3_, s32[1,2048]{1,0:T(1,128)S(1)} %bitcast.7, s32[1,2048]{1,0:T(1,128)S(1)} %bitcast.10), custom_call_target="tpu_custom_call" | custom-call | flops 3221225472 | tf_op jit(solution)/shard_map/pallas_call | solution.py:23
  23.4 0.0 copy-start
  23.4 2.4 %collective-permute-start.8 = (bf16[1040,128]{1,0:T(8,128)(2,1)S(1)}, bf16[1040,128]{1,0:T(8,128)(2,1)S(1)}, u32[]{:S(2)}, u32[]{:S(2)}) collective-permute-start(bf16[1040,128]{1,0:T(8,128)(2,1)S(1)} %shard_map.97.refs_6_), channel_id=1, source_target_pairs={{0,24},{8,16},{16,8},{24,0},{1,25},{9,17},{17,9},{25,1},{2,26},{10... | collective-permute-start | bytes 798728 | tf_op jit(solution)/shard_map/ppermute | solution.py:410
  25.9 4.9 %shard_map.98 = (bf16[1040,128]{1,0:T(8,128)(2,1)S(1)}, bf16[1040,128]{1,0:T(8,128)(2,1)S(1)}) custom-call(bf16[576,128]{1,0:T(8,128)(2,1)S(1)} %collective-permute-done.5.refs_0_.refs_2_, bf16[576,128]{1,0:T(8,128)(2,1)S(1)} %collective-permute-done.6.refs_1_, bf16[2048,512]{1,0:T(8,128)(2,1)S(1)} %shard_map.95.refs_1_.refs_2_, ...), custom_call_target="tpu_custom_call" | custom-call | flops 6442450944 | tf_op jit(solution)/shard_map/pallas_call | solution.py:23
  30.7 0.6 %collective-permute-start.10 = (bf16[1040,128]{1,0:T(8,128)(2,1)S(1)}, bf16[1040,128]{1,0:T(8,128)(2,1)S(1)}, u32[]{:S(2)}, u32[]{:S(2)}) collective-permute-start(bf16[1040,128]{1,0:T(8,128)(2,1)S(1)} %get-tuple-element.24.refs_7_.refs_5_), channel_id=1, source_target_pairs={{0,8},{8,0},{16,24},{24,16},{1,9},{9,1},{17,25},{25,17},{2,10},{10... | collective-permute-start | bytes 798728 | tf_op jit(solution)/shard_map/ppermute | solution.py:410
  31.4 0.6 %collective-permute-start.9 = (bf16[1040,128]{1,0:T(8,128)(2,1)S(1)}, bf16[1040,128]{1,0:T(8,128)(2,1)S(1)}, u32[]{:S(2)}, u32[]{:S(2)}) collective-permute-start(bf16[1040,128]{1,0:T(8,128)(2,1)S(1)} %get-tuple-element.23.refs_6_.refs_4_), channel_id=1, source_target_pairs={{0,16},{8,24},{16,0},{24,8},{1,17},{9,25},{17,1},{25,9},{2,18},{10... | collective-permute-start | bytes 798728 | tf_op jit(solution)/shard_map/ppermute | solution.py:410
  31.9 3.0 %shard_map.99 = (f32[1040,128]{1,0:T(8,128)S(1)}, bf16[2048,512]{1,0:T(8,128)(2,1)}) custom-call(bf16[576,128]{1,0:T(8,128)(2,1)S(1)} %shard_map.94.refs_0_, bf16[2048,512]{1,0:T(8,128)(2,1)S(1)} %shard_map.95.refs_1_.refs_2_, bf16[2048,512]{1,0:T(8,128)(2,1)S(1)} %shard_map.96.refs_2_.refs_3_, s32[1,2048]{1,0:T(1,128)S(1)} %bitcast.9, ...), custom_call_target="tpu_custom_call" | custom-call | flops 3221225472 | tf_op jit(solution)/shard_map/pallas_call | solution.py:23
  34.9 2.3 %collective-permute-done.10.refs_3_ = bf16[1040,128]{1,0:T(8,128)(2,1)S(1)} collective-permute-done((bf16[1040,128]{1,0:T(8,128)(2,1)S(1)}, bf16[1040,128]{1,0:T(8,128)(2,1)S(1)}, u32[]{:S(2)}, u32[]{:S(2)}) %collective-permute-start.10) | collective-permute-done | bytes 266272 | tf_op jit(solution)/shard_map/ppermute | solution.py:410
  37.2 0.5 %collective-permute-done.9.refs_2_ = bf16[1040,128]{1,0:T(8,128)(2,1)S(1)} collective-permute-done((bf16[1040,128]{1,0:T(8,128)(2,1)S(1)}, bf16[1040,128]{1,0:T(8,128)(2,1)S(1)}, u32[]{:S(2)}, u32[]{:S(2)}) %collective-permute-start.9) | collective-permute-done | bytes 266272 | tf_op jit(solution)/shard_map/ppermute | solution.py:410
  37.8 0.1 shard_map.101
  37.9 0.6 %collective-permute-start.12 = (bf16[272,128]{1,0:T(8,128)(2,1)S(1)}, bf16[272,128]{1,0:T(8,128)(2,1)S(1)}, u32[]{:S(2)}, u32[]{:S(2)}) collective-permute-start(bf16[272,128]{1,0:T(8,128)(2,1)S(1)} %get-tuple-element.27), channel_id=1, source_target_pairs={{0,6},{1,7},{2,4},{3,5},{4,2},{5,3},{6,0},{7,1},{8,14},{9,15},{10,... | collective-permute-start | bytes 208904 | tf_op jit(solution)/shard_map/ppermute | solution.py:412
  38.5 0.0 collective-permute-start.13
  38.5 3.9 %collective-permute-start.14 = (bf16[272,128]{1,0:T(8,128)(2,1)S(1)}, bf16[272,128]{1,0:T(8,128)(2,1)S(1)}, u32[]{:S(2)}, u32[]{:S(2)}) collective-permute-start(bf16[272,128]{1,0:T(8,128)(2,1)S(1)} %get-tuple-element.29), channel_id=1, source_target_pairs={{0,2},{1,3},{2,0},{3,1},{4,6},{5,7},{6,4},{7,5},{8,10},{9,11},{10,... | collective-permute-start | bytes 208904 | tf_op jit(solution)/shard_map/ppermute | solution.py:412
  42.4 1.2 %shard_map.103 = (bf16[2048,512]{1,0:T(8,128)(2,1)}, s32[16,128]{1,0:T(8,128)}) custom-call(s32[1]{0:T(128)S(6)} %copy.12.step_ref, bf16[2048,512]{1,0:T(8,128)(2,1)} %get-tuple-element.34.stored_ref, s32[16,128]{1,0:T(8,128)S(1)} %get-tuple-element.35.labels_ref, bf16[144,128]{1,0:T(8,128)(2,1)S(1)} %shard_map.100.refs_4_.refs_0_, ...), custom_call_target="tpu_custom_call", output_to_operand_aliasing={{0}: (1, {})} | custom-call | tf_op jit(solution)/shard_map/pallas_call | solution.py:23
  43.6 0.6 %collective-permute-done.12.refs_1_ = bf16[272,128]{1,0:T(8,128)(2,1)S(1)} collective-permute-done((bf16[272,128]{1,0:T(8,128)(2,1)S(1)}, bf16[272,128]{1,0:T(8,128)(2,1)S(1)}, u32[]{:S(2)}, u32[]{:S(2)}) %collective-permute-start.12) | collective-permute-done | bytes 69664 | tf_op jit(solution)/shard_map/ppermute | solution.py:412
  44.2 1.0 %collective-permute-done.13.refs_2_ = bf16[272,128]{1,0:T(8,128)(2,1)S(1)} collective-permute-done((bf16[272,128]{1,0:T(8,128)(2,1)S(1)}, bf16[272,128]{1,0:T(8,128)(2,1)S(1)}, u32[]{:S(2)}, u32[]{:S(2)}) %collective-permute-start.13) | collective-permute-done | bytes 69664 | tf_op jit(solution)/shard_map/ppermute | solution.py:412
  45.2 0.9 %shard_map.102 = (f32[32,512]{1,0:T(8,128)}, f32[1,32]{1,0:T(1,128)}) custom-call(f32[272,128]{1,0:T(8,128)S(1)} %get-tuple-element.26.refs_0_, bf16[272,128]{1,0:T(8,128)(2,1)S(1)} %collective-permute-done.12.refs_1_, bf16[272,128]{1,0:T(8,128)(2,1)S(1)} %collective-permute-done.13.refs_2_, bf16[272,128]{1,0:T(8,128)(2,1)S(1)} %collective-permute-done.14.refs_3_, ...), custom_call_target="tpu_custom_call" | custom-call | tf_op jit(solution)/shard_map/pallas_call | solution.py:23
  (11 shorter events, 0.0 us)
Async XLA Ops:
  1.5 6.9 %collective-permute-start = (bf16[144,128]{1,0:T(8,128)(2,1)S(1)}, bf16[144,128]{1,0:T(8,128)(2,1)S(1)}, u32[]{:S(2)}, u32[]{:S(2)}) collective-permute-start(bf16[144,128]{1,0:T(8,128)(2,1)S(1)} %get-tuple-element.21.refs_0_), channel_id=1, source_target_pairs={{0,2},{1,3},{2,0},{3,1},{4,6},{5,7},{6,4},{7,5},{8,10},{9,11},{10,... | collective-permute-start | bytes 110600 | tf_op jit(solution)/shard_map/ppermute | solution.py:412
  4.6 5.5 %collective-permute-start.1 = (bf16[144,128]{1,0:T(8,128)(2,1)S(1)}, bf16[144,128]{1,0:T(8,128)(2,1)S(1)}, u32[]{:S(2)}, u32[]{:S(2)}) collective-permute-start(bf16[144,128]{1,0:T(8,128)(2,1)S(1)} %get-tuple-element.21.refs_0_), channel_id=1, source_target_pairs={{0,4},{1,5},{2,6},{3,7},{4,0},{5,1},{6,2},{7,3},{8,12},{9,13},{10,... | collective-permute-start | bytes 110600 | tf_op jit(solution)/shard_map/ppermute | solution.py:412
  7.2 5.8 %collective-permute-start.2 = (bf16[144,128]{1,0:T(8,128)(2,1)S(1)}, bf16[144,128]{1,0:T(8,128)(2,1)S(1)}, u32[]{:S(2)}, u32[]{:S(2)}) collective-permute-start(bf16[144,128]{1,0:T(8,128)(2,1)S(1)} %get-tuple-element.21.refs_0_), channel_id=1, source_target_pairs={{0,6},{1,7},{2,4},{3,5},{4,2},{5,3},{6,0},{7,1},{8,14},{9,15},{10,... | collective-permute-start | bytes 110600 | tf_op jit(solution)/shard_map/ppermute | solution.py:412
  7.2 1.2 %collective-permute-start.3 = (s32[16,128]{1,0:T(8,128)S(1)}, s32[16,128]{1,0:T(8,128)S(1)}, u32[]{:S(2)}, u32[]{:S(2)}) collective-permute-start(s32[16,128]{1,0:T(8,128)S(1)} %get-tuple-element.22.refs_4_), channel_id=1, source_target_pairs={{0,1},{1,0},{2,3},{3,2},{4,5},{5,4},{6,7},{7,6},{8,9},{9,8},{10,11... | collective-permute-start | bytes 24584 | tf_op jit(solution)/shard_map/ppermute | solution.py:412
  7.2 12.2 %collective-permute-start.4 = (bf16[2048,512]{1,0:T(8,128)(2,1)}, bf16[2048,512]{1,0:T(8,128)(2,1)S(1)}, u32[]{:S(2)}, u32[]{:S(2)}) collective-permute-start(bf16[2048,512]{1,0:T(8,128)(2,1)} %refs_5_.1), channel_id=1, source_target_pairs={{0,1},{1,0},{2,3},{3,2},{4,5},{5,4},{6,7},{7,6},{8,9},{9,8},{10,11... | collective-permute-start | bytes 6291464 | tf_op jit(solution)/shard_map/ppermute | solution.py:412
  13.0 7.5 %collective-permute-start.7 = (bf16[576,128]{1,0:T(8,128)(2,1)S(1)}, bf16[576,128]{1,0:T(8,128)(2,1)S(1)}, u32[]{:S(2)}, u32[]{:S(2)}) collective-permute-start(bf16[576,128]{1,0:T(8,128)(2,1)S(1)} %shard_map.94.refs_0_), channel_id=1, source_target_pairs={{0,24},{8,16},{16,8},{24,0},{1,25},{9,17},{17,9},{25,1},{2,26},{10... | collective-permute-start | bytes 442376 | tf_op jit(solution)/shard_map/ppermute | solution.py:410
  15.5 10.4 %collective-permute-start.5 = (bf16[576,128]{1,0:T(8,128)(2,1)S(1)}, bf16[576,128]{1,0:T(8,128)(2,1)S(1)}, u32[]{:S(2)}, u32[]{:S(2)}) collective-permute-start(bf16[576,128]{1,0:T(8,128)(2,1)S(1)} %shard_map.94.refs_0_), channel_id=1, source_target_pairs={{0,16},{8,24},{16,0},{24,8},{1,17},{9,25},{17,1},{25,9},{2,18},{10... | collective-permute-start | bytes 442376 | tf_op jit(solution)/shard_map/ppermute | solution.py:410
  16.0 9.9 %collective-permute-start.6 = (bf16[576,128]{1,0:T(8,128)(2,1)S(1)}, bf16[576,128]{1,0:T(8,128)(2,1)S(1)}, u32[]{:S(2)}, u32[]{:S(2)}) collective-permute-start(bf16[576,128]{1,0:T(8,128)(2,1)S(1)} %shard_map.94.refs_0_), channel_id=1, source_target_pairs={{0,8},{8,0},{16,24},{24,16},{1,9},{9,1},{17,25},{25,17},{2,10},{10... | collective-permute-start | bytes 442376 | tf_op jit(solution)/shard_map/ppermute | solution.py:410
  23.4 8.5 %copy-start = (bf16[2048,512]{1,0:T(8,128)(2,1)S(1)}, bf16[2048,512]{1,0:T(8,128)(2,1)}, u32[]{:S(2)}) copy-start(bf16[2048,512]{1,0:T(8,128)(2,1)} %refs_5_.1) | copy-start | bytes 6291460
  23.4 14.3 %collective-permute-start.8 = (bf16[1040,128]{1,0:T(8,128)(2,1)S(1)}, bf16[1040,128]{1,0:T(8,128)(2,1)S(1)}, u32[]{:S(2)}, u32[]{:S(2)}) collective-permute-start(bf16[1040,128]{1,0:T(8,128)(2,1)S(1)} %shard_map.97.refs_6_), channel_id=1, source_target_pairs={{0,24},{8,16},{16,8},{24,0},{1,25},{9,17},{17,9},{25,1},{2,26},{10... | collective-permute-start | bytes 798728 | tf_op jit(solution)/shard_map/ppermute | solution.py:410
  30.7 6.5 %collective-permute-start.10 = (bf16[1040,128]{1,0:T(8,128)(2,1)S(1)}, bf16[1040,128]{1,0:T(8,128)(2,1)S(1)}, u32[]{:S(2)}, u32[]{:S(2)}) collective-permute-start(bf16[1040,128]{1,0:T(8,128)(2,1)S(1)} %get-tuple-element.24.refs_7_.refs_5_), channel_id=1, source_target_pairs={{0,8},{8,0},{16,24},{24,16},{1,9},{9,1},{17,25},{25,17},{2,10},{10... | collective-permute-start | bytes 798728 | tf_op jit(solution)/shard_map/ppermute | solution.py:410
  31.4 6.4 %collective-permute-start.9 = (bf16[1040,128]{1,0:T(8,128)(2,1)S(1)}, bf16[1040,128]{1,0:T(8,128)(2,1)S(1)}, u32[]{:S(2)}, u32[]{:S(2)}) collective-permute-start(bf16[1040,128]{1,0:T(8,128)(2,1)S(1)} %get-tuple-element.23.refs_6_.refs_4_), channel_id=1, source_target_pairs={{0,16},{8,24},{16,0},{24,8},{1,17},{9,25},{17,1},{25,9},{2,18},{10... | collective-permute-start | bytes 798728 | tf_op jit(solution)/shard_map/ppermute | solution.py:410
  31.9 3.0 %collective-permute-start.11 = (bf16[144,128]{1,0:T(8,128)(2,1)S(1)}, bf16[144,128]{1,0:T(8,128)(2,1)S(1)}, u32[]{:S(2)}, u32[]{:S(2)}) collective-permute-start(bf16[144,128]{1,0:T(8,128)(2,1)S(1)} %shard_map.100.refs_4_.refs_0_), channel_id=1, source_target_pairs={{0,1},{1,0},{2,3},{3,2},{4,5},{5,4},{6,7},{7,6},{8,9},{9,8},{10,11... | collective-permute-start | bytes 110600 | tf_op jit(solution)/shard_map/ppermute | solution.py:412
  37.9 6.3 %collective-permute-start.12 = (bf16[272,128]{1,0:T(8,128)(2,1)S(1)}, bf16[272,128]{1,0:T(8,128)(2,1)S(1)}, u32[]{:S(2)}, u32[]{:S(2)}) collective-permute-start(bf16[272,128]{1,0:T(8,128)(2,1)S(1)} %get-tuple-element.27), channel_id=1, source_target_pairs={{0,6},{1,7},{2,4},{3,5},{4,2},{5,3},{6,0},{7,1},{8,14},{9,15},{10,... | collective-permute-start | bytes 208904 | tf_op jit(solution)/shard_map/ppermute | solution.py:412
  38.5 6.7 %collective-permute-start.13 = (bf16[272,128]{1,0:T(8,128)(2,1)S(1)}, bf16[272,128]{1,0:T(8,128)(2,1)S(1)}, u32[]{:S(2)}, u32[]{:S(2)}) collective-permute-start(bf16[272,128]{1,0:T(8,128)(2,1)S(1)} %get-tuple-element.28), channel_id=1, source_target_pairs={{0,4},{1,5},{2,6},{3,7},{4,0},{5,1},{6,2},{7,3},{8,12},{9,13},{10,... | collective-permute-start | bytes 208904 | tf_op jit(solution)/shard_map/ppermute | solution.py:412
  38.5 6.7 %collective-permute-start.14 = (bf16[272,128]{1,0:T(8,128)(2,1)S(1)}, bf16[272,128]{1,0:T(8,128)(2,1)S(1)}, u32[]{:S(2)}, u32[]{:S(2)}) collective-permute-start(bf16[272,128]{1,0:T(8,128)(2,1)S(1)} %get-tuple-element.29), channel_id=1, source_target_pairs={{0,2},{1,3},{2,0},{3,1},{4,6},{5,7},{6,4},{7,5},{8,10},{9,11},{10,... | collective-permute-start | bytes 208904 | tf_op jit(solution)/shard_map/ppermute | solution.py:412

commit v11 on v10

--- a/solution.py
+++ b/solution.py
@@ -114,37 +114,21 @@
 
 def join_kernel(blocks, *refs):
     block_refs, out_ref = refs[:blocks], refs[-1]
-    size = block_refs[0].shape[0]
-    for place, ref in enumerate(block_refs):
-        out_ref[place * size : (place + 1) * size, :] = ref[...]
+    first = 0
+    for ref in block_refs:
+        out_ref[first : first + ref.shape[0], :] = ref[...]
+        first += ref.shape[0]
 
 
 def join(blocks, after):
-    size, width = blocks[0].shape
+    rows = sum(block.shape[0] for block in blocks)
     return call(
         functools.partial(join_kernel, len(blocks)),
-        [shaped((size * len(blocks), width), blocks[0].dtype)],
+        [shaped((rows, blocks[0].shape[1]), blocks[0].dtype)],
         *blocks, *after,
         in_specs=[pl.BlockSpec(memory_space=pltpu.VMEM)] * len(blocks)
         + [pl.BlockSpec(memory_space=pl.ANY)] * len(after),
     )[0]
-
-
-def other_keys_kernel(block, memory_ref, rows_ref, keys_ref, same_ref):
-    same_ref[...] = rows_ref[...]
-
-    @pl.loop(0, memory_ref.shape[0] // block)
-    def _(i):
-        part = pl.ds(pl.multiple_of(i * block, block), block)
-        keys_ref[part, :] = normalized(memory_ref[part, :])
-
-
-def other_keys(memory, rows):
-    return call(
-        functools.partial(other_keys_kernel, math.gcd(256, memory.shape[0])),
-        [shaped(memory.shape, bf16), shaped(rows.shape, bf16)],
-        memory, rows,
-    )
 
 
 def positions(step, count, slots, groups, line, cores):
@@ -158,7 +142,8 @@
     source = lax.rem(target + devices_all - lax.rem(step, devices_all), devices_all)
     source_grp = lax.div(source, members)
     source_line = lax.div(lax.rem(source, members), cores)
-    return first, crossing, grp ^ source_grp, lax.div(dev, cores) ^ source_line
+    step = lax.div(dev, cores) ^ source_line
+    return first, crossing, grp ^ source_grp, lax.rem(line - step, line)
 
 
 def pick_kernel(groups, sizes, step_ref, *refs):
@@ -319,7 +304,7 @@
     anywhere = pl.BlockSpec(memory_space=pl.ANY)
     vmem = pl.BlockSpec(memory_space=pltpu.VMEM)
     return call(
-        functools.partial(block_kernel, len(blocks), len(keys), math.gcd(512, slots), count, len(copied)),
+        functools.partial(block_kernel, len(blocks), len(keys), math.gcd(1024, slots), count, len(copied)),
         [shaped((2 * parts * size + sum_rows(size), lanes), dtype)] * len(blocks)
         + [shaped(value.shape, value.dtype) for value in copied],
         *blocks, *[in_vmem(k) for k in keys], *labels, *copied, *after,
@@ -429,10 +414,9 @@
     labels = [slot_labels] + [exchange(slot_labels, "core", s) for s in range(1, cores)]
     memories = [memory] + [exchange(memory, "core", s) for s in range(1, cores)]
 
-    near = [packed] + [None] * (line - 1)
+    part = packed
     for s in range(line - 1, 0, -1):
-        near[s] = exchange(packed, "line", s)
-    part = join(near, labels)
+        part = join([part, exchange(packed, "line", s)], labels if s == 1 else [])
     labels = [value.reshape(1, slots) for value in labels]
     blocks = [part] + [None] * (groups - 1)
     for s in range(groups - 1, 0, -1):
@@ -453,7 +437,7 @@
     choices = [moved] + [exchange(moved, "core", s) for s in range(1, cores)]
 
     sums, *others = add(held, arrived, size, count, 2 * parts, choices)
-    arrived = [exchange(others[s - 1], "line", s) for s in range(line - 1, 0, -1)]
+    arrived = [exchange(value, "line", line - at) for at, value in enumerate(others, 1)]
     grad_batch, loss = call(
         functools.partial(finish_kernel, len(arrived)),
         [shaped((count, width), f32), shaped((1, count), f32)],

time: 46.3 us -> 45.5 us (0.983)
  waiting for transfers between devices: 9.1 us -> 7.84 us
    ppermute x9, waiting for transfers between devices: 6.16 us -> 5.07 us  [exchange(): return lax.ppermute(value, 'dev', [(i, i ^ jump) for i in range(members)])]
    pallas_call x11 -> x13, Pallas kernels: 17.7 us -> 18.1 us  [call(): pl.pallas_call(body, out_shape=outs, compiler_params=pltpu.CompilerParams...]
  transfers between devices with their start and end apart: 15 -> 15, of which waited for: 7 -> 7; matrix products, arithmetic and copies ran while one was open for 0% -> 0% of each run, Pallas kernels for 34% -> 36%
where the time goes in v11:
time: 45.5 us; the launch traced here: 45.3 us
  Pallas kernels  18.1 us (40%)
  starting transfers between devices  17.9 us (39%)
  waiting for transfers between devices  7.84 us (17%)
  between operations  1.4 us (3%)
    pallas_call x13, Pallas kernels, call(): pl.pallas_call(body, out_shape=outs, compiler_params=pltpu.CompilerParams...  18.1 us
    ppermute x9, starting transfers between devices, exchange(): return lax.ppermute(value, 'dev', [(i, i ^ jump) for i in range(members)])  10.7 us
    ppermute x6, starting transfers between devices, exchange(): return lax.ppermute(value, 'grp', [(i, i ^ step) for i in range(groups)])  7.16 us
    ppermute x9, waiting for transfers between devices, exchange(): return lax.ppermute(value, 'dev', [(i, i ^ jump) for i in range(members)])  5.07 us
    ppermute x6, waiting for transfers between devices, exchange(): return lax.ppermute(value, 'grp', [(i, i ^ step) for i in range(groups)])  2.76 us
  transfers between devices with their start and end apart: 15, of which 7 were waited for; matrix products, arithmetic and copies ran while one was open for 0% of the time, Pallas kernels for 36%

profile of v11, /device:TPU:0, one launch (start us, length us, event | category | flops | bytes accessed | tf_op | source)
XLA Modules:
  0.0 45.3 jit_solution(16428314948110642505)
XLA Ops:
  0.6 0.9 %shard_map.93 = (bf16[144,128]{1,0:T(8,128)(2,1)S(1)}, f32[32,512]{1,0:T(8,128)S(1)}, f32[32,128]{1,0:T(8,128)S(1)}, s32[16,128]{1,0:T(8,128)S(1)}, s32[16,128]{1,0:T(8,128)S(1)}) custom-call(bf16[32,512]{1,0:T(8,128)(2,1)} %rows_ref.1, s32[1,32]{1,0:T(1,128)} %bitcast.15, s32[16,128]{1,0:T(8,128)} %bitcast.13, s32[16,128]{1,0:T(8,128)} %bitcast.14), custom_call_target="tpu_custom_call" | custom-call | tf_op jit(solution)/shard_map/pallas_call | solution.py:23
  1.5 5.1 %collective-permute-start = (bf16[144,128]{1,0:T(8,128)(2,1)S(1)}, bf16[144,128]{1,0:T(8,128)(2,1)S(1)}, u32[]{:S(2)}, u32[]{:S(2)}) collective-permute-start(bf16[144,128]{1,0:T(8,128)(2,1)S(1)} %get-tuple-element.21.refs_0_), channel_id=1, source_target_pairs={{0,6},{1,7},{2,4},{3,5},{4,2},{5,3},{6,0},{7,1},{8,14},{9,15},{10,... | collective-permute-start | bytes 110600 | tf_op jit(solution)/shard_map/ppermute | solution.py:397
  6.6 0.0 collective-permute-start.1
  6.6 0.6 %collective-permute-start.2 = (bf16[144,128]{1,0:T(8,128)(2,1)S(1)}, bf16[144,128]{1,0:T(8,128)(2,1)S(1)}, u32[]{:S(2)}, u32[]{:S(2)}) collective-permute-start(bf16[144,128]{1,0:T(8,128)(2,1)S(1)} %get-tuple-element.21.refs_0_), channel_id=1, source_target_pairs={{0,2},{1,3},{2,0},{3,1},{4,6},{5,7},{6,4},{7,5},{8,10},{9,11},{10,... | collective-permute-start | bytes 110600 | tf_op jit(solution)/shard_map/ppermute | solution.py:397
  7.3 0.5 %collective-permute-start.4 = (bf16[2048,512]{1,0:T(8,128)(2,1)}, bf16[2048,512]{1,0:T(8,128)(2,1)S(1)}, u32[]{:S(2)}, u32[]{:S(2)}) collective-permute-start(bf16[2048,512]{1,0:T(8,128)(2,1)} %refs_5_.1), channel_id=1, source_target_pairs={{0,1},{1,0},{2,3},{3,2},{4,5},{5,4},{6,7},{7,6},{8,9},{9,8},{10,11... | collective-permute-start | bytes 6291464 | tf_op jit(solution)/shard_map/ppermute | solution.py:397
  8.4 0.1 collective-permute-done.refs_1_
  8.6 2.9 %collective-permute-done.1.refs_1_ = bf16[144,128]{1,0:T(8,128)(2,1)S(1)} collective-permute-done((bf16[144,128]{1,0:T(8,128)(2,1)S(1)}, bf16[144,128]{1,0:T(8,128)(2,1)S(1)}, u32[]{:S(2)}, u32[]{:S(2)}) %collective-permute-start.1) | collective-permute-done | bytes 36896 | tf_op jit(solution)/shard_map/ppermute | solution.py:397
  11.5 0.0 collective-permute-done.3.refs_3_
  11.5 0.0 collective-permute-done.2.refs_1_
  11.5 2.5 %collective-permute-start.7 = (bf16[576,128]{1,0:T(8,128)(2,1)S(1)}, bf16[576,128]{1,0:T(8,128)(2,1)S(1)}, u32[]{:S(2)}, u32[]{:S(2)}) collective-permute-start(bf16[576,128]{1,0:T(8,128)(2,1)S(1)} %shard_map.96.refs_0_), channel_id=1, source_target_pairs={{0,24},{8,16},{16,8},{24,0},{1,25},{9,17},{17,9},{25,1},{2,26},{10... | collective-permute-start | bytes 442376 | tf_op jit(solution)/shard_map/ppermute | solution.py:395
  14.1 0.5 %collective-permute-start.5 = (bf16[576,128]{1,0:T(8,128)(2,1)S(1)}, bf16[576,128]{1,0:T(8,128)(2,1)S(1)}, u32[]{:S(2)}, u32[]{:S(2)}) collective-permute-start(bf16[576,128]{1,0:T(8,128)(2,1)S(1)} %shard_map.96.refs_0_), channel_id=1, source_target_pairs={{0,16},{8,24},{16,0},{24,8},{1,17},{9,25},{17,1},{25,9},{2,18},{10... | collective-permute-start | bytes 442376 | tf_op jit(solution)/shard_map/ppermute | solution.py:395
  14.6 0.5 %collective-permute-start.6 = (bf16[576,128]{1,0:T(8,128)(2,1)S(1)}, bf16[576,128]{1,0:T(8,128)(2,1)S(1)}, u32[]{:S(2)}, u32[]{:S(2)}) collective-permute-start(bf16[576,128]{1,0:T(8,128)(2,1)S(1)} %shard_map.96.refs_0_), channel_id=1, source_target_pairs={{0,8},{8,0},{16,24},{24,16},{1,9},{9,1},{17,25},{25,17},{2,10},{10... | collective-permute-start | bytes 442376 | tf_op jit(solution)/shard_map/ppermute | solution.py:395
  15.1 2.9 %shard_map.97.refs_1_.refs_2_ = bf16[2048,512]{1,0:T(8,128)(2,1)S(1)} custom-call(bf16[2048,512]{1,0:T(8,128)(2,1)} %refs_5_.1, bf16[576,128]{1,0:T(8,128)(2,1)S(1)} %shard_map.96.refs_0_), custom_call_target="tpu_custom_call" | custom-call | flops 34359738368 | tf_op jit(solution)/shard_map/pallas_call | solution.py:23
  18.0 1.0 %shard_map.98.refs_2_.refs_3_ = bf16[2048,512]{1,0:T(8,128)(2,1)S(1)} custom-call(bf16[2048,512]{1,0:T(8,128)(2,1)S(1)} %collective-permute-done.4.memory_ref, bf16[576,128]{1,0:T(8,128)(2,1)S(1)} %shard_map.96.refs_0_), custom_call_target="tpu_custom_call" | custom-call | flops 34359738368 | tf_op jit(solution)/shard_map/pallas_call | solution.py:23
  19.0 0.3 collective-permute-done.7.refs_0_.refs_3_
  19.2 3.1 %shard_map.99.refs_6_ = bf16[1040,128]{1,0:T(8,128)(2,1)S(1)} custom-call(bf16[576,128]{1,0:T(8,128)(2,1)S(1)} %collective-permute-done.7.refs_0_.refs_3_, bf16[2048,512]{1,0:T(8,128)(2,1)S(1)} %shard_map.97.refs_1_.refs_2_, bf16[2048,512]{1,0:T(8,128)(2,1)S(1)} %shard_map.98.refs_2_.refs_3_, s32[1,2048]{1,0:T(1,128)S(1)} %bitcast.7, s32[1,2048]{1,0:T(1,128)S(1)} %bitcast.10), custom_call_target="tpu_custom_call" | custom-call | flops 3221225472 | tf_op jit(solution)/shard_map/pallas_call | solution.py:23
  22.4 0.0 copy-start
  22.4 2.3 %collective-permute-start.8 = (bf16[1040,128]{1,0:T(8,128)(2,1)S(1)}, bf16[1040,128]{1,0:T(8,128)(2,1)S(1)}, u32[]{:S(2)}, u32[]{:S(2)}) collective-permute-start(bf16[1040,128]{1,0:T(8,128)(2,1)S(1)} %shard_map.99.refs_6_), channel_id=1, source_target_pairs={{0,24},{8,16},{16,8},{24,0},{1,25},{9,17},{17,9},{25,1},{2,26},{10... | collective-permute-start | bytes 798728 | tf_op jit(solution)/shard_map/ppermute | solution.py:395
  24.7 4.9 %shard_map.100 = (bf16[1040,128]{1,0:T(8,128)(2,1)S(1)}, bf16[1040,128]{1,0:T(8,128)(2,1)S(1)}) custom-call(bf16[576,128]{1,0:T(8,128)(2,1)S(1)} %collective-permute-done.5.refs_0_.refs_2_, bf16[576,128]{1,0:T(8,128)(2,1)S(1)} %collective-permute-done.6.refs_1_, bf16[2048,512]{1,0:T(8,128)(2,1)S(1)} %shard_map.97.refs_1_.refs_2_, ...), custom_call_target="tpu_custom_call" | custom-call | flops 6442450944 | tf_op jit(solution)/shard_map/pallas_call | solution.py:23
  29.5 0.6 %collective-permute-start.10 = (bf16[1040,128]{1,0:T(8,128)(2,1)S(1)}, bf16[1040,128]{1,0:T(8,128)(2,1)S(1)}, u32[]{:S(2)}, u32[]{:S(2)}) collective-permute-start(bf16[1040,128]{1,0:T(8,128)(2,1)S(1)} %get-tuple-element.24.refs_7_.refs_5_), channel_id=1, source_target_pairs={{0,8},{8,0},{16,24},{24,16},{1,9},{9,1},{17,25},{25,17},{2,10},{10... | collective-permute-start | bytes 798728 | tf_op jit(solution)/shard_map/ppermute | solution.py:395
  30.1 0.7 %collective-permute-start.9 = (bf16[1040,128]{1,0:T(8,128)(2,1)S(1)}, bf16[1040,128]{1,0:T(8,128)(2,1)S(1)}, u32[]{:S(2)}, u32[]{:S(2)}) collective-permute-start(bf16[1040,128]{1,0:T(8,128)(2,1)S(1)} %get-tuple-element.23.refs_6_.refs_4_), channel_id=1, source_target_pairs={{0,16},{8,24},{16,0},{24,8},{1,17},{9,25},{17,1},{25,9},{2,18},{10... | collective-permute-start | bytes 798728 | tf_op jit(solution)/shard_map/ppermute | solution.py:395
  30.9 3.1 %shard_map.101 = (f32[1040,128]{1,0:T(8,128)S(1)}, bf16[2048,512]{1,0:T(8,128)(2,1)}) custom-call(bf16[576,128]{1,0:T(8,128)(2,1)S(1)} %shard_map.96.refs_0_, bf16[2048,512]{1,0:T(8,128)(2,1)S(1)} %shard_map.97.refs_1_.refs_2_, bf16[2048,512]{1,0:T(8,128)(2,1)S(1)} %shard_map.98.refs_2_.refs_3_, s32[1,2048]{1,0:T(1,128)S(1)} %bitcast.9, ...), custom_call_target="tpu_custom_call" | custom-call | flops 3221225472 | tf_op jit(solution)/shard_map/pallas_call | solution.py:23
  34.0 2.0 %collective-permute-done.10.refs_3_ = bf16[1040,128]{1,0:T(8,128)(2,1)S(1)} collective-permute-done((bf16[1040,128]{1,0:T(8,128)(2,1)S(1)}, bf16[1040,128]{1,0:T(8,128)(2,1)S(1)}, u32[]{:S(2)}, u32[]{:S(2)}) %collective-permute-start.10) | collective-permute-done | bytes 266272 | tf_op jit(solution)/shard_map/ppermute | solution.py:395
  36.0 0.5 %collective-permute-done.9.refs_2_ = bf16[1040,128]{1,0:T(8,128)(2,1)S(1)} collective-permute-done((bf16[1040,128]{1,0:T(8,128)(2,1)S(1)}, bf16[1040,128]{1,0:T(8,128)(2,1)S(1)}, u32[]{:S(2)}, u32[]{:S(2)}) %collective-permute-start.9) | collective-permute-done | bytes 266272 | tf_op jit(solution)/shard_map/ppermute | solution.py:395
  36.5 0.1 shard_map.103
  36.7 1.8 %collective-permute-start.12 = (bf16[272,128]{1,0:T(8,128)(2,1)S(1)}, bf16[272,128]{1,0:T(8,128)(2,1)S(1)}, u32[]{:S(2)}, u32[]{:S(2)}) collective-permute-start(bf16[272,128]{1,0:T(8,128)(2,1)S(1)} %get-tuple-element.27), channel_id=1, source_target_pairs={{0,6},{1,7},{2,4},{3,5},{4,2},{5,3},{6,0},{7,1},{8,14},{9,15},{10,... | collective-permute-start | bytes 208904 | tf_op jit(solution)/shard_map/ppermute | solution.py:397
  38.4 0.4 collective-permute-start.13
  38.8 2.3 %collective-permute-start.14 = (bf16[272,128]{1,0:T(8,128)(2,1)S(1)}, bf16[272,128]{1,0:T(8,128)(2,1)S(1)}, u32[]{:S(2)}, u32[]{:S(2)}) collective-permute-start(bf16[272,128]{1,0:T(8,128)(2,1)S(1)} %get-tuple-element.29), channel_id=1, source_target_pairs={{0,2},{1,3},{2,0},{3,1},{4,6},{5,7},{6,4},{7,5},{8,10},{9,11},{10,... | collective-permute-start | bytes 208904 | tf_op jit(solution)/shard_map/ppermute | solution.py:397
  41.1 1.2 %shard_map.105 = (bf16[2048,512]{1,0:T(8,128)(2,1)}, s32[16,128]{1,0:T(8,128)}) custom-call(s32[1]{0:T(128)S(6)} %copy.12.step_ref, bf16[2048,512]{1,0:T(8,128)(2,1)} %get-tuple-element.34.stored_ref, s32[16,128]{1,0:T(8,128)S(1)} %get-tuple-element.35.labels_ref, bf16[144,128]{1,0:T(8,128)(2,1)S(1)} %shard_map.102.refs_4_.refs_0_, ...), custom_call_target="tpu_custom_call", output_to_operand_aliasing={{0}: (1, {})} | custom-call | tf_op jit(solution)/shard_map/pallas_call | solution.py:23
  42.4 0.5 %collective-permute-done.12.refs_1_ = bf16[272,128]{1,0:T(8,128)(2,1)S(1)} collective-permute-done((bf16[272,128]{1,0:T(8,128)(2,1)S(1)}, bf16[272,128]{1,0:T(8,128)(2,1)S(1)}, u32[]{:S(2)}, u32[]{:S(2)}) %collective-permute-start.12) | collective-permute-done | bytes 69664 | tf_op jit(solution)/shard_map/ppermute | solution.py:397
  42.9 1.5 %collective-permute-done.13.refs_2_ = bf16[272,128]{1,0:T(8,128)(2,1)S(1)} collective-permute-done((bf16[272,128]{1,0:T(8,128)(2,1)S(1)}, bf16[272,128]{1,0:T(8,128)(2,1)S(1)}, u32[]{:S(2)}, u32[]{:S(2)}) %collective-permute-start.13) | collective-permute-done | bytes 69664 | tf_op jit(solution)/shard_map/ppermute | solution.py:397
  44.4 0.9 %shard_map.104 = (f32[32,512]{1,0:T(8,128)}, f32[1,32]{1,0:T(1,128)}) custom-call(f32[272,128]{1,0:T(8,128)S(1)} %get-tuple-element.26.refs_0_, bf16[272,128]{1,0:T(8,128)(2,1)S(1)} %collective-permute-done.12.refs_1_, bf16[272,128]{1,0:T(8,128)(2,1)S(1)} %collective-permute-done.13.refs_2_, bf16[272,128]{1,0:T(8,128)(2,1)S(1)} %collective-permute-done.14.refs_3_, ...), custom_call_target="tpu_custom_call" | custom-call | tf_op jit(solution)/shard_map/pallas_call | solution.py:23
  (13 shorter events, 0.1 us)
Async XLA Ops:
  1.5 7.1 %collective-permute-start = (bf16[144,128]{1,0:T(8,128)(2,1)S(1)}, bf16[144,128]{1,0:T(8,128)(2,1)S(1)}, u32[]{:S(2)}, u32[]{:S(2)}) collective-permute-start(bf16[144,128]{1,0:T(8,128)(2,1)S(1)} %get-tuple-element.21.refs_0_), channel_id=1, source_target_pairs={{0,6},{1,7},{2,4},{3,5},{4,2},{5,3},{6,0},{7,1},{8,14},{9,15},{10,... | collective-permute-start | bytes 110600 | tf_op jit(solution)/shard_map/ppermute | solution.py:397
  6.6 4.9 %collective-permute-start.1 = (bf16[144,128]{1,0:T(8,128)(2,1)S(1)}, bf16[144,128]{1,0:T(8,128)(2,1)S(1)}, u32[]{:S(2)}, u32[]{:S(2)}) collective-permute-start(bf16[144,128]{1,0:T(8,128)(2,1)S(1)} %get-tuple-element.21.refs_0_), channel_id=1, source_target_pairs={{0,4},{1,5},{2,6},{3,7},{4,0},{5,1},{6,2},{7,3},{8,12},{9,13},{10,... | collective-permute-start | bytes 110600 | tf_op jit(solution)/shard_map/ppermute | solution.py:397
  6.6 4.9 %collective-permute-start.2 = (bf16[144,128]{1,0:T(8,128)(2,1)S(1)}, bf16[144,128]{1,0:T(8,128)(2,1)S(1)}, u32[]{:S(2)}, u32[]{:S(2)}) collective-permute-start(bf16[144,128]{1,0:T(8,128)(2,1)S(1)} %get-tuple-element.21.refs_0_), channel_id=1, source_target_pairs={{0,2},{1,3},{2,0},{3,1},{4,6},{5,7},{6,4},{7,5},{8,10},{9,11},{10,... | collective-permute-start | bytes 110600 | tf_op jit(solution)/shard_map/ppermute | solution.py:397
  7.3 4.2 %collective-permute-start.3 = (s32[16,128]{1,0:T(8,128)S(1)}, s32[16,128]{1,0:T(8,128)S(1)}, u32[]{:S(2)}, u32[]{:S(2)}) collective-permute-start(s32[16,128]{1,0:T(8,128)S(1)} %get-tuple-element.22.refs_2_), channel_id=1, source_target_pairs={{0,1},{1,0},{2,3},{3,2},{4,5},{5,4},{6,7},{7,6},{8,9},{9,8},{10,11... | collective-permute-start | bytes 24584 | tf_op jit(solution)/shard_map/ppermute | solution.py:397
  7.3 10.7 %collective-permute-start.4 = (bf16[2048,512]{1,0:T(8,128)(2,1)}, bf16[2048,512]{1,0:T(8,128)(2,1)S(1)}, u32[]{:S(2)}, u32[]{:S(2)}) collective-permute-start(bf16[2048,512]{1,0:T(8,128)(2,1)} %refs_5_.1), channel_id=1, source_target_pairs={{0,1},{1,0},{2,3},{3,2},{4,5},{5,4},{6,7},{7,6},{8,9},{9,8},{10,11... | collective-permute-start | bytes 6291464 | tf_op jit(solution)/shard_map/ppermute | solution.py:397
  11.5 7.7 %collective-permute-start.7 = (bf16[576,128]{1,0:T(8,128)(2,1)S(1)}, bf16[576,128]{1,0:T(8,128)(2,1)S(1)}, u32[]{:S(2)}, u32[]{:S(2)}) collective-permute-start(bf16[576,128]{1,0:T(8,128)(2,1)S(1)} %shard_map.96.refs_0_), channel_id=1, source_target_pairs={{0,24},{8,16},{16,8},{24,0},{1,25},{9,17},{17,9},{25,1},{2,26},{10... | collective-permute-start | bytes 442376 | tf_op jit(solution)/shard_map/ppermute | solution.py:395
  14.1 10.6 %collective-permute-start.5 = (bf16[576,128]{1,0:T(8,128)(2,1)S(1)}, bf16[576,128]{1,0:T(8,128)(2,1)S(1)}, u32[]{:S(2)}, u32[]{:S(2)}) collective-permute-start(bf16[576,128]{1,0:T(8,128)(2,1)S(1)} %shard_map.96.refs_0_), channel_id=1, source_target_pairs={{0,16},{8,24},{16,0},{24,8},{1,17},{9,25},{17,1},{25,9},{2,18},{10... | collective-permute-start | bytes 442376 | tf_op jit(solution)/shard_map/ppermute | solution.py:395
  14.6 10.1 %collective-permute-start.6 = (bf16[576,128]{1,0:T(8,128)(2,1)S(1)}, bf16[576,128]{1,0:T(8,128)(2,1)S(1)}, u32[]{:S(2)}, u32[]{:S(2)}) collective-permute-start(bf16[576,128]{1,0:T(8,128)(2,1)S(1)} %shard_map.96.refs_0_), channel_id=1, source_target_pairs={{0,8},{8,0},{16,24},{24,16},{1,9},{9,1},{17,25},{25,17},{2,10},{10... | collective-permute-start | bytes 442376 | tf_op jit(solution)/shard_map/ppermute | solution.py:395
  22.4 8.5 %copy-start = (bf16[2048,512]{1,0:T(8,128)(2,1)S(1)}, bf16[2048,512]{1,0:T(8,128)(2,1)}, u32[]{:S(2)}) copy-start(bf16[2048,512]{1,0:T(8,128)(2,1)} %refs_5_.1) | copy-start | bytes 6291460
  22.4 14.2 %collective-permute-start.8 = (bf16[1040,128]{1,0:T(8,128)(2,1)S(1)}, bf16[1040,128]{1,0:T(8,128)(2,1)S(1)}, u32[]{:S(2)}, u32[]{:S(2)}) collective-permute-start(bf16[1040,128]{1,0:T(8,128)(2,1)S(1)} %shard_map.99.refs_6_), channel_id=1, source_target_pairs={{0,24},{8,16},{16,8},{24,0},{1,25},{9,17},{17,9},{25,1},{2,26},{10... | collective-permute-start | bytes 798728 | tf_op jit(solution)/shard_map/ppermute | solution.py:395
  29.5 6.5 %collective-permute-start.10 = (bf16[1040,128]{1,0:T(8,128)(2,1)S(1)}, bf16[1040,128]{1,0:T(8,128)(2,1)S(1)}, u32[]{:S(2)}, u32[]{:S(2)}) collective-permute-start(bf16[1040,128]{1,0:T(8,128)(2,1)S(1)} %get-tuple-element.24.refs_7_.refs_5_), channel_id=1, source_target_pairs={{0,8},{8,0},{16,24},{24,16},{1,9},{9,1},{17,25},{25,17},{2,10},{10... | collective-permute-start | bytes 798728 | tf_op jit(solution)/shard_map/ppermute | solution.py:395
  30.1 6.4 %collective-permute-start.9 = (bf16[1040,128]{1,0:T(8,128)(2,1)S(1)}, bf16[1040,128]{1,0:T(8,128)(2,1)S(1)}, u32[]{:S(2)}, u32[]{:S(2)}) collective-permute-start(bf16[1040,128]{1,0:T(8,128)(2,1)S(1)} %get-tuple-element.23.refs_6_.refs_4_), channel_id=1, source_target_pairs={{0,16},{8,24},{16,0},{24,8},{1,17},{9,25},{17,1},{25,9},{2,18},{10... | collective-permute-start | bytes 798728 | tf_op jit(solution)/shard_map/ppermute | solution.py:395
  30.9 3.2 %collective-permute-start.11 = (bf16[144,128]{1,0:T(8,128)(2,1)S(1)}, bf16[144,128]{1,0:T(8,128)(2,1)S(1)}, u32[]{:S(2)}, u32[]{:S(2)}) collective-permute-start(bf16[144,128]{1,0:T(8,128)(2,1)S(1)} %shard_map.102.refs_4_.refs_0_), channel_id=1, source_target_pairs={{0,1},{1,0},{2,3},{3,2},{4,5},{5,4},{6,7},{7,6},{8,9},{9,8},{10,11... | collective-permute-start | bytes 110600 | tf_op jit(solution)/shard_map/ppermute | solution.py:397
  36.7 6.2 %collective-permute-start.12 = (bf16[272,128]{1,0:T(8,128)(2,1)S(1)}, bf16[272,128]{1,0:T(8,128)(2,1)S(1)}, u32[]{:S(2)}, u32[]{:S(2)}) collective-permute-start(bf16[272,128]{1,0:T(8,128)(2,1)S(1)} %get-tuple-element.27), channel_id=1, source_target_pairs={{0,6},{1,7},{2,4},{3,5},{4,2},{5,3},{6,0},{7,1},{8,14},{9,15},{10,... | collective-permute-start | bytes 208904 | tf_op jit(solution)/shard_map/ppermute | solution.py:397
  38.4 6.0 %collective-permute-start.13 = (bf16[272,128]{1,0:T(8,128)(2,1)S(1)}, bf16[272,128]{1,0:T(8,128)(2,1)S(1)}, u32[]{:S(2)}, u32[]{:S(2)}) collective-permute-start(bf16[272,128]{1,0:T(8,128)(2,1)S(1)} %get-tuple-element.28), channel_id=1, source_target_pairs={{0,4},{1,5},{2,6},{3,7},{4,0},{5,1},{6,2},{7,3},{8,12},{9,13},{10,... | collective-permute-start | bytes 208904 | tf_op jit(solution)/shard_map/ppermute | solution.py:397
  38.8 5.6 %collective-permute-start.14 = (bf16[272,128]{1,0:T(8,128)(2,1)S(1)}, bf16[272,128]{1,0:T(8,128)(2,1)S(1)}, u32[]{:S(2)}, u32[]{:S(2)}) collective-permute-start(bf16[272,128]{1,0:T(8,128)(2,1)S(1)} %get-tuple-element.29), channel_id=1, source_target_pairs={{0,2},{1,3},{2,0},{3,1},{4,6},{5,7},{6,4},{7,5},{8,10},{9,11},{10,... | collective-permute-start | bytes 208904 | tf_op jit(solution)/shard_map/ppermute | solution.py:397

commit v12 on v11

--- a/solution.py
+++ b/solution.py
@@ -213,16 +213,18 @@
     return rounded_up(8 * (rounded_up(size, lanes) // lanes), 16)
 
 
-def block_kernel(blocks, sides, chunk, count, copies, *refs):
+def block_kernel(blocks, sides, unit, count, copies, scratch, *refs):
     if copies:
-        source_ref, target_ref, sem = refs[blocks + 2 * sides], refs[-3], refs[-1]
+        source_ref, target_ref, sem = refs[blocks + 2 * sides], refs[-scratch - 1], refs[-1]
         copy = pltpu.make_async_copy(source_ref, target_ref, sem)
         copy.start()
-        refs = refs[:-3] + refs[-2:-1]
+        refs = refs[: -scratch - 1] + refs[-scratch : -1]
+        scratch -= 1
     rows_refs, keys_refs = refs[:blocks], refs[blocks : blocks + sides]
     label_refs = refs[blocks + sides : blocks + 2 * sides]
-    out_refs = refs[-1 - blocks : -1]
-    anchors_ref = refs[-1]
+    out_refs = refs[-scratch - blocks : -scratch]
+    anchors_ref, labels_ref, total_ref, pos_ref, neg_ref = refs[-scratch:-4]
+    scores_refs, weight_refs = refs[-4:-2], refs[-2:]
     slots, width = keys_refs[0].shape
     parts = blocks_of(width)
     packed = rows_refs[0].shape[0]
@@ -239,36 +241,66 @@
                 ]
             digits = ref[first + parts * count : first + parts * count + 16, :].astype(f32)
             columns.append(to_column((digits[0:1, :] * 256.0 + digits[1:2, :])[:, :count]))
-    labels = jnp.concatenate(columns, axis=0)
+    rows = blocks * size
+    labels_ref[...] = jnp.broadcast_to(jnp.concatenate(columns, axis=0), labels_ref.shape)
+    pos_ref[...] = jnp.zeros_like(pos_ref)
+    neg_ref[...] = jnp.zeros_like(neg_ref)
     anchors = anchors_ref[...]
-    rows = blocks * size
-    pos_sum = jnp.zeros((rows, 1), f32)
-    neg_sum = jnp.zeros((rows, 1), f32)
-    total = None
-    chunks = [(side, slice(at, at + chunk)) for side in range(sides) for at in range(0, slots, chunk)]
-
-    def scores_of(side, part):
-        return lax.dot_general(
-            anchors, keys_refs[side][part, :], (((1,), (1,)), ((), ())), preferred_element_type=f32
+    units = [(side, at) for side in range(sides) for at in range(0, slots, unit)]
+    quarter = rows // 4
+
+    def score_unit(at):
+        side, first = units[at]
+        scores_refs[at % 2][...] = lax.dot_general(
+            anchors, keys_refs[side][first : first + unit, :], (((1,), (1,)), ((), ())), preferred_element_type=f32
         )
 
-    scores = scores_of(*chunks[0])
-    for at, (side, part) in enumerate(chunks):
-        following = scores_of(*chunks[at + 1]) if at + 1 < len(chunks) else None
-        slot_labels = label_refs[side][:, part].astype(f32)
-        neg_shift = jnp.where(slot_labels < 0.0, -1e30, -neg_scale * margin * log2e)
-        same = labels == slot_labels
-        slope = jnp.where(same, -pos_scale * log2e, neg_scale * log2e)
-        shift = jnp.where(same, pos_scale * margin * log2e, neg_shift)
-        term = jnp.exp2(scores * slope + shift)
-        pos = jnp.where(same, term, 0.0)
-        neg = jnp.where(same, 0.0, term)
-        pos_sum += jnp.sum(pos, axis=1, keepdims=True)
-        neg_sum += jnp.sum(neg, axis=1, keepdims=True)
-        weights = jnp.concatenate([neg.astype(bf16), pos.astype(bf16)], axis=0)
-        more = jnp.dot(weights, keys_refs[side][part, :], preferred_element_type=f32)
-        total = more if total is None else total + more
-        scores = following
+    def term_unit(at, which):
+        side, first = units[at]
+        part = slice(which * quarter, (which + 1) * quarter)
+        weights_ref = weight_refs[at // 2 % 2]
+        wanted = labels_ref[part, :]
+        pos_sum, neg_sum = pos_ref[part, :], neg_ref[part, :]
+        for piece in range(0, unit, lanes):
+            slot_labels = label_refs[side][:, first + piece : first + piece + lanes].astype(f32)
+            neg_shift = jnp.where(slot_labels < 0.0, -1e30, -neg_scale * margin * log2e)
+            same = wanted == slot_labels
+            slope = jnp.where(same, -pos_scale * log2e, neg_scale * log2e)
+            shift = jnp.where(same, pos_scale * margin * log2e, neg_shift)
+            term = jnp.exp2(scores_refs[at % 2][part, piece : piece + lanes] * slope + shift)
+            pos = jnp.where(same, term, 0.0)
+            neg = jnp.where(same, 0.0, term)
+            pos_sum += pos
+            neg_sum += neg
+            to = slice(at % 2 * unit + piece, at % 2 * unit + piece + lanes)
+            weights_ref[part, to] = neg.astype(bf16)
+            weights_ref[rows + which * quarter : rows + (which + 1) * quarter, to] = pos.astype(bf16)
+        pos_ref[part, :] = pos_sum
+        neg_ref[part, :] = neg_sum
+
+    def weigh_half(pair, half):
+        side, first = units[2 * pair]
+        part = slice(half * (width // 2), (half + 1) * (width // 2))
+        more = jnp.dot(
+            weight_refs[pair % 2][...], keys_refs[side][first : first + 2 * unit, part], preferred_element_type=f32
+        )
+        total_ref[:, part] = more if pair == 0 else total_ref[:, part] + more
+
+    score_unit(0)
+    for at in range(len(units)):
+        term_unit(at, 0)
+        if at + 1 < len(units):
+            score_unit(at + 1)
+        term_unit(at, 1)
+        term_unit(at, 2)
+        if at >= 2:
+            weigh_half(at // 2 - 1, at % 2)
+        term_unit(at, 3)
+    weigh_half(len(units) // 2 - 1, 0)
+    weigh_half(len(units) // 2 - 1, 1)
+    total = total_ref[...]
+    pos_sum = jnp.sum(pos_ref[...], axis=1, keepdims=True)
+    neg_sum = jnp.sum(neg_ref[...], axis=1, keepdims=True)
     floats = anchors.astype(f32)
     sums = [pos_sum, neg_sum]
     for which in range(2):
@@ -301,17 +333,29 @@
     slots, width = keys[0].shape
     parts = blocks_of(width)
     size = blocks[0].shape[0] // (parts * count + 16) * count
+    rows = len(blocks) * size
+    unit = math.gcd(256, slots // 2)
     anywhere = pl.BlockSpec(memory_space=pl.ANY)
     vmem = pl.BlockSpec(memory_space=pltpu.VMEM)
     return call(
-        functools.partial(block_kernel, len(blocks), len(keys), math.gcd(1024, slots), count, len(copied)),
+        functools.partial(block_kernel, len(blocks), len(keys), unit, count, len(copied), 9 + len(copied)),
         [shaped((2 * parts * size + sum_rows(size), lanes), dtype)] * len(blocks)
         + [shaped(value.shape, value.dtype) for value in copied],
         *blocks, *[in_vmem(k) for k in keys], *labels, *copied, *after,
         work=12 * size * len(blocks) * slots * len(keys) * width,
         in_specs=[vmem] * (len(blocks) + 2 * len(keys)) + [anywhere] * (len(copied) + len(after)),
         out_specs=[vmem] * len(blocks) + [anywhere] * len(copied),
-        scratch_shapes=[pltpu.VMEM((len(blocks) * size, width), bf16)]
+        scratch_shapes=[
+            pltpu.VMEM((rows, width), bf16),
+            pltpu.VMEM((rows, lanes), f32),
+            pltpu.VMEM((2 * rows, width), f32),
+            pltpu.VMEM((rows, lanes), f32),
+            pltpu.VMEM((rows, lanes), f32),
+            pltpu.VMEM((rows, unit), f32),
+            pltpu.VMEM((rows, unit), f32),
+            pltpu.VMEM((2 * rows, 2 * unit), bf16),
+            pltpu.VMEM((2 * rows, 2 * unit), bf16),
+        ]
         + [pltpu.SemaphoreType.DMA] * len(copied),
     )
 

time: 45.5 us -> 44.8 us (0.985)
  Pallas kernels: 18.1 us -> 17.3 us
    pallas_call x13, Pallas kernels: 18.1 us -> 17.3 us  [call(): pl.pallas_call(body, out_shape=outs, compiler_params=pltpu.CompilerParams...]
  transfers between devices with their start and end apart: 15 -> 15, of which waited for: 7 -> 7; matrix products, arithmetic and copies ran while one was open for 0% -> 0% of each run, Pallas kernels for 36% -> 35%
where the time goes in v12:
time: 44.8 us; the launch traced here: 44.5 us
  starting transfers between devices  17.9 us (40%)
  Pallas kernels  17.3 us (39%)
  waiting for transfers between devices  7.91 us (18%)
  between operations  1.4 us (3%)
    pallas_call x13, Pallas kernels, call(): pl.pallas_call(body, out_shape=outs, compiler_params=pltpu.CompilerParams...  17.3 us
    ppermute x9, starting transfers between devices, exchange(): return lax.ppermute(value, 'dev', [(i, i ^ jump) for i in range(members)])  10.7 us
    ppermute x6, starting transfers between devices, exchange(): return lax.ppermute(value, 'grp', [(i, i ^ step) for i in range(groups)])  7.17 us
    ppermute x9, waiting for transfers between devices, exchange(): return lax.ppermute(value, 'dev', [(i, i ^ jump) for i in range(members)])  5.08 us
    ppermute x6, waiting for transfers between devices, exchange(): return lax.ppermute(value, 'grp', [(i, i ^ step) for i in range(groups)])  2.83 us
  transfers between devices with their start and end apart: 15, of which 7 were waited for; matrix products, arithmetic and copies ran while one was open for 0% of the time, Pallas kernels for 35%

profile of v12, /device:TPU:0, one launch (start us, length us, event | category | flops | bytes accessed | tf_op | source)
XLA Modules:
  0.0 44.5 jit_solution(4751357928187065515)
XLA Ops:
  0.6 0.9 %shard_map.93 = (bf16[144,128]{1,0:T(8,128)(2,1)S(1)}, f32[32,512]{1,0:T(8,128)S(1)}, f32[32,128]{1,0:T(8,128)S(1)}, s32[16,128]{1,0:T(8,128)S(1)}, s32[16,128]{1,0:T(8,128)S(1)}) custom-call(bf16[32,512]{1,0:T(8,128)(2,1)} %rows_ref.1, s32[1,32]{1,0:T(1,128)} %bitcast.15, s32[16,128]{1,0:T(8,128)} %bitcast.13, s32[16,128]{1,0:T(8,128)} %bitcast.14), custom_call_target="tpu_custom_call" | custom-call | tf_op jit(solution)/shard_map/pallas_call | solution.py:23
  1.5 5.1 %collective-permute-start = (bf16[144,128]{1,0:T(8,128)(2,1)S(1)}, bf16[144,128]{1,0:T(8,128)(2,1)S(1)}, u32[]{:S(2)}, u32[]{:S(2)}) collective-permute-start(bf16[144,128]{1,0:T(8,128)(2,1)S(1)} %get-tuple-element.21.refs_0_), channel_id=1, source_target_pairs={{0,6},{1,7},{2,4},{3,5},{4,2},{5,3},{6,0},{7,1},{8,14},{9,15},{10,... | collective-permute-start | bytes 110600 | tf_op jit(solution)/shard_map/ppermute | solution.py:441
  6.6 0.0 collective-permute-start.1
  6.6 0.6 %collective-permute-start.2 = (bf16[144,128]{1,0:T(8,128)(2,1)S(1)}, bf16[144,128]{1,0:T(8,128)(2,1)S(1)}, u32[]{:S(2)}, u32[]{:S(2)}) collective-permute-start(bf16[144,128]{1,0:T(8,128)(2,1)S(1)} %get-tuple-element.21.refs_0_), channel_id=1, source_target_pairs={{0,2},{1,3},{2,0},{3,1},{4,6},{5,7},{6,4},{7,5},{8,10},{9,11},{10,... | collective-permute-start | bytes 110600 | tf_op jit(solution)/shard_map/ppermute | solution.py:441
  7.3 0.0 collective-permute-start.3
  7.3 0.5 %collective-permute-start.4 = (bf16[2048,512]{1,0:T(8,128)(2,1)}, bf16[2048,512]{1,0:T(8,128)(2,1)S(1)}, u32[]{:S(2)}, u32[]{:S(2)}) collective-permute-start(bf16[2048,512]{1,0:T(8,128)(2,1)} %refs_5_.1), channel_id=1, source_target_pairs={{0,1},{1,0},{2,3},{3,2},{4,5},{5,4},{6,7},{7,6},{8,9},{9,8},{10,11... | collective-permute-start | bytes 6291464 | tf_op jit(solution)/shard_map/ppermute | solution.py:441
  8.4 0.1 collective-permute-done.refs_1_
  8.6 2.9 %collective-permute-done.1.refs_1_ = bf16[144,128]{1,0:T(8,128)(2,1)S(1)} collective-permute-done((bf16[144,128]{1,0:T(8,128)(2,1)S(1)}, bf16[144,128]{1,0:T(8,128)(2,1)S(1)}, u32[]{:S(2)}, u32[]{:S(2)}) %collective-permute-start.1) | collective-permute-done | bytes 36896 | tf_op jit(solution)/shard_map/ppermute | solution.py:441
  11.5 0.0 collective-permute-done.3.refs_3_
  11.5 2.5 %collective-permute-start.7 = (bf16[576,128]{1,0:T(8,128)(2,1)S(1)}, bf16[576,128]{1,0:T(8,128)(2,1)S(1)}, u32[]{:S(2)}, u32[]{:S(2)}) collective-permute-start(bf16[576,128]{1,0:T(8,128)(2,1)S(1)} %shard_map.96.refs_0_), channel_id=1, source_target_pairs={{0,24},{8,16},{16,8},{24,0},{1,25},{9,17},{17,9},{25,1},{2,26},{10... | collective-permute-start | bytes 442376 | tf_op jit(solution)/shard_map/ppermute | solution.py:439
  14.1 0.5 %collective-permute-start.5 = (bf16[576,128]{1,0:T(8,128)(2,1)S(1)}, bf16[576,128]{1,0:T(8,128)(2,1)S(1)}, u32[]{:S(2)}, u32[]{:S(2)}) collective-permute-start(bf16[576,128]{1,0:T(8,128)(2,1)S(1)} %shard_map.96.refs_0_), channel_id=1, source_target_pairs={{0,16},{8,24},{16,0},{24,8},{1,17},{9,25},{17,1},{25,9},{2,18},{10... | collective-permute-start | bytes 442376 | tf_op jit(solution)/shard_map/ppermute | solution.py:439
  14.6 0.5 %collective-permute-start.6 = (bf16[576,128]{1,0:T(8,128)(2,1)S(1)}, bf16[576,128]{1,0:T(8,128)(2,1)S(1)}, u32[]{:S(2)}, u32[]{:S(2)}) collective-permute-start(bf16[576,128]{1,0:T(8,128)(2,1)S(1)} %shard_map.96.refs_0_), channel_id=1, source_target_pairs={{0,8},{8,0},{16,24},{24,16},{1,9},{9,1},{17,25},{25,17},{2,10},{10... | collective-permute-start | bytes 442376 | tf_op jit(solution)/shard_map/ppermute | solution.py:439
  15.1 2.9 %shard_map.97.refs_1_.refs_2_ = bf16[2048,512]{1,0:T(8,128)(2,1)S(1)} custom-call(bf16[2048,512]{1,0:T(8,128)(2,1)} %refs_5_.1, bf16[576,128]{1,0:T(8,128)(2,1)S(1)} %shard_map.96.refs_0_), custom_call_target="tpu_custom_call" | custom-call | flops 34359738368 | tf_op jit(solution)/shard_map/pallas_call | solution.py:23
  18.0 1.0 %shard_map.98.refs_2_.refs_3_ = bf16[2048,512]{1,0:T(8,128)(2,1)S(1)} custom-call(bf16[2048,512]{1,0:T(8,128)(2,1)S(1)} %collective-permute-done.4.memory_ref, bf16[576,128]{1,0:T(8,128)(2,1)S(1)} %shard_map.96.refs_0_), custom_call_target="tpu_custom_call" | custom-call | flops 34359738368 | tf_op jit(solution)/shard_map/pallas_call | solution.py:23
  19.0 0.3 collective-permute-done.7.refs_0_.refs_3_
  19.2 3.0 %shard_map.99.refs_6_ = bf16[1040,128]{1,0:T(8,128)(2,1)S(1)} custom-call(bf16[576,128]{1,0:T(8,128)(2,1)S(1)} %collective-permute-done.7.refs_0_.refs_3_, bf16[2048,512]{1,0:T(8,128)(2,1)S(1)} %shard_map.97.refs_1_.refs_2_, bf16[2048,512]{1,0:T(8,128)(2,1)S(1)} %shard_map.98.refs_2_.refs_3_, s32[1,2048]{1,0:T(1,128)S(1)} %bitcast.7, s32[1,2048]{1,0:T(1,128)S(1)} %bitcast.10), custom_call_target="tpu_custom_call" | custom-call | flops 3221225472 | tf_op jit(solution)/shard_map/pallas_call | solution.py:23
  22.3 0.0 copy-start
  22.3 2.3 %collective-permute-start.8 = (bf16[1040,128]{1,0:T(8,128)(2,1)S(1)}, bf16[1040,128]{1,0:T(8,128)(2,1)S(1)}, u32[]{:S(2)}, u32[]{:S(2)}) collective-permute-start(bf16[1040,128]{1,0:T(8,128)(2,1)S(1)} %shard_map.99.refs_6_), channel_id=1, source_target_pairs={{0,24},{8,16},{16,8},{24,0},{1,25},{9,17},{17,9},{25,1},{2,26},{10... | collective-permute-start | bytes 798728 | tf_op jit(solution)/shard_map/ppermute | solution.py:439
  24.6 4.2 %shard_map.100 = (bf16[1040,128]{1,0:T(8,128)(2,1)S(1)}, bf16[1040,128]{1,0:T(8,128)(2,1)S(1)}) custom-call(bf16[576,128]{1,0:T(8,128)(2,1)S(1)} %collective-permute-done.5.refs_0_.refs_2_, bf16[576,128]{1,0:T(8,128)(2,1)S(1)} %collective-permute-done.6.refs_1_, bf16[2048,512]{1,0:T(8,128)(2,1)S(1)} %shard_map.97.refs_1_.refs_2_, ...), custom_call_target="tpu_custom_call" | custom-call | flops 6442450944 | tf_op jit(solution)/shard_map/pallas_call | solution.py:23
  28.8 0.6 %collective-permute-start.10 = (bf16[1040,128]{1,0:T(8,128)(2,1)S(1)}, bf16[1040,128]{1,0:T(8,128)(2,1)S(1)}, u32[]{:S(2)}, u32[]{:S(2)}) collective-permute-start(bf16[1040,128]{1,0:T(8,128)(2,1)S(1)} %get-tuple-element.24.refs_7_.refs_5_), channel_id=1, source_target_pairs={{0,8},{8,0},{16,24},{24,16},{1,9},{9,1},{17,25},{25,17},{2,10},{10... | collective-permute-start | bytes 798728 | tf_op jit(solution)/shard_map/ppermute | solution.py:439
  29.4 0.8 %collective-permute-start.9 = (bf16[1040,128]{1,0:T(8,128)(2,1)S(1)}, bf16[1040,128]{1,0:T(8,128)(2,1)S(1)}, u32[]{:S(2)}, u32[]{:S(2)}) collective-permute-start(bf16[1040,128]{1,0:T(8,128)(2,1)S(1)} %get-tuple-element.23.refs_6_.refs_4_), channel_id=1, source_target_pairs={{0,16},{8,24},{16,0},{24,8},{1,17},{9,25},{17,1},{25,9},{2,18},{10... | collective-permute-start | bytes 798728 | tf_op jit(solution)/shard_map/ppermute | solution.py:439
  30.2 3.1 %shard_map.101 = (f32[1040,128]{1,0:T(8,128)S(1)}, bf16[2048,512]{1,0:T(8,128)(2,1)}) custom-call(bf16[576,128]{1,0:T(8,128)(2,1)S(1)} %shard_map.96.refs_0_, bf16[2048,512]{1,0:T(8,128)(2,1)S(1)} %shard_map.97.refs_1_.refs_2_, bf16[2048,512]{1,0:T(8,128)(2,1)S(1)} %shard_map.98.refs_2_.refs_3_, s32[1,2048]{1,0:T(1,128)S(1)} %bitcast.9, ...), custom_call_target="tpu_custom_call" | custom-call | flops 3221225472 | tf_op jit(solution)/shard_map/pallas_call | solution.py:23
  33.2 2.0 %collective-permute-done.10.refs_3_ = bf16[1040,128]{1,0:T(8,128)(2,1)S(1)} collective-permute-done((bf16[1040,128]{1,0:T(8,128)(2,1)S(1)}, bf16[1040,128]{1,0:T(8,128)(2,1)S(1)}, u32[]{:S(2)}, u32[]{:S(2)}) %collective-permute-start.10) | collective-permute-done | bytes 266272 | tf_op jit(solution)/shard_map/ppermute | solution.py:439
  35.3 0.5 %collective-permute-done.9.refs_2_ = bf16[1040,128]{1,0:T(8,128)(2,1)S(1)} collective-permute-done((bf16[1040,128]{1,0:T(8,128)(2,1)S(1)}, bf16[1040,128]{1,0:T(8,128)(2,1)S(1)}, u32[]{:S(2)}, u32[]{:S(2)}) %collective-permute-start.9) | collective-permute-done | bytes 266272 | tf_op jit(solution)/shard_map/ppermute | solution.py:439
  35.8 0.1 shard_map.103
  35.9 1.8 %collective-permute-start.12 = (bf16[272,128]{1,0:T(8,128)(2,1)S(1)}, bf16[272,128]{1,0:T(8,128)(2,1)S(1)}, u32[]{:S(2)}, u32[]{:S(2)}) collective-permute-start(bf16[272,128]{1,0:T(8,128)(2,1)S(1)} %get-tuple-element.27), channel_id=1, source_target_pairs={{0,6},{1,7},{2,4},{3,5},{4,2},{5,3},{6,0},{7,1},{8,14},{9,15},{10,... | collective-permute-start | bytes 208904 | tf_op jit(solution)/shard_map/ppermute | solution.py:441
  37.7 0.4 collective-permute-start.13
  38.1 2.3 %collective-permute-start.14 = (bf16[272,128]{1,0:T(8,128)(2,1)S(1)}, bf16[272,128]{1,0:T(8,128)(2,1)S(1)}, u32[]{:S(2)}, u32[]{:S(2)}) collective-permute-start(bf16[272,128]{1,0:T(8,128)(2,1)S(1)} %get-tuple-element.29), channel_id=1, source_target_pairs={{0,2},{1,3},{2,0},{3,1},{4,6},{5,7},{6,4},{7,5},{8,10},{9,11},{10,... | collective-permute-start | bytes 208904 | tf_op jit(solution)/shard_map/ppermute | solution.py:441
  40.4 1.2 %shard_map.105 = (bf16[2048,512]{1,0:T(8,128)(2,1)}, s32[16,128]{1,0:T(8,128)}) custom-call(s32[1]{0:T(128)S(6)} %copy.12.step_ref, bf16[2048,512]{1,0:T(8,128)(2,1)} %get-tuple-element.34.stored_ref, s32[16,128]{1,0:T(8,128)S(1)} %get-tuple-element.35.labels_ref, bf16[144,128]{1,0:T(8,128)(2,1)S(1)} %shard_map.102.refs_4_.refs_0_, ...), custom_call_target="tpu_custom_call", output_to_operand_aliasing={{0}: (1, {})} | custom-call | tf_op jit(solution)/shard_map/pallas_call | solution.py:23
  41.6 0.5 %collective-permute-done.12.refs_1_ = bf16[272,128]{1,0:T(8,128)(2,1)S(1)} collective-permute-done((bf16[272,128]{1,0:T(8,128)(2,1)S(1)}, bf16[272,128]{1,0:T(8,128)(2,1)S(1)}, u32[]{:S(2)}, u32[]{:S(2)}) %collective-permute-start.12) | collective-permute-done | bytes 69664 | tf_op jit(solution)/shard_map/ppermute | solution.py:441
  42.1 1.5 %collective-permute-done.13.refs_2_ = bf16[272,128]{1,0:T(8,128)(2,1)S(1)} collective-permute-done((bf16[272,128]{1,0:T(8,128)(2,1)S(1)}, bf16[272,128]{1,0:T(8,128)(2,1)S(1)}, u32[]{:S(2)}, u32[]{:S(2)}) %collective-permute-start.13) | collective-permute-done | bytes 69664 | tf_op jit(solution)/shard_map/ppermute | solution.py:441
  43.7 0.9 %shard_map.104 = (f32[32,512]{1,0:T(8,128)}, f32[1,32]{1,0:T(1,128)}) custom-call(f32[272,128]{1,0:T(8,128)S(1)} %get-tuple-element.26.refs_0_, bf16[272,128]{1,0:T(8,128)(2,1)S(1)} %collective-permute-done.12.refs_1_, bf16[272,128]{1,0:T(8,128)(2,1)S(1)} %collective-permute-done.13.refs_2_, bf16[272,128]{1,0:T(8,128)(2,1)S(1)} %collective-permute-done.14.refs_3_, ...), custom_call_target="tpu_custom_call" | custom-call | tf_op jit(solution)/shard_map/pallas_call | solution.py:23
  (13 shorter events, 0.1 us)
Async XLA Ops:
  1.5 7.1 %collective-permute-start = (bf16[144,128]{1,0:T(8,128)(2,1)S(1)}, bf16[144,128]{1,0:T(8,128)(2,1)S(1)}, u32[]{:S(2)}, u32[]{:S(2)}) collective-permute-start(bf16[144,128]{1,0:T(8,128)(2,1)S(1)} %get-tuple-element.21.refs_0_), channel_id=1, source_target_pairs={{0,6},{1,7},{2,4},{3,5},{4,2},{5,3},{6,0},{7,1},{8,14},{9,15},{10,... | collective-permute-start | bytes 110600 | tf_op jit(solution)/shard_map/ppermute | solution.py:441
  6.6 4.9 %collective-permute-start.1 = (bf16[144,128]{1,0:T(8,128)(2,1)S(1)}, bf16[144,128]{1,0:T(8,128)(2,1)S(1)}, u32[]{:S(2)}, u32[]{:S(2)}) collective-permute-start(bf16[144,128]{1,0:T(8,128)(2,1)S(1)} %get-tuple-element.21.refs_0_), channel_id=1, source_target_pairs={{0,4},{1,5},{2,6},{3,7},{4,0},{5,1},{6,2},{7,3},{8,12},{9,13},{10,... | collective-permute-start | bytes 110600 | tf_op jit(solution)/shard_map/ppermute | solution.py:441
  6.6 4.9 %collective-permute-start.2 = (bf16[144,128]{1,0:T(8,128)(2,1)S(1)}, bf16[144,128]{1,0:T(8,128)(2,1)S(1)}, u32[]{:S(2)}, u32[]{:S(2)}) collective-permute-start(bf16[144,128]{1,0:T(8,128)(2,1)S(1)} %get-tuple-element.21.refs_0_), channel_id=1, source_target_pairs={{0,2},{1,3},{2,0},{3,1},{4,6},{5,7},{6,4},{7,5},{8,10},{9,11},{10,... | collective-permute-start | bytes 110600 | tf_op jit(solution)/shard_map/ppermute | solution.py:441
  7.3 4.2 %collective-permute-start.3 = (s32[16,128]{1,0:T(8,128)S(1)}, s32[16,128]{1,0:T(8,128)S(1)}, u32[]{:S(2)}, u32[]{:S(2)}) collective-permute-start(s32[16,128]{1,0:T(8,128)S(1)} %get-tuple-element.22.refs_2_), channel_id=1, source_target_pairs={{0,1},{1,0},{2,3},{3,2},{4,5},{5,4},{6,7},{7,6},{8,9},{9,8},{10,11... | collective-permute-start | bytes 24584 | tf_op jit(solution)/shard_map/ppermute | solution.py:441
  7.3 10.7 %collective-permute-start.4 = (bf16[2048,512]{1,0:T(8,128)(2,1)}, bf16[2048,512]{1,0:T(8,128)(2,1)S(1)}, u32[]{:S(2)}, u32[]{:S(2)}) collective-permute-start(bf16[2048,512]{1,0:T(8,128)(2,1)} %refs_5_.1), channel_id=1, source_target_pairs={{0,1},{1,0},{2,3},{3,2},{4,5},{5,4},{6,7},{7,6},{8,9},{9,8},{10,11... | collective-permute-start | bytes 6291464 | tf_op jit(solution)/shard_map/ppermute | solution.py:441
  11.5 7.7 %collective-permute-start.7 = (bf16[576,128]{1,0:T(8,128)(2,1)S(1)}, bf16[576,128]{1,0:T(8,128)(2,1)S(1)}, u32[]{:S(2)}, u32[]{:S(2)}) collective-permute-start(bf16[576,128]{1,0:T(8,128)(2,1)S(1)} %shard_map.96.refs_0_), channel_id=1, source_target_pairs={{0,24},{8,16},{16,8},{24,0},{1,25},{9,17},{17,9},{25,1},{2,26},{10... | collective-permute-start | bytes 442376 | tf_op jit(solution)/shard_map/ppermute | solution.py:439
  14.1 10.5 %collective-permute-start.5 = (bf16[576,128]{1,0:T(8,128)(2,1)S(1)}, bf16[576,128]{1,0:T(8,128)(2,1)S(1)}, u32[]{:S(2)}, u32[]{:S(2)}) collective-permute-start(bf16[576,128]{1,0:T(8,128)(2,1)S(1)} %shard_map.96.refs_0_), channel_id=1, source_target_pairs={{0,16},{8,24},{16,0},{24,8},{1,17},{9,25},{17,1},{25,9},{2,18},{10... | collective-permute-start | bytes 442376 | tf_op jit(solution)/shard_map/ppermute | solution.py:439
  14.6 10.0 %collective-permute-start.6 = (bf16[576,128]{1,0:T(8,128)(2,1)S(1)}, bf16[576,128]{1,0:T(8,128)(2,1)S(1)}, u32[]{:S(2)}, u32[]{:S(2)}) collective-permute-start(bf16[576,128]{1,0:T(8,128)(2,1)S(1)} %shard_map.96.refs_0_), channel_id=1, source_target_pairs={{0,8},{8,0},{16,24},{24,16},{1,9},{9,1},{17,25},{25,17},{2,10},{10... | collective-permute-start | bytes 442376 | tf_op jit(solution)/shard_map/ppermute | solution.py:439
  22.3 7.9 %copy-start = (bf16[2048,512]{1,0:T(8,128)(2,1)S(1)}, bf16[2048,512]{1,0:T(8,128)(2,1)}, u32[]{:S(2)}) copy-start(bf16[2048,512]{1,0:T(8,128)(2,1)} %refs_5_.1) | copy-start | bytes 6291460
  22.3 13.5 %collective-permute-start.8 = (bf16[1040,128]{1,0:T(8,128)(2,1)S(1)}, bf16[1040,128]{1,0:T(8,128)(2,1)S(1)}, u32[]{:S(2)}, u32[]{:S(2)}) collective-permute-start(bf16[1040,128]{1,0:T(8,128)(2,1)S(1)} %shard_map.99.refs_6_), channel_id=1, source_target_pairs={{0,24},{8,16},{16,8},{24,0},{1,25},{9,17},{17,9},{25,1},{2,26},{10... | collective-permute-start | bytes 798728 | tf_op jit(solution)/shard_map/ppermute | solution.py:439
  28.8 6.5 %collective-permute-start.10 = (bf16[1040,128]{1,0:T(8,128)(2,1)S(1)}, bf16[1040,128]{1,0:T(8,128)(2,1)S(1)}, u32[]{:S(2)}, u32[]{:S(2)}) collective-permute-start(bf16[1040,128]{1,0:T(8,128)(2,1)S(1)} %get-tuple-element.24.refs_7_.refs_5_), channel_id=1, source_target_pairs={{0,8},{8,0},{16,24},{24,16},{1,9},{9,1},{17,25},{25,17},{2,10},{10... | collective-permute-start | bytes 798728 | tf_op jit(solution)/shard_map/ppermute | solution.py:439
  29.4 6.4 %collective-permute-start.9 = (bf16[1040,128]{1,0:T(8,128)(2,1)S(1)}, bf16[1040,128]{1,0:T(8,128)(2,1)S(1)}, u32[]{:S(2)}, u32[]{:S(2)}) collective-permute-start(bf16[1040,128]{1,0:T(8,128)(2,1)S(1)} %get-tuple-element.23.refs_6_.refs_4_), channel_id=1, source_target_pairs={{0,16},{8,24},{16,0},{24,8},{1,17},{9,25},{17,1},{25,9},{2,18},{10... | collective-permute-start | bytes 798728 | tf_op jit(solution)/shard_map/ppermute | solution.py:439
  30.1 3.1 %collective-permute-start.11 = (bf16[144,128]{1,0:T(8,128)(2,1)S(1)}, bf16[144,128]{1,0:T(8,128)(2,1)S(1)}, u32[]{:S(2)}, u32[]{:S(2)}) collective-permute-start(bf16[144,128]{1,0:T(8,128)(2,1)S(1)} %shard_map.102.refs_4_.refs_0_), channel_id=1, source_target_pairs={{0,1},{1,0},{2,3},{3,2},{4,5},{5,4},{6,7},{7,6},{8,9},{9,8},{10,11... | collective-permute-start | bytes 110600 | tf_op jit(solution)/shard_map/ppermute | solution.py:441
  35.9 6.2 %collective-permute-start.12 = (bf16[272,128]{1,0:T(8,128)(2,1)S(1)}, bf16[272,128]{1,0:T(8,128)(2,1)S(1)}, u32[]{:S(2)}, u32[]{:S(2)}) collective-permute-start(bf16[272,128]{1,0:T(8,128)(2,1)S(1)} %get-tuple-element.27), channel_id=1, source_target_pairs={{0,6},{1,7},{2,4},{3,5},{4,2},{5,3},{6,0},{7,1},{8,14},{9,15},{10,... | collective-permute-start | bytes 208904 | tf_op jit(solution)/shard_map/ppermute | solution.py:441
  37.7 6.0 %collective-permute-start.13 = (bf16[272,128]{1,0:T(8,128)(2,1)S(1)}, bf16[272,128]{1,0:T(8,128)(2,1)S(1)}, u32[]{:S(2)}, u32[]{:S(2)}) collective-permute-start(bf16[272,128]{1,0:T(8,128)(2,1)S(1)} %get-tuple-element.28), channel_id=1, source_target_pairs={{0,4},{1,5},{2,6},{3,7},{4,0},{5,1},{6,2},{7,3},{8,12},{9,13},{10,... | collective-permute-start | bytes 208904 | tf_op jit(solution)/shard_map/ppermute | solution.py:441
  38.1 5.6 %collective-permute-start.14 = (bf16[272,128]{1,0:T(8,128)(2,1)S(1)}, bf16[272,128]{1,0:T(8,128)(2,1)S(1)}, u32[]{:S(2)}, u32[]{:S(2)}) collective-permute-start(bf16[272,128]{1,0:T(8,128)(2,1)S(1)} %get-tuple-element.29), channel_id=1, source_target_pairs={{0,2},{1,3},{2,0},{3,1},{4,6},{5,7},{6,4},{7,5},{8,10},{9,11},{10,... | collective-permute-start | bytes 208904 | tf_op jit(solution)/shard_map/ppermute | solution.py:441

commit v13 on v12

--- a/solution.py
+++ b/solution.py
@@ -412,16 +412,15 @@
         sums.append((total[row : row + 1, :] + total[row + 1 : row + 2, :])[:, :count])
     pos, neg = sums[:2]
     loss_ref[...] = jnp.log(1.0 + pos) / pos_scale + jnp.log(1.0 + neg) / neg_scale
-    pos, neg, push_along, pull_along = [to_column(row) for row in sums]
+    scales = [to_column(1.0 / (1.0 + row)) for row in (neg, pos)]
+    alongs = [to_column(row) for row in sums[2:]]
     unit = unit_ref[...]
     anchors = unit.astype(bf16).astype(f32)
     push, pull = [
         jnp.concatenate([total[(first + at) * count : (first + at + 1) * count, :] for at in range(parts)], axis=1)
         for first in (0, parts)
     ]
-    push = push + push_along * anchors
-    pull = pull + pull_along * anchors
-    grad_unit = push / (1.0 + neg) - pull / (1.0 + pos)
+    grad_unit = (push + alongs[0] * anchors) * scales[0] - (pull + alongs[1] * anchors) * scales[1]
     along = jnp.sum(unit * grad_unit, axis=1, keepdims=True)
     grad_ref[...] = (grad_unit - unit * along) / radius_ref[:, :1]
 
@@ -481,7 +480,8 @@
     choices = [moved] + [exchange(moved, "core", s) for s in range(1, cores)]
 
     sums, *others = add(held, arrived, size, count, 2 * parts, choices)
-    arrived = [exchange(value, "line", line - at) for at, value in enumerate(others, 1)]
+    order = sorted(range(1, line), key=lambda step: (step != line // 2, -step))
+    arrived = [exchange(others[line - 1 - step], "line", step) for step in order]
     grad_batch, loss = call(
         functools.partial(finish_kernel, len(arrived)),
         [shaped((count, width), f32), shaped((1, count), f32)],

time: 44.8 us -> 45.2 us (level)
  waiting for transfers between devices: 7.91 us -> 9.26 us
  starting transfers between devices: 17.9 us -> 17 us
    ppermute x9, waiting for transfers between devices: 5.08 us -> 6.43 us  [exchange(): return lax.ppermute(value, 'dev', [(i, i ^ jump) for i in range(members)])]
    ppermute x9, starting transfers between devices: 10.7 us -> 9.82 us  [exchange(): return lax.ppermute(value, 'dev', [(i, i ^ jump) for i in range(members)])]
  transfers between devices with their start and end apart: 15 -> 15, of which waited for: 7 -> 7; matrix products, arithmetic and copies ran while one was open for 0% -> 0% of each run, Pallas kernels for 35% -> 34%
where the time goes in v13:
time: 45.2 us; the launch traced here: 45 us
  Pallas kernels  17.3 us (38%)
  starting transfers between devices  17 us (38%)
  waiting for transfers between devices  9.26 us (20%)
  between operations  1.4 us (3%)
    pallas_call x13, Pallas kernels, call(): pl.pallas_call(body, out_shape=outs, compiler_params=pltpu.CompilerParams...  17.3 us
    ppermute x9, starting transfers between devices, exchange(): return lax.ppermute(value, 'dev', [(i, i ^ jump) for i in range(members)])  9.82 us
    ppermute x6, starting transfers between devices, exchange(): return lax.ppermute(value, 'grp', [(i, i ^ step) for i in range(groups)])  7.17 us
    ppermute x9, waiting for transfers between devices, exchange(): return lax.ppermute(value, 'dev', [(i, i ^ jump) for i in range(members)])  6.43 us
    ppermute x6, waiting for transfers between devices, exchange(): return lax.ppermute(value, 'grp', [(i, i ^ step) for i in range(groups)])  2.83 us
  transfers between devices with their start and end apart: 15, of which 7 were waited for; matrix products, arithmetic and copies ran while one was open for 0% of the time, Pallas kernels for 34%

profile of v13, /device:TPU:0, one launch (start us, length us, event | category | flops | bytes accessed | tf_op | source)
XLA Modules:
  0.0 45.0 jit_solution(13271561201987376946)
XLA Ops:
  0.6 0.9 %shard_map.93 = (bf16[144,128]{1,0:T(8,128)(2,1)S(1)}, f32[32,512]{1,0:T(8,128)S(1)}, f32[32,128]{1,0:T(8,128)S(1)}, s32[16,128]{1,0:T(8,128)S(1)}, s32[16,128]{1,0:T(8,128)S(1)}) custom-call(bf16[32,512]{1,0:T(8,128)(2,1)} %rows_ref.1, s32[1,32]{1,0:T(1,128)} %bitcast.15, s32[16,128]{1,0:T(8,128)} %bitcast.13, s32[16,128]{1,0:T(8,128)} %bitcast.14), custom_call_target="tpu_custom_call" | custom-call | tf_op jit(solution)/shard_map/pallas_call | solution.py:23
  1.5 5.1 %collective-permute-start = (bf16[144,128]{1,0:T(8,128)(2,1)S(1)}, bf16[144,128]{1,0:T(8,128)(2,1)S(1)}, u32[]{:S(2)}, u32[]{:S(2)}) collective-permute-start(bf16[144,128]{1,0:T(8,128)(2,1)S(1)} %get-tuple-element.21.refs_0_), channel_id=1, source_target_pairs={{0,6},{1,7},{2,4},{3,5},{4,2},{5,3},{6,0},{7,1},{8,14},{9,15},{10,... | collective-permute-start | bytes 110600 | tf_op jit(solution)/shard_map/ppermute | solution.py:440
  6.6 0.6 %collective-permute-start.2 = (bf16[144,128]{1,0:T(8,128)(2,1)S(1)}, bf16[144,128]{1,0:T(8,128)(2,1)S(1)}, u32[]{:S(2)}, u32[]{:S(2)}) collective-permute-start(bf16[144,128]{1,0:T(8,128)(2,1)S(1)} %get-tuple-element.21.refs_0_), channel_id=1, source_target_pairs={{0,2},{1,3},{2,0},{3,1},{4,6},{5,7},{6,4},{7,5},{8,10},{9,11},{10,... | collective-permute-start | bytes 110600 | tf_op jit(solution)/shard_map/ppermute | solution.py:440
  7.3 0.0 collective-permute-start.3
  7.3 0.5 %collective-permute-start.4 = (bf16[2048,512]{1,0:T(8,128)(2,1)}, bf16[2048,512]{1,0:T(8,128)(2,1)S(1)}, u32[]{:S(2)}, u32[]{:S(2)}) collective-permute-start(bf16[2048,512]{1,0:T(8,128)(2,1)} %refs_5_.1), channel_id=1, source_target_pairs={{0,1},{1,0},{2,3},{3,2},{4,5},{5,4},{6,7},{7,6},{8,9},{9,8},{10,11... | collective-permute-start | bytes 6291464 | tf_op jit(solution)/shard_map/ppermute | solution.py:440
  8.4 0.1 collective-permute-done.refs_1_
  8.6 2.9 %collective-permute-done.1.refs_1_ = bf16[144,128]{1,0:T(8,128)(2,1)S(1)} collective-permute-done((bf16[144,128]{1,0:T(8,128)(2,1)S(1)}, bf16[144,128]{1,0:T(8,128)(2,1)S(1)}, u32[]{:S(2)}, u32[]{:S(2)}) %collective-permute-start.1) | collective-permute-done | bytes 36896 | tf_op jit(solution)/shard_map/ppermute | solution.py:440
  11.5 2.5 %collective-permute-start.7 = (bf16[576,128]{1,0:T(8,128)(2,1)S(1)}, bf16[576,128]{1,0:T(8,128)(2,1)S(1)}, u32[]{:S(2)}, u32[]{:S(2)}) collective-permute-start(bf16[576,128]{1,0:T(8,128)(2,1)S(1)} %shard_map.96.refs_0_), channel_id=1, source_target_pairs={{0,24},{8,16},{16,8},{24,0},{1,25},{9,17},{17,9},{25,1},{2,26},{10... | collective-permute-start | bytes 442376 | tf_op jit(solution)/shard_map/ppermute | solution.py:438
  14.1 0.5 %collective-permute-start.5 = (bf16[576,128]{1,0:T(8,128)(2,1)S(1)}, bf16[576,128]{1,0:T(8,128)(2,1)S(1)}, u32[]{:S(2)}, u32[]{:S(2)}) collective-permute-start(bf16[576,128]{1,0:T(8,128)(2,1)S(1)} %shard_map.96.refs_0_), channel_id=1, source_target_pairs={{0,16},{8,24},{16,0},{24,8},{1,17},{9,25},{17,1},{25,9},{2,18},{10... | collective-permute-start | bytes 442376 | tf_op jit(solution)/shard_map/ppermute | solution.py:438
  14.6 0.5 %collective-permute-start.6 = (bf16[576,128]{1,0:T(8,128)(2,1)S(1)}, bf16[576,128]{1,0:T(8,128)(2,1)S(1)}, u32[]{:S(2)}, u32[]{:S(2)}) collective-permute-start(bf16[576,128]{1,0:T(8,128)(2,1)S(1)} %shard_map.96.refs_0_), channel_id=1, source_target_pairs={{0,8},{8,0},{16,24},{24,16},{1,9},{9,1},{17,25},{25,17},{2,10},{10... | collective-permute-start | bytes 442376 | tf_op jit(solution)/shard_map/ppermute | solution.py:438
  15.1 2.9 %shard_map.97.refs_1_.refs_2_ = bf16[2048,512]{1,0:T(8,128)(2,1)S(1)} custom-call(bf16[2048,512]{1,0:T(8,128)(2,1)} %refs_5_.1, bf16[576,128]{1,0:T(8,128)(2,1)S(1)} %shard_map.96.refs_0_), custom_call_target="tpu_custom_call" | custom-call | flops 34359738368 | tf_op jit(solution)/shard_map/pallas_call | solution.py:23
  18.0 1.0 %shard_map.98.refs_2_.refs_3_ = bf16[2048,512]{1,0:T(8,128)(2,1)S(1)} custom-call(bf16[2048,512]{1,0:T(8,128)(2,1)S(1)} %collective-permute-done.4.memory_ref, bf16[576,128]{1,0:T(8,128)(2,1)S(1)} %shard_map.96.refs_0_), custom_call_target="tpu_custom_call" | custom-call | flops 34359738368 | tf_op jit(solution)/shard_map/pallas_call | solution.py:23
  19.0 0.3 collective-permute-done.7.refs_0_.refs_3_
  19.2 3.0 %shard_map.99.refs_6_ = bf16[1040,128]{1,0:T(8,128)(2,1)S(1)} custom-call(bf16[576,128]{1,0:T(8,128)(2,1)S(1)} %collective-permute-done.7.refs_0_.refs_3_, bf16[2048,512]{1,0:T(8,128)(2,1)S(1)} %shard_map.97.refs_1_.refs_2_, bf16[2048,512]{1,0:T(8,128)(2,1)S(1)} %shard_map.98.refs_2_.refs_3_, s32[1,2048]{1,0:T(1,128)S(1)} %bitcast.7, s32[1,2048]{1,0:T(1,128)S(1)} %bitcast.10), custom_call_target="tpu_custom_call" | custom-call | flops 3221225472 | tf_op jit(solution)/shard_map/pallas_call | solution.py:23
  22.3 0.0 copy-start
  22.3 2.3 %collective-permute-start.8 = (bf16[1040,128]{1,0:T(8,128)(2,1)S(1)}, bf16[1040,128]{1,0:T(8,128)(2,1)S(1)}, u32[]{:S(2)}, u32[]{:S(2)}) collective-permute-start(bf16[1040,128]{1,0:T(8,128)(2,1)S(1)} %shard_map.99.refs_6_), channel_id=1, source_target_pairs={{0,24},{8,16},{16,8},{24,0},{1,25},{9,17},{17,9},{25,1},{2,26},{10... | collective-permute-start | bytes 798728 | tf_op jit(solution)/shard_map/ppermute | solution.py:438
  24.6 0.0 collective-permute-done.5.refs_0_.refs_2_
  24.6 0.0 collective-permute-done.6.refs_1_
  24.6 4.2 %shard_map.100 = (bf16[1040,128]{1,0:T(8,128)(2,1)S(1)}, bf16[1040,128]{1,0:T(8,128)(2,1)S(1)}) custom-call(bf16[576,128]{1,0:T(8,128)(2,1)S(1)} %collective-permute-done.5.refs_0_.refs_2_, bf16[576,128]{1,0:T(8,128)(2,1)S(1)} %collective-permute-done.6.refs_1_, bf16[2048,512]{1,0:T(8,128)(2,1)S(1)} %shard_map.97.refs_1_.refs_2_, ...), custom_call_target="tpu_custom_call" | custom-call | flops 6442450944 | tf_op jit(solution)/shard_map/pallas_call | solution.py:23
  28.8 0.6 %collective-permute-start.10 = (bf16[1040,128]{1,0:T(8,128)(2,1)S(1)}, bf16[1040,128]{1,0:T(8,128)(2,1)S(1)}, u32[]{:S(2)}, u32[]{:S(2)}) collective-permute-start(bf16[1040,128]{1,0:T(8,128)(2,1)S(1)} %get-tuple-element.24.refs_7_.refs_5_), channel_id=1, source_target_pairs={{0,8},{8,0},{16,24},{24,16},{1,9},{9,1},{17,25},{25,17},{2,10},{10... | collective-permute-start | bytes 798728 | tf_op jit(solution)/shard_map/ppermute | solution.py:438
  29.4 0.8 %collective-permute-start.9 = (bf16[1040,128]{1,0:T(8,128)(2,1)S(1)}, bf16[1040,128]{1,0:T(8,128)(2,1)S(1)}, u32[]{:S(2)}, u32[]{:S(2)}) collective-permute-start(bf16[1040,128]{1,0:T(8,128)(2,1)S(1)} %get-tuple-element.23.refs_6_.refs_4_), channel_id=1, source_target_pairs={{0,16},{8,24},{16,0},{24,8},{1,17},{9,25},{17,1},{25,9},{2,18},{10... | collective-permute-start | bytes 798728 | tf_op jit(solution)/shard_map/ppermute | solution.py:438
  30.2 3.1 %shard_map.101 = (f32[1040,128]{1,0:T(8,128)S(1)}, bf16[2048,512]{1,0:T(8,128)(2,1)}) custom-call(bf16[576,128]{1,0:T(8,128)(2,1)S(1)} %shard_map.96.refs_0_, bf16[2048,512]{1,0:T(8,128)(2,1)S(1)} %shard_map.97.refs_1_.refs_2_, bf16[2048,512]{1,0:T(8,128)(2,1)S(1)} %shard_map.98.refs_2_.refs_3_, s32[1,2048]{1,0:T(1,128)S(1)} %bitcast.9, ...), custom_call_target="tpu_custom_call" | custom-call | flops 3221225472 | tf_op jit(solution)/shard_map/pallas_call | solution.py:23
  33.2 2.0 %collective-permute-done.10.refs_3_ = bf16[1040,128]{1,0:T(8,128)(2,1)S(1)} collective-permute-done((bf16[1040,128]{1,0:T(8,128)(2,1)S(1)}, bf16[1040,128]{1,0:T(8,128)(2,1)S(1)}, u32[]{:S(2)}, u32[]{:S(2)}) %collective-permute-start.10) | collective-permute-done | bytes 266272 | tf_op jit(solution)/shard_map/ppermute | solution.py:438
  35.3 0.5 %collective-permute-done.9.refs_2_ = bf16[1040,128]{1,0:T(8,128)(2,1)S(1)} collective-permute-done((bf16[1040,128]{1,0:T(8,128)(2,1)S(1)}, bf16[1040,128]{1,0:T(8,128)(2,1)S(1)}, u32[]{:S(2)}, u32[]{:S(2)}) %collective-permute-start.9) | collective-permute-done | bytes 266272 | tf_op jit(solution)/shard_map/ppermute | solution.py:438
  35.8 0.1 shard_map.103
  35.9 2.1 %collective-permute-start.12 = (bf16[272,128]{1,0:T(8,128)(2,1)S(1)}, bf16[272,128]{1,0:T(8,128)(2,1)S(1)}, u32[]{:S(2)}, u32[]{:S(2)}) collective-permute-start(bf16[272,128]{1,0:T(8,128)(2,1)S(1)} %get-tuple-element.27), channel_id=1, source_target_pairs={{0,4},{1,5},{2,6},{3,7},{4,0},{5,1},{6,2},{7,3},{8,12},{9,13},{10,... | collective-permute-start | bytes 208904 | tf_op jit(solution)/shard_map/ppermute | solution.py:440
  38.0 0.3 collective-permute-start.13
  38.3 1.2 %collective-permute-start.14 = (bf16[272,128]{1,0:T(8,128)(2,1)S(1)}, bf16[272,128]{1,0:T(8,128)(2,1)S(1)}, u32[]{:S(2)}, u32[]{:S(2)}) collective-permute-start(bf16[272,128]{1,0:T(8,128)(2,1)S(1)} %get-tuple-element.29), channel_id=1, source_target_pairs={{0,2},{1,3},{2,0},{3,1},{4,6},{5,7},{6,4},{7,5},{8,10},{9,11},{10,... | collective-permute-start | bytes 208904 | tf_op jit(solution)/shard_map/ppermute | solution.py:440
  39.5 1.2 %shard_map.105 = (bf16[2048,512]{1,0:T(8,128)(2,1)}, s32[16,128]{1,0:T(8,128)}) custom-call(s32[1]{0:T(128)S(6)} %copy.12.step_ref, bf16[2048,512]{1,0:T(8,128)(2,1)} %get-tuple-element.34.stored_ref, s32[16,128]{1,0:T(8,128)S(1)} %get-tuple-element.35.labels_ref, bf16[144,128]{1,0:T(8,128)(2,1)S(1)} %shard_map.102.refs_4_.refs_0_, ...), custom_call_target="tpu_custom_call", output_to_operand_aliasing={{0}: (1, {})} | custom-call | tf_op jit(solution)/shard_map/pallas_call | solution.py:23
  40.7 1.3 %collective-permute-done.12.refs_1_ = bf16[272,128]{1,0:T(8,128)(2,1)S(1)} collective-permute-done((bf16[272,128]{1,0:T(8,128)(2,1)S(1)}, bf16[272,128]{1,0:T(8,128)(2,1)S(1)}, u32[]{:S(2)}, u32[]{:S(2)}) %collective-permute-start.12) | collective-permute-done | bytes 69664 | tf_op jit(solution)/shard_map/ppermute | solution.py:440
  42.1 2.0 %collective-permute-done.13.refs_2_ = bf16[272,128]{1,0:T(8,128)(2,1)S(1)} collective-permute-done((bf16[272,128]{1,0:T(8,128)(2,1)S(1)}, bf16[272,128]{1,0:T(8,128)(2,1)S(1)}, u32[]{:S(2)}, u32[]{:S(2)}) %collective-permute-start.13) | collective-permute-done | bytes 69664 | tf_op jit(solution)/shard_map/ppermute | solution.py:440
  44.1 0.9 %shard_map.104 = (f32[32,512]{1,0:T(8,128)}, f32[1,32]{1,0:T(1,128)}) custom-call(f32[272,128]{1,0:T(8,128)S(1)} %get-tuple-element.26.refs_0_, bf16[272,128]{1,0:T(8,128)(2,1)S(1)} %collective-permute-done.12.refs_1_, bf16[272,128]{1,0:T(8,128)(2,1)S(1)} %collective-permute-done.13.refs_2_, bf16[272,128]{1,0:T(8,128)(2,1)S(1)} %collective-permute-done.14.refs_3_, ...), custom_call_target="tpu_custom_call" | custom-call | tf_op jit(solution)/shard_map/pallas_call | solution.py:23
  (13 shorter events, 0.1 us)
Async XLA Ops:
  1.5 7.1 %collective-permute-start = (bf16[144,128]{1,0:T(8,128)(2,1)S(1)}, bf16[144,128]{1,0:T(8,128)(2,1)S(1)}, u32[]{:S(2)}, u32[]{:S(2)}) collective-permute-start(bf16[144,128]{1,0:T(8,128)(2,1)S(1)} %get-tuple-element.21.refs_0_), channel_id=1, source_target_pairs={{0,6},{1,7},{2,4},{3,5},{4,2},{5,3},{6,0},{7,1},{8,14},{9,15},{10,... | collective-permute-start | bytes 110600 | tf_op jit(solution)/shard_map/ppermute | solution.py:440
  6.6 4.9 %collective-permute-start.1 = (bf16[144,128]{1,0:T(8,128)(2,1)S(1)}, bf16[144,128]{1,0:T(8,128)(2,1)S(1)}, u32[]{:S(2)}, u32[]{:S(2)}) collective-permute-start(bf16[144,128]{1,0:T(8,128)(2,1)S(1)} %get-tuple-element.21.refs_0_), channel_id=1, source_target_pairs={{0,4},{1,5},{2,6},{3,7},{4,0},{5,1},{6,2},{7,3},{8,12},{9,13},{10,... | collective-permute-start | bytes 110600 | tf_op jit(solution)/shard_map/ppermute | solution.py:440
  6.6 4.9 %collective-permute-start.2 = (bf16[144,128]{1,0:T(8,128)(2,1)S(1)}, bf16[144,128]{1,0:T(8,128)(2,1)S(1)}, u32[]{:S(2)}, u32[]{:S(2)}) collective-permute-start(bf16[144,128]{1,0:T(8,128)(2,1)S(1)} %get-tuple-element.21.refs_0_), channel_id=1, source_target_pairs={{0,2},{1,3},{2,0},{3,1},{4,6},{5,7},{6,4},{7,5},{8,10},{9,11},{10,... | collective-permute-start | bytes 110600 | tf_op jit(solution)/shard_map/ppermute | solution.py:440
  7.3 4.2 %collective-permute-start.3 = (s32[16,128]{1,0:T(8,128)S(1)}, s32[16,128]{1,0:T(8,128)S(1)}, u32[]{:S(2)}, u32[]{:S(2)}) collective-permute-start(s32[16,128]{1,0:T(8,128)S(1)} %get-tuple-element.22.refs_2_), channel_id=1, source_target_pairs={{0,1},{1,0},{2,3},{3,2},{4,5},{5,4},{6,7},{7,6},{8,9},{9,8},{10,11... | collective-permute-start | bytes 24584 | tf_op jit(solution)/shard_map/ppermute | solution.py:440
  7.3 10.7 %collective-permute-start.4 = (bf16[2048,512]{1,0:T(8,128)(2,1)}, bf16[2048,512]{1,0:T(8,128)(2,1)S(1)}, u32[]{:S(2)}, u32[]{:S(2)}) collective-permute-start(bf16[2048,512]{1,0:T(8,128)(2,1)} %refs_5_.1), channel_id=1, source_target_pairs={{0,1},{1,0},{2,3},{3,2},{4,5},{5,4},{6,7},{7,6},{8,9},{9,8},{10,11... | collective-permute-start | bytes 6291464 | tf_op jit(solution)/shard_map/ppermute | solution.py:440
  11.5 7.7 %collective-permute-start.7 = (bf16[576,128]{1,0:T(8,128)(2,1)S(1)}, bf16[576,128]{1,0:T(8,128)(2,1)S(1)}, u32[]{:S(2)}, u32[]{:S(2)}) collective-permute-start(bf16[576,128]{1,0:T(8,128)(2,1)S(1)} %shard_map.96.refs_0_), channel_id=1, source_target_pairs={{0,24},{8,16},{16,8},{24,0},{1,25},{9,17},{17,9},{25,1},{2,26},{10... | collective-permute-start | bytes 442376 | tf_op jit(solution)/shard_map/ppermute | solution.py:438
  14.1 10.5 %collective-permute-start.5 = (bf16[576,128]{1,0:T(8,128)(2,1)S(1)}, bf16[576,128]{1,0:T(8,128)(2,1)S(1)}, u32[]{:S(2)}, u32[]{:S(2)}) collective-permute-start(bf16[576,128]{1,0:T(8,128)(2,1)S(1)} %shard_map.96.refs_0_), channel_id=1, source_target_pairs={{0,16},{8,24},{16,0},{24,8},{1,17},{9,25},{17,1},{25,9},{2,18},{10... | collective-permute-start | bytes 442376 | tf_op jit(solution)/shard_map/ppermute | solution.py:438
  14.6 10.0 %collective-permute-start.6 = (bf16[576,128]{1,0:T(8,128)(2,1)S(1)}, bf16[576,128]{1,0:T(8,128)(2,1)S(1)}, u32[]{:S(2)}, u32[]{:S(2)}) collective-permute-start(bf16[576,128]{1,0:T(8,128)(2,1)S(1)} %shard_map.96.refs_0_), channel_id=1, source_target_pairs={{0,8},{8,0},{16,24},{24,16},{1,9},{9,1},{17,25},{25,17},{2,10},{10... | collective-permute-start | bytes 442376 | tf_op jit(solution)/shard_map/ppermute | solution.py:438
  22.3 7.9 %copy-start = (bf16[2048,512]{1,0:T(8,128)(2,1)S(1)}, bf16[2048,512]{1,0:T(8,128)(2,1)}, u32[]{:S(2)}) copy-start(bf16[2048,512]{1,0:T(8,128)(2,1)} %refs_5_.1) | copy-start | bytes 6291460
  22.3 13.5 %collective-permute-start.8 = (bf16[1040,128]{1,0:T(8,128)(2,1)S(1)}, bf16[1040,128]{1,0:T(8,128)(2,1)S(1)}, u32[]{:S(2)}, u32[]{:S(2)}) collective-permute-start(bf16[1040,128]{1,0:T(8,128)(2,1)S(1)} %shard_map.99.refs_6_), channel_id=1, source_target_pairs={{0,24},{8,16},{16,8},{24,0},{1,25},{9,17},{17,9},{25,1},{2,26},{10... | collective-permute-start | bytes 798728 | tf_op jit(solution)/shard_map/ppermute | solution.py:438
  28.8 6.5 %collective-permute-start.10 = (bf16[1040,128]{1,0:T(8,128)(2,1)S(1)}, bf16[1040,128]{1,0:T(8,128)(2,1)S(1)}, u32[]{:S(2)}, u32[]{:S(2)}) collective-permute-start(bf16[1040,128]{1,0:T(8,128)(2,1)S(1)} %get-tuple-element.24.refs_7_.refs_5_), channel_id=1, source_target_pairs={{0,8},{8,0},{16,24},{24,16},{1,9},{9,1},{17,25},{25,17},{2,10},{10... | collective-permute-start | bytes 798728 | tf_op jit(solution)/shard_map/ppermute | solution.py:438
  29.4 6.4 %collective-permute-start.9 = (bf16[1040,128]{1,0:T(8,128)(2,1)S(1)}, bf16[1040,128]{1,0:T(8,128)(2,1)S(1)}, u32[]{:S(2)}, u32[]{:S(2)}) collective-permute-start(bf16[1040,128]{1,0:T(8,128)(2,1)S(1)} %get-tuple-element.23.refs_6_.refs_4_), channel_id=1, source_target_pairs={{0,16},{8,24},{16,0},{24,8},{1,17},{9,25},{17,1},{25,9},{2,18},{10... | collective-permute-start | bytes 798728 | tf_op jit(solution)/shard_map/ppermute | solution.py:438
  30.1 3.1 %collective-permute-start.11 = (bf16[144,128]{1,0:T(8,128)(2,1)S(1)}, bf16[144,128]{1,0:T(8,128)(2,1)S(1)}, u32[]{:S(2)}, u32[]{:S(2)}) collective-permute-start(bf16[144,128]{1,0:T(8,128)(2,1)S(1)} %shard_map.102.refs_4_.refs_0_), channel_id=1, source_target_pairs={{0,1},{1,0},{2,3},{3,2},{4,5},{5,4},{6,7},{7,6},{8,9},{9,8},{10,11... | collective-permute-start | bytes 110600 | tf_op jit(solution)/shard_map/ppermute | solution.py:440
  35.9 6.1 %collective-permute-start.12 = (bf16[272,128]{1,0:T(8,128)(2,1)S(1)}, bf16[272,128]{1,0:T(8,128)(2,1)S(1)}, u32[]{:S(2)}, u32[]{:S(2)}) collective-permute-start(bf16[272,128]{1,0:T(8,128)(2,1)S(1)} %get-tuple-element.27), channel_id=1, source_target_pairs={{0,4},{1,5},{2,6},{3,7},{4,0},{5,1},{6,2},{7,3},{8,12},{9,13},{10,... | collective-permute-start | bytes 208904 | tf_op jit(solution)/shard_map/ppermute | solution.py:440
  38.0 6.1 %collective-permute-start.13 = (bf16[272,128]{1,0:T(8,128)(2,1)S(1)}, bf16[272,128]{1,0:T(8,128)(2,1)S(1)}, u32[]{:S(2)}, u32[]{:S(2)}) collective-permute-start(bf16[272,128]{1,0:T(8,128)(2,1)S(1)} %get-tuple-element.28), channel_id=1, source_target_pairs={{0,6},{1,7},{2,4},{3,5},{4,2},{5,3},{6,0},{7,1},{8,14},{9,15},{10,... | collective-permute-start | bytes 208904 | tf_op jit(solution)/shard_map/ppermute | solution.py:440
  38.3 5.8 %collective-permute-start.14 = (bf16[272,128]{1,0:T(8,128)(2,1)S(1)}, bf16[272,128]{1,0:T(8,128)(2,1)S(1)}, u32[]{:S(2)}, u32[]{:S(2)}) collective-permute-start(bf16[272,128]{1,0:T(8,128)(2,1)S(1)} %get-tuple-element.29), channel_id=1, source_target_pairs={{0,2},{1,3},{2,0},{3,1},{4,6},{5,7},{6,4},{7,5},{8,10},{9,11},{10,... | collective-permute-start | bytes 208904 | tf_op jit(solution)/shard_map/ppermute | solution.py:440

commit v14 on v13

--- a/solution.py
+++ b/solution.py
@@ -223,7 +223,7 @@
     rows_refs, keys_refs = refs[:blocks], refs[blocks : blocks + sides]
     label_refs = refs[blocks + sides : blocks + 2 * sides]
     out_refs = refs[-scratch - blocks : -scratch]
-    anchors_ref, labels_ref, total_ref, pos_ref, neg_ref = refs[-scratch:-4]
+    anchors_ref, labels_ref, total_ref, *sum_refs = refs[-scratch:-4]
     scores_refs, weight_refs = refs[-4:-2], refs[-2:]
     slots, width = keys_refs[0].shape
     parts = blocks_of(width)
@@ -243,8 +243,8 @@
             columns.append(to_column((digits[0:1, :] * 256.0 + digits[1:2, :])[:, :count]))
     rows = blocks * size
     labels_ref[...] = jnp.broadcast_to(jnp.concatenate(columns, axis=0), labels_ref.shape)
-    pos_ref[...] = jnp.zeros_like(pos_ref)
-    neg_ref[...] = jnp.zeros_like(neg_ref)
+    for ref in sum_refs:
+        ref[...] = jnp.zeros_like(ref)
     anchors = anchors_ref[...]
     units = [(side, at) for side in range(sides) for at in range(0, slots, unit)]
     quarter = rows // 4
@@ -260,23 +260,26 @@
         part = slice(which * quarter, (which + 1) * quarter)
         weights_ref = weight_refs[at // 2 % 2]
         wanted = labels_ref[part, :]
-        pos_sum, neg_sum = pos_ref[part, :], neg_ref[part, :]
+        pos_sum, neg_sum, push_along, pull_along = [ref[part, :] for ref in sum_refs]
         for piece in range(0, unit, lanes):
             slot_labels = label_refs[side][:, first + piece : first + piece + lanes].astype(f32)
             neg_shift = jnp.where(slot_labels < 0.0, -1e30, -neg_scale * margin * log2e)
             same = wanted == slot_labels
             slope = jnp.where(same, -pos_scale * log2e, neg_scale * log2e)
             shift = jnp.where(same, pos_scale * margin * log2e, neg_shift)
-            term = jnp.exp2(scores_refs[at % 2][part, piece : piece + lanes] * slope + shift)
+            scores = scores_refs[at % 2][part, piece : piece + lanes]
+            term = jnp.exp2(scores * slope + shift)
             pos = jnp.where(same, term, 0.0)
             neg = jnp.where(same, 0.0, term)
             pos_sum += pos
             neg_sum += neg
+            push_along += neg * scores
+            pull_along += pos * scores
             to = slice(at % 2 * unit + piece, at % 2 * unit + piece + lanes)
             weights_ref[part, to] = neg.astype(bf16)
             weights_ref[rows + which * quarter : rows + (which + 1) * quarter, to] = pos.astype(bf16)
-        pos_ref[part, :] = pos_sum
-        neg_ref[part, :] = neg_sum
+        for ref, value in zip(sum_refs, (pos_sum, neg_sum, push_along, pull_along)):
+            ref[part, :] = value
 
     def weigh_half(pair, half):
         side, first = units[2 * pair]
@@ -296,24 +299,17 @@
         if at >= 2:
             weigh_half(at // 2 - 1, at % 2)
         term_unit(at, 3)
-    weigh_half(len(units) // 2 - 1, 0)
-    weigh_half(len(units) // 2 - 1, 1)
-    total = total_ref[...]
-    pos_sum = jnp.sum(pos_ref[...], axis=1, keepdims=True)
-    neg_sum = jnp.sum(neg_ref[...], axis=1, keepdims=True)
+    sums = [jnp.sum(ref[...], axis=1, keepdims=True) for ref in sum_refs]
     floats = anchors.astype(f32)
-    sums = [pos_sum, neg_sum]
-    for which in range(2):
-        value = total[which * rows : (which + 1) * rows, :]
-        along = jnp.sum(value * floats, axis=1, keepdims=True)
-        sums.append(along)
-        rest = value - along * floats
-        for block, ref in enumerate(out_refs):
-            for at in range(parts):
+    for half in range(2):
+        weigh_half(len(units) // 2 - 1, half)
+        for which in range(2):
+            for at in range(half * parts // 2, (half + 1) * parts // 2):
+                columns = slice(at * lanes, (at + 1) * lanes)
+                rest = total_ref[which * rows : (which + 1) * rows, columns] - sums[2 + which] * floats[:, columns]
                 first = (which * parts + at) * size
-                ref[first : first + size, :] = rest[
-                    block * size : (block + 1) * size, at * lanes : (at + 1) * lanes
-                ].astype(ref.dtype)
+                for block, ref in enumerate(out_refs):
+                    ref[first : first + size, :] = rest[block * size : (block + 1) * size, :].astype(ref.dtype)
     for block, ref in enumerate(out_refs):
         lines = []
         for first in range(0, size, lanes):
@@ -338,7 +334,7 @@
     anywhere = pl.BlockSpec(memory_space=pl.ANY)
     vmem = pl.BlockSpec(memory_space=pltpu.VMEM)
     return call(
-        functools.partial(block_kernel, len(blocks), len(keys), unit, count, len(copied), 9 + len(copied)),
+        functools.partial(block_kernel, len(blocks), len(keys), unit, count, len(copied), 11 + len(copied)),
         [shaped((2 * parts * size + sum_rows(size), lanes), dtype)] * len(blocks)
         + [shaped(value.shape, value.dtype) for value in copied],
         *blocks, *[in_vmem(k) for k in keys], *labels, *copied, *after,
@@ -349,6 +345,8 @@
             pltpu.VMEM((rows, width), bf16),
             pltpu.VMEM((rows, lanes), f32),
             pltpu.VMEM((2 * rows, width), f32),
+            pltpu.VMEM((rows, lanes), f32),
+            pltpu.VMEM((rows, lanes), f32),
             pltpu.VMEM((rows, lanes), f32),
             pltpu.VMEM((rows, lanes), f32),
             pltpu.VMEM((rows, unit), f32),
@@ -480,8 +478,7 @@
     choices = [moved] + [exchange(moved, "core", s) for s in range(1, cores)]
 
     sums, *others = add(held, arrived, size, count, 2 * parts, choices)
-    order = sorted(range(1, line), key=lambda step: (step != line // 2, -step))
-    arrived = [exchange(others[line - 1 - step], "line", step) for step in order]
+    arrived = [exchange(value, "line", line - at) for at, value in enumerate(others, 1)]
     grad_batch, loss = call(
         functools.partial(finish_kernel, len(arrived)),
         [shaped((count, width), f32), shaped((1, count), f32)],

time: 45.2 us -> 45.2 us (level)
  waiting for transfers between devices: 9.26 us -> 7.84 us
  starting transfers between devices: 17 us -> 17.9 us
  Pallas kernels: 17.3 us -> 17.8 us
    ppermute x9, waiting for transfers between devices: 6.43 us -> 5.08 us  [exchange(): return lax.ppermute(value, 'dev', [(i, i ^ jump) for i in range(members)])]
    ppermute x9, starting transfers between devices: 9.82 us -> 10.7 us  [exchange(): return lax.ppermute(value, 'dev', [(i, i ^ jump) for i in range(members)])]
    pallas_call x13, Pallas kernels: 17.3 us -> 17.8 us  [call(): pl.pallas_call(body, out_shape=outs, compiler_params=pltpu.CompilerParams...]
  transfers between devices with their start and end apart: 15 -> 15, of which waited for: 7 -> 7; matrix products, arithmetic and copies ran while one was open for 0% -> 0% of each run, Pallas kernels for 34% -> 35%
where the time goes in v14:
time: 45.2 us; the launch traced here: 45 us
  starting transfers between devices  17.9 us (40%)
  Pallas kernels  17.8 us (39%)
  waiting for transfers between devices  7.84 us (17%)
  between operations  1.41 us (3%)
    pallas_call x13, Pallas kernels, call(): pl.pallas_call(body, out_shape=outs, compiler_params=pltpu.CompilerParams...  17.8 us
    ppermute x9, starting transfers between devices, exchange(): return lax.ppermute(value, 'dev', [(i, i ^ jump) for i in range(members)])  10.7 us
    ppermute x6, starting transfers between devices, exchange(): return lax.ppermute(value, 'grp', [(i, i ^ step) for i in range(groups)])  7.17 us
    ppermute x9, waiting for transfers between devices, exchange(): return lax.ppermute(value, 'dev', [(i, i ^ jump) for i in range(members)])  5.08 us
    ppermute x6, waiting for transfers between devices, exchange(): return lax.ppermute(value, 'grp', [(i, i ^ step) for i in range(groups)])  2.75 us
  transfers between devices with their start and end apart: 15, of which 7 were waited for; matrix products, arithmetic and copies ran while one was open for 0% of the time, Pallas kernels for 35%

profile of v14, /device:TPU:0, one launch (start us, length us, event | category | flops | bytes accessed | tf_op | source)
XLA Modules:
  0.0 45.0 jit_solution(4004790843074689727)
XLA Ops:
  0.6 0.9 %shard_map.93 = (bf16[144,128]{1,0:T(8,128)(2,1)S(1)}, f32[32,512]{1,0:T(8,128)S(1)}, f32[32,128]{1,0:T(8,128)S(1)}, s32[16,128]{1,0:T(8,128)S(1)}, s32[16,128]{1,0:T(8,128)S(1)}) custom-call(bf16[32,512]{1,0:T(8,128)(2,1)} %rows_ref.1, s32[1,32]{1,0:T(1,128)} %bitcast.15, s32[16,128]{1,0:T(8,128)} %bitcast.13, s32[16,128]{1,0:T(8,128)} %bitcast.14), custom_call_target="tpu_custom_call" | custom-call | tf_op jit(solution)/shard_map/pallas_call | solution.py:23
  1.5 5.1 %collective-permute-start = (bf16[144,128]{1,0:T(8,128)(2,1)S(1)}, bf16[144,128]{1,0:T(8,128)(2,1)S(1)}, u32[]{:S(2)}, u32[]{:S(2)}) collective-permute-start(bf16[144,128]{1,0:T(8,128)(2,1)S(1)} %get-tuple-element.21.refs_0_), channel_id=1, source_target_pairs={{0,6},{1,7},{2,4},{3,5},{4,2},{5,3},{6,0},{7,1},{8,14},{9,15},{10,... | collective-permute-start | bytes 110600 | tf_op jit(solution)/shard_map/ppermute | solution.py:438
  6.6 0.0 collective-permute-start.1
  6.6 0.6 %collective-permute-start.2 = (bf16[144,128]{1,0:T(8,128)(2,1)S(1)}, bf16[144,128]{1,0:T(8,128)(2,1)S(1)}, u32[]{:S(2)}, u32[]{:S(2)}) collective-permute-start(bf16[144,128]{1,0:T(8,128)(2,1)S(1)} %get-tuple-element.21.refs_0_), channel_id=1, source_target_pairs={{0,2},{1,3},{2,0},{3,1},{4,6},{5,7},{6,4},{7,5},{8,10},{9,11},{10,... | collective-permute-start | bytes 110600 | tf_op jit(solution)/shard_map/ppermute | solution.py:438
  7.3 0.0 collective-permute-start.3
  7.3 0.5 %collective-permute-start.4 = (bf16[2048,512]{1,0:T(8,128)(2,1)}, bf16[2048,512]{1,0:T(8,128)(2,1)S(1)}, u32[]{:S(2)}, u32[]{:S(2)}) collective-permute-start(bf16[2048,512]{1,0:T(8,128)(2,1)} %refs_5_.1), channel_id=1, source_target_pairs={{0,1},{1,0},{2,3},{3,2},{4,5},{5,4},{6,7},{7,6},{8,9},{9,8},{10,11... | collective-permute-start | bytes 6291464 | tf_op jit(solution)/shard_map/ppermute | solution.py:438
  8.4 0.1 collective-permute-done.refs_1_
  8.6 2.9 %collective-permute-done.1.refs_1_ = bf16[144,128]{1,0:T(8,128)(2,1)S(1)} collective-permute-done((bf16[144,128]{1,0:T(8,128)(2,1)S(1)}, bf16[144,128]{1,0:T(8,128)(2,1)S(1)}, u32[]{:S(2)}, u32[]{:S(2)}) %collective-permute-start.1) | collective-permute-done | bytes 36896 | tf_op jit(solution)/shard_map/ppermute | solution.py:438
  11.5 0.0 collective-permute-done.3.refs_3_
  11.5 2.5 %collective-permute-start.7 = (bf16[576,128]{1,0:T(8,128)(2,1)S(1)}, bf16[576,128]{1,0:T(8,128)(2,1)S(1)}, u32[]{:S(2)}, u32[]{:S(2)}) collective-permute-start(bf16[576,128]{1,0:T(8,128)(2,1)S(1)} %shard_map.96.refs_0_), channel_id=1, source_target_pairs={{0,24},{8,16},{16,8},{24,0},{1,25},{9,17},{17,9},{25,1},{2,26},{10... | collective-permute-start | bytes 442376 | tf_op jit(solution)/shard_map/ppermute | solution.py:436
  14.1 0.5 %collective-permute-start.5 = (bf16[576,128]{1,0:T(8,128)(2,1)S(1)}, bf16[576,128]{1,0:T(8,128)(2,1)S(1)}, u32[]{:S(2)}, u32[]{:S(2)}) collective-permute-start(bf16[576,128]{1,0:T(8,128)(2,1)S(1)} %shard_map.96.refs_0_), channel_id=1, source_target_pairs={{0,16},{8,24},{16,0},{24,8},{1,17},{9,25},{17,1},{25,9},{2,18},{10... | collective-permute-start | bytes 442376 | tf_op jit(solution)/shard_map/ppermute | solution.py:436
  14.6 0.5 %collective-permute-start.6 = (bf16[576,128]{1,0:T(8,128)(2,1)S(1)}, bf16[576,128]{1,0:T(8,128)(2,1)S(1)}, u32[]{:S(2)}, u32[]{:S(2)}) collective-permute-start(bf16[576,128]{1,0:T(8,128)(2,1)S(1)} %shard_map.96.refs_0_), channel_id=1, source_target_pairs={{0,8},{8,0},{16,24},{24,16},{1,9},{9,1},{17,25},{25,17},{2,10},{10... | collective-permute-start | bytes 442376 | tf_op jit(solution)/shard_map/ppermute | solution.py:436
  15.1 2.9 %shard_map.97.refs_1_.refs_2_ = bf16[2048,512]{1,0:T(8,128)(2,1)S(1)} custom-call(bf16[2048,512]{1,0:T(8,128)(2,1)} %refs_5_.1, bf16[576,128]{1,0:T(8,128)(2,1)S(1)} %shard_map.96.refs_0_), custom_call_target="tpu_custom_call" | custom-call | flops 34359738368 | tf_op jit(solution)/shard_map/pallas_call | solution.py:23
  18.0 1.0 %shard_map.98.refs_2_.refs_3_ = bf16[2048,512]{1,0:T(8,128)(2,1)S(1)} custom-call(bf16[2048,512]{1,0:T(8,128)(2,1)S(1)} %collective-permute-done.4.memory_ref, bf16[576,128]{1,0:T(8,128)(2,1)S(1)} %shard_map.96.refs_0_), custom_call_target="tpu_custom_call" | custom-call | flops 34359738368 | tf_op jit(solution)/shard_map/pallas_call | solution.py:23
  19.0 0.3 collective-permute-done.7.refs_0_.refs_3_
  19.2 3.1 %shard_map.99.refs_6_ = bf16[1040,128]{1,0:T(8,128)(2,1)S(1)} custom-call(bf16[576,128]{1,0:T(8,128)(2,1)S(1)} %collective-permute-done.7.refs_0_.refs_3_, bf16[2048,512]{1,0:T(8,128)(2,1)S(1)} %shard_map.97.refs_1_.refs_2_, bf16[2048,512]{1,0:T(8,128)(2,1)S(1)} %shard_map.98.refs_2_.refs_3_, s32[1,2048]{1,0:T(1,128)S(1)} %bitcast.7, s32[1,2048]{1,0:T(1,128)S(1)} %bitcast.10), custom_call_target="tpu_custom_call" | custom-call | flops 3221225472 | tf_op jit(solution)/shard_map/pallas_call | solution.py:23
  22.4 0.0 copy-start
  22.4 2.3 %collective-permute-start.8 = (bf16[1040,128]{1,0:T(8,128)(2,1)S(1)}, bf16[1040,128]{1,0:T(8,128)(2,1)S(1)}, u32[]{:S(2)}, u32[]{:S(2)}) collective-permute-start(bf16[1040,128]{1,0:T(8,128)(2,1)S(1)} %shard_map.99.refs_6_), channel_id=1, source_target_pairs={{0,24},{8,16},{16,8},{24,0},{1,25},{9,17},{17,9},{25,1},{2,26},{10... | collective-permute-start | bytes 798728 | tf_op jit(solution)/shard_map/ppermute | solution.py:436
  24.6 4.6 %shard_map.100 = (bf16[1040,128]{1,0:T(8,128)(2,1)S(1)}, bf16[1040,128]{1,0:T(8,128)(2,1)S(1)}) custom-call(bf16[576,128]{1,0:T(8,128)(2,1)S(1)} %collective-permute-done.5.refs_0_.refs_2_, bf16[576,128]{1,0:T(8,128)(2,1)S(1)} %collective-permute-done.6.refs_1_, bf16[2048,512]{1,0:T(8,128)(2,1)S(1)} %shard_map.97.refs_1_.refs_2_, ...), custom_call_target="tpu_custom_call" | custom-call | flops 6442450944 | tf_op jit(solution)/shard_map/pallas_call | solution.py:23
  29.2 0.6 %collective-permute-start.10 = (bf16[1040,128]{1,0:T(8,128)(2,1)S(1)}, bf16[1040,128]{1,0:T(8,128)(2,1)S(1)}, u32[]{:S(2)}, u32[]{:S(2)}) collective-permute-start(bf16[1040,128]{1,0:T(8,128)(2,1)S(1)} %get-tuple-element.24.refs_7_.refs_5_), channel_id=1, source_target_pairs={{0,8},{8,0},{16,24},{24,16},{1,9},{9,1},{17,25},{25,17},{2,10},{10... | collective-permute-start | bytes 798728 | tf_op jit(solution)/shard_map/ppermute | solution.py:436
  29.8 0.7 %collective-permute-start.9 = (bf16[1040,128]{1,0:T(8,128)(2,1)S(1)}, bf16[1040,128]{1,0:T(8,128)(2,1)S(1)}, u32[]{:S(2)}, u32[]{:S(2)}) collective-permute-start(bf16[1040,128]{1,0:T(8,128)(2,1)S(1)} %get-tuple-element.23.refs_6_.refs_4_), channel_id=1, source_target_pairs={{0,16},{8,24},{16,0},{24,8},{1,17},{9,25},{17,1},{25,9},{2,18},{10... | collective-permute-start | bytes 798728 | tf_op jit(solution)/shard_map/ppermute | solution.py:436
  30.6 3.1 %shard_map.101 = (f32[1040,128]{1,0:T(8,128)S(1)}, bf16[2048,512]{1,0:T(8,128)(2,1)}) custom-call(bf16[576,128]{1,0:T(8,128)(2,1)S(1)} %shard_map.96.refs_0_, bf16[2048,512]{1,0:T(8,128)(2,1)S(1)} %shard_map.97.refs_1_.refs_2_, bf16[2048,512]{1,0:T(8,128)(2,1)S(1)} %shard_map.98.refs_2_.refs_3_, s32[1,2048]{1,0:T(1,128)S(1)} %bitcast.9, ...), custom_call_target="tpu_custom_call" | custom-call | flops 3221225472 | tf_op jit(solution)/shard_map/pallas_call | solution.py:23
  33.8 2.0 %collective-permute-done.10.refs_3_ = bf16[1040,128]{1,0:T(8,128)(2,1)S(1)} collective-permute-done((bf16[1040,128]{1,0:T(8,128)(2,1)S(1)}, bf16[1040,128]{1,0:T(8,128)(2,1)S(1)}, u32[]{:S(2)}, u32[]{:S(2)}) %collective-permute-start.10) | collective-permute-done | bytes 266272 | tf_op jit(solution)/shard_map/ppermute | solution.py:436
  35.7 0.5 %collective-permute-done.9.refs_2_ = bf16[1040,128]{1,0:T(8,128)(2,1)S(1)} collective-permute-done((bf16[1040,128]{1,0:T(8,128)(2,1)S(1)}, bf16[1040,128]{1,0:T(8,128)(2,1)S(1)}, u32[]{:S(2)}, u32[]{:S(2)}) %collective-permute-start.9) | collective-permute-done | bytes 266272 | tf_op jit(solution)/shard_map/ppermute | solution.py:436
  36.3 0.1 shard_map.103
  36.4 1.8 %collective-permute-start.12 = (bf16[272,128]{1,0:T(8,128)(2,1)S(1)}, bf16[272,128]{1,0:T(8,128)(2,1)S(1)}, u32[]{:S(2)}, u32[]{:S(2)}) collective-permute-start(bf16[272,128]{1,0:T(8,128)(2,1)S(1)} %get-tuple-element.27), channel_id=1, source_target_pairs={{0,6},{1,7},{2,4},{3,5},{4,2},{5,3},{6,0},{7,1},{8,14},{9,15},{10,... | collective-permute-start | bytes 208904 | tf_op jit(solution)/shard_map/ppermute | solution.py:438
  38.2 0.4 collective-permute-start.13
  38.5 2.3 %collective-permute-start.14 = (bf16[272,128]{1,0:T(8,128)(2,1)S(1)}, bf16[272,128]{1,0:T(8,128)(2,1)S(1)}, u32[]{:S(2)}, u32[]{:S(2)}) collective-permute-start(bf16[272,128]{1,0:T(8,128)(2,1)S(1)} %get-tuple-element.29), channel_id=1, source_target_pairs={{0,2},{1,3},{2,0},{3,1},{4,6},{5,7},{6,4},{7,5},{8,10},{9,11},{10,... | collective-permute-start | bytes 208904 | tf_op jit(solution)/shard_map/ppermute | solution.py:438
  40.9 1.2 %shard_map.105 = (bf16[2048,512]{1,0:T(8,128)(2,1)}, s32[16,128]{1,0:T(8,128)}) custom-call(s32[1]{0:T(128)S(6)} %copy.12.step_ref, bf16[2048,512]{1,0:T(8,128)(2,1)} %get-tuple-element.34.stored_ref, s32[16,128]{1,0:T(8,128)S(1)} %get-tuple-element.35.labels_ref, bf16[144,128]{1,0:T(8,128)(2,1)S(1)} %shard_map.102.refs_4_.refs_0_, ...), custom_call_target="tpu_custom_call", output_to_operand_aliasing={{0}: (1, {})} | custom-call | tf_op jit(solution)/shard_map/pallas_call | solution.py:23
  42.1 0.6 %collective-permute-done.12.refs_1_ = bf16[272,128]{1,0:T(8,128)(2,1)S(1)} collective-permute-done((bf16[272,128]{1,0:T(8,128)(2,1)S(1)}, bf16[272,128]{1,0:T(8,128)(2,1)S(1)}, u32[]{:S(2)}, u32[]{:S(2)}) %collective-permute-start.12) | collective-permute-done | bytes 69664 | tf_op jit(solution)/shard_map/ppermute | solution.py:438
  42.6 1.5 %collective-permute-done.13.refs_2_ = bf16[272,128]{1,0:T(8,128)(2,1)S(1)} collective-permute-done((bf16[272,128]{1,0:T(8,128)(2,1)S(1)}, bf16[272,128]{1,0:T(8,128)(2,1)S(1)}, u32[]{:S(2)}, u32[]{:S(2)}) %collective-permute-start.13) | collective-permute-done | bytes 69664 | tf_op jit(solution)/shard_map/ppermute | solution.py:438
  44.1 0.9 %shard_map.104 = (f32[32,512]{1,0:T(8,128)}, f32[1,32]{1,0:T(1,128)}) custom-call(f32[272,128]{1,0:T(8,128)S(1)} %get-tuple-element.26.refs_0_, bf16[272,128]{1,0:T(8,128)(2,1)S(1)} %collective-permute-done.12.refs_1_, bf16[272,128]{1,0:T(8,128)(2,1)S(1)} %collective-permute-done.13.refs_2_, bf16[272,128]{1,0:T(8,128)(2,1)S(1)} %collective-permute-done.14.refs_3_, ...), custom_call_target="tpu_custom_call" | custom-call | tf_op jit(solution)/shard_map/pallas_call | solution.py:23
  (13 shorter events, 0.1 us)
Async XLA Ops:
  1.5 7.1 %collective-permute-start = (bf16[144,128]{1,0:T(8,128)(2,1)S(1)}, bf16[144,128]{1,0:T(8,128)(2,1)S(1)}, u32[]{:S(2)}, u32[]{:S(2)}) collective-permute-start(bf16[144,128]{1,0:T(8,128)(2,1)S(1)} %get-tuple-element.21.refs_0_), channel_id=1, source_target_pairs={{0,6},{1,7},{2,4},{3,5},{4,2},{5,3},{6,0},{7,1},{8,14},{9,15},{10,... | collective-permute-start | bytes 110600 | tf_op jit(solution)/shard_map/ppermute | solution.py:438
  6.6 4.9 %collective-permute-start.1 = (bf16[144,128]{1,0:T(8,128)(2,1)S(1)}, bf16[144,128]{1,0:T(8,128)(2,1)S(1)}, u32[]{:S(2)}, u32[]{:S(2)}) collective-permute-start(bf16[144,128]{1,0:T(8,128)(2,1)S(1)} %get-tuple-element.21.refs_0_), channel_id=1, source_target_pairs={{0,4},{1,5},{2,6},{3,7},{4,0},{5,1},{6,2},{7,3},{8,12},{9,13},{10,... | collective-permute-start | bytes 110600 | tf_op jit(solution)/shard_map/ppermute | solution.py:438
  6.6 4.9 %collective-permute-start.2 = (bf16[144,128]{1,0:T(8,128)(2,1)S(1)}, bf16[144,128]{1,0:T(8,128)(2,1)S(1)}, u32[]{:S(2)}, u32[]{:S(2)}) collective-permute-start(bf16[144,128]{1,0:T(8,128)(2,1)S(1)} %get-tuple-element.21.refs_0_), channel_id=1, source_target_pairs={{0,2},{1,3},{2,0},{3,1},{4,6},{5,7},{6,4},{7,5},{8,10},{9,11},{10,... | collective-permute-start | bytes 110600 | tf_op jit(solution)/shard_map/ppermute | solution.py:438
  7.3 4.2 %collective-permute-start.3 = (s32[16,128]{1,0:T(8,128)S(1)}, s32[16,128]{1,0:T(8,128)S(1)}, u32[]{:S(2)}, u32[]{:S(2)}) collective-permute-start(s32[16,128]{1,0:T(8,128)S(1)} %get-tuple-element.22.refs_2_), channel_id=1, source_target_pairs={{0,1},{1,0},{2,3},{3,2},{4,5},{5,4},{6,7},{7,6},{8,9},{9,8},{10,11... | collective-permute-start | bytes 24584 | tf_op jit(solution)/shard_map/ppermute | solution.py:438
  7.3 10.7 %collective-permute-start.4 = (bf16[2048,512]{1,0:T(8,128)(2,1)}, bf16[2048,512]{1,0:T(8,128)(2,1)S(1)}, u32[]{:S(2)}, u32[]{:S(2)}) collective-permute-start(bf16[2048,512]{1,0:T(8,128)(2,1)} %refs_5_.1), channel_id=1, source_target_pairs={{0,1},{1,0},{2,3},{3,2},{4,5},{5,4},{6,7},{7,6},{8,9},{9,8},{10,11... | collective-permute-start | bytes 6291464 | tf_op jit(solution)/shard_map/ppermute | solution.py:438
  11.5 7.7 %collective-permute-start.7 = (bf16[576,128]{1,0:T(8,128)(2,1)S(1)}, bf16[576,128]{1,0:T(8,128)(2,1)S(1)}, u32[]{:S(2)}, u32[]{:S(2)}) collective-permute-start(bf16[576,128]{1,0:T(8,128)(2,1)S(1)} %shard_map.96.refs_0_), channel_id=1, source_target_pairs={{0,24},{8,16},{16,8},{24,0},{1,25},{9,17},{17,9},{25,1},{2,26},{10... | collective-permute-start | bytes 442376 | tf_op jit(solution)/shard_map/ppermute | solution.py:436
  14.1 10.6 %collective-permute-start.5 = (bf16[576,128]{1,0:T(8,128)(2,1)S(1)}, bf16[576,128]{1,0:T(8,128)(2,1)S(1)}, u32[]{:S(2)}, u32[]{:S(2)}) collective-permute-start(bf16[576,128]{1,0:T(8,128)(2,1)S(1)} %shard_map.96.refs_0_), channel_id=1, source_target_pairs={{0,16},{8,24},{16,0},{24,8},{1,17},{9,25},{17,1},{25,9},{2,18},{10... | collective-permute-start | bytes 442376 | tf_op jit(solution)/shard_map/ppermute | solution.py:436
  14.6 10.1 %collective-permute-start.6 = (bf16[576,128]{1,0:T(8,128)(2,1)S(1)}, bf16[576,128]{1,0:T(8,128)(2,1)S(1)}, u32[]{:S(2)}, u32[]{:S(2)}) collective-permute-start(bf16[576,128]{1,0:T(8,128)(2,1)S(1)} %shard_map.96.refs_0_), channel_id=1, source_target_pairs={{0,8},{8,0},{16,24},{24,16},{1,9},{9,1},{17,25},{25,17},{2,10},{10... | collective-permute-start | bytes 442376 | tf_op jit(solution)/shard_map/ppermute | solution.py:436
  22.4 8.2 %copy-start = (bf16[2048,512]{1,0:T(8,128)(2,1)S(1)}, bf16[2048,512]{1,0:T(8,128)(2,1)}, u32[]{:S(2)}) copy-start(bf16[2048,512]{1,0:T(8,128)(2,1)} %refs_5_.1) | copy-start | bytes 6291460
  22.4 13.9 %collective-permute-start.8 = (bf16[1040,128]{1,0:T(8,128)(2,1)S(1)}, bf16[1040,128]{1,0:T(8,128)(2,1)S(1)}, u32[]{:S(2)}, u32[]{:S(2)}) collective-permute-start(bf16[1040,128]{1,0:T(8,128)(2,1)S(1)} %shard_map.99.refs_6_), channel_id=1, source_target_pairs={{0,24},{8,16},{16,8},{24,0},{1,25},{9,17},{17,9},{25,1},{2,26},{10... | collective-permute-start | bytes 798728 | tf_op jit(solution)/shard_map/ppermute | solution.py:436
  29.2 6.5 %collective-permute-start.10 = (bf16[1040,128]{1,0:T(8,128)(2,1)S(1)}, bf16[1040,128]{1,0:T(8,128)(2,1)S(1)}, u32[]{:S(2)}, u32[]{:S(2)}) collective-permute-start(bf16[1040,128]{1,0:T(8,128)(2,1)S(1)} %get-tuple-element.24.refs_7_.refs_5_), channel_id=1, source_target_pairs={{0,8},{8,0},{16,24},{24,16},{1,9},{9,1},{17,25},{25,17},{2,10},{10... | collective-permute-start | bytes 798728 | tf_op jit(solution)/shard_map/ppermute | solution.py:436
  29.8 6.4 %collective-permute-start.9 = (bf16[1040,128]{1,0:T(8,128)(2,1)S(1)}, bf16[1040,128]{1,0:T(8,128)(2,1)S(1)}, u32[]{:S(2)}, u32[]{:S(2)}) collective-permute-start(bf16[1040,128]{1,0:T(8,128)(2,1)S(1)} %get-tuple-element.23.refs_6_.refs_4_), channel_id=1, source_target_pairs={{0,16},{8,24},{16,0},{24,8},{1,17},{9,25},{17,1},{25,9},{2,18},{10... | collective-permute-start | bytes 798728 | tf_op jit(solution)/shard_map/ppermute | solution.py:436
  30.6 3.2 %collective-permute-start.11 = (bf16[144,128]{1,0:T(8,128)(2,1)S(1)}, bf16[144,128]{1,0:T(8,128)(2,1)S(1)}, u32[]{:S(2)}, u32[]{:S(2)}) collective-permute-start(bf16[144,128]{1,0:T(8,128)(2,1)S(1)} %shard_map.102.refs_4_.refs_0_), channel_id=1, source_target_pairs={{0,1},{1,0},{2,3},{3,2},{4,5},{5,4},{6,7},{7,6},{8,9},{9,8},{10,11... | collective-permute-start | bytes 110600 | tf_op jit(solution)/shard_map/ppermute | solution.py:438
  36.4 6.2 %collective-permute-start.12 = (bf16[272,128]{1,0:T(8,128)(2,1)S(1)}, bf16[272,128]{1,0:T(8,128)(2,1)S(1)}, u32[]{:S(2)}, u32[]{:S(2)}) collective-permute-start(bf16[272,128]{1,0:T(8,128)(2,1)S(1)} %get-tuple-element.27), channel_id=1, source_target_pairs={{0,6},{1,7},{2,4},{3,5},{4,2},{5,3},{6,0},{7,1},{8,14},{9,15},{10,... | collective-permute-start | bytes 208904 | tf_op jit(solution)/shard_map/ppermute | solution.py:438
  38.2 6.0 %collective-permute-start.13 = (bf16[272,128]{1,0:T(8,128)(2,1)S(1)}, bf16[272,128]{1,0:T(8,128)(2,1)S(1)}, u32[]{:S(2)}, u32[]{:S(2)}) collective-permute-start(bf16[272,128]{1,0:T(8,128)(2,1)S(1)} %get-tuple-element.28), channel_id=1, source_target_pairs={{0,4},{1,5},{2,6},{3,7},{4,0},{5,1},{6,2},{7,3},{8,12},{9,13},{10,... | collective-permute-start | bytes 208904 | tf_op jit(solution)/shard_map/ppermute | solution.py:438
  38.5 5.6 %collective-permute-start.14 = (bf16[272,128]{1,0:T(8,128)(2,1)S(1)}, bf16[272,128]{1,0:T(8,128)(2,1)S(1)}, u32[]{:S(2)}, u32[]{:S(2)}) collective-permute-start(bf16[272,128]{1,0:T(8,128)(2,1)S(1)} %get-tuple-element.29), channel_id=1, source_target_pairs={{0,2},{1,3},{2,0},{3,1},{4,6},{5,7},{6,4},{7,5},{8,10},{9,11},{10,... | collective-permute-start | bytes 208904 | tf_op jit(solution)/shard_map/ppermute | solution.py:438

commit v15 on v13

--- a/solution.py
+++ b/solution.py
@@ -223,7 +223,7 @@
     rows_refs, keys_refs = refs[:blocks], refs[blocks : blocks + sides]
     label_refs = refs[blocks + sides : blocks + 2 * sides]
     out_refs = refs[-scratch - blocks : -scratch]
-    anchors_ref, labels_ref, total_ref, pos_ref, neg_ref = refs[-scratch:-4]
+    anchors_ref, labels_ref, total_ref, pos_ref, neg_ref, wanted_ref, bias_ref = refs[-scratch:-4]
     scores_refs, weight_refs = refs[-4:-2], refs[-2:]
     slots, width = keys_refs[0].shape
     parts = blocks_of(width)
@@ -247,7 +247,11 @@
     neg_ref[...] = jnp.zeros_like(neg_ref)
     anchors = anchors_ref[...]
     units = [(side, at) for side in range(sides) for at in range(0, slots, unit)]
-    quarter = rows // 4
+    some = min(64, rows)
+    for side in range(sides):
+        slot_labels = label_refs[side][...].astype(f32)
+        wanted_ref[side : side + 1, :] = slot_labels
+        bias_ref[side : side + 1, :] = jnp.where(slot_labels < 0.0, -1e30, 0.0)
 
     def score_unit(at):
         side, first = units[at]
@@ -257,24 +261,23 @@
 
     def term_unit(at, which):
         side, first = units[at]
-        part = slice(which * quarter, (which + 1) * quarter)
+        part = slice(which * some, (which + 1) * some)
         weights_ref = weight_refs[at // 2 % 2]
         wanted = labels_ref[part, :]
         pos_sum, neg_sum = pos_ref[part, :], neg_ref[part, :]
         for piece in range(0, unit, lanes):
-            slot_labels = label_refs[side][:, first + piece : first + piece + lanes].astype(f32)
-            neg_shift = jnp.where(slot_labels < 0.0, -1e30, -neg_scale * margin * log2e)
-            same = wanted == slot_labels
+            columns = slice(first + piece, first + piece + lanes)
+            same = wanted == wanted_ref[side : side + 1, columns]
             slope = jnp.where(same, -pos_scale * log2e, neg_scale * log2e)
-            shift = jnp.where(same, pos_scale * margin * log2e, neg_shift)
-            term = jnp.exp2(scores_refs[at % 2][part, piece : piece + lanes] * slope + shift)
+            scores = scores_refs[at % 2][part, piece : piece + lanes]
+            term = jnp.exp2(scores * slope + bias_ref[side : side + 1, columns])
             pos = jnp.where(same, term, 0.0)
             neg = jnp.where(same, 0.0, term)
             pos_sum += pos
             neg_sum += neg
             to = slice(at % 2 * unit + piece, at % 2 * unit + piece + lanes)
             weights_ref[part, to] = neg.astype(bf16)
-            weights_ref[rows + which * quarter : rows + (which + 1) * quarter, to] = pos.astype(bf16)
+            weights_ref[rows + which * some : rows + (which + 1) * some, to] = pos.astype(bf16)
         pos_ref[part, :] = pos_sum
         neg_ref[part, :] = neg_sum
 
@@ -288,14 +291,13 @@
 
     score_unit(0)
     for at in range(len(units)):
-        term_unit(at, 0)
-        if at + 1 < len(units):
-            score_unit(at + 1)
-        term_unit(at, 1)
-        term_unit(at, 2)
-        if at >= 2:
-            weigh_half(at // 2 - 1, at % 2)
-        term_unit(at, 3)
+        groups = rows // some
+        for which in range(groups):
+            term_unit(at, which)
+            if which == 0 and at + 1 < len(units):
+                score_unit(at + 1)
+            if which == max(groups - 2, 0) and at >= 2:
+                weigh_half(at // 2 - 1, at % 2)
     weigh_half(len(units) // 2 - 1, 0)
     weigh_half(len(units) // 2 - 1, 1)
     total = total_ref[...]
@@ -338,7 +340,7 @@
     anywhere = pl.BlockSpec(memory_space=pl.ANY)
     vmem = pl.BlockSpec(memory_space=pltpu.VMEM)
     return call(
-        functools.partial(block_kernel, len(blocks), len(keys), unit, count, len(copied), 9 + len(copied)),
+        functools.partial(block_kernel, len(blocks), len(keys), unit, count, len(copied), 11 + len(copied)),
         [shaped((2 * parts * size + sum_rows(size), lanes), dtype)] * len(blocks)
         + [shaped(value.shape, value.dtype) for value in copied],
         *blocks, *[in_vmem(k) for k in keys], *labels, *copied, *after,
@@ -351,6 +353,8 @@
             pltpu.VMEM((2 * rows, width), f32),
             pltpu.VMEM((rows, lanes), f32),
             pltpu.VMEM((rows, lanes), f32),
+            pltpu.VMEM((len(keys), slots), f32),
+            pltpu.VMEM((len(keys), slots), f32),
             pltpu.VMEM((rows, unit), f32),
             pltpu.VMEM((rows, unit), f32),
             pltpu.VMEM((2 * rows, 2 * unit), bf16),
@@ -410,9 +414,12 @@
     for which in range(4):
         row = 2 * parts * count + 2 * which
         sums.append((total[row : row + 1, :] + total[row + 1 : row + 2, :])[:, :count])
-    pos, neg = sums[:2]
+    pos, neg = [row * math.exp(scale) for row, scale in zip(sums, (pos_scale * margin, -neg_scale * margin))]
     loss_ref[...] = jnp.log(1.0 + pos) / pos_scale + jnp.log(1.0 + neg) / neg_scale
-    scales = [to_column(1.0 / (1.0 + row)) for row in (neg, pos)]
+    scales = [
+        to_column(math.exp(-neg_scale * margin) / (1.0 + neg)),
+        to_column(math.exp(pos_scale * margin) / (1.0 + pos)),
+    ]
     alongs = [to_column(row) for row in sums[2:]]
     unit = unit_ref[...]
     anchors = unit.astype(bf16).astype(f32)
@@ -480,8 +487,7 @@
     choices = [moved] + [exchange(moved, "core", s) for s in range(1, cores)]
 
     sums, *others = add(held, arrived, size, count, 2 * parts, choices)
-    order = sorted(range(1, line), key=lambda step: (step != line // 2, -step))
-    arrived = [exchange(others[line - 1 - step], "line", step) for step in order]
+    arrived = [exchange(value, "line", line - at) for at, value in enumerate(others, 1)]
     grad_batch, loss = call(
         functools.partial(finish_kernel, len(arrived)),
         [shaped((count, width), f32), shaped((1, count), f32)],

time: 45.2 us -> 44.9 us (level)
  waiting for transfers between devices: 9.26 us -> 7.85 us
  starting transfers between devices: 17 us -> 17.9 us
    ppermute x9, waiting for transfers between devices: 6.43 us -> 5.08 us  [exchange(): return lax.ppermute(value, 'dev', [(i, i ^ jump) for i in range(members)])]
    ppermute x9, starting transfers between devices: 9.82 us -> 10.7 us  [exchange(): return lax.ppermute(value, 'dev', [(i, i ^ jump) for i in range(members)])]
  transfers between devices with their start and end apart: 15 -> 15, of which waited for: 7 -> 7; matrix products, arithmetic and copies ran while one was open for 0% -> 0% of each run, Pallas kernels for 34% -> 35%
where the time goes in v15:
time: 44.9 us; the launch traced here: 44.7 us
  starting transfers between devices  17.9 us (40%)
  Pallas kernels  17.5 us (39%)
  waiting for transfers between devices  7.85 us (17%)
  between operations  1.4 us (3%)
    pallas_call x13, Pallas kernels, call(): pl.pallas_call(body, out_shape=outs, compiler_params=pltpu.CompilerParams...  17.5 us
    ppermute x9, starting transfers between devices, exchange(): return lax.ppermute(value, 'dev', [(i, i ^ jump) for i in range(members)])  10.7 us
    ppermute x6, starting transfers between devices, exchange(): return lax.ppermute(value, 'grp', [(i, i ^ step) for i in range(groups)])  7.17 us
    ppermute x9, waiting for transfers between devices, exchange(): return lax.ppermute(value, 'dev', [(i, i ^ jump) for i in range(members)])  5.08 us
    ppermute x6, waiting for transfers between devices, exchange(): return lax.ppermute(value, 'grp', [(i, i ^ step) for i in range(groups)])  2.77 us
  transfers between devices with their start and end apart: 15, of which 7 were waited for; matrix products, arithmetic and copies ran while one was open for 0% of the time, Pallas kernels for 35%

profile of v15, /device:TPU:0, one launch (start us, length us, event | category | flops | bytes accessed | tf_op | source)
XLA Modules:
  0.0 44.7 jit_solution(8641291163956269158)
XLA Ops:
  0.6 0.9 %shard_map.93 = (bf16[144,128]{1,0:T(8,128)(2,1)S(1)}, f32[32,512]{1,0:T(8,128)S(1)}, f32[32,128]{1,0:T(8,128)S(1)}, s32[16,128]{1,0:T(8,128)S(1)}, s32[16,128]{1,0:T(8,128)S(1)}) custom-call(bf16[32,512]{1,0:T(8,128)(2,1)} %rows_ref.1, s32[1,32]{1,0:T(1,128)} %bitcast.15, s32[16,128]{1,0:T(8,128)} %bitcast.13, s32[16,128]{1,0:T(8,128)} %bitcast.14), custom_call_target="tpu_custom_call" | custom-call | tf_op jit(solution)/shard_map/pallas_call | solution.py:23
  1.5 5.1 %collective-permute-start = (bf16[144,128]{1,0:T(8,128)(2,1)S(1)}, bf16[144,128]{1,0:T(8,128)(2,1)S(1)}, u32[]{:S(2)}, u32[]{:S(2)}) collective-permute-start(bf16[144,128]{1,0:T(8,128)(2,1)S(1)} %get-tuple-element.21.refs_0_), channel_id=1, source_target_pairs={{0,6},{1,7},{2,4},{3,5},{4,2},{5,3},{6,0},{7,1},{8,14},{9,15},{10,... | collective-permute-start | bytes 110600 | tf_op jit(solution)/shard_map/ppermute | solution.py:447
  6.6 0.6 %collective-permute-start.2 = (bf16[144,128]{1,0:T(8,128)(2,1)S(1)}, bf16[144,128]{1,0:T(8,128)(2,1)S(1)}, u32[]{:S(2)}, u32[]{:S(2)}) collective-permute-start(bf16[144,128]{1,0:T(8,128)(2,1)S(1)} %get-tuple-element.21.refs_0_), channel_id=1, source_target_pairs={{0,2},{1,3},{2,0},{3,1},{4,6},{5,7},{6,4},{7,5},{8,10},{9,11},{10,... | collective-permute-start | bytes 110600 | tf_op jit(solution)/shard_map/ppermute | solution.py:447
  7.3 0.0 collective-permute-start.3
  7.3 0.5 %collective-permute-start.4 = (bf16[2048,512]{1,0:T(8,128)(2,1)}, bf16[2048,512]{1,0:T(8,128)(2,1)S(1)}, u32[]{:S(2)}, u32[]{:S(2)}) collective-permute-start(bf16[2048,512]{1,0:T(8,128)(2,1)} %refs_5_.1), channel_id=1, source_target_pairs={{0,1},{1,0},{2,3},{3,2},{4,5},{5,4},{6,7},{7,6},{8,9},{9,8},{10,11... | collective-permute-start | bytes 6291464 | tf_op jit(solution)/shard_map/ppermute | solution.py:447
  8.4 0.1 collective-permute-done.refs_1_
  8.6 2.9 %collective-permute-done.1.refs_1_ = bf16[144,128]{1,0:T(8,128)(2,1)S(1)} collective-permute-done((bf16[144,128]{1,0:T(8,128)(2,1)S(1)}, bf16[144,128]{1,0:T(8,128)(2,1)S(1)}, u32[]{:S(2)}, u32[]{:S(2)}) %collective-permute-start.1) | collective-permute-done | bytes 36896 | tf_op jit(solution)/shard_map/ppermute | solution.py:447
  11.5 2.5 %collective-permute-start.7 = (bf16[576,128]{1,0:T(8,128)(2,1)S(1)}, bf16[576,128]{1,0:T(8,128)(2,1)S(1)}, u32[]{:S(2)}, u32[]{:S(2)}) collective-permute-start(bf16[576,128]{1,0:T(8,128)(2,1)S(1)} %shard_map.96.refs_0_), channel_id=1, source_target_pairs={{0,24},{8,16},{16,8},{24,0},{1,25},{9,17},{17,9},{25,1},{2,26},{10... | collective-permute-start | bytes 442376 | tf_op jit(solution)/shard_map/ppermute | solution.py:445
  14.1 0.5 %collective-permute-start.5 = (bf16[576,128]{1,0:T(8,128)(2,1)S(1)}, bf16[576,128]{1,0:T(8,128)(2,1)S(1)}, u32[]{:S(2)}, u32[]{:S(2)}) collective-permute-start(bf16[576,128]{1,0:T(8,128)(2,1)S(1)} %shard_map.96.refs_0_), channel_id=1, source_target_pairs={{0,16},{8,24},{16,0},{24,8},{1,17},{9,25},{17,1},{25,9},{2,18},{10... | collective-permute-start | bytes 442376 | tf_op jit(solution)/shard_map/ppermute | solution.py:445
  14.6 0.5 %collective-permute-start.6 = (bf16[576,128]{1,0:T(8,128)(2,1)S(1)}, bf16[576,128]{1,0:T(8,128)(2,1)S(1)}, u32[]{:S(2)}, u32[]{:S(2)}) collective-permute-start(bf16[576,128]{1,0:T(8,128)(2,1)S(1)} %shard_map.96.refs_0_), channel_id=1, source_target_pairs={{0,8},{8,0},{16,24},{24,16},{1,9},{9,1},{17,25},{25,17},{2,10},{10... | collective-permute-start | bytes 442376 | tf_op jit(solution)/shard_map/ppermute | solution.py:445
  15.1 2.9 %shard_map.97.refs_1_.refs_2_ = bf16[2048,512]{1,0:T(8,128)(2,1)S(1)} custom-call(bf16[2048,512]{1,0:T(8,128)(2,1)} %refs_5_.1, bf16[576,128]{1,0:T(8,128)(2,1)S(1)} %shard_map.96.refs_0_), custom_call_target="tpu_custom_call" | custom-call | flops 34359738368 | tf_op jit(solution)/shard_map/pallas_call | solution.py:23
  18.0 1.0 %shard_map.98.refs_2_.refs_3_ = bf16[2048,512]{1,0:T(8,128)(2,1)S(1)} custom-call(bf16[2048,512]{1,0:T(8,128)(2,1)S(1)} %collective-permute-done.4.memory_ref, bf16[576,128]{1,0:T(8,128)(2,1)S(1)} %shard_map.96.refs_0_), custom_call_target="tpu_custom_call" | custom-call | flops 34359738368 | tf_op jit(solution)/shard_map/pallas_call | solution.py:23
  19.0 0.3 collective-permute-done.7.refs_0_.refs_3_
  19.2 3.1 %shard_map.99.refs_6_ = bf16[1040,128]{1,0:T(8,128)(2,1)S(1)} custom-call(bf16[576,128]{1,0:T(8,128)(2,1)S(1)} %collective-permute-done.7.refs_0_.refs_3_, bf16[2048,512]{1,0:T(8,128)(2,1)S(1)} %shard_map.97.refs_1_.refs_2_, bf16[2048,512]{1,0:T(8,128)(2,1)S(1)} %shard_map.98.refs_2_.refs_3_, s32[1,2048]{1,0:T(1,128)S(1)} %bitcast.7, s32[1,2048]{1,0:T(1,128)S(1)} %bitcast.10), custom_call_target="tpu_custom_call" | custom-call | flops 3221225472 | tf_op jit(solution)/shard_map/pallas_call | solution.py:23
  22.3 0.0 copy-start
  22.3 2.3 %collective-permute-start.8 = (bf16[1040,128]{1,0:T(8,128)(2,1)S(1)}, bf16[1040,128]{1,0:T(8,128)(2,1)S(1)}, u32[]{:S(2)}, u32[]{:S(2)}) collective-permute-start(bf16[1040,128]{1,0:T(8,128)(2,1)S(1)} %shard_map.99.refs_6_), channel_id=1, source_target_pairs={{0,24},{8,16},{16,8},{24,0},{1,25},{9,17},{17,9},{25,1},{2,26},{10... | collective-permute-start | bytes 798728 | tf_op jit(solution)/shard_map/ppermute | solution.py:445
  24.6 0.0 collective-permute-done.5.refs_0_.refs_2_
  24.6 0.0 collective-permute-done.6.refs_1_
  24.6 4.3 %shard_map.100 = (bf16[1040,128]{1,0:T(8,128)(2,1)S(1)}, bf16[1040,128]{1,0:T(8,128)(2,1)S(1)}) custom-call(bf16[576,128]{1,0:T(8,128)(2,1)S(1)} %collective-permute-done.5.refs_0_.refs_2_, bf16[576,128]{1,0:T(8,128)(2,1)S(1)} %collective-permute-done.6.refs_1_, bf16[2048,512]{1,0:T(8,128)(2,1)S(1)} %shard_map.97.refs_1_.refs_2_, ...), custom_call_target="tpu_custom_call" | custom-call | flops 6442450944 | tf_op jit(solution)/shard_map/pallas_call | solution.py:23
  28.9 0.6 %collective-permute-start.10 = (bf16[1040,128]{1,0:T(8,128)(2,1)S(1)}, bf16[1040,128]{1,0:T(8,128)(2,1)S(1)}, u32[]{:S(2)}, u32[]{:S(2)}) collective-permute-start(bf16[1040,128]{1,0:T(8,128)(2,1)S(1)} %get-tuple-element.24.refs_7_.refs_5_), channel_id=1, source_target_pairs={{0,8},{8,0},{16,24},{24,16},{1,9},{9,1},{17,25},{25,17},{2,10},{10... | collective-permute-start | bytes 798728 | tf_op jit(solution)/shard_map/ppermute | solution.py:445
  29.5 0.7 %collective-permute-start.9 = (bf16[1040,128]{1,0:T(8,128)(2,1)S(1)}, bf16[1040,128]{1,0:T(8,128)(2,1)S(1)}, u32[]{:S(2)}, u32[]{:S(2)}) collective-permute-start(bf16[1040,128]{1,0:T(8,128)(2,1)S(1)} %get-tuple-element.23.refs_6_.refs_4_), channel_id=1, source_target_pairs={{0,16},{8,24},{16,0},{24,8},{1,17},{9,25},{17,1},{25,9},{2,18},{10... | collective-permute-start | bytes 798728 | tf_op jit(solution)/shard_map/ppermute | solution.py:445
  30.3 3.1 %shard_map.101 = (f32[1040,128]{1,0:T(8,128)S(1)}, bf16[2048,512]{1,0:T(8,128)(2,1)}) custom-call(bf16[576,128]{1,0:T(8,128)(2,1)S(1)} %shard_map.96.refs_0_, bf16[2048,512]{1,0:T(8,128)(2,1)S(1)} %shard_map.97.refs_1_.refs_2_, bf16[2048,512]{1,0:T(8,128)(2,1)S(1)} %shard_map.98.refs_2_.refs_3_, s32[1,2048]{1,0:T(1,128)S(1)} %bitcast.9, ...), custom_call_target="tpu_custom_call" | custom-call | flops 3221225472 | tf_op jit(solution)/shard_map/pallas_call | solution.py:23
  33.4 2.0 %collective-permute-done.10.refs_3_ = bf16[1040,128]{1,0:T(8,128)(2,1)S(1)} collective-permute-done((bf16[1040,128]{1,0:T(8,128)(2,1)S(1)}, bf16[1040,128]{1,0:T(8,128)(2,1)S(1)}, u32[]{:S(2)}, u32[]{:S(2)}) %collective-permute-start.10) | collective-permute-done | bytes 266272 | tf_op jit(solution)/shard_map/ppermute | solution.py:445
  35.4 0.5 %collective-permute-done.9.refs_2_ = bf16[1040,128]{1,0:T(8,128)(2,1)S(1)} collective-permute-done((bf16[1040,128]{1,0:T(8,128)(2,1)S(1)}, bf16[1040,128]{1,0:T(8,128)(2,1)S(1)}, u32[]{:S(2)}, u32[]{:S(2)}) %collective-permute-start.9) | collective-permute-done | bytes 266272 | tf_op jit(solution)/shard_map/ppermute | solution.py:445
  35.9 0.1 shard_map.103
  36.1 1.8 %collective-permute-start.12 = (bf16[272,128]{1,0:T(8,128)(2,1)S(1)}, bf16[272,128]{1,0:T(8,128)(2,1)S(1)}, u32[]{:S(2)}, u32[]{:S(2)}) collective-permute-start(bf16[272,128]{1,0:T(8,128)(2,1)S(1)} %get-tuple-element.27), channel_id=1, source_target_pairs={{0,6},{1,7},{2,4},{3,5},{4,2},{5,3},{6,0},{7,1},{8,14},{9,15},{10,... | collective-permute-start | bytes 208904 | tf_op jit(solution)/shard_map/ppermute | solution.py:447
  37.8 0.4 collective-permute-start.13
  38.2 2.3 %collective-permute-start.14 = (bf16[272,128]{1,0:T(8,128)(2,1)S(1)}, bf16[272,128]{1,0:T(8,128)(2,1)S(1)}, u32[]{:S(2)}, u32[]{:S(2)}) collective-permute-start(bf16[272,128]{1,0:T(8,128)(2,1)S(1)} %get-tuple-element.29), channel_id=1, source_target_pairs={{0,2},{1,3},{2,0},{3,1},{4,6},{5,7},{6,4},{7,5},{8,10},{9,11},{10,... | collective-permute-start | bytes 208904 | tf_op jit(solution)/shard_map/ppermute | solution.py:447
  40.5 1.2 %shard_map.105 = (bf16[2048,512]{1,0:T(8,128)(2,1)}, s32[16,128]{1,0:T(8,128)}) custom-call(s32[1]{0:T(128)S(6)} %copy.12.step_ref, bf16[2048,512]{1,0:T(8,128)(2,1)} %get-tuple-element.34.stored_ref, s32[16,128]{1,0:T(8,128)S(1)} %get-tuple-element.35.labels_ref, bf16[144,128]{1,0:T(8,128)(2,1)S(1)} %shard_map.102.refs_4_.refs_0_, ...), custom_call_target="tpu_custom_call", output_to_operand_aliasing={{0}: (1, {})} | custom-call | tf_op jit(solution)/shard_map/pallas_call | solution.py:23
  41.8 0.5 %collective-permute-done.12.refs_1_ = bf16[272,128]{1,0:T(8,128)(2,1)S(1)} collective-permute-done((bf16[272,128]{1,0:T(8,128)(2,1)S(1)}, bf16[272,128]{1,0:T(8,128)(2,1)S(1)}, u32[]{:S(2)}, u32[]{:S(2)}) %collective-permute-start.12) | collective-permute-done | bytes 69664 | tf_op jit(solution)/shard_map/ppermute | solution.py:447
  42.3 1.5 %collective-permute-done.13.refs_2_ = bf16[272,128]{1,0:T(8,128)(2,1)S(1)} collective-permute-done((bf16[272,128]{1,0:T(8,128)(2,1)S(1)}, bf16[272,128]{1,0:T(8,128)(2,1)S(1)}, u32[]{:S(2)}, u32[]{:S(2)}) %collective-permute-start.13) | collective-permute-done | bytes 69664 | tf_op jit(solution)/shard_map/ppermute | solution.py:447
  43.8 0.9 %shard_map.104 = (f32[32,512]{1,0:T(8,128)}, f32[1,32]{1,0:T(1,128)}) custom-call(f32[272,128]{1,0:T(8,128)S(1)} %get-tuple-element.26.refs_0_, bf16[272,128]{1,0:T(8,128)(2,1)S(1)} %collective-permute-done.12.refs_1_, bf16[272,128]{1,0:T(8,128)(2,1)S(1)} %collective-permute-done.13.refs_2_, bf16[272,128]{1,0:T(8,128)(2,1)S(1)} %collective-permute-done.14.refs_3_, ...), custom_call_target="tpu_custom_call" | custom-call | tf_op jit(solution)/shard_map/pallas_call | solution.py:23
  (13 shorter events, 0.1 us)
Async XLA Ops:
  1.5 7.1 %collective-permute-start = (bf16[144,128]{1,0:T(8,128)(2,1)S(1)}, bf16[144,128]{1,0:T(8,128)(2,1)S(1)}, u32[]{:S(2)}, u32[]{:S(2)}) collective-permute-start(bf16[144,128]{1,0:T(8,128)(2,1)S(1)} %get-tuple-element.21.refs_0_), channel_id=1, source_target_pairs={{0,6},{1,7},{2,4},{3,5},{4,2},{5,3},{6,0},{7,1},{8,14},{9,15},{10,... | collective-permute-start | bytes 110600 | tf_op jit(solution)/shard_map/ppermute | solution.py:447
  6.6 4.9 %collective-permute-start.1 = (bf16[144,128]{1,0:T(8,128)(2,1)S(1)}, bf16[144,128]{1,0:T(8,128)(2,1)S(1)}, u32[]{:S(2)}, u32[]{:S(2)}) collective-permute-start(bf16[144,128]{1,0:T(8,128)(2,1)S(1)} %get-tuple-element.21.refs_0_), channel_id=1, source_target_pairs={{0,4},{1,5},{2,6},{3,7},{4,0},{5,1},{6,2},{7,3},{8,12},{9,13},{10,... | collective-permute-start | bytes 110600 | tf_op jit(solution)/shard_map/ppermute | solution.py:447
  6.6 4.9 %collective-permute-start.2 = (bf16[144,128]{1,0:T(8,128)(2,1)S(1)}, bf16[144,128]{1,0:T(8,128)(2,1)S(1)}, u32[]{:S(2)}, u32[]{:S(2)}) collective-permute-start(bf16[144,128]{1,0:T(8,128)(2,1)S(1)} %get-tuple-element.21.refs_0_), channel_id=1, source_target_pairs={{0,2},{1,3},{2,0},{3,1},{4,6},{5,7},{6,4},{7,5},{8,10},{9,11},{10,... | collective-permute-start | bytes 110600 | tf_op jit(solution)/shard_map/ppermute | solution.py:447
  7.3 4.2 %collective-permute-start.3 = (s32[16,128]{1,0:T(8,128)S(1)}, s32[16,128]{1,0:T(8,128)S(1)}, u32[]{:S(2)}, u32[]{:S(2)}) collective-permute-start(s32[16,128]{1,0:T(8,128)S(1)} %get-tuple-element.22.refs_2_), channel_id=1, source_target_pairs={{0,1},{1,0},{2,3},{3,2},{4,5},{5,4},{6,7},{7,6},{8,9},{9,8},{10,11... | collective-permute-start | bytes 24584 | tf_op jit(solution)/shard_map/ppermute | solution.py:447
  7.3 10.7 %collective-permute-start.4 = (bf16[2048,512]{1,0:T(8,128)(2,1)}, bf16[2048,512]{1,0:T(8,128)(2,1)S(1)}, u32[]{:S(2)}, u32[]{:S(2)}) collective-permute-start(bf16[2048,512]{1,0:T(8,128)(2,1)} %refs_5_.1), channel_id=1, source_target_pairs={{0,1},{1,0},{2,3},{3,2},{4,5},{5,4},{6,7},{7,6},{8,9},{9,8},{10,11... | collective-permute-start | bytes 6291464 | tf_op jit(solution)/shard_map/ppermute | solution.py:447
  11.5 7.7 %collective-permute-start.7 = (bf16[576,128]{1,0:T(8,128)(2,1)S(1)}, bf16[576,128]{1,0:T(8,128)(2,1)S(1)}, u32[]{:S(2)}, u32[]{:S(2)}) collective-permute-start(bf16[576,128]{1,0:T(8,128)(2,1)S(1)} %shard_map.96.refs_0_), channel_id=1, source_target_pairs={{0,24},{8,16},{16,8},{24,0},{1,25},{9,17},{17,9},{25,1},{2,26},{10... | collective-permute-start | bytes 442376 | tf_op jit(solution)/shard_map/ppermute | solution.py:445
  14.1 10.6 %collective-permute-start.5 = (bf16[576,128]{1,0:T(8,128)(2,1)S(1)}, bf16[576,128]{1,0:T(8,128)(2,1)S(1)}, u32[]{:S(2)}, u32[]{:S(2)}) collective-permute-start(bf16[576,128]{1,0:T(8,128)(2,1)S(1)} %shard_map.96.refs_0_), channel_id=1, source_target_pairs={{0,16},{8,24},{16,0},{24,8},{1,17},{9,25},{17,1},{25,9},{2,18},{10... | collective-permute-start | bytes 442376 | tf_op jit(solution)/shard_map/ppermute | solution.py:445
  14.6 10.1 %collective-permute-start.6 = (bf16[576,128]{1,0:T(8,128)(2,1)S(1)}, bf16[576,128]{1,0:T(8,128)(2,1)S(1)}, u32[]{:S(2)}, u32[]{:S(2)}) collective-permute-start(bf16[576,128]{1,0:T(8,128)(2,1)S(1)} %shard_map.96.refs_0_), channel_id=1, source_target_pairs={{0,8},{8,0},{16,24},{24,16},{1,9},{9,1},{17,25},{25,17},{2,10},{10... | collective-permute-start | bytes 442376 | tf_op jit(solution)/shard_map/ppermute | solution.py:445
  22.3 7.9 %copy-start = (bf16[2048,512]{1,0:T(8,128)(2,1)S(1)}, bf16[2048,512]{1,0:T(8,128)(2,1)}, u32[]{:S(2)}) copy-start(bf16[2048,512]{1,0:T(8,128)(2,1)} %refs_5_.1) | copy-start | bytes 6291460
  22.3 13.6 %collective-permute-start.8 = (bf16[1040,128]{1,0:T(8,128)(2,1)S(1)}, bf16[1040,128]{1,0:T(8,128)(2,1)S(1)}, u32[]{:S(2)}, u32[]{:S(2)}) collective-permute-start(bf16[1040,128]{1,0:T(8,128)(2,1)S(1)} %shard_map.99.refs_6_), channel_id=1, source_target_pairs={{0,24},{8,16},{16,8},{24,0},{1,25},{9,17},{17,9},{25,1},{2,26},{10... | collective-permute-start | bytes 798728 | tf_op jit(solution)/shard_map/ppermute | solution.py:445
  28.9 6.5 %collective-permute-start.10 = (bf16[1040,128]{1,0:T(8,128)(2,1)S(1)}, bf16[1040,128]{1,0:T(8,128)(2,1)S(1)}, u32[]{:S(2)}, u32[]{:S(2)}) collective-permute-start(bf16[1040,128]{1,0:T(8,128)(2,1)S(1)} %get-tuple-element.24.refs_7_.refs_5_), channel_id=1, source_target_pairs={{0,8},{8,0},{16,24},{24,16},{1,9},{9,1},{17,25},{25,17},{2,10},{10... | collective-permute-start | bytes 798728 | tf_op jit(solution)/shard_map/ppermute | solution.py:445
  29.5 6.4 %collective-permute-start.9 = (bf16[1040,128]{1,0:T(8,128)(2,1)S(1)}, bf16[1040,128]{1,0:T(8,128)(2,1)S(1)}, u32[]{:S(2)}, u32[]{:S(2)}) collective-permute-start(bf16[1040,128]{1,0:T(8,128)(2,1)S(1)} %get-tuple-element.23.refs_6_.refs_4_), channel_id=1, source_target_pairs={{0,16},{8,24},{16,0},{24,8},{1,17},{9,25},{17,1},{25,9},{2,18},{10... | collective-permute-start | bytes 798728 | tf_op jit(solution)/shard_map/ppermute | solution.py:445
  30.3 3.1 %collective-permute-start.11 = (bf16[144,128]{1,0:T(8,128)(2,1)S(1)}, bf16[144,128]{1,0:T(8,128)(2,1)S(1)}, u32[]{:S(2)}, u32[]{:S(2)}) collective-permute-start(bf16[144,128]{1,0:T(8,128)(2,1)S(1)} %shard_map.102.refs_4_.refs_0_), channel_id=1, source_target_pairs={{0,1},{1,0},{2,3},{3,2},{4,5},{5,4},{6,7},{7,6},{8,9},{9,8},{10,11... | collective-permute-start | bytes 110600 | tf_op jit(solution)/shard_map/ppermute | solution.py:447
  36.1 6.2 %collective-permute-start.12 = (bf16[272,128]{1,0:T(8,128)(2,1)S(1)}, bf16[272,128]{1,0:T(8,128)(2,1)S(1)}, u32[]{:S(2)}, u32[]{:S(2)}) collective-permute-start(bf16[272,128]{1,0:T(8,128)(2,1)S(1)} %get-tuple-element.27), channel_id=1, source_target_pairs={{0,6},{1,7},{2,4},{3,5},{4,2},{5,3},{6,0},{7,1},{8,14},{9,15},{10,... | collective-permute-start | bytes 208904 | tf_op jit(solution)/shard_map/ppermute | solution.py:447
  37.8 6.0 %collective-permute-start.13 = (bf16[272,128]{1,0:T(8,128)(2,1)S(1)}, bf16[272,128]{1,0:T(8,128)(2,1)S(1)}, u32[]{:S(2)}, u32[]{:S(2)}) collective-permute-start(bf16[272,128]{1,0:T(8,128)(2,1)S(1)} %get-tuple-element.28), channel_id=1, source_target_pairs={{0,4},{1,5},{2,6},{3,7},{4,0},{5,1},{6,2},{7,3},{8,12},{9,13},{10,... | collective-permute-start | bytes 208904 | tf_op jit(solution)/shard_map/ppermute | solution.py:447
  38.2 5.6 %collective-permute-start.14 = (bf16[272,128]{1,0:T(8,128)(2,1)S(1)}, bf16[272,128]{1,0:T(8,128)(2,1)S(1)}, u32[]{:S(2)}, u32[]{:S(2)}) collective-permute-start(bf16[272,128]{1,0:T(8,128)(2,1)S(1)} %get-tuple-element.29), channel_id=1, source_target_pairs={{0,2},{1,3},{2,0},{3,1},{4,6},{5,7},{6,4},{7,5},{8,10},{9,11},{10,... | collective-permute-start | bytes 208904 | tf_op jit(solution)/shard_map/ppermute | solution.py:447

commit v16 on v13

--- a/solution.py
+++ b/solution.py
@@ -247,6 +247,17 @@
     neg_ref[...] = jnp.zeros_like(neg_ref)
     anchors = anchors_ref[...]
     units = [(side, at) for side in range(sides) for at in range(0, slots, unit)]
+    runs = []
+    for side in range(sides):
+        left = slots // unit
+        while left:
+            length = min(4, left)
+            if side == sides - 1 and length == left and left > 1:
+                length -= 1
+            runs.append(length)
+            left -= length
+    starts = [sum(runs[:run]) for run in range(len(runs))]
+    run_of = [run for run, length in enumerate(runs) for _ in range(length)]
     quarter = rows // 4
 
     def score_unit(at):
@@ -258,7 +269,8 @@
     def term_unit(at, which):
         side, first = units[at]
         part = slice(which * quarter, (which + 1) * quarter)
-        weights_ref = weight_refs[at // 2 % 2]
+        weights_ref = weight_refs[run_of[at] % 2]
+        base = (at - starts[run_of[at]]) * unit
         wanted = labels_ref[part, :]
         pos_sum, neg_sum = pos_ref[part, :], neg_ref[part, :]
         for piece in range(0, unit, lanes):
@@ -272,32 +284,38 @@
             neg = jnp.where(same, 0.0, term)
             pos_sum += pos
             neg_sum += neg
-            to = slice(at % 2 * unit + piece, at % 2 * unit + piece + lanes)
+            to = slice(base + piece, base + piece + lanes)
             weights_ref[part, to] = neg.astype(bf16)
             weights_ref[rows + which * quarter : rows + (which + 1) * quarter, to] = pos.astype(bf16)
         pos_ref[part, :] = pos_sum
         neg_ref[part, :] = neg_sum
 
-    def weigh_half(pair, half):
-        side, first = units[2 * pair]
+    def weigh_half(run, half):
+        side, first = units[starts[run]]
+        span = runs[run] * unit
         part = slice(half * (width // 2), (half + 1) * (width // 2))
         more = jnp.dot(
-            weight_refs[pair % 2][...], keys_refs[side][first : first + 2 * unit, part], preferred_element_type=f32
+            weight_refs[run % 2][:, :span], keys_refs[side][first : first + span, part], preferred_element_type=f32
         )
-        total_ref[:, part] = more if pair == 0 else total_ref[:, part] + more
+        total_ref[:, part] = more if run == 0 else total_ref[:, part] + more
 
     score_unit(0)
+    waiting = []
     for at in range(len(units)):
+        if at in starts and at:
+            waiting += [(run_of[at] - 1, 0), (run_of[at] - 1, 1)]
+        left = runs[run_of[at]] - (at - starts[run_of[at]])
+        now, waiting = waiting[: -(-len(waiting) // left)], waiting[-(-len(waiting) // left) :]
         term_unit(at, 0)
         if at + 1 < len(units):
             score_unit(at + 1)
         term_unit(at, 1)
         term_unit(at, 2)
-        if at >= 2:
-            weigh_half(at // 2 - 1, at % 2)
+        for run, half in now:
+            weigh_half(run, half)
         term_unit(at, 3)
-    weigh_half(len(units) // 2 - 1, 0)
-    weigh_half(len(units) // 2 - 1, 1)
+    weigh_half(len(runs) - 1, 0)
+    weigh_half(len(runs) - 1, 1)
     total = total_ref[...]
     pos_sum = jnp.sum(pos_ref[...], axis=1, keepdims=True)
     neg_sum = jnp.sum(neg_ref[...], axis=1, keepdims=True)
@@ -353,8 +371,8 @@
             pltpu.VMEM((rows, lanes), f32),
             pltpu.VMEM((rows, unit), f32),
             pltpu.VMEM((rows, unit), f32),
-            pltpu.VMEM((2 * rows, 2 * unit), bf16),
-            pltpu.VMEM((2 * rows, 2 * unit), bf16),
+            pltpu.VMEM((2 * rows, 4 * unit), bf16),
+            pltpu.VMEM((2 * rows, 4 * unit), bf16),
         ]
         + [pltpu.SemaphoreType.DMA] * len(copied),
     )
@@ -480,8 +498,7 @@
     choices = [moved] + [exchange(moved, "core", s) for s in range(1, cores)]
 
     sums, *others = add(held, arrived, size, count, 2 * parts, choices)
-    order = sorted(range(1, line), key=lambda step: (step != line // 2, -step))
-    arrived = [exchange(others[line - 1 - step], "line", step) for step in order]
+    arrived = [exchange(value, "line", line - at) for at, value in enumerate(others, 1)]
     grad_batch, loss = call(
         functools.partial(finish_kernel, len(arrived)),
         [shaped((count, width), f32), shaped((1, count), f32)],

time: 45.2 us -> 45 us (level)
  waiting for transfers between devices: 9.26 us -> 8.06 us
  starting transfers between devices: 17 us -> 17.9 us
    ppermute x9, waiting for transfers between devices: 6.43 us -> 5.06 us  [exchange(): return lax.ppermute(value, 'dev', [(i, i ^ jump) for i in range(members)])]
    ppermute x9, starting transfers between devices: 9.82 us -> 10.7 us  [exchange(): return lax.ppermute(value, 'dev', [(i, i ^ jump) for i in range(members)])]
  transfers between devices with their start and end apart: 15 -> 15, of which waited for: 7 -> 7; matrix products, arithmetic and copies ran while one was open for 0% -> 0% of each run, Pallas kernels for 34% -> 35%
where the time goes in v16:
time: 45 us; the launch traced here: 44.7 us
  starting transfers between devices  17.9 us (40%)
  Pallas kernels  17.4 us (39%)
  waiting for transfers between devices  8.06 us (18%)
  between operations  1.4 us (3%)
    pallas_call x13, Pallas kernels, call(): pl.pallas_call(body, out_shape=outs, compiler_params=pltpu.CompilerParams...  17.4 us
    ppermute x9, starting transfers between devices, exchange(): return lax.ppermute(value, 'dev', [(i, i ^ jump) for i in range(members)])  10.7 us
    ppermute x6, starting transfers between devices, exchange(): return lax.ppermute(value, 'grp', [(i, i ^ step) for i in range(groups)])  7.17 us
    ppermute x9, waiting for transfers between devices, exchange(): return lax.ppermute(value, 'dev', [(i, i ^ jump) for i in range(members)])  5.06 us
    ppermute x6, waiting for transfers between devices, exchange(): return lax.ppermute(value, 'grp', [(i, i ^ step) for i in range(groups)])  2.99 us
  transfers between devices with their start and end apart: 15, of which 7 were waited for; matrix products, arithmetic and copies ran while one was open for 0% of the time, Pallas kernels for 35%

profile of v16, /device:TPU:0, one launch (start us, length us, event | category | flops | bytes accessed | tf_op | source)
XLA Modules:
  0.0 44.7 jit_solution(4555892894546569971)
XLA Ops:
  0.6 0.9 %shard_map.93 = (bf16[144,128]{1,0:T(8,128)(2,1)S(1)}, f32[32,512]{1,0:T(8,128)S(1)}, f32[32,128]{1,0:T(8,128)S(1)}, s32[16,128]{1,0:T(8,128)S(1)}, s32[16,128]{1,0:T(8,128)S(1)}) custom-call(bf16[32,512]{1,0:T(8,128)(2,1)} %rows_ref.1, s32[1,32]{1,0:T(1,128)} %bitcast.15, s32[16,128]{1,0:T(8,128)} %bitcast.13, s32[16,128]{1,0:T(8,128)} %bitcast.14), custom_call_target="tpu_custom_call" | custom-call | tf_op jit(solution)/shard_map/pallas_call | solution.py:23
  1.5 5.1 %collective-permute-start = (bf16[144,128]{1,0:T(8,128)(2,1)S(1)}, bf16[144,128]{1,0:T(8,128)(2,1)S(1)}, u32[]{:S(2)}, u32[]{:S(2)}) collective-permute-start(bf16[144,128]{1,0:T(8,128)(2,1)S(1)} %get-tuple-element.21.refs_0_), channel_id=1, source_target_pairs={{0,6},{1,7},{2,4},{3,5},{4,2},{5,3},{6,0},{7,1},{8,14},{9,15},{10,... | collective-permute-start | bytes 110600 | tf_op jit(solution)/shard_map/ppermute | solution.py:458
  6.6 0.6 %collective-permute-start.2 = (bf16[144,128]{1,0:T(8,128)(2,1)S(1)}, bf16[144,128]{1,0:T(8,128)(2,1)S(1)}, u32[]{:S(2)}, u32[]{:S(2)}) collective-permute-start(bf16[144,128]{1,0:T(8,128)(2,1)S(1)} %get-tuple-element.21.refs_0_), channel_id=1, source_target_pairs={{0,2},{1,3},{2,0},{3,1},{4,6},{5,7},{6,4},{7,5},{8,10},{9,11},{10,... | collective-permute-start | bytes 110600 | tf_op jit(solution)/shard_map/ppermute | solution.py:458
  7.3 0.5 %collective-permute-start.4 = (bf16[2048,512]{1,0:T(8,128)(2,1)}, bf16[2048,512]{1,0:T(8,128)(2,1)S(1)}, u32[]{:S(2)}, u32[]{:S(2)}) collective-permute-start(bf16[2048,512]{1,0:T(8,128)(2,1)} %refs_5_.1), channel_id=1, source_target_pairs={{0,1},{1,0},{2,3},{3,2},{4,5},{5,4},{6,7},{7,6},{8,9},{9,8},{10,11... | collective-permute-start | bytes 6291464 | tf_op jit(solution)/shard_map/ppermute | solution.py:458
  8.4 0.1 collective-permute-done.refs_1_
  8.6 2.9 %collective-permute-done.1.refs_1_ = bf16[144,128]{1,0:T(8,128)(2,1)S(1)} collective-permute-done((bf16[144,128]{1,0:T(8,128)(2,1)S(1)}, bf16[144,128]{1,0:T(8,128)(2,1)S(1)}, u32[]{:S(2)}, u32[]{:S(2)}) %collective-permute-start.1) | collective-permute-done | bytes 36896 | tf_op jit(solution)/shard_map/ppermute | solution.py:458
  11.5 0.0 collective-permute-done.2.refs_1_
  11.5 2.5 %collective-permute-start.7 = (bf16[576,128]{1,0:T(8,128)(2,1)S(1)}, bf16[576,128]{1,0:T(8,128)(2,1)S(1)}, u32[]{:S(2)}, u32[]{:S(2)}) collective-permute-start(bf16[576,128]{1,0:T(8,128)(2,1)S(1)} %shard_map.96.refs_0_), channel_id=1, source_target_pairs={{0,24},{8,16},{16,8},{24,0},{1,25},{9,17},{17,9},{25,1},{2,26},{10... | collective-permute-start | bytes 442376 | tf_op jit(solution)/shard_map/ppermute | solution.py:456
  14.1 0.5 %collective-permute-start.5 = (bf16[576,128]{1,0:T(8,128)(2,1)S(1)}, bf16[576,128]{1,0:T(8,128)(2,1)S(1)}, u32[]{:S(2)}, u32[]{:S(2)}) collective-permute-start(bf16[576,128]{1,0:T(8,128)(2,1)S(1)} %shard_map.96.refs_0_), channel_id=1, source_target_pairs={{0,16},{8,24},{16,0},{24,8},{1,17},{9,25},{17,1},{25,9},{2,18},{10... | collective-permute-start | bytes 442376 | tf_op jit(solution)/shard_map/ppermute | solution.py:456
  14.6 0.5 %collective-permute-start.6 = (bf16[576,128]{1,0:T(8,128)(2,1)S(1)}, bf16[576,128]{1,0:T(8,128)(2,1)S(1)}, u32[]{:S(2)}, u32[]{:S(2)}) collective-permute-start(bf16[576,128]{1,0:T(8,128)(2,1)S(1)} %shard_map.96.refs_0_), channel_id=1, source_target_pairs={{0,8},{8,0},{16,24},{24,16},{1,9},{9,1},{17,25},{25,17},{2,10},{10... | collective-permute-start | bytes 442376 | tf_op jit(solution)/shard_map/ppermute | solution.py:456
  15.1 2.9 %shard_map.97.refs_1_.refs_2_ = bf16[2048,512]{1,0:T(8,128)(2,1)S(1)} custom-call(bf16[2048,512]{1,0:T(8,128)(2,1)} %refs_5_.1, bf16[576,128]{1,0:T(8,128)(2,1)S(1)} %shard_map.96.refs_0_), custom_call_target="tpu_custom_call" | custom-call | flops 34359738368 | tf_op jit(solution)/shard_map/pallas_call | solution.py:23
  18.0 0.0 collective-permute-done.4.memory_ref
  18.0 1.0 %shard_map.98.refs_2_.refs_3_ = bf16[2048,512]{1,0:T(8,128)(2,1)S(1)} custom-call(bf16[2048,512]{1,0:T(8,128)(2,1)S(1)} %collective-permute-done.4.memory_ref, bf16[576,128]{1,0:T(8,128)(2,1)S(1)} %shard_map.96.refs_0_), custom_call_target="tpu_custom_call" | custom-call | flops 34359738368 | tf_op jit(solution)/shard_map/pallas_call | solution.py:23
  19.0 0.3 collective-permute-done.7.refs_0_.refs_3_
  19.2 2.9 %shard_map.99.refs_6_ = bf16[1040,128]{1,0:T(8,128)(2,1)S(1)} custom-call(bf16[576,128]{1,0:T(8,128)(2,1)S(1)} %collective-permute-done.7.refs_0_.refs_3_, bf16[2048,512]{1,0:T(8,128)(2,1)S(1)} %shard_map.97.refs_1_.refs_2_, bf16[2048,512]{1,0:T(8,128)(2,1)S(1)} %shard_map.98.refs_2_.refs_3_, s32[1,2048]{1,0:T(1,128)S(1)} %bitcast.7, s32[1,2048]{1,0:T(1,128)S(1)} %bitcast.10), custom_call_target="tpu_custom_call" | custom-call | flops 3221225472 | tf_op jit(solution)/shard_map/pallas_call | solution.py:23
  22.1 0.0 copy-start
  22.1 2.3 %collective-permute-start.8 = (bf16[1040,128]{1,0:T(8,128)(2,1)S(1)}, bf16[1040,128]{1,0:T(8,128)(2,1)S(1)}, u32[]{:S(2)}, u32[]{:S(2)}) collective-permute-start(bf16[1040,128]{1,0:T(8,128)(2,1)S(1)} %shard_map.99.refs_6_), channel_id=1, source_target_pairs={{0,24},{8,16},{16,8},{24,0},{1,25},{9,17},{17,9},{25,1},{2,26},{10... | collective-permute-start | bytes 798728 | tf_op jit(solution)/shard_map/ppermute | solution.py:456
  24.4 0.0 collective-permute-done.5.refs_0_.refs_2_
  24.4 4.6 %shard_map.100 = (bf16[1040,128]{1,0:T(8,128)(2,1)S(1)}, bf16[1040,128]{1,0:T(8,128)(2,1)S(1)}) custom-call(bf16[576,128]{1,0:T(8,128)(2,1)S(1)} %collective-permute-done.5.refs_0_.refs_2_, bf16[576,128]{1,0:T(8,128)(2,1)S(1)} %collective-permute-done.6.refs_1_, bf16[2048,512]{1,0:T(8,128)(2,1)S(1)} %shard_map.97.refs_1_.refs_2_, ...), custom_call_target="tpu_custom_call" | custom-call | flops 6442450944 | tf_op jit(solution)/shard_map/pallas_call | solution.py:23
  29.0 0.6 %collective-permute-start.10 = (bf16[1040,128]{1,0:T(8,128)(2,1)S(1)}, bf16[1040,128]{1,0:T(8,128)(2,1)S(1)}, u32[]{:S(2)}, u32[]{:S(2)}) collective-permute-start(bf16[1040,128]{1,0:T(8,128)(2,1)S(1)} %get-tuple-element.24.refs_7_.refs_5_), channel_id=1, source_target_pairs={{0,8},{8,0},{16,24},{24,16},{1,9},{9,1},{17,25},{25,17},{2,10},{10... | collective-permute-start | bytes 798728 | tf_op jit(solution)/shard_map/ppermute | solution.py:456
  29.6 0.7 %collective-permute-start.9 = (bf16[1040,128]{1,0:T(8,128)(2,1)S(1)}, bf16[1040,128]{1,0:T(8,128)(2,1)S(1)}, u32[]{:S(2)}, u32[]{:S(2)}) collective-permute-start(bf16[1040,128]{1,0:T(8,128)(2,1)S(1)} %get-tuple-element.23.refs_6_.refs_4_), channel_id=1, source_target_pairs={{0,16},{8,24},{16,0},{24,8},{1,17},{9,25},{17,1},{25,9},{2,18},{10... | collective-permute-start | bytes 798728 | tf_op jit(solution)/shard_map/ppermute | solution.py:456
  30.3 2.9 %shard_map.101 = (f32[1040,128]{1,0:T(8,128)S(1)}, bf16[2048,512]{1,0:T(8,128)(2,1)}) custom-call(bf16[576,128]{1,0:T(8,128)(2,1)S(1)} %shard_map.96.refs_0_, bf16[2048,512]{1,0:T(8,128)(2,1)S(1)} %shard_map.97.refs_1_.refs_2_, bf16[2048,512]{1,0:T(8,128)(2,1)S(1)} %shard_map.98.refs_2_.refs_3_, s32[1,2048]{1,0:T(1,128)S(1)} %bitcast.9, ...), custom_call_target="tpu_custom_call" | custom-call | flops 3221225472 | tf_op jit(solution)/shard_map/pallas_call | solution.py:23
  33.3 2.2 %collective-permute-done.10.refs_3_ = bf16[1040,128]{1,0:T(8,128)(2,1)S(1)} collective-permute-done((bf16[1040,128]{1,0:T(8,128)(2,1)S(1)}, bf16[1040,128]{1,0:T(8,128)(2,1)S(1)}, u32[]{:S(2)}, u32[]{:S(2)}) %collective-permute-start.10) | collective-permute-done | bytes 266272 | tf_op jit(solution)/shard_map/ppermute | solution.py:456
  35.5 0.5 %collective-permute-done.9.refs_2_ = bf16[1040,128]{1,0:T(8,128)(2,1)S(1)} collective-permute-done((bf16[1040,128]{1,0:T(8,128)(2,1)S(1)}, bf16[1040,128]{1,0:T(8,128)(2,1)S(1)}, u32[]{:S(2)}, u32[]{:S(2)}) %collective-permute-start.9) | collective-permute-done | bytes 266272 | tf_op jit(solution)/shard_map/ppermute | solution.py:456
  36.0 0.1 shard_map.103
  36.1 1.7 %collective-permute-start.12 = (bf16[272,128]{1,0:T(8,128)(2,1)S(1)}, bf16[272,128]{1,0:T(8,128)(2,1)S(1)}, u32[]{:S(2)}, u32[]{:S(2)}) collective-permute-start(bf16[272,128]{1,0:T(8,128)(2,1)S(1)} %get-tuple-element.27), channel_id=1, source_target_pairs={{0,6},{1,7},{2,4},{3,5},{4,2},{5,3},{6,0},{7,1},{8,14},{9,15},{10,... | collective-permute-start | bytes 208904 | tf_op jit(solution)/shard_map/ppermute | solution.py:458
  37.9 0.4 collective-permute-start.13
  38.3 2.3 %collective-permute-start.14 = (bf16[272,128]{1,0:T(8,128)(2,1)S(1)}, bf16[272,128]{1,0:T(8,128)(2,1)S(1)}, u32[]{:S(2)}, u32[]{:S(2)}) collective-permute-start(bf16[272,128]{1,0:T(8,128)(2,1)S(1)} %get-tuple-element.29), channel_id=1, source_target_pairs={{0,2},{1,3},{2,0},{3,1},{4,6},{5,7},{6,4},{7,5},{8,10},{9,11},{10,... | collective-permute-start | bytes 208904 | tf_op jit(solution)/shard_map/ppermute | solution.py:458
  40.6 1.2 %shard_map.105 = (bf16[2048,512]{1,0:T(8,128)(2,1)}, s32[16,128]{1,0:T(8,128)}) custom-call(s32[1]{0:T(128)S(6)} %copy.12.step_ref, bf16[2048,512]{1,0:T(8,128)(2,1)} %get-tuple-element.34.stored_ref, s32[16,128]{1,0:T(8,128)S(1)} %get-tuple-element.35.labels_ref, bf16[144,128]{1,0:T(8,128)(2,1)S(1)} %shard_map.102.refs_4_.refs_0_, ...), custom_call_target="tpu_custom_call", output_to_operand_aliasing={{0}: (1, {})} | custom-call | tf_op jit(solution)/shard_map/pallas_call | solution.py:23
  41.8 0.5 %collective-permute-done.12.refs_1_ = bf16[272,128]{1,0:T(8,128)(2,1)S(1)} collective-permute-done((bf16[272,128]{1,0:T(8,128)(2,1)S(1)}, bf16[272,128]{1,0:T(8,128)(2,1)S(1)}, u32[]{:S(2)}, u32[]{:S(2)}) %collective-permute-start.12) | collective-permute-done | bytes 69664 | tf_op jit(solution)/shard_map/ppermute | solution.py:458
  42.3 1.5 %collective-permute-done.13.refs_2_ = bf16[272,128]{1,0:T(8,128)(2,1)S(1)} collective-permute-done((bf16[272,128]{1,0:T(8,128)(2,1)S(1)}, bf16[272,128]{1,0:T(8,128)(2,1)S(1)}, u32[]{:S(2)}, u32[]{:S(2)}) %collective-permute-start.13) | collective-permute-done | bytes 69664 | tf_op jit(solution)/shard_map/ppermute | solution.py:458
  43.8 0.9 %shard_map.104 = (f32[32,512]{1,0:T(8,128)}, f32[1,32]{1,0:T(1,128)}) custom-call(f32[272,128]{1,0:T(8,128)S(1)} %get-tuple-element.26.refs_0_, bf16[272,128]{1,0:T(8,128)(2,1)S(1)} %collective-permute-done.12.refs_1_, bf16[272,128]{1,0:T(8,128)(2,1)S(1)} %collective-permute-done.13.refs_2_, bf16[272,128]{1,0:T(8,128)(2,1)S(1)} %collective-permute-done.14.refs_3_, ...), custom_call_target="tpu_custom_call" | custom-call | tf_op jit(solution)/shard_map/pallas_call | solution.py:23
  (13 shorter events, 0.1 us)
Async XLA Ops:
  1.5 7.1 %collective-permute-start = (bf16[144,128]{1,0:T(8,128)(2,1)S(1)}, bf16[144,128]{1,0:T(8,128)(2,1)S(1)}, u32[]{:S(2)}, u32[]{:S(2)}) collective-permute-start(bf16[144,128]{1,0:T(8,128)(2,1)S(1)} %get-tuple-element.21.refs_0_), channel_id=1, source_target_pairs={{0,6},{1,7},{2,4},{3,5},{4,2},{5,3},{6,0},{7,1},{8,14},{9,15},{10,... | collective-permute-start | bytes 110600 | tf_op jit(solution)/shard_map/ppermute | solution.py:458
  6.6 4.9 %collective-permute-start.1 = (bf16[144,128]{1,0:T(8,128)(2,1)S(1)}, bf16[144,128]{1,0:T(8,128)(2,1)S(1)}, u32[]{:S(2)}, u32[]{:S(2)}) collective-permute-start(bf16[144,128]{1,0:T(8,128)(2,1)S(1)} %get-tuple-element.21.refs_0_), channel_id=1, source_target_pairs={{0,4},{1,5},{2,6},{3,7},{4,0},{5,1},{6,2},{7,3},{8,12},{9,13},{10,... | collective-permute-start | bytes 110600 | tf_op jit(solution)/shard_map/ppermute | solution.py:458
  6.6 4.9 %collective-permute-start.2 = (bf16[144,128]{1,0:T(8,128)(2,1)S(1)}, bf16[144,128]{1,0:T(8,128)(2,1)S(1)}, u32[]{:S(2)}, u32[]{:S(2)}) collective-permute-start(bf16[144,128]{1,0:T(8,128)(2,1)S(1)} %get-tuple-element.21.refs_0_), channel_id=1, source_target_pairs={{0,2},{1,3},{2,0},{3,1},{4,6},{5,7},{6,4},{7,5},{8,10},{9,11},{10,... | collective-permute-start | bytes 110600 | tf_op jit(solution)/shard_map/ppermute | solution.py:458
  7.3 4.2 %collective-permute-start.3 = (s32[16,128]{1,0:T(8,128)S(1)}, s32[16,128]{1,0:T(8,128)S(1)}, u32[]{:S(2)}, u32[]{:S(2)}) collective-permute-start(s32[16,128]{1,0:T(8,128)S(1)} %get-tuple-element.22.refs_2_), channel_id=1, source_target_pairs={{0,1},{1,0},{2,3},{3,2},{4,5},{5,4},{6,7},{7,6},{8,9},{9,8},{10,11... | collective-permute-start | bytes 24584 | tf_op jit(solution)/shard_map/ppermute | solution.py:458
  7.3 10.7 %collective-permute-start.4 = (bf16[2048,512]{1,0:T(8,128)(2,1)}, bf16[2048,512]{1,0:T(8,128)(2,1)S(1)}, u32[]{:S(2)}, u32[]{:S(2)}) collective-permute-start(bf16[2048,512]{1,0:T(8,128)(2,1)} %refs_5_.1), channel_id=1, source_target_pairs={{0,1},{1,0},{2,3},{3,2},{4,5},{5,4},{6,7},{7,6},{8,9},{9,8},{10,11... | collective-permute-start | bytes 6291464 | tf_op jit(solution)/shard_map/ppermute | solution.py:458
  11.5 7.7 %collective-permute-start.7 = (bf16[576,128]{1,0:T(8,128)(2,1)S(1)}, bf16[576,128]{1,0:T(8,128)(2,1)S(1)}, u32[]{:S(2)}, u32[]{:S(2)}) collective-permute-start(bf16[576,128]{1,0:T(8,128)(2,1)S(1)} %shard_map.96.refs_0_), channel_id=1, source_target_pairs={{0,24},{8,16},{16,8},{24,0},{1,25},{9,17},{17,9},{25,1},{2,26},{10... | collective-permute-start | bytes 442376 | tf_op jit(solution)/shard_map/ppermute | solution.py:456
  14.1 10.4 %collective-permute-start.5 = (bf16[576,128]{1,0:T(8,128)(2,1)S(1)}, bf16[576,128]{1,0:T(8,128)(2,1)S(1)}, u32[]{:S(2)}, u32[]{:S(2)}) collective-permute-start(bf16[576,128]{1,0:T(8,128)(2,1)S(1)} %shard_map.96.refs_0_), channel_id=1, source_target_pairs={{0,16},{8,24},{16,0},{24,8},{1,17},{9,25},{17,1},{25,9},{2,18},{10... | collective-permute-start | bytes 442376 | tf_op jit(solution)/shard_map/ppermute | solution.py:456
  14.6 9.9 %collective-permute-start.6 = (bf16[576,128]{1,0:T(8,128)(2,1)S(1)}, bf16[576,128]{1,0:T(8,128)(2,1)S(1)}, u32[]{:S(2)}, u32[]{:S(2)}) collective-permute-start(bf16[576,128]{1,0:T(8,128)(2,1)S(1)} %shard_map.96.refs_0_), channel_id=1, source_target_pairs={{0,8},{8,0},{16,24},{24,16},{1,9},{9,1},{17,25},{25,17},{2,10},{10... | collective-permute-start | bytes 442376 | tf_op jit(solution)/shard_map/ppermute | solution.py:456
  22.1 8.2 %copy-start = (bf16[2048,512]{1,0:T(8,128)(2,1)S(1)}, bf16[2048,512]{1,0:T(8,128)(2,1)}, u32[]{:S(2)}) copy-start(bf16[2048,512]{1,0:T(8,128)(2,1)} %refs_5_.1) | copy-start | bytes 6291460
  22.1 13.9 %collective-permute-start.8 = (bf16[1040,128]{1,0:T(8,128)(2,1)S(1)}, bf16[1040,128]{1,0:T(8,128)(2,1)S(1)}, u32[]{:S(2)}, u32[]{:S(2)}) collective-permute-start(bf16[1040,128]{1,0:T(8,128)(2,1)S(1)} %shard_map.99.refs_6_), channel_id=1, source_target_pairs={{0,24},{8,16},{16,8},{24,0},{1,25},{9,17},{17,9},{25,1},{2,26},{10... | collective-permute-start | bytes 798728 | tf_op jit(solution)/shard_map/ppermute | solution.py:456
  29.0 6.5 %collective-permute-start.10 = (bf16[1040,128]{1,0:T(8,128)(2,1)S(1)}, bf16[1040,128]{1,0:T(8,128)(2,1)S(1)}, u32[]{:S(2)}, u32[]{:S(2)}) collective-permute-start(bf16[1040,128]{1,0:T(8,128)(2,1)S(1)} %get-tuple-element.24.refs_7_.refs_5_), channel_id=1, source_target_pairs={{0,8},{8,0},{16,24},{24,16},{1,9},{9,1},{17,25},{25,17},{2,10},{10... | collective-permute-start | bytes 798728 | tf_op jit(solution)/shard_map/ppermute | solution.py:456
  29.6 6.4 %collective-permute-start.9 = (bf16[1040,128]{1,0:T(8,128)(2,1)S(1)}, bf16[1040,128]{1,0:T(8,128)(2,1)S(1)}, u32[]{:S(2)}, u32[]{:S(2)}) collective-permute-start(bf16[1040,128]{1,0:T(8,128)(2,1)S(1)} %get-tuple-element.23.refs_6_.refs_4_), channel_id=1, source_target_pairs={{0,16},{8,24},{16,0},{24,8},{1,17},{9,25},{17,1},{25,9},{2,18},{10... | collective-permute-start | bytes 798728 | tf_op jit(solution)/shard_map/ppermute | solution.py:456
  30.3 2.9 %collective-permute-start.11 = (bf16[144,128]{1,0:T(8,128)(2,1)S(1)}, bf16[144,128]{1,0:T(8,128)(2,1)S(1)}, u32[]{:S(2)}, u32[]{:S(2)}) collective-permute-start(bf16[144,128]{1,0:T(8,128)(2,1)S(1)} %shard_map.102.refs_4_.refs_0_), channel_id=1, source_target_pairs={{0,1},{1,0},{2,3},{3,2},{4,5},{5,4},{6,7},{7,6},{8,9},{9,8},{10,11... | collective-permute-start | bytes 110600 | tf_op jit(solution)/shard_map/ppermute | solution.py:458
  36.1 6.2 %collective-permute-start.12 = (bf16[272,128]{1,0:T(8,128)(2,1)S(1)}, bf16[272,128]{1,0:T(8,128)(2,1)S(1)}, u32[]{:S(2)}, u32[]{:S(2)}) collective-permute-start(bf16[272,128]{1,0:T(8,128)(2,1)S(1)} %get-tuple-element.27), channel_id=1, source_target_pairs={{0,6},{1,7},{2,4},{3,5},{4,2},{5,3},{6,0},{7,1},{8,14},{9,15},{10,... | collective-permute-start | bytes 208904 | tf_op jit(solution)/shard_map/ppermute | solution.py:458
  37.9 6.0 %collective-permute-start.13 = (bf16[272,128]{1,0:T(8,128)(2,1)S(1)}, bf16[272,128]{1,0:T(8,128)(2,1)S(1)}, u32[]{:S(2)}, u32[]{:S(2)}) collective-permute-start(bf16[272,128]{1,0:T(8,128)(2,1)S(1)} %get-tuple-element.28), channel_id=1, source_target_pairs={{0,4},{1,5},{2,6},{3,7},{4,0},{5,1},{6,2},{7,3},{8,12},{9,13},{10,... | collective-permute-start | bytes 208904 | tf_op jit(solution)/shard_map/ppermute | solution.py:458
  38.3 5.6 %collective-permute-start.14 = (bf16[272,128]{1,0:T(8,128)(2,1)S(1)}, bf16[272,128]{1,0:T(8,128)(2,1)S(1)}, u32[]{:S(2)}, u32[]{:S(2)}) collective-permute-start(bf16[272,128]{1,0:T(8,128)(2,1)S(1)} %get-tuple-element.29), channel_id=1, source_target_pairs={{0,2},{1,3},{2,0},{3,1},{4,6},{5,7},{6,4},{7,5},{8,10},{9,11},{10,... | collective-permute-start | bytes 208904 | tf_op jit(solution)/shard_map/ppermute | solution.py:458

commit v17 on v16

--- a/solution.py
+++ b/solution.py
@@ -247,12 +247,13 @@
     neg_ref[...] = jnp.zeros_like(neg_ref)
     anchors = anchors_ref[...]
     units = [(side, at) for side in range(sides) for at in range(0, slots, unit)]
+    longest = 4 if blocks == 1 else 2
     runs = []
     for side in range(sides):
         left = slots // unit
         while left:
-            length = min(4, left)
-            if side == sides - 1 and length == left and left > 1:
+            length = min(longest, left)
+            if blocks == 1 and side == sides - 1 and length == left and left > 1:
                 length -= 1
             runs.append(length)
             left -= length
@@ -371,8 +372,8 @@
             pltpu.VMEM((rows, lanes), f32),
             pltpu.VMEM((rows, unit), f32),
             pltpu.VMEM((rows, unit), f32),
-            pltpu.VMEM((2 * rows, 4 * unit), bf16),
-            pltpu.VMEM((2 * rows, 4 * unit), bf16),
+            pltpu.VMEM((2 * rows, (4 if len(blocks) == 1 else 2) * unit), bf16),
+            pltpu.VMEM((2 * rows, (4 if len(blocks) == 1 else 2) * unit), bf16),
         ]
         + [pltpu.SemaphoreType.DMA] * len(copied),
     )

time: 45 us -> 44.6 us (level)
  transfers between devices with their start and end apart: 15 -> 15, of which waited for: 7 -> 7; matrix products, arithmetic and copies ran while one was open for 0% -> 0% of each run, Pallas kernels for 35% -> 34%
where the time goes in v17:
time: 44.6 us; the launch traced here: 44.4 us
  starting transfers between devices  17.9 us (40%)
  Pallas kernels  17 us (38%)
  waiting for transfers between devices  8.06 us (18%)
  between operations  1.4 us (3%)
    pallas_call x13, Pallas kernels, call(): pl.pallas_call(body, out_shape=outs, compiler_params=pltpu.CompilerParams...  17 us
    ppermute x9, starting transfers between devices, exchange(): return lax.ppermute(value, 'dev', [(i, i ^ jump) for i in range(members)])  10.7 us
    ppermute x6, starting transfers between devices, exchange(): return lax.ppermute(value, 'grp', [(i, i ^ step) for i in range(groups)])  7.18 us
    ppermute x9, waiting for transfers between devices, exchange(): return lax.ppermute(value, 'dev', [(i, i ^ jump) for i in range(members)])  5.07 us
    ppermute x6, waiting for transfers between devices, exchange(): return lax.ppermute(value, 'grp', [(i, i ^ step) for i in range(groups)])  2.99 us
  transfers between devices with their start and end apart: 15, of which 7 were waited for; matrix products, arithmetic and copies ran while one was open for 0% of the time, Pallas kernels for 34%

profile of v17, /device:TPU:0, one launch (start us, length us, event | category | flops | bytes accessed | tf_op | source)
XLA Modules:
  0.0 44.4 jit_solution(16053848739963553034)
XLA Ops:
  0.6 0.9 %shard_map.93 = (bf16[144,128]{1,0:T(8,128)(2,1)S(1)}, f32[32,512]{1,0:T(8,128)S(1)}, f32[32,128]{1,0:T(8,128)S(1)}, s32[16,128]{1,0:T(8,128)S(1)}, s32[16,128]{1,0:T(8,128)S(1)}) custom-call(bf16[32,512]{1,0:T(8,128)(2,1)} %rows_ref.1, s32[1,32]{1,0:T(1,128)} %bitcast.15, s32[16,128]{1,0:T(8,128)} %bitcast.13, s32[16,128]{1,0:T(8,128)} %bitcast.14), custom_call_target="tpu_custom_call" | custom-call | tf_op jit(solution)/shard_map/pallas_call | solution.py:23
  1.5 5.1 %collective-permute-start = (bf16[144,128]{1,0:T(8,128)(2,1)S(1)}, bf16[144,128]{1,0:T(8,128)(2,1)S(1)}, u32[]{:S(2)}, u32[]{:S(2)}) collective-permute-start(bf16[144,128]{1,0:T(8,128)(2,1)S(1)} %get-tuple-element.21.refs_0_), channel_id=1, source_target_pairs={{0,6},{1,7},{2,4},{3,5},{4,2},{5,3},{6,0},{7,1},{8,14},{9,15},{10,... | collective-permute-start | bytes 110600 | tf_op jit(solution)/shard_map/ppermute | solution.py:459
  6.6 0.0 collective-permute-start.1
  6.6 0.6 %collective-permute-start.2 = (bf16[144,128]{1,0:T(8,128)(2,1)S(1)}, bf16[144,128]{1,0:T(8,128)(2,1)S(1)}, u32[]{:S(2)}, u32[]{:S(2)}) collective-permute-start(bf16[144,128]{1,0:T(8,128)(2,1)S(1)} %get-tuple-element.21.refs_0_), channel_id=1, source_target_pairs={{0,2},{1,3},{2,0},{3,1},{4,6},{5,7},{6,4},{7,5},{8,10},{9,11},{10,... | collective-permute-start | bytes 110600 | tf_op jit(solution)/shard_map/ppermute | solution.py:459
  7.3 0.0 collective-permute-start.3
  7.3 0.5 %collective-permute-start.4 = (bf16[2048,512]{1,0:T(8,128)(2,1)}, bf16[2048,512]{1,0:T(8,128)(2,1)S(1)}, u32[]{:S(2)}, u32[]{:S(2)}) collective-permute-start(bf16[2048,512]{1,0:T(8,128)(2,1)} %refs_5_.1), channel_id=1, source_target_pairs={{0,1},{1,0},{2,3},{3,2},{4,5},{5,4},{6,7},{7,6},{8,9},{9,8},{10,11... | collective-permute-start | bytes 6291464 | tf_op jit(solution)/shard_map/ppermute | solution.py:459
  8.4 0.1 collective-permute-done.refs_1_
  8.6 2.9 %collective-permute-done.1.refs_1_ = bf16[144,128]{1,0:T(8,128)(2,1)S(1)} collective-permute-done((bf16[144,128]{1,0:T(8,128)(2,1)S(1)}, bf16[144,128]{1,0:T(8,128)(2,1)S(1)}, u32[]{:S(2)}, u32[]{:S(2)}) %collective-permute-start.1) | collective-permute-done | bytes 36896 | tf_op jit(solution)/shard_map/ppermute | solution.py:459
  11.5 0.0 collective-permute-done.3.refs_3_
  11.5 2.5 %collective-permute-start.7 = (bf16[576,128]{1,0:T(8,128)(2,1)S(1)}, bf16[576,128]{1,0:T(8,128)(2,1)S(1)}, u32[]{:S(2)}, u32[]{:S(2)}) collective-permute-start(bf16[576,128]{1,0:T(8,128)(2,1)S(1)} %shard_map.96.refs_0_), channel_id=1, source_target_pairs={{0,24},{8,16},{16,8},{24,0},{1,25},{9,17},{17,9},{25,1},{2,26},{10... | collective-permute-start | bytes 442376 | tf_op jit(solution)/shard_map/ppermute | solution.py:457
  14.1 0.5 %collective-permute-start.5 = (bf16[576,128]{1,0:T(8,128)(2,1)S(1)}, bf16[576,128]{1,0:T(8,128)(2,1)S(1)}, u32[]{:S(2)}, u32[]{:S(2)}) collective-permute-start(bf16[576,128]{1,0:T(8,128)(2,1)S(1)} %shard_map.96.refs_0_), channel_id=1, source_target_pairs={{0,16},{8,24},{16,0},{24,8},{1,17},{9,25},{17,1},{25,9},{2,18},{10... | collective-permute-start | bytes 442376 | tf_op jit(solution)/shard_map/ppermute | solution.py:457
  14.6 0.5 %collective-permute-start.6 = (bf16[576,128]{1,0:T(8,128)(2,1)S(1)}, bf16[576,128]{1,0:T(8,128)(2,1)S(1)}, u32[]{:S(2)}, u32[]{:S(2)}) collective-permute-start(bf16[576,128]{1,0:T(8,128)(2,1)S(1)} %shard_map.96.refs_0_), channel_id=1, source_target_pairs={{0,8},{8,0},{16,24},{24,16},{1,9},{9,1},{17,25},{25,17},{2,10},{10... | collective-permute-start | bytes 442376 | tf_op jit(solution)/shard_map/ppermute | solution.py:457
  15.1 2.9 %shard_map.97.refs_1_.refs_2_ = bf16[2048,512]{1,0:T(8,128)(2,1)S(1)} custom-call(bf16[2048,512]{1,0:T(8,128)(2,1)} %refs_5_.1, bf16[576,128]{1,0:T(8,128)(2,1)S(1)} %shard_map.96.refs_0_), custom_call_target="tpu_custom_call" | custom-call | flops 34359738368 | tf_op jit(solution)/shard_map/pallas_call | solution.py:23
  18.0 1.0 %shard_map.98.refs_2_.refs_3_ = bf16[2048,512]{1,0:T(8,128)(2,1)S(1)} custom-call(bf16[2048,512]{1,0:T(8,128)(2,1)S(1)} %collective-permute-done.4.memory_ref, bf16[576,128]{1,0:T(8,128)(2,1)S(1)} %shard_map.96.refs_0_), custom_call_target="tpu_custom_call" | custom-call | flops 34359738368 | tf_op jit(solution)/shard_map/pallas_call | solution.py:23
  19.0 0.3 collective-permute-done.7.refs_0_.refs_3_
  19.2 2.9 %shard_map.99.refs_6_ = bf16[1040,128]{1,0:T(8,128)(2,1)S(1)} custom-call(bf16[576,128]{1,0:T(8,128)(2,1)S(1)} %collective-permute-done.7.refs_0_.refs_3_, bf16[2048,512]{1,0:T(8,128)(2,1)S(1)} %shard_map.97.refs_1_.refs_2_, bf16[2048,512]{1,0:T(8,128)(2,1)S(1)} %shard_map.98.refs_2_.refs_3_, s32[1,2048]{1,0:T(1,128)S(1)} %bitcast.7, s32[1,2048]{1,0:T(1,128)S(1)} %bitcast.10), custom_call_target="tpu_custom_call" | custom-call | flops 3221225472 | tf_op jit(solution)/shard_map/pallas_call | solution.py:23
  22.1 0.0 copy-start
  22.1 2.3 %collective-permute-start.8 = (bf16[1040,128]{1,0:T(8,128)(2,1)S(1)}, bf16[1040,128]{1,0:T(8,128)(2,1)S(1)}, u32[]{:S(2)}, u32[]{:S(2)}) collective-permute-start(bf16[1040,128]{1,0:T(8,128)(2,1)S(1)} %shard_map.99.refs_6_), channel_id=1, source_target_pairs={{0,24},{8,16},{16,8},{24,0},{1,25},{9,17},{17,9},{25,1},{2,26},{10... | collective-permute-start | bytes 798728 | tf_op jit(solution)/shard_map/ppermute | solution.py:457
  24.4 4.2 %shard_map.100 = (bf16[1040,128]{1,0:T(8,128)(2,1)S(1)}, bf16[1040,128]{1,0:T(8,128)(2,1)S(1)}) custom-call(bf16[576,128]{1,0:T(8,128)(2,1)S(1)} %collective-permute-done.5.refs_0_.refs_2_, bf16[576,128]{1,0:T(8,128)(2,1)S(1)} %collective-permute-done.6.refs_1_, bf16[2048,512]{1,0:T(8,128)(2,1)S(1)} %shard_map.97.refs_1_.refs_2_, ...), custom_call_target="tpu_custom_call" | custom-call | flops 6442450944 | tf_op jit(solution)/shard_map/pallas_call | solution.py:23
  28.6 0.6 %collective-permute-start.10 = (bf16[1040,128]{1,0:T(8,128)(2,1)S(1)}, bf16[1040,128]{1,0:T(8,128)(2,1)S(1)}, u32[]{:S(2)}, u32[]{:S(2)}) collective-permute-start(bf16[1040,128]{1,0:T(8,128)(2,1)S(1)} %get-tuple-element.24.refs_7_.refs_5_), channel_id=1, source_target_pairs={{0,8},{8,0},{16,24},{24,16},{1,9},{9,1},{17,25},{25,17},{2,10},{10... | collective-permute-start | bytes 798728 | tf_op jit(solution)/shard_map/ppermute | solution.py:457
  29.2 0.7 %collective-permute-start.9 = (bf16[1040,128]{1,0:T(8,128)(2,1)S(1)}, bf16[1040,128]{1,0:T(8,128)(2,1)S(1)}, u32[]{:S(2)}, u32[]{:S(2)}) collective-permute-start(bf16[1040,128]{1,0:T(8,128)(2,1)S(1)} %get-tuple-element.23.refs_6_.refs_4_), channel_id=1, source_target_pairs={{0,16},{8,24},{16,0},{24,8},{1,17},{9,25},{17,1},{25,9},{2,18},{10... | collective-permute-start | bytes 798728 | tf_op jit(solution)/shard_map/ppermute | solution.py:457
  30.0 2.9 %shard_map.101 = (f32[1040,128]{1,0:T(8,128)S(1)}, bf16[2048,512]{1,0:T(8,128)(2,1)}) custom-call(bf16[576,128]{1,0:T(8,128)(2,1)S(1)} %shard_map.96.refs_0_, bf16[2048,512]{1,0:T(8,128)(2,1)S(1)} %shard_map.97.refs_1_.refs_2_, bf16[2048,512]{1,0:T(8,128)(2,1)S(1)} %shard_map.98.refs_2_.refs_3_, s32[1,2048]{1,0:T(1,128)S(1)} %bitcast.9, ...), custom_call_target="tpu_custom_call" | custom-call | flops 3221225472 | tf_op jit(solution)/shard_map/pallas_call | solution.py:23
  32.9 2.2 %collective-permute-done.10.refs_3_ = bf16[1040,128]{1,0:T(8,128)(2,1)S(1)} collective-permute-done((bf16[1040,128]{1,0:T(8,128)(2,1)S(1)}, bf16[1040,128]{1,0:T(8,128)(2,1)S(1)}, u32[]{:S(2)}, u32[]{:S(2)}) %collective-permute-start.10) | collective-permute-done | bytes 266272 | tf_op jit(solution)/shard_map/ppermute | solution.py:457
  35.1 0.5 %collective-permute-done.9.refs_2_ = bf16[1040,128]{1,0:T(8,128)(2,1)S(1)} collective-permute-done((bf16[1040,128]{1,0:T(8,128)(2,1)S(1)}, bf16[1040,128]{1,0:T(8,128)(2,1)S(1)}, u32[]{:S(2)}, u32[]{:S(2)}) %collective-permute-start.9) | collective-permute-done | bytes 266272 | tf_op jit(solution)/shard_map/ppermute | solution.py:457
  35.7 0.1 shard_map.103
  35.8 1.8 %collective-permute-start.12 = (bf16[272,128]{1,0:T(8,128)(2,1)S(1)}, bf16[272,128]{1,0:T(8,128)(2,1)S(1)}, u32[]{:S(2)}, u32[]{:S(2)}) collective-permute-start(bf16[272,128]{1,0:T(8,128)(2,1)S(1)} %get-tuple-element.27), channel_id=1, source_target_pairs={{0,6},{1,7},{2,4},{3,5},{4,2},{5,3},{6,0},{7,1},{8,14},{9,15},{10,... | collective-permute-start | bytes 208904 | tf_op jit(solution)/shard_map/ppermute | solution.py:459
  37.5 0.4 collective-permute-start.13
  37.9 2.3 %collective-permute-start.14 = (bf16[272,128]{1,0:T(8,128)(2,1)S(1)}, bf16[272,128]{1,0:T(8,128)(2,1)S(1)}, u32[]{:S(2)}, u32[]{:S(2)}) collective-permute-start(bf16[272,128]{1,0:T(8,128)(2,1)S(1)} %get-tuple-element.29), channel_id=1, source_target_pairs={{0,2},{1,3},{2,0},{3,1},{4,6},{5,7},{6,4},{7,5},{8,10},{9,11},{10,... | collective-permute-start | bytes 208904 | tf_op jit(solution)/shard_map/ppermute | solution.py:459
  40.2 1.2 %shard_map.105 = (bf16[2048,512]{1,0:T(8,128)(2,1)}, s32[16,128]{1,0:T(8,128)}) custom-call(s32[1]{0:T(128)S(6)} %copy.12.step_ref, bf16[2048,512]{1,0:T(8,128)(2,1)} %get-tuple-element.34.stored_ref, s32[16,128]{1,0:T(8,128)S(1)} %get-tuple-element.35.labels_ref, bf16[144,128]{1,0:T(8,128)(2,1)S(1)} %shard_map.102.refs_4_.refs_0_, ...), custom_call_target="tpu_custom_call", output_to_operand_aliasing={{0}: (1, {})} | custom-call | tf_op jit(solution)/shard_map/pallas_call | solution.py:23
  41.5 0.5 %collective-permute-done.12.refs_1_ = bf16[272,128]{1,0:T(8,128)(2,1)S(1)} collective-permute-done((bf16[272,128]{1,0:T(8,128)(2,1)S(1)}, bf16[272,128]{1,0:T(8,128)(2,1)S(1)}, u32[]{:S(2)}, u32[]{:S(2)}) %collective-permute-start.12) | collective-permute-done | bytes 69664 | tf_op jit(solution)/shard_map/ppermute | solution.py:459
  42.0 1.5 %collective-permute-done.13.refs_2_ = bf16[272,128]{1,0:T(8,128)(2,1)S(1)} collective-permute-done((bf16[272,128]{1,0:T(8,128)(2,1)S(1)}, bf16[272,128]{1,0:T(8,128)(2,1)S(1)}, u32[]{:S(2)}, u32[]{:S(2)}) %collective-permute-start.13) | collective-permute-done | bytes 69664 | tf_op jit(solution)/shard_map/ppermute | solution.py:459
  43.5 0.9 %shard_map.104 = (f32[32,512]{1,0:T(8,128)}, f32[1,32]{1,0:T(1,128)}) custom-call(f32[272,128]{1,0:T(8,128)S(1)} %get-tuple-element.26.refs_0_, bf16[272,128]{1,0:T(8,128)(2,1)S(1)} %collective-permute-done.12.refs_1_, bf16[272,128]{1,0:T(8,128)(2,1)S(1)} %collective-permute-done.13.refs_2_, bf16[272,128]{1,0:T(8,128)(2,1)S(1)} %collective-permute-done.14.refs_3_, ...), custom_call_target="tpu_custom_call" | custom-call | tf_op jit(solution)/shard_map/pallas_call | solution.py:23
  (13 shorter events, 0.1 us)
Async XLA Ops:
  1.5 7.1 %collective-permute-start = (bf16[144,128]{1,0:T(8,128)(2,1)S(1)}, bf16[144,128]{1,0:T(8,128)(2,1)S(1)}, u32[]{:S(2)}, u32[]{:S(2)}) collective-permute-start(bf16[144,128]{1,0:T(8,128)(2,1)S(1)} %get-tuple-element.21.refs_0_), channel_id=1, source_target_pairs={{0,6},{1,7},{2,4},{3,5},{4,2},{5,3},{6,0},{7,1},{8,14},{9,15},{10,... | collective-permute-start | bytes 110600 | tf_op jit(solution)/shard_map/ppermute | solution.py:459
  6.6 4.9 %collective-permute-start.1 = (bf16[144,128]{1,0:T(8,128)(2,1)S(1)}, bf16[144,128]{1,0:T(8,128)(2,1)S(1)}, u32[]{:S(2)}, u32[]{:S(2)}) collective-permute-start(bf16[144,128]{1,0:T(8,128)(2,1)S(1)} %get-tuple-element.21.refs_0_), channel_id=1, source_target_pairs={{0,4},{1,5},{2,6},{3,7},{4,0},{5,1},{6,2},{7,3},{8,12},{9,13},{10,... | collective-permute-start | bytes 110600 | tf_op jit(solution)/shard_map/ppermute | solution.py:459
  6.6 4.9 %collective-permute-start.2 = (bf16[144,128]{1,0:T(8,128)(2,1)S(1)}, bf16[144,128]{1,0:T(8,128)(2,1)S(1)}, u32[]{:S(2)}, u32[]{:S(2)}) collective-permute-start(bf16[144,128]{1,0:T(8,128)(2,1)S(1)} %get-tuple-element.21.refs_0_), channel_id=1, source_target_pairs={{0,2},{1,3},{2,0},{3,1},{4,6},{5,7},{6,4},{7,5},{8,10},{9,11},{10,... | collective-permute-start | bytes 110600 | tf_op jit(solution)/shard_map/ppermute | solution.py:459
  7.3 4.2 %collective-permute-start.3 = (s32[16,128]{1,0:T(8,128)S(1)}, s32[16,128]{1,0:T(8,128)S(1)}, u32[]{:S(2)}, u32[]{:S(2)}) collective-permute-start(s32[16,128]{1,0:T(8,128)S(1)} %get-tuple-element.22.refs_2_), channel_id=1, source_target_pairs={{0,1},{1,0},{2,3},{3,2},{4,5},{5,4},{6,7},{7,6},{8,9},{9,8},{10,11... | collective-permute-start | bytes 24584 | tf_op jit(solution)/shard_map/ppermute | solution.py:459
  7.3 10.7 %collective-permute-start.4 = (bf16[2048,512]{1,0:T(8,128)(2,1)}, bf16[2048,512]{1,0:T(8,128)(2,1)S(1)}, u32[]{:S(2)}, u32[]{:S(2)}) collective-permute-start(bf16[2048,512]{1,0:T(8,128)(2,1)} %refs_5_.1), channel_id=1, source_target_pairs={{0,1},{1,0},{2,3},{3,2},{4,5},{5,4},{6,7},{7,6},{8,9},{9,8},{10,11... | collective-permute-start | bytes 6291464 | tf_op jit(solution)/shard_map/ppermute | solution.py:459
  11.5 7.7 %collective-permute-start.7 = (bf16[576,128]{1,0:T(8,128)(2,1)S(1)}, bf16[576,128]{1,0:T(8,128)(2,1)S(1)}, u32[]{:S(2)}, u32[]{:S(2)}) collective-permute-start(bf16[576,128]{1,0:T(8,128)(2,1)S(1)} %shard_map.96.refs_0_), channel_id=1, source_target_pairs={{0,24},{8,16},{16,8},{24,0},{1,25},{9,17},{17,9},{25,1},{2,26},{10... | collective-permute-start | bytes 442376 | tf_op jit(solution)/shard_map/ppermute | solution.py:457
  14.1 10.4 %collective-permute-start.5 = (bf16[576,128]{1,0:T(8,128)(2,1)S(1)}, bf16[576,128]{1,0:T(8,128)(2,1)S(1)}, u32[]{:S(2)}, u32[]{:S(2)}) collective-permute-start(bf16[576,128]{1,0:T(8,128)(2,1)S(1)} %shard_map.96.refs_0_), channel_id=1, source_target_pairs={{0,16},{8,24},{16,0},{24,8},{1,17},{9,25},{17,1},{25,9},{2,18},{10... | collective-permute-start | bytes 442376 | tf_op jit(solution)/shard_map/ppermute | solution.py:457
  14.6 9.9 %collective-permute-start.6 = (bf16[576,128]{1,0:T(8,128)(2,1)S(1)}, bf16[576,128]{1,0:T(8,128)(2,1)S(1)}, u32[]{:S(2)}, u32[]{:S(2)}) collective-permute-start(bf16[576,128]{1,0:T(8,128)(2,1)S(1)} %shard_map.96.refs_0_), channel_id=1, source_target_pairs={{0,8},{8,0},{16,24},{24,16},{1,9},{9,1},{17,25},{25,17},{2,10},{10... | collective-permute-start | bytes 442376 | tf_op jit(solution)/shard_map/ppermute | solution.py:457
  22.1 7.9 %copy-start = (bf16[2048,512]{1,0:T(8,128)(2,1)S(1)}, bf16[2048,512]{1,0:T(8,128)(2,1)}, u32[]{:S(2)}) copy-start(bf16[2048,512]{1,0:T(8,128)(2,1)} %refs_5_.1) | copy-start | bytes 6291460
  22.1 13.5 %collective-permute-start.8 = (bf16[1040,128]{1,0:T(8,128)(2,1)S(1)}, bf16[1040,128]{1,0:T(8,128)(2,1)S(1)}, u32[]{:S(2)}, u32[]{:S(2)}) collective-permute-start(bf16[1040,128]{1,0:T(8,128)(2,1)S(1)} %shard_map.99.refs_6_), channel_id=1, source_target_pairs={{0,24},{8,16},{16,8},{24,0},{1,25},{9,17},{17,9},{25,1},{2,26},{10... | collective-permute-start | bytes 798728 | tf_op jit(solution)/shard_map/ppermute | solution.py:457
  28.6 6.5 %collective-permute-start.10 = (bf16[1040,128]{1,0:T(8,128)(2,1)S(1)}, bf16[1040,128]{1,0:T(8,128)(2,1)S(1)}, u32[]{:S(2)}, u32[]{:S(2)}) collective-permute-start(bf16[1040,128]{1,0:T(8,128)(2,1)S(1)} %get-tuple-element.24.refs_7_.refs_5_), channel_id=1, source_target_pairs={{0,8},{8,0},{16,24},{24,16},{1,9},{9,1},{17,25},{25,17},{2,10},{10... | collective-permute-start | bytes 798728 | tf_op jit(solution)/shard_map/ppermute | solution.py:457
  29.2 6.4 %collective-permute-start.9 = (bf16[1040,128]{1,0:T(8,128)(2,1)S(1)}, bf16[1040,128]{1,0:T(8,128)(2,1)S(1)}, u32[]{:S(2)}, u32[]{:S(2)}) collective-permute-start(bf16[1040,128]{1,0:T(8,128)(2,1)S(1)} %get-tuple-element.23.refs_6_.refs_4_), channel_id=1, source_target_pairs={{0,16},{8,24},{16,0},{24,8},{1,17},{9,25},{17,1},{25,9},{2,18},{10... | collective-permute-start | bytes 798728 | tf_op jit(solution)/shard_map/ppermute | solution.py:457
  30.0 2.9 %collective-permute-start.11 = (bf16[144,128]{1,0:T(8,128)(2,1)S(1)}, bf16[144,128]{1,0:T(8,128)(2,1)S(1)}, u32[]{:S(2)}, u32[]{:S(2)}) collective-permute-start(bf16[144,128]{1,0:T(8,128)(2,1)S(1)} %shard_map.102.refs_4_.refs_0_), channel_id=1, source_target_pairs={{0,1},{1,0},{2,3},{3,2},{4,5},{5,4},{6,7},{7,6},{8,9},{9,8},{10,11... | collective-permute-start | bytes 110600 | tf_op jit(solution)/shard_map/ppermute | solution.py:459
  35.8 6.2 %collective-permute-start.12 = (bf16[272,128]{1,0:T(8,128)(2,1)S(1)}, bf16[272,128]{1,0:T(8,128)(2,1)S(1)}, u32[]{:S(2)}, u32[]{:S(2)}) collective-permute-start(bf16[272,128]{1,0:T(8,128)(2,1)S(1)} %get-tuple-element.27), channel_id=1, source_target_pairs={{0,6},{1,7},{2,4},{3,5},{4,2},{5,3},{6,0},{7,1},{8,14},{9,15},{10,... | collective-permute-start | bytes 208904 | tf_op jit(solution)/shard_map/ppermute | solution.py:459
  37.5 6.0 %collective-permute-start.13 = (bf16[272,128]{1,0:T(8,128)(2,1)S(1)}, bf16[272,128]{1,0:T(8,128)(2,1)S(1)}, u32[]{:S(2)}, u32[]{:S(2)}) collective-permute-start(bf16[272,128]{1,0:T(8,128)(2,1)S(1)} %get-tuple-element.28), channel_id=1, source_target_pairs={{0,4},{1,5},{2,6},{3,7},{4,0},{5,1},{6,2},{7,3},{8,12},{9,13},{10,... | collective-permute-start | bytes 208904 | tf_op jit(solution)/shard_map/ppermute | solution.py:459
  37.9 5.6 %collective-permute-start.14 = (bf16[272,128]{1,0:T(8,128)(2,1)S(1)}, bf16[272,128]{1,0:T(8,128)(2,1)S(1)}, u32[]{:S(2)}, u32[]{:S(2)}) collective-permute-start(bf16[272,128]{1,0:T(8,128)(2,1)S(1)} %get-tuple-element.29), channel_id=1, source_target_pairs={{0,2},{1,3},{2,0},{3,1},{4,6},{5,7},{6,4},{7,5},{8,10},{9,11},{10,... | collective-permute-start | bytes 208904 | tf_op jit(solution)/shard_map/ppermute | solution.py:459

commit v18 on v17

--- a/solution.py
+++ b/solution.py
@@ -53,10 +53,8 @@
     return out
 
 
-def prepare_kernel(rows_ref, labels_ref, stored_ref, keep_ref, packed_ref, unit_ref, radius_ref, slot_ref, copy_ref):
-    stored = stored_ref[...]
-    slot_ref[...] = jnp.where(keep_ref[...] > 0, stored, -1)
-    copy_ref[...] = stored
+def prepare_kernel(rows_ref, labels_ref, stored_ref, keep_ref, packed_ref, unit_ref, radius_ref, slot_ref):
+    slot_ref[...] = jnp.where(keep_ref[...] > 0, stored_ref[...], -1)
     rows = rows_ref[...].astype(f32)
     count, width = rows.shape
     radius = jnp.sqrt(jnp.sum(rows * rows, axis=1, keepdims=True) + 1e-06)
@@ -259,7 +257,8 @@
             left -= length
     starts = [sum(runs[:run]) for run in range(len(runs))]
     run_of = [run for run, length in enumerate(runs) for _ in range(length)]
-    quarter = rows // 4
+    cuts = max(rows // 32, 4)
+    quarter = rows // cuts
 
     def score_unit(at):
         side, first = units[at]
@@ -307,14 +306,13 @@
             waiting += [(run_of[at] - 1, 0), (run_of[at] - 1, 1)]
         left = runs[run_of[at]] - (at - starts[run_of[at]])
         now, waiting = waiting[: -(-len(waiting) // left)], waiting[-(-len(waiting) // left) :]
-        term_unit(at, 0)
-        if at + 1 < len(units):
-            score_unit(at + 1)
-        term_unit(at, 1)
-        term_unit(at, 2)
-        for run, half in now:
-            weigh_half(run, half)
-        term_unit(at, 3)
+        for which in range(cuts):
+            if which == cuts // 4 and at + 1 < len(units):
+                score_unit(at + 1)
+            if which == cuts - cuts // 4:
+                for run, half in now:
+                    weigh_half(run, half)
+            term_unit(at, which)
     weigh_half(len(runs) - 1, 0)
     weigh_half(len(runs) - 1, 1)
     total = total_ref[...]
@@ -460,13 +458,12 @@
 
     folded = (slots // lanes, lanes)
     parts = blocks_of(width)
-    packed, unit, radius, slot_labels, copied_labels = call(
+    packed, unit, radius, slot_labels = call(
         prepare_kernel,
         [
             pltpu.VMEM((parts * count + 16, lanes), bf16),
             pltpu.VMEM((count, width), f32),
             pltpu.VMEM((count, lanes), f32),
-            pltpu.VMEM(folded, jnp.int32),
             pltpu.VMEM(folded, jnp.int32),
         ],
         batch_rows, batch_labels.reshape(1, count), memory_labels.reshape(folded), keep_bits.reshape(folded),
@@ -506,7 +503,7 @@
         sums, *arrived, unit, radius,
     )
 
-    new_memory, new_labels = patch(copied, copied_labels, choices, step_index, sizes)
+    new_memory, new_labels = patch(copied, memory_labels.reshape(folded), choices, step_index, sizes)
     return (grad_batch, loss.reshape(count), new_memory, new_labels.reshape(slots))
 
 

time: 44.6 us -> 44.6 us (level)
  no operation moved by 1% of the time
where the time goes in v18:
time: 44.6 us; the launch traced here: 44.4 us
  starting transfers between devices  17.9 us (40%)
  Pallas kernels  17 us (38%)
  waiting for transfers between devices  8.04 us (18%)
  between operations  1.41 us (3%)
    pallas_call x13, Pallas kernels, call(): pl.pallas_call(body, out_shape=outs, compiler_params=pltpu.CompilerParams...  17 us
    ppermute x9, starting transfers between devices, exchange(): return lax.ppermute(value, 'dev', [(i, i ^ jump) for i in range(members)])  10.7 us
    ppermute x6, starting transfers between devices, exchange(): return lax.ppermute(value, 'grp', [(i, i ^ step) for i in range(groups)])  7.18 us
    ppermute x9, waiting for transfers between devices, exchange(): return lax.ppermute(value, 'dev', [(i, i ^ jump) for i in range(members)])  5.07 us
    ppermute x6, waiting for transfers between devices, exchange(): return lax.ppermute(value, 'grp', [(i, i ^ step) for i in range(groups)])  2.98 us
  transfers between devices with their start and end apart: 15, of which 7 were waited for; matrix products, arithmetic and copies ran while one was open for 0% of the time, Pallas kernels for 34%

profile of v18, /device:TPU:0, one launch (start us, length us, event | category | flops | bytes accessed | tf_op | source)
XLA Modules:
  0.0 44.4 jit_solution(18089882802697831055)
XLA Ops:
  0.6 0.9 %shard_map.93 = (bf16[144,128]{1,0:T(8,128)(2,1)S(1)}, f32[32,512]{1,0:T(8,128)S(1)}, f32[32,128]{1,0:T(8,128)S(1)}, s32[16,128]{1,0:T(8,128)S(1)}) custom-call(bf16[32,512]{1,0:T(8,128)(2,1)} %rows_ref.1, s32[1,32]{1,0:T(1,128)} %bitcast.16, s32[16,128]{1,0:T(8,128)} %bitcast.7, s32[16,128]{1,0:T(8,128)} %bitcast.15), custom_call_target="tpu_custom_call" | custom-call | tf_op jit(solution)/shard_map/pallas_call | solution.py:23
  1.5 5.1 %collective-permute-start = (bf16[144,128]{1,0:T(8,128)(2,1)S(1)}, bf16[144,128]{1,0:T(8,128)(2,1)S(1)}, u32[]{:S(2)}, u32[]{:S(2)}) collective-permute-start(bf16[144,128]{1,0:T(8,128)(2,1)S(1)} %get-tuple-element.20.refs_0_), channel_id=1, source_target_pairs={{0,6},{1,7},{2,4},{3,5},{4,2},{5,3},{6,0},{7,1},{8,14},{9,15},{10,... | collective-permute-start | bytes 110600 | tf_op jit(solution)/shard_map/ppermute | solution.py:457
  6.6 0.0 collective-permute-start.1
  6.6 0.6 %collective-permute-start.2 = (bf16[144,128]{1,0:T(8,128)(2,1)S(1)}, bf16[144,128]{1,0:T(8,128)(2,1)S(1)}, u32[]{:S(2)}, u32[]{:S(2)}) collective-permute-start(bf16[144,128]{1,0:T(8,128)(2,1)S(1)} %get-tuple-element.20.refs_0_), channel_id=1, source_target_pairs={{0,2},{1,3},{2,0},{3,1},{4,6},{5,7},{6,4},{7,5},{8,10},{9,11},{10,... | collective-permute-start | bytes 110600 | tf_op jit(solution)/shard_map/ppermute | solution.py:457
  7.3 0.0 collective-permute-start.3
  7.3 0.5 %collective-permute-start.4 = (bf16[2048,512]{1,0:T(8,128)(2,1)}, bf16[2048,512]{1,0:T(8,128)(2,1)S(1)}, u32[]{:S(2)}, u32[]{:S(2)}) collective-permute-start(bf16[2048,512]{1,0:T(8,128)(2,1)} %refs_5_.1), channel_id=1, source_target_pairs={{0,1},{1,0},{2,3},{3,2},{4,5},{5,4},{6,7},{7,6},{8,9},{9,8},{10,11... | collective-permute-start | bytes 6291464 | tf_op jit(solution)/shard_map/ppermute | solution.py:457
  8.4 0.1 collective-permute-done.refs_1_
  8.6 2.9 %collective-permute-done.1.refs_1_ = bf16[144,128]{1,0:T(8,128)(2,1)S(1)} collective-permute-done((bf16[144,128]{1,0:T(8,128)(2,1)S(1)}, bf16[144,128]{1,0:T(8,128)(2,1)S(1)}, u32[]{:S(2)}, u32[]{:S(2)}) %collective-permute-start.1) | collective-permute-done | bytes 36896 | tf_op jit(solution)/shard_map/ppermute | solution.py:457
  11.5 0.0 collective-permute-done.3.refs_3_
  11.5 2.5 %collective-permute-start.7 = (bf16[576,128]{1,0:T(8,128)(2,1)S(1)}, bf16[576,128]{1,0:T(8,128)(2,1)S(1)}, u32[]{:S(2)}, u32[]{:S(2)}) collective-permute-start(bf16[576,128]{1,0:T(8,128)(2,1)S(1)} %shard_map.96.refs_0_), channel_id=1, source_target_pairs={{0,24},{8,16},{16,8},{24,0},{1,25},{9,17},{17,9},{25,1},{2,26},{10... | collective-permute-start | bytes 442376 | tf_op jit(solution)/shard_map/ppermute | solution.py:455
  14.1 0.5 %collective-permute-start.5 = (bf16[576,128]{1,0:T(8,128)(2,1)S(1)}, bf16[576,128]{1,0:T(8,128)(2,1)S(1)}, u32[]{:S(2)}, u32[]{:S(2)}) collective-permute-start(bf16[576,128]{1,0:T(8,128)(2,1)S(1)} %shard_map.96.refs_0_), channel_id=1, source_target_pairs={{0,16},{8,24},{16,0},{24,8},{1,17},{9,25},{17,1},{25,9},{2,18},{10... | collective-permute-start | bytes 442376 | tf_op jit(solution)/shard_map/ppermute | solution.py:455
  14.6 0.5 %collective-permute-start.6 = (bf16[576,128]{1,0:T(8,128)(2,1)S(1)}, bf16[576,128]{1,0:T(8,128)(2,1)S(1)}, u32[]{:S(2)}, u32[]{:S(2)}) collective-permute-start(bf16[576,128]{1,0:T(8,128)(2,1)S(1)} %shard_map.96.refs_0_), channel_id=1, source_target_pairs={{0,8},{8,0},{16,24},{24,16},{1,9},{9,1},{17,25},{25,17},{2,10},{10... | collective-permute-start | bytes 442376 | tf_op jit(solution)/shard_map/ppermute | solution.py:455
  15.1 2.9 %shard_map.97.refs_1_.refs_2_ = bf16[2048,512]{1,0:T(8,128)(2,1)S(1)} custom-call(bf16[2048,512]{1,0:T(8,128)(2,1)} %refs_5_.1, bf16[576,128]{1,0:T(8,128)(2,1)S(1)} %shard_map.96.refs_0_), custom_call_target="tpu_custom_call" | custom-call | flops 34359738368 | tf_op jit(solution)/shard_map/pallas_call | solution.py:23
  18.0 1.0 %shard_map.98.refs_2_.refs_3_ = bf16[2048,512]{1,0:T(8,128)(2,1)S(1)} custom-call(bf16[2048,512]{1,0:T(8,128)(2,1)S(1)} %collective-permute-done.4.memory_ref, bf16[576,128]{1,0:T(8,128)(2,1)S(1)} %shard_map.96.refs_0_), custom_call_target="tpu_custom_call" | custom-call | flops 34359738368 | tf_op jit(solution)/shard_map/pallas_call | solution.py:23
  19.0 0.3 collective-permute-done.7.refs_0_.refs_3_
  19.2 2.9 %shard_map.99.refs_6_ = bf16[1040,128]{1,0:T(8,128)(2,1)S(1)} custom-call(bf16[576,128]{1,0:T(8,128)(2,1)S(1)} %collective-permute-done.7.refs_0_.refs_3_, bf16[2048,512]{1,0:T(8,128)(2,1)S(1)} %shard_map.97.refs_1_.refs_2_, bf16[2048,512]{1,0:T(8,128)(2,1)S(1)} %shard_map.98.refs_2_.refs_3_, s32[1,2048]{1,0:T(1,128)S(1)} %bitcast.9, s32[1,2048]{1,0:T(1,128)S(1)} %bitcast.12), custom_call_target="tpu_custom_call" | custom-call | flops 3221225472 | tf_op jit(solution)/shard_map/pallas_call | solution.py:23
  22.1 0.0 copy-start.1
  22.1 2.3 %collective-permute-start.8 = (bf16[1040,128]{1,0:T(8,128)(2,1)S(1)}, bf16[1040,128]{1,0:T(8,128)(2,1)S(1)}, u32[]{:S(2)}, u32[]{:S(2)}) collective-permute-start(bf16[1040,128]{1,0:T(8,128)(2,1)S(1)} %shard_map.99.refs_6_), channel_id=1, source_target_pairs={{0,24},{8,16},{16,8},{24,0},{1,25},{9,17},{17,9},{25,1},{2,26},{10... | collective-permute-start | bytes 798728 | tf_op jit(solution)/shard_map/ppermute | solution.py:455
  24.4 4.2 %shard_map.100 = (bf16[1040,128]{1,0:T(8,128)(2,1)S(1)}, bf16[1040,128]{1,0:T(8,128)(2,1)S(1)}) custom-call(bf16[576,128]{1,0:T(8,128)(2,1)S(1)} %collective-permute-done.5.refs_0_.refs_2_, bf16[576,128]{1,0:T(8,128)(2,1)S(1)} %collective-permute-done.6.refs_1_, bf16[2048,512]{1,0:T(8,128)(2,1)S(1)} %shard_map.97.refs_1_.refs_2_, ...), custom_call_target="tpu_custom_call" | custom-call | flops 6442450944 | tf_op jit(solution)/shard_map/pallas_call | solution.py:23
  28.6 0.6 %collective-permute-start.10 = (bf16[1040,128]{1,0:T(8,128)(2,1)S(1)}, bf16[1040,128]{1,0:T(8,128)(2,1)S(1)}, u32[]{:S(2)}, u32[]{:S(2)}) collective-permute-start(bf16[1040,128]{1,0:T(8,128)(2,1)S(1)} %get-tuple-element.23.refs_7_.refs_5_), channel_id=1, source_target_pairs={{0,8},{8,0},{16,24},{24,16},{1,9},{9,1},{17,25},{25,17},{2,10},{10... | collective-permute-start | bytes 798728 | tf_op jit(solution)/shard_map/ppermute | solution.py:455
  29.2 0.7 %collective-permute-start.9 = (bf16[1040,128]{1,0:T(8,128)(2,1)S(1)}, bf16[1040,128]{1,0:T(8,128)(2,1)S(1)}, u32[]{:S(2)}, u32[]{:S(2)}) collective-permute-start(bf16[1040,128]{1,0:T(8,128)(2,1)S(1)} %get-tuple-element.22.refs_6_.refs_4_), channel_id=1, source_target_pairs={{0,16},{8,24},{16,0},{24,8},{1,17},{9,25},{17,1},{25,9},{2,18},{10... | collective-permute-start | bytes 798728 | tf_op jit(solution)/shard_map/ppermute | solution.py:455
  30.0 2.9 %shard_map.101 = (f32[1040,128]{1,0:T(8,128)S(1)}, bf16[2048,512]{1,0:T(8,128)(2,1)}) custom-call(bf16[576,128]{1,0:T(8,128)(2,1)S(1)} %shard_map.96.refs_0_, bf16[2048,512]{1,0:T(8,128)(2,1)S(1)} %shard_map.97.refs_1_.refs_2_, bf16[2048,512]{1,0:T(8,128)(2,1)S(1)} %shard_map.98.refs_2_.refs_3_, s32[1,2048]{1,0:T(1,128)S(1)} %bitcast.11, ...), custom_call_target="tpu_custom_call" | custom-call | flops 3221225472 | tf_op jit(solution)/shard_map/pallas_call | solution.py:23
  32.9 2.2 %collective-permute-done.10.refs_3_ = bf16[1040,128]{1,0:T(8,128)(2,1)S(1)} collective-permute-done((bf16[1040,128]{1,0:T(8,128)(2,1)S(1)}, bf16[1040,128]{1,0:T(8,128)(2,1)S(1)}, u32[]{:S(2)}, u32[]{:S(2)}) %collective-permute-start.10) | collective-permute-done | bytes 266272 | tf_op jit(solution)/shard_map/ppermute | solution.py:455
  35.1 0.5 %collective-permute-done.9.refs_2_ = bf16[1040,128]{1,0:T(8,128)(2,1)S(1)} collective-permute-done((bf16[1040,128]{1,0:T(8,128)(2,1)S(1)}, bf16[1040,128]{1,0:T(8,128)(2,1)S(1)}, u32[]{:S(2)}, u32[]{:S(2)}) %collective-permute-start.9) | collective-permute-done | bytes 266272 | tf_op jit(solution)/shard_map/ppermute | solution.py:455
  35.7 0.1 shard_map.103
  35.8 1.8 %collective-permute-start.12 = (bf16[272,128]{1,0:T(8,128)(2,1)S(1)}, bf16[272,128]{1,0:T(8,128)(2,1)S(1)}, u32[]{:S(2)}, u32[]{:S(2)}) collective-permute-start(bf16[272,128]{1,0:T(8,128)(2,1)S(1)} %get-tuple-element.26), channel_id=1, source_target_pairs={{0,6},{1,7},{2,4},{3,5},{4,2},{5,3},{6,0},{7,1},{8,14},{9,15},{10,... | collective-permute-start | bytes 208904 | tf_op jit(solution)/shard_map/ppermute | solution.py:457
  37.5 0.4 collective-permute-start.13
  37.9 2.3 %collective-permute-start.14 = (bf16[272,128]{1,0:T(8,128)(2,1)S(1)}, bf16[272,128]{1,0:T(8,128)(2,1)S(1)}, u32[]{:S(2)}, u32[]{:S(2)}) collective-permute-start(bf16[272,128]{1,0:T(8,128)(2,1)S(1)} %get-tuple-element.28), channel_id=1, source_target_pairs={{0,2},{1,3},{2,0},{3,1},{4,6},{5,7},{6,4},{7,5},{8,10},{9,11},{10,... | collective-permute-start | bytes 208904 | tf_op jit(solution)/shard_map/ppermute | solution.py:457
  40.2 1.2 %shard_map.105 = (bf16[2048,512]{1,0:T(8,128)(2,1)}, s32[16,128]{1,0:T(8,128)}) custom-call(s32[1]{0:T(128)S(6)} %copy.12.step_ref, bf16[2048,512]{1,0:T(8,128)(2,1)} %get-tuple-element.33.stored_ref, s32[16,128]{1,0:T(8,128)S(1)} %bitcast.8, bf16[144,128]{1,0:T(8,128)(2,1)S(1)} %shard_map.102.refs_4_.refs_0_, ...), custom_call_target="tpu_custom_call", output_to_operand_aliasing={{0}: (1, {})} | custom-call | tf_op jit(solution)/shard_map/pallas_call | solution.py:23
  41.5 0.5 %collective-permute-done.12.refs_1_ = bf16[272,128]{1,0:T(8,128)(2,1)S(1)} collective-permute-done((bf16[272,128]{1,0:T(8,128)(2,1)S(1)}, bf16[272,128]{1,0:T(8,128)(2,1)S(1)}, u32[]{:S(2)}, u32[]{:S(2)}) %collective-permute-start.12) | collective-permute-done | bytes 69664 | tf_op jit(solution)/shard_map/ppermute | solution.py:457
  42.0 1.5 %collective-permute-done.13.refs_2_ = bf16[272,128]{1,0:T(8,128)(2,1)S(1)} collective-permute-done((bf16[272,128]{1,0:T(8,128)(2,1)S(1)}, bf16[272,128]{1,0:T(8,128)(2,1)S(1)}, u32[]{:S(2)}, u32[]{:S(2)}) %collective-permute-start.13) | collective-permute-done | bytes 69664 | tf_op jit(solution)/shard_map/ppermute | solution.py:457
  43.5 0.9 %shard_map.104 = (f32[32,512]{1,0:T(8,128)}, f32[1,32]{1,0:T(1,128)}) custom-call(f32[272,128]{1,0:T(8,128)S(1)} %get-tuple-element.25.refs_0_, bf16[272,128]{1,0:T(8,128)(2,1)S(1)} %collective-permute-done.12.refs_1_, bf16[272,128]{1,0:T(8,128)(2,1)S(1)} %collective-permute-done.13.refs_2_, bf16[272,128]{1,0:T(8,128)(2,1)S(1)} %collective-permute-done.14.refs_3_, ...), custom_call_target="tpu_custom_call" | custom-call | tf_op jit(solution)/shard_map/pallas_call | solution.py:23
  (15 shorter events, 0.1 us)
Async XLA Ops:
  1.5 7.1 %collective-permute-start = (bf16[144,128]{1,0:T(8,128)(2,1)S(1)}, bf16[144,128]{1,0:T(8,128)(2,1)S(1)}, u32[]{:S(2)}, u32[]{:S(2)}) collective-permute-start(bf16[144,128]{1,0:T(8,128)(2,1)S(1)} %get-tuple-element.20.refs_0_), channel_id=1, source_target_pairs={{0,6},{1,7},{2,4},{3,5},{4,2},{5,3},{6,0},{7,1},{8,14},{9,15},{10,... | collective-permute-start | bytes 110600 | tf_op jit(solution)/shard_map/ppermute | solution.py:457
  6.6 4.9 %collective-permute-start.1 = (bf16[144,128]{1,0:T(8,128)(2,1)S(1)}, bf16[144,128]{1,0:T(8,128)(2,1)S(1)}, u32[]{:S(2)}, u32[]{:S(2)}) collective-permute-start(bf16[144,128]{1,0:T(8,128)(2,1)S(1)} %get-tuple-element.20.refs_0_), channel_id=1, source_target_pairs={{0,4},{1,5},{2,6},{3,7},{4,0},{5,1},{6,2},{7,3},{8,12},{9,13},{10,... | collective-permute-start | bytes 110600 | tf_op jit(solution)/shard_map/ppermute | solution.py:457
  6.6 4.9 %collective-permute-start.2 = (bf16[144,128]{1,0:T(8,128)(2,1)S(1)}, bf16[144,128]{1,0:T(8,128)(2,1)S(1)}, u32[]{:S(2)}, u32[]{:S(2)}) collective-permute-start(bf16[144,128]{1,0:T(8,128)(2,1)S(1)} %get-tuple-element.20.refs_0_), channel_id=1, source_target_pairs={{0,2},{1,3},{2,0},{3,1},{4,6},{5,7},{6,4},{7,5},{8,10},{9,11},{10,... | collective-permute-start | bytes 110600 | tf_op jit(solution)/shard_map/ppermute | solution.py:457
  7.3 4.2 %collective-permute-start.3 = (s32[16,128]{1,0:T(8,128)S(1)}, s32[16,128]{1,0:T(8,128)S(1)}, u32[]{:S(2)}, u32[]{:S(2)}) collective-permute-start(s32[16,128]{1,0:T(8,128)S(1)} %get-tuple-element.21.refs_2_), channel_id=1, source_target_pairs={{0,1},{1,0},{2,3},{3,2},{4,5},{5,4},{6,7},{7,6},{8,9},{9,8},{10,11... | collective-permute-start | bytes 24584 | tf_op jit(solution)/shard_map/ppermute | solution.py:457
  7.3 10.7 %collective-permute-start.4 = (bf16[2048,512]{1,0:T(8,128)(2,1)}, bf16[2048,512]{1,0:T(8,128)(2,1)S(1)}, u32[]{:S(2)}, u32[]{:S(2)}) collective-permute-start(bf16[2048,512]{1,0:T(8,128)(2,1)} %refs_5_.1), channel_id=1, source_target_pairs={{0,1},{1,0},{2,3},{3,2},{4,5},{5,4},{6,7},{7,6},{8,9},{9,8},{10,11... | collective-permute-start | bytes 6291464 | tf_op jit(solution)/shard_map/ppermute | solution.py:457
  11.5 7.7 %collective-permute-start.7 = (bf16[576,128]{1,0:T(8,128)(2,1)S(1)}, bf16[576,128]{1,0:T(8,128)(2,1)S(1)}, u32[]{:S(2)}, u32[]{:S(2)}) collective-permute-start(bf16[576,128]{1,0:T(8,128)(2,1)S(1)} %shard_map.96.refs_0_), channel_id=1, source_target_pairs={{0,24},{8,16},{16,8},{24,0},{1,25},{9,17},{17,9},{25,1},{2,26},{10... | collective-permute-start | bytes 442376 | tf_op jit(solution)/shard_map/ppermute | solution.py:455
  14.1 10.4 %collective-permute-start.5 = (bf16[576,128]{1,0:T(8,128)(2,1)S(1)}, bf16[576,128]{1,0:T(8,128)(2,1)S(1)}, u32[]{:S(2)}, u32[]{:S(2)}) collective-permute-start(bf16[576,128]{1,0:T(8,128)(2,1)S(1)} %shard_map.96.refs_0_), channel_id=1, source_target_pairs={{0,16},{8,24},{16,0},{24,8},{1,17},{9,25},{17,1},{25,9},{2,18},{10... | collective-permute-start | bytes 442376 | tf_op jit(solution)/shard_map/ppermute | solution.py:455
  14.6 9.9 %collective-permute-start.6 = (bf16[576,128]{1,0:T(8,128)(2,1)S(1)}, bf16[576,128]{1,0:T(8,128)(2,1)S(1)}, u32[]{:S(2)}, u32[]{:S(2)}) collective-permute-start(bf16[576,128]{1,0:T(8,128)(2,1)S(1)} %shard_map.96.refs_0_), channel_id=1, source_target_pairs={{0,8},{8,0},{16,24},{24,16},{1,9},{9,1},{17,25},{25,17},{2,10},{10... | collective-permute-start | bytes 442376 | tf_op jit(solution)/shard_map/ppermute | solution.py:455
  22.1 7.9 %copy-start.1 = (bf16[2048,512]{1,0:T(8,128)(2,1)S(1)}, bf16[2048,512]{1,0:T(8,128)(2,1)}, u32[]{:S(2)}) copy-start(bf16[2048,512]{1,0:T(8,128)(2,1)} %refs_5_.1) | copy-start | bytes 6291460
  22.1 13.5 %collective-permute-start.8 = (bf16[1040,128]{1,0:T(8,128)(2,1)S(1)}, bf16[1040,128]{1,0:T(8,128)(2,1)S(1)}, u32[]{:S(2)}, u32[]{:S(2)}) collective-permute-start(bf16[1040,128]{1,0:T(8,128)(2,1)S(1)} %shard_map.99.refs_6_), channel_id=1, source_target_pairs={{0,24},{8,16},{16,8},{24,0},{1,25},{9,17},{17,9},{25,1},{2,26},{10... | collective-permute-start | bytes 798728 | tf_op jit(solution)/shard_map/ppermute | solution.py:455
  28.6 6.5 %collective-permute-start.10 = (bf16[1040,128]{1,0:T(8,128)(2,1)S(1)}, bf16[1040,128]{1,0:T(8,128)(2,1)S(1)}, u32[]{:S(2)}, u32[]{:S(2)}) collective-permute-start(bf16[1040,128]{1,0:T(8,128)(2,1)S(1)} %get-tuple-element.23.refs_7_.refs_5_), channel_id=1, source_target_pairs={{0,8},{8,0},{16,24},{24,16},{1,9},{9,1},{17,25},{25,17},{2,10},{10... | collective-permute-start | bytes 798728 | tf_op jit(solution)/shard_map/ppermute | solution.py:455
  29.2 6.4 %collective-permute-start.9 = (bf16[1040,128]{1,0:T(8,128)(2,1)S(1)}, bf16[1040,128]{1,0:T(8,128)(2,1)S(1)}, u32[]{:S(2)}, u32[]{:S(2)}) collective-permute-start(bf16[1040,128]{1,0:T(8,128)(2,1)S(1)} %get-tuple-element.22.refs_6_.refs_4_), channel_id=1, source_target_pairs={{0,16},{8,24},{16,0},{24,8},{1,17},{9,25},{17,1},{25,9},{2,18},{10... | collective-permute-start | bytes 798728 | tf_op jit(solution)/shard_map/ppermute | solution.py:455
  30.0 10.3 %copy-start = (s32[2048]{0:T(1024)S(1)}, s32[2048]{0:T(1024)}, u32[]{:S(2)}) copy-start(s32[2048]{0:T(1024)} %param.9) | copy-start | bytes 24580
  30.0 2.9 %collective-permute-start.11 = (bf16[144,128]{1,0:T(8,128)(2,1)S(1)}, bf16[144,128]{1,0:T(8,128)(2,1)S(1)}, u32[]{:S(2)}, u32[]{:S(2)}) collective-permute-start(bf16[144,128]{1,0:T(8,128)(2,1)S(1)} %shard_map.102.refs_4_.refs_0_), channel_id=1, source_target_pairs={{0,1},{1,0},{2,3},{3,2},{4,5},{5,4},{6,7},{7,6},{8,9},{9,8},{10,11... | collective-permute-start | bytes 110600 | tf_op jit(solution)/shard_map/ppermute | solution.py:457
  35.8 6.2 %collective-permute-start.12 = (bf16[272,128]{1,0:T(8,128)(2,1)S(1)}, bf16[272,128]{1,0:T(8,128)(2,1)S(1)}, u32[]{:S(2)}, u32[]{:S(2)}) collective-permute-start(bf16[272,128]{1,0:T(8,128)(2,1)S(1)} %get-tuple-element.26), channel_id=1, source_target_pairs={{0,6},{1,7},{2,4},{3,5},{4,2},{5,3},{6,0},{7,1},{8,14},{9,15},{10,... | collective-permute-start | bytes 208904 | tf_op jit(solution)/shard_map/ppermute | solution.py:457
  37.5 6.0 %collective-permute-start.13 = (bf16[272,128]{1,0:T(8,128)(2,1)S(1)}, bf16[272,128]{1,0:T(8,128)(2,1)S(1)}, u32[]{:S(2)}, u32[]{:S(2)}) collective-permute-start(bf16[272,128]{1,0:T(8,128)(2,1)S(1)} %get-tuple-element.27), channel_id=1, source_target_pairs={{0,4},{1,5},{2,6},{3,7},{4,0},{5,1},{6,2},{7,3},{8,12},{9,13},{10,... | collective-permute-start | bytes 208904 | tf_op jit(solution)/shard_map/ppermute | solution.py:457
  37.9 5.6 %collective-permute-start.14 = (bf16[272,128]{1,0:T(8,128)(2,1)S(1)}, bf16[272,128]{1,0:T(8,128)(2,1)S(1)}, u32[]{:S(2)}, u32[]{:S(2)}) collective-permute-start(bf16[272,128]{1,0:T(8,128)(2,1)S(1)} %get-tuple-element.28), channel_id=1, source_target_pairs={{0,2},{1,3},{2,0},{3,1},{4,6},{5,7},{6,4},{7,5},{8,10},{9,11},{10,... | collective-permute-start | bytes 208904 | tf_op jit(solution)/shard_map/ppermute | solution.py:457

commit v19 on v18

--- a/solution.py
+++ b/solution.py
@@ -97,7 +97,7 @@
 
 def keys_of(memory, place, after):
     slots, width = memory.shape
-    block = math.gcd(512, slots)
+    block = math.gcd(256 if place == pltpu.HBM else 512, slots)
     spec = pl.BlockSpec((block, width), lambda i: (i, 0))
     return call(
         keys_kernel,

time: 44.6 us -> 46.4 us (1.040)
  Pallas kernels: 17 us -> 18.9 us
    pallas_call x13, Pallas kernels: 17 us -> 18.9 us  [call(): pl.pallas_call(body, out_shape=outs, compiler_params=pltpu.CompilerParams...]
  transfers between devices with their start and end apart: 15 -> 15, of which waited for: 7 -> 6; matrix products, arithmetic and copies ran while one was open for 0% -> 0% of each run, Pallas kernels for 34% -> 37%
where the time goes in v19:
time: 46.4 us; the launch traced here: 46.2 us
  Pallas kernels  18.9 us (41%)
  starting transfers between devices  17.9 us (39%)
  waiting for transfers between devices  7.99 us (17%)
  between operations  1.42 us (3%)
    pallas_call x13, Pallas kernels, call(): pl.pallas_call(body, out_shape=outs, compiler_params=pltpu.CompilerParams...  18.9 us
    ppermute x9, starting transfers between devices, exchange(): return lax.ppermute(value, 'dev', [(i, i ^ jump) for i in range(members)])  10.7 us
    ppermute x6, starting transfers between devices, exchange(): return lax.ppermute(value, 'grp', [(i, i ^ step) for i in range(groups)])  7.17 us
    ppermute x9, waiting for transfers between devices, exchange(): return lax.ppermute(value, 'dev', [(i, i ^ jump) for i in range(members)])  5.03 us
    ppermute x6, waiting for transfers between devices, exchange(): return lax.ppermute(value, 'grp', [(i, i ^ step) for i in range(groups)])  2.96 us
  transfers between devices with their start and end apart: 15, of which 6 were waited for; matrix products, arithmetic and copies ran while one was open for 0% of the time, Pallas kernels for 37%

profile of v19, /device:TPU:0, one launch (start us, length us, event | category | flops | bytes accessed | tf_op | source)
XLA Modules:
  0.0 46.2 jit_solution(9828755043524582087)
XLA Ops:
  0.6 0.9 %shard_map.93 = (bf16[144,128]{1,0:T(8,128)(2,1)S(1)}, f32[32,512]{1,0:T(8,128)S(1)}, f32[32,128]{1,0:T(8,128)S(1)}, s32[16,128]{1,0:T(8,128)S(1)}) custom-call(bf16[32,512]{1,0:T(8,128)(2,1)} %rows_ref.1, s32[1,32]{1,0:T(1,128)} %bitcast.16, s32[16,128]{1,0:T(8,128)} %bitcast.7, s32[16,128]{1,0:T(8,128)} %bitcast.15), custom_call_target="tpu_custom_call" | custom-call | tf_op jit(solution)/shard_map/pallas_call | solution.py:23
  1.5 5.1 %collective-permute-start = (bf16[144,128]{1,0:T(8,128)(2,1)S(1)}, bf16[144,128]{1,0:T(8,128)(2,1)S(1)}, u32[]{:S(2)}, u32[]{:S(2)}) collective-permute-start(bf16[144,128]{1,0:T(8,128)(2,1)S(1)} %get-tuple-element.20.refs_0_), channel_id=1, source_target_pairs={{0,6},{1,7},{2,4},{3,5},{4,2},{5,3},{6,0},{7,1},{8,14},{9,15},{10,... | collective-permute-start | bytes 110600 | tf_op jit(solution)/shard_map/ppermute | solution.py:457
  6.6 0.0 collective-permute-start.1
  6.6 0.6 %collective-permute-start.2 = (bf16[144,128]{1,0:T(8,128)(2,1)S(1)}, bf16[144,128]{1,0:T(8,128)(2,1)S(1)}, u32[]{:S(2)}, u32[]{:S(2)}) collective-permute-start(bf16[144,128]{1,0:T(8,128)(2,1)S(1)} %get-tuple-element.20.refs_0_), channel_id=1, source_target_pairs={{0,2},{1,3},{2,0},{3,1},{4,6},{5,7},{6,4},{7,5},{8,10},{9,11},{10,... | collective-permute-start | bytes 110600 | tf_op jit(solution)/shard_map/ppermute | solution.py:457
  7.3 0.0 collective-permute-start.3
  7.3 0.5 %collective-permute-start.4 = (bf16[2048,512]{1,0:T(8,128)(2,1)}, bf16[2048,512]{1,0:T(8,128)(2,1)S(1)}, u32[]{:S(2)}, u32[]{:S(2)}) collective-permute-start(bf16[2048,512]{1,0:T(8,128)(2,1)} %refs_5_.1), channel_id=1, source_target_pairs={{0,1},{1,0},{2,3},{3,2},{4,5},{5,4},{6,7},{7,6},{8,9},{9,8},{10,11... | collective-permute-start | bytes 6291464 | tf_op jit(solution)/shard_map/ppermute | solution.py:457
  8.4 0.1 collective-permute-done.refs_1_
  8.6 2.9 %collective-permute-done.1.refs_1_ = bf16[144,128]{1,0:T(8,128)(2,1)S(1)} collective-permute-done((bf16[144,128]{1,0:T(8,128)(2,1)S(1)}, bf16[144,128]{1,0:T(8,128)(2,1)S(1)}, u32[]{:S(2)}, u32[]{:S(2)}) %collective-permute-start.1) | collective-permute-done | bytes 36896 | tf_op jit(solution)/shard_map/ppermute | solution.py:457
  11.5 0.0 collective-permute-done.3.refs_3_
  11.5 2.5 %collective-permute-start.7 = (bf16[576,128]{1,0:T(8,128)(2,1)S(1)}, bf16[576,128]{1,0:T(8,128)(2,1)S(1)}, u32[]{:S(2)}, u32[]{:S(2)}) collective-permute-start(bf16[576,128]{1,0:T(8,128)(2,1)S(1)} %shard_map.96.refs_0_), channel_id=1, source_target_pairs={{0,24},{8,16},{16,8},{24,0},{1,25},{9,17},{17,9},{25,1},{2,26},{10... | collective-permute-start | bytes 442376 | tf_op jit(solution)/shard_map/ppermute | solution.py:455
  14.1 0.5 %collective-permute-start.5 = (bf16[576,128]{1,0:T(8,128)(2,1)S(1)}, bf16[576,128]{1,0:T(8,128)(2,1)S(1)}, u32[]{:S(2)}, u32[]{:S(2)}) collective-permute-start(bf16[576,128]{1,0:T(8,128)(2,1)S(1)} %shard_map.96.refs_0_), channel_id=1, source_target_pairs={{0,16},{8,24},{16,0},{24,8},{1,17},{9,25},{17,1},{25,9},{2,18},{10... | collective-permute-start | bytes 442376 | tf_op jit(solution)/shard_map/ppermute | solution.py:455
  14.6 0.5 %collective-permute-start.6 = (bf16[576,128]{1,0:T(8,128)(2,1)S(1)}, bf16[576,128]{1,0:T(8,128)(2,1)S(1)}, u32[]{:S(2)}, u32[]{:S(2)}) collective-permute-start(bf16[576,128]{1,0:T(8,128)(2,1)S(1)} %shard_map.96.refs_0_), channel_id=1, source_target_pairs={{0,8},{8,0},{16,24},{24,16},{1,9},{9,1},{17,25},{25,17},{2,10},{10... | collective-permute-start | bytes 442376 | tf_op jit(solution)/shard_map/ppermute | solution.py:455
  15.1 4.7 %shard_map.97.refs_1_.refs_2_ = bf16[2048,512]{1,0:T(8,128)(2,1)S(1)} custom-call(bf16[2048,512]{1,0:T(8,128)(2,1)} %refs_5_.1, bf16[576,128]{1,0:T(8,128)(2,1)S(1)} %shard_map.96.refs_0_), custom_call_target="tpu_custom_call" | custom-call | flops 34359738368 | tf_op jit(solution)/shard_map/pallas_call | solution.py:23
  19.8 1.0 %shard_map.98.refs_2_.refs_3_ = bf16[2048,512]{1,0:T(8,128)(2,1)S(1)} custom-call(bf16[2048,512]{1,0:T(8,128)(2,1)S(1)} %collective-permute-done.4.memory_ref, bf16[576,128]{1,0:T(8,128)(2,1)S(1)} %shard_map.96.refs_0_), custom_call_target="tpu_custom_call" | custom-call | flops 34359738368 | tf_op jit(solution)/shard_map/pallas_call | solution.py:23
  20.8 2.9 %shard_map.99.refs_6_ = bf16[1040,128]{1,0:T(8,128)(2,1)S(1)} custom-call(bf16[576,128]{1,0:T(8,128)(2,1)S(1)} %collective-permute-done.7.refs_0_.refs_3_, bf16[2048,512]{1,0:T(8,128)(2,1)S(1)} %shard_map.97.refs_1_.refs_2_, bf16[2048,512]{1,0:T(8,128)(2,1)S(1)} %shard_map.98.refs_2_.refs_3_, s32[1,2048]{1,0:T(1,128)S(1)} %bitcast.9, s32[1,2048]{1,0:T(1,128)S(1)} %bitcast.12), custom_call_target="tpu_custom_call" | custom-call | flops 3221225472 | tf_op jit(solution)/shard_map/pallas_call | solution.py:23
  23.7 0.0 copy-start.1
  23.7 2.5 %collective-permute-start.8 = (bf16[1040,128]{1,0:T(8,128)(2,1)S(1)}, bf16[1040,128]{1,0:T(8,128)(2,1)S(1)}, u32[]{:S(2)}, u32[]{:S(2)}) collective-permute-start(bf16[1040,128]{1,0:T(8,128)(2,1)S(1)} %shard_map.99.refs_6_), channel_id=1, source_target_pairs={{0,24},{8,16},{16,8},{24,0},{1,25},{9,17},{17,9},{25,1},{2,26},{10... | collective-permute-start | bytes 798728 | tf_op jit(solution)/shard_map/ppermute | solution.py:455
  26.3 4.2 %shard_map.100 = (bf16[1040,128]{1,0:T(8,128)(2,1)S(1)}, bf16[1040,128]{1,0:T(8,128)(2,1)S(1)}) custom-call(bf16[576,128]{1,0:T(8,128)(2,1)S(1)} %collective-permute-done.5.refs_0_.refs_2_, bf16[576,128]{1,0:T(8,128)(2,1)S(1)} %collective-permute-done.6.refs_1_, bf16[2048,512]{1,0:T(8,128)(2,1)S(1)} %shard_map.97.refs_1_.refs_2_, ...), custom_call_target="tpu_custom_call" | custom-call | flops 6442450944 | tf_op jit(solution)/shard_map/pallas_call | solution.py:23
  30.5 0.6 %collective-permute-start.10 = (bf16[1040,128]{1,0:T(8,128)(2,1)S(1)}, bf16[1040,128]{1,0:T(8,128)(2,1)S(1)}, u32[]{:S(2)}, u32[]{:S(2)}) collective-permute-start(bf16[1040,128]{1,0:T(8,128)(2,1)S(1)} %get-tuple-element.23.refs_7_.refs_5_), channel_id=1, source_target_pairs={{0,8},{8,0},{16,24},{24,16},{1,9},{9,1},{17,25},{25,17},{2,10},{10... | collective-permute-start | bytes 798728 | tf_op jit(solution)/shard_map/ppermute | solution.py:455
  31.1 0.5 %collective-permute-start.9 = (bf16[1040,128]{1,0:T(8,128)(2,1)S(1)}, bf16[1040,128]{1,0:T(8,128)(2,1)S(1)}, u32[]{:S(2)}, u32[]{:S(2)}) collective-permute-start(bf16[1040,128]{1,0:T(8,128)(2,1)S(1)} %get-tuple-element.22.refs_6_.refs_4_), channel_id=1, source_target_pairs={{0,16},{8,24},{16,0},{24,8},{1,17},{9,25},{17,1},{25,9},{2,18},{10... | collective-permute-start | bytes 798728 | tf_op jit(solution)/shard_map/ppermute | solution.py:455
  31.6 2.9 %shard_map.101 = (f32[1040,128]{1,0:T(8,128)S(1)}, bf16[2048,512]{1,0:T(8,128)(2,1)}) custom-call(bf16[576,128]{1,0:T(8,128)(2,1)S(1)} %shard_map.96.refs_0_, bf16[2048,512]{1,0:T(8,128)(2,1)S(1)} %shard_map.97.refs_1_.refs_2_, bf16[2048,512]{1,0:T(8,128)(2,1)S(1)} %shard_map.98.refs_2_.refs_3_, s32[1,2048]{1,0:T(1,128)S(1)} %bitcast.11, ...), custom_call_target="tpu_custom_call" | custom-call | flops 3221225472 | tf_op jit(solution)/shard_map/pallas_call | solution.py:23
  34.5 2.4 %collective-permute-done.10.refs_3_ = bf16[1040,128]{1,0:T(8,128)(2,1)S(1)} collective-permute-done((bf16[1040,128]{1,0:T(8,128)(2,1)S(1)}, bf16[1040,128]{1,0:T(8,128)(2,1)S(1)}, u32[]{:S(2)}, u32[]{:S(2)}) %collective-permute-start.10) | collective-permute-done | bytes 266272 | tf_op jit(solution)/shard_map/ppermute | solution.py:455
  37.0 0.5 %collective-permute-done.9.refs_2_ = bf16[1040,128]{1,0:T(8,128)(2,1)S(1)} collective-permute-done((bf16[1040,128]{1,0:T(8,128)(2,1)S(1)}, bf16[1040,128]{1,0:T(8,128)(2,1)S(1)}, u32[]{:S(2)}, u32[]{:S(2)}) %collective-permute-start.9) | collective-permute-done | bytes 266272 | tf_op jit(solution)/shard_map/ppermute | solution.py:455
  37.5 0.1 shard_map.103
  37.6 1.5 %collective-permute-start.12 = (bf16[272,128]{1,0:T(8,128)(2,1)S(1)}, bf16[272,128]{1,0:T(8,128)(2,1)S(1)}, u32[]{:S(2)}, u32[]{:S(2)}) collective-permute-start(bf16[272,128]{1,0:T(8,128)(2,1)S(1)} %get-tuple-element.26), channel_id=1, source_target_pairs={{0,6},{1,7},{2,4},{3,5},{4,2},{5,3},{6,0},{7,1},{8,14},{9,15},{10,... | collective-permute-start | bytes 208904 | tf_op jit(solution)/shard_map/ppermute | solution.py:457
  39.1 0.6 %collective-permute-start.13 = (bf16[272,128]{1,0:T(8,128)(2,1)S(1)}, bf16[272,128]{1,0:T(8,128)(2,1)S(1)}, u32[]{:S(2)}, u32[]{:S(2)}) collective-permute-start(bf16[272,128]{1,0:T(8,128)(2,1)S(1)} %get-tuple-element.27), channel_id=1, source_target_pairs={{0,4},{1,5},{2,6},{3,7},{4,0},{5,1},{6,2},{7,3},{8,12},{9,13},{10,... | collective-permute-start | bytes 208904 | tf_op jit(solution)/shard_map/ppermute | solution.py:457
  39.8 2.3 %collective-permute-start.14 = (bf16[272,128]{1,0:T(8,128)(2,1)S(1)}, bf16[272,128]{1,0:T(8,128)(2,1)S(1)}, u32[]{:S(2)}, u32[]{:S(2)}) collective-permute-start(bf16[272,128]{1,0:T(8,128)(2,1)S(1)} %get-tuple-element.28), channel_id=1, source_target_pairs={{0,2},{1,3},{2,0},{3,1},{4,6},{5,7},{6,4},{7,5},{8,10},{9,11},{10,... | collective-permute-start | bytes 208904 | tf_op jit(solution)/shard_map/ppermute | solution.py:457
  42.1 1.2 %shard_map.105 = (bf16[2048,512]{1,0:T(8,128)(2,1)}, s32[16,128]{1,0:T(8,128)}) custom-call(s32[1]{0:T(128)S(6)} %copy.12.step_ref, bf16[2048,512]{1,0:T(8,128)(2,1)} %get-tuple-element.33.stored_ref, s32[16,128]{1,0:T(8,128)S(1)} %bitcast.8, bf16[144,128]{1,0:T(8,128)(2,1)S(1)} %shard_map.102.refs_4_.refs_0_, ...), custom_call_target="tpu_custom_call", output_to_operand_aliasing={{0}: (1, {})} | custom-call | tf_op jit(solution)/shard_map/pallas_call | solution.py:23
  43.3 0.5 %collective-permute-done.12.refs_1_ = bf16[272,128]{1,0:T(8,128)(2,1)S(1)} collective-permute-done((bf16[272,128]{1,0:T(8,128)(2,1)S(1)}, bf16[272,128]{1,0:T(8,128)(2,1)S(1)}, u32[]{:S(2)}, u32[]{:S(2)}) %collective-permute-start.12) | collective-permute-done | bytes 69664 | tf_op jit(solution)/shard_map/ppermute | solution.py:457
  43.8 1.5 %collective-permute-done.13.refs_2_ = bf16[272,128]{1,0:T(8,128)(2,1)S(1)} collective-permute-done((bf16[272,128]{1,0:T(8,128)(2,1)S(1)}, bf16[272,128]{1,0:T(8,128)(2,1)S(1)}, u32[]{:S(2)}, u32[]{:S(2)}) %collective-permute-start.13) | collective-permute-done | bytes 69664 | tf_op jit(solution)/shard_map/ppermute | solution.py:457
  45.3 0.0 collective-permute-done.14.refs_3_
  45.3 0.9 %shard_map.104 = (f32[32,512]{1,0:T(8,128)}, f32[1,32]{1,0:T(1,128)}) custom-call(f32[272,128]{1,0:T(8,128)S(1)} %get-tuple-element.25.refs_0_, bf16[272,128]{1,0:T(8,128)(2,1)S(1)} %collective-permute-done.12.refs_1_, bf16[272,128]{1,0:T(8,128)(2,1)S(1)} %collective-permute-done.13.refs_2_, bf16[272,128]{1,0:T(8,128)(2,1)S(1)} %collective-permute-done.14.refs_3_, ...), custom_call_target="tpu_custom_call" | custom-call | tf_op jit(solution)/shard_map/pallas_call | solution.py:23
  (15 shorter events, 0.1 us)
Async XLA Ops:
  1.5 7.1 %collective-permute-start = (bf16[144,128]{1,0:T(8,128)(2,1)S(1)}, bf16[144,128]{1,0:T(8,128)(2,1)S(1)}, u32[]{:S(2)}, u32[]{:S(2)}) collective-permute-start(bf16[144,128]{1,0:T(8,128)(2,1)S(1)} %get-tuple-element.20.refs_0_), channel_id=1, source_target_pairs={{0,6},{1,7},{2,4},{3,5},{4,2},{5,3},{6,0},{7,1},{8,14},{9,15},{10,... | collective-permute-start | bytes 110600 | tf_op jit(solution)/shard_map/ppermute | solution.py:457
  6.6 4.9 %collective-permute-start.1 = (bf16[144,128]{1,0:T(8,128)(2,1)S(1)}, bf16[144,128]{1,0:T(8,128)(2,1)S(1)}, u32[]{:S(2)}, u32[]{:S(2)}) collective-permute-start(bf16[144,128]{1,0:T(8,128)(2,1)S(1)} %get-tuple-element.20.refs_0_), channel_id=1, source_target_pairs={{0,4},{1,5},{2,6},{3,7},{4,0},{5,1},{6,2},{7,3},{8,12},{9,13},{10,... | collective-permute-start | bytes 110600 | tf_op jit(solution)/shard_map/ppermute | solution.py:457
  6.6 4.9 %collective-permute-start.2 = (bf16[144,128]{1,0:T(8,128)(2,1)S(1)}, bf16[144,128]{1,0:T(8,128)(2,1)S(1)}, u32[]{:S(2)}, u32[]{:S(2)}) collective-permute-start(bf16[144,128]{1,0:T(8,128)(2,1)S(1)} %get-tuple-element.20.refs_0_), channel_id=1, source_target_pairs={{0,2},{1,3},{2,0},{3,1},{4,6},{5,7},{6,4},{7,5},{8,10},{9,11},{10,... | collective-permute-start | bytes 110600 | tf_op jit(solution)/shard_map/ppermute | solution.py:457
  7.3 4.2 %collective-permute-start.3 = (s32[16,128]{1,0:T(8,128)S(1)}, s32[16,128]{1,0:T(8,128)S(1)}, u32[]{:S(2)}, u32[]{:S(2)}) collective-permute-start(s32[16,128]{1,0:T(8,128)S(1)} %get-tuple-element.21.refs_2_), channel_id=1, source_target_pairs={{0,1},{1,0},{2,3},{3,2},{4,5},{5,4},{6,7},{7,6},{8,9},{9,8},{10,11... | collective-permute-start | bytes 24584 | tf_op jit(solution)/shard_map/ppermute | solution.py:457
  7.3 12.5 %collective-permute-start.4 = (bf16[2048,512]{1,0:T(8,128)(2,1)}, bf16[2048,512]{1,0:T(8,128)(2,1)S(1)}, u32[]{:S(2)}, u32[]{:S(2)}) collective-permute-start(bf16[2048,512]{1,0:T(8,128)(2,1)} %refs_5_.1), channel_id=1, source_target_pairs={{0,1},{1,0},{2,3},{3,2},{4,5},{5,4},{6,7},{7,6},{8,9},{9,8},{10,11... | collective-permute-start | bytes 6291464 | tf_op jit(solution)/shard_map/ppermute | solution.py:457
  11.5 9.3 %collective-permute-start.7 = (bf16[576,128]{1,0:T(8,128)(2,1)S(1)}, bf16[576,128]{1,0:T(8,128)(2,1)S(1)}, u32[]{:S(2)}, u32[]{:S(2)}) collective-permute-start(bf16[576,128]{1,0:T(8,128)(2,1)S(1)} %shard_map.96.refs_0_), channel_id=1, source_target_pairs={{0,24},{8,16},{16,8},{24,0},{1,25},{9,17},{17,9},{25,1},{2,26},{10... | collective-permute-start | bytes 442376 | tf_op jit(solution)/shard_map/ppermute | solution.py:455
  14.1 12.2 %collective-permute-start.5 = (bf16[576,128]{1,0:T(8,128)(2,1)S(1)}, bf16[576,128]{1,0:T(8,128)(2,1)S(1)}, u32[]{:S(2)}, u32[]{:S(2)}) collective-permute-start(bf16[576,128]{1,0:T(8,128)(2,1)S(1)} %shard_map.96.refs_0_), channel_id=1, source_target_pairs={{0,16},{8,24},{16,0},{24,8},{1,17},{9,25},{17,1},{25,9},{2,18},{10... | collective-permute-start | bytes 442376 | tf_op jit(solution)/shard_map/ppermute | solution.py:455
  14.6 11.7 %collective-permute-start.6 = (bf16[576,128]{1,0:T(8,128)(2,1)S(1)}, bf16[576,128]{1,0:T(8,128)(2,1)S(1)}, u32[]{:S(2)}, u32[]{:S(2)}) collective-permute-start(bf16[576,128]{1,0:T(8,128)(2,1)S(1)} %shard_map.96.refs_0_), channel_id=1, source_target_pairs={{0,8},{8,0},{16,24},{24,16},{1,9},{9,1},{17,25},{25,17},{2,10},{10... | collective-permute-start | bytes 442376 | tf_op jit(solution)/shard_map/ppermute | solution.py:455
  23.7 7.9 %copy-start.1 = (bf16[2048,512]{1,0:T(8,128)(2,1)S(1)}, bf16[2048,512]{1,0:T(8,128)(2,1)}, u32[]{:S(2)}) copy-start(bf16[2048,512]{1,0:T(8,128)(2,1)} %refs_5_.1) | copy-start | bytes 6291460
  23.7 13.8 %collective-permute-start.8 = (bf16[1040,128]{1,0:T(8,128)(2,1)S(1)}, bf16[1040,128]{1,0:T(8,128)(2,1)S(1)}, u32[]{:S(2)}, u32[]{:S(2)}) collective-permute-start(bf16[1040,128]{1,0:T(8,128)(2,1)S(1)} %shard_map.99.refs_6_), channel_id=1, source_target_pairs={{0,24},{8,16},{16,8},{24,0},{1,25},{9,17},{17,9},{25,1},{2,26},{10... | collective-permute-start | bytes 798728 | tf_op jit(solution)/shard_map/ppermute | solution.py:455
  30.5 6.5 %collective-permute-start.10 = (bf16[1040,128]{1,0:T(8,128)(2,1)S(1)}, bf16[1040,128]{1,0:T(8,128)(2,1)S(1)}, u32[]{:S(2)}, u32[]{:S(2)}) collective-permute-start(bf16[1040,128]{1,0:T(8,128)(2,1)S(1)} %get-tuple-element.23.refs_7_.refs_5_), channel_id=1, source_target_pairs={{0,8},{8,0},{16,24},{24,16},{1,9},{9,1},{17,25},{25,17},{2,10},{10... | collective-permute-start | bytes 798728 | tf_op jit(solution)/shard_map/ppermute | solution.py:455
  31.1 6.4 %collective-permute-start.9 = (bf16[1040,128]{1,0:T(8,128)(2,1)S(1)}, bf16[1040,128]{1,0:T(8,128)(2,1)S(1)}, u32[]{:S(2)}, u32[]{:S(2)}) collective-permute-start(bf16[1040,128]{1,0:T(8,128)(2,1)S(1)} %get-tuple-element.22.refs_6_.refs_4_), channel_id=1, source_target_pairs={{0,16},{8,24},{16,0},{24,8},{1,17},{9,25},{17,1},{25,9},{2,18},{10... | collective-permute-start | bytes 798728 | tf_op jit(solution)/shard_map/ppermute | solution.py:455
  31.6 10.5 %copy-start = (s32[2048]{0:T(1024)S(1)}, s32[2048]{0:T(1024)}, u32[]{:S(2)}) copy-start(s32[2048]{0:T(1024)} %param.9) | copy-start | bytes 24580
  31.6 2.9 %collective-permute-start.11 = (bf16[144,128]{1,0:T(8,128)(2,1)S(1)}, bf16[144,128]{1,0:T(8,128)(2,1)S(1)}, u32[]{:S(2)}, u32[]{:S(2)}) collective-permute-start(bf16[144,128]{1,0:T(8,128)(2,1)S(1)} %shard_map.102.refs_4_.refs_0_), channel_id=1, source_target_pairs={{0,1},{1,0},{2,3},{3,2},{4,5},{5,4},{6,7},{7,6},{8,9},{9,8},{10,11... | collective-permute-start | bytes 110600 | tf_op jit(solution)/shard_map/ppermute | solution.py:457
  37.6 6.2 %collective-permute-start.12 = (bf16[272,128]{1,0:T(8,128)(2,1)S(1)}, bf16[272,128]{1,0:T(8,128)(2,1)S(1)}, u32[]{:S(2)}, u32[]{:S(2)}) collective-permute-start(bf16[272,128]{1,0:T(8,128)(2,1)S(1)} %get-tuple-element.26), channel_id=1, source_target_pairs={{0,6},{1,7},{2,4},{3,5},{4,2},{5,3},{6,0},{7,1},{8,14},{9,15},{10,... | collective-permute-start | bytes 208904 | tf_op jit(solution)/shard_map/ppermute | solution.py:457
  39.1 6.2 %collective-permute-start.13 = (bf16[272,128]{1,0:T(8,128)(2,1)S(1)}, bf16[272,128]{1,0:T(8,128)(2,1)S(1)}, u32[]{:S(2)}, u32[]{:S(2)}) collective-permute-start(bf16[272,128]{1,0:T(8,128)(2,1)S(1)} %get-tuple-element.27), channel_id=1, source_target_pairs={{0,4},{1,5},{2,6},{3,7},{4,0},{5,1},{6,2},{7,3},{8,12},{9,13},{10,... | collective-permute-start | bytes 208904 | tf_op jit(solution)/shard_map/ppermute | solution.py:457
  39.8 5.5 %collective-permute-start.14 = (bf16[272,128]{1,0:T(8,128)(2,1)S(1)}, bf16[272,128]{1,0:T(8,128)(2,1)S(1)}, u32[]{:S(2)}, u32[]{:S(2)}) collective-permute-start(bf16[272,128]{1,0:T(8,128)(2,1)S(1)} %get-tuple-element.28), channel_id=1, source_target_pairs={{0,2},{1,3},{2,0},{3,1},{4,6},{5,7},{6,4},{7,5},{8,10},{9,11},{10,... | collective-permute-start | bytes 208904 | tf_op jit(solution)/shard_map/ppermute | solution.py:457

commit v20 on v19

--- a/solution.py
+++ b/solution.py
@@ -97,7 +97,7 @@
 
 def keys_of(memory, place, after):
     slots, width = memory.shape
-    block = math.gcd(256 if place == pltpu.HBM else 512, slots)
+    block = math.gcd(1024, slots)
     spec = pl.BlockSpec((block, width), lambda i: (i, 0))
     return call(
         keys_kernel,

time: 46.4 us -> 44.6 us (0.961)
  Pallas kernels: 18.9 us -> 16.4 us
  waiting for transfers between devices: 7.99 us -> 8.64 us
    pallas_call x13, Pallas kernels: 18.9 us -> 16.4 us  [call(): pl.pallas_call(body, out_shape=outs, compiler_params=pltpu.CompilerParams...]
  transfers between devices with their start and end apart: 15 -> 15, of which waited for: 6 -> 7; matrix products, arithmetic and copies ran while one was open for 0% -> 0% of each run, Pallas kernels for 37% -> 33%
where the time goes in v20:
time: 44.6 us; the launch traced here: 44.4 us
  starting transfers between devices  17.9 us (40%)
  Pallas kernels  16.4 us (37%)
  waiting for transfers between devices  8.64 us (19%)
  between operations  1.41 us (3%)
    pallas_call x13, Pallas kernels, call(): pl.pallas_call(body, out_shape=outs, compiler_params=pltpu.CompilerParams...  16.4 us
    ppermute x9, starting transfers between devices, exchange(): return lax.ppermute(value, 'dev', [(i, i ^ jump) for i in range(members)])  10.7 us
    ppermute x6, starting transfers between devices, exchange(): return lax.ppermute(value, 'grp', [(i, i ^ step) for i in range(groups)])  7.18 us
    ppermute x9, waiting for transfers between devices, exchange(): return lax.ppermute(value, 'dev', [(i, i ^ jump) for i in range(members)])  5.36 us
    ppermute x6, waiting for transfers between devices, exchange(): return lax.ppermute(value, 'grp', [(i, i ^ step) for i in range(groups)])  3.28 us
  transfers between devices with their start and end apart: 15, of which 7 were waited for; matrix products, arithmetic and copies ran while one was open for 0% of the time, Pallas kernels for 33%

profile of v20, /device:TPU:0, one launch (start us, length us, event | category | flops | bytes accessed | tf_op | source)
XLA Modules:
  0.0 44.4 jit_solution(10053639664843588062)
XLA Ops:
  0.6 0.9 %shard_map.93 = (bf16[144,128]{1,0:T(8,128)(2,1)S(1)}, f32[32,512]{1,0:T(8,128)S(1)}, f32[32,128]{1,0:T(8,128)S(1)}, s32[16,128]{1,0:T(8,128)S(1)}) custom-call(bf16[32,512]{1,0:T(8,128)(2,1)} %rows_ref.1, s32[1,32]{1,0:T(1,128)} %bitcast.16, s32[16,128]{1,0:T(8,128)} %bitcast.7, s32[16,128]{1,0:T(8,128)} %bitcast.15), custom_call_target="tpu_custom_call" | custom-call | tf_op jit(solution)/shard_map/pallas_call | solution.py:23
  1.5 5.1 %collective-permute-start = (bf16[144,128]{1,0:T(8,128)(2,1)S(1)}, bf16[144,128]{1,0:T(8,128)(2,1)S(1)}, u32[]{:S(2)}, u32[]{:S(2)}) collective-permute-start(bf16[144,128]{1,0:T(8,128)(2,1)S(1)} %get-tuple-element.20.refs_0_), channel_id=1, source_target_pairs={{0,6},{1,7},{2,4},{3,5},{4,2},{5,3},{6,0},{7,1},{8,14},{9,15},{10,... | collective-permute-start | bytes 110600 | tf_op jit(solution)/shard_map/ppermute | solution.py:457
  6.6 0.0 collective-permute-start.1
  6.6 0.6 %collective-permute-start.2 = (bf16[144,128]{1,0:T(8,128)(2,1)S(1)}, bf16[144,128]{1,0:T(8,128)(2,1)S(1)}, u32[]{:S(2)}, u32[]{:S(2)}) collective-permute-start(bf16[144,128]{1,0:T(8,128)(2,1)S(1)} %get-tuple-element.20.refs_0_), channel_id=1, source_target_pairs={{0,2},{1,3},{2,0},{3,1},{4,6},{5,7},{6,4},{7,5},{8,10},{9,11},{10,... | collective-permute-start | bytes 110600 | tf_op jit(solution)/shard_map/ppermute | solution.py:457
  7.3 0.0 collective-permute-start.3
  7.3 0.5 %collective-permute-start.4 = (bf16[2048,512]{1,0:T(8,128)(2,1)}, bf16[2048,512]{1,0:T(8,128)(2,1)S(1)}, u32[]{:S(2)}, u32[]{:S(2)}) collective-permute-start(bf16[2048,512]{1,0:T(8,128)(2,1)} %refs_5_.1), channel_id=1, source_target_pairs={{0,1},{1,0},{2,3},{3,2},{4,5},{5,4},{6,7},{7,6},{8,9},{9,8},{10,11... | collective-permute-start | bytes 6291464 | tf_op jit(solution)/shard_map/ppermute | solution.py:457
  8.4 0.1 collective-permute-done.refs_1_
  8.6 2.9 %collective-permute-done.1.refs_1_ = bf16[144,128]{1,0:T(8,128)(2,1)S(1)} collective-permute-done((bf16[144,128]{1,0:T(8,128)(2,1)S(1)}, bf16[144,128]{1,0:T(8,128)(2,1)S(1)}, u32[]{:S(2)}, u32[]{:S(2)}) %collective-permute-start.1) | collective-permute-done | bytes 36896 | tf_op jit(solution)/shard_map/ppermute | solution.py:457
  11.5 0.0 collective-permute-done.3.refs_3_
  11.5 2.5 %collective-permute-start.7 = (bf16[576,128]{1,0:T(8,128)(2,1)S(1)}, bf16[576,128]{1,0:T(8,128)(2,1)S(1)}, u32[]{:S(2)}, u32[]{:S(2)}) collective-permute-start(bf16[576,128]{1,0:T(8,128)(2,1)S(1)} %shard_map.96.refs_0_), channel_id=1, source_target_pairs={{0,24},{8,16},{16,8},{24,0},{1,25},{9,17},{17,9},{25,1},{2,26},{10... | collective-permute-start | bytes 442376 | tf_op jit(solution)/shard_map/ppermute | solution.py:455
  14.1 0.5 %collective-permute-start.5 = (bf16[576,128]{1,0:T(8,128)(2,1)S(1)}, bf16[576,128]{1,0:T(8,128)(2,1)S(1)}, u32[]{:S(2)}, u32[]{:S(2)}) collective-permute-start(bf16[576,128]{1,0:T(8,128)(2,1)S(1)} %shard_map.96.refs_0_), channel_id=1, source_target_pairs={{0,16},{8,24},{16,0},{24,8},{1,17},{9,25},{17,1},{25,9},{2,18},{10... | collective-permute-start | bytes 442376 | tf_op jit(solution)/shard_map/ppermute | solution.py:455
  14.6 0.5 %collective-permute-start.6 = (bf16[576,128]{1,0:T(8,128)(2,1)S(1)}, bf16[576,128]{1,0:T(8,128)(2,1)S(1)}, u32[]{:S(2)}, u32[]{:S(2)}) collective-permute-start(bf16[576,128]{1,0:T(8,128)(2,1)S(1)} %shard_map.96.refs_0_), channel_id=1, source_target_pairs={{0,8},{8,0},{16,24},{24,16},{1,9},{9,1},{17,25},{25,17},{2,10},{10... | collective-permute-start | bytes 442376 | tf_op jit(solution)/shard_map/ppermute | solution.py:455
  15.1 2.2 %shard_map.97.refs_1_.refs_2_ = bf16[2048,512]{1,0:T(8,128)(2,1)S(1)} custom-call(bf16[2048,512]{1,0:T(8,128)(2,1)} %refs_5_.1, bf16[576,128]{1,0:T(8,128)(2,1)S(1)} %shard_map.96.refs_0_), custom_call_target="tpu_custom_call" | custom-call | flops 34359738368 | tf_op jit(solution)/shard_map/pallas_call | solution.py:23
  17.4 1.0 %shard_map.98.refs_2_.refs_3_ = bf16[2048,512]{1,0:T(8,128)(2,1)S(1)} custom-call(bf16[2048,512]{1,0:T(8,128)(2,1)S(1)} %collective-permute-done.4.memory_ref, bf16[576,128]{1,0:T(8,128)(2,1)S(1)} %shard_map.96.refs_0_), custom_call_target="tpu_custom_call" | custom-call | flops 34359738368 | tf_op jit(solution)/shard_map/pallas_call | solution.py:23
  18.4 0.8 %collective-permute-done.7.refs_0_.refs_3_ = bf16[576,128]{1,0:T(8,128)(2,1)S(1)} collective-permute-done((bf16[576,128]{1,0:T(8,128)(2,1)S(1)}, bf16[576,128]{1,0:T(8,128)(2,1)S(1)}, u32[]{:S(2)}, u32[]{:S(2)}) %collective-permute-start.7) | collective-permute-done | bytes 147488 | tf_op jit(solution)/shard_map/ppermute | solution.py:455
  19.2 2.9 %shard_map.99.refs_6_ = bf16[1040,128]{1,0:T(8,128)(2,1)S(1)} custom-call(bf16[576,128]{1,0:T(8,128)(2,1)S(1)} %collective-permute-done.7.refs_0_.refs_3_, bf16[2048,512]{1,0:T(8,128)(2,1)S(1)} %shard_map.97.refs_1_.refs_2_, bf16[2048,512]{1,0:T(8,128)(2,1)S(1)} %shard_map.98.refs_2_.refs_3_, s32[1,2048]{1,0:T(1,128)S(1)} %bitcast.9, s32[1,2048]{1,0:T(1,128)S(1)} %bitcast.12), custom_call_target="tpu_custom_call" | custom-call | flops 3221225472 | tf_op jit(solution)/shard_map/pallas_call | solution.py:23
  22.1 0.0 copy-start.1
  22.1 1.7 %collective-permute-start.8 = (bf16[1040,128]{1,0:T(8,128)(2,1)S(1)}, bf16[1040,128]{1,0:T(8,128)(2,1)S(1)}, u32[]{:S(2)}, u32[]{:S(2)}) collective-permute-start(bf16[1040,128]{1,0:T(8,128)(2,1)S(1)} %shard_map.99.refs_6_), channel_id=1, source_target_pairs={{0,24},{8,16},{16,8},{24,0},{1,25},{9,17},{17,9},{25,1},{2,26},{10... | collective-permute-start | bytes 798728 | tf_op jit(solution)/shard_map/ppermute | solution.py:455
  23.8 4.2 %shard_map.100 = (bf16[1040,128]{1,0:T(8,128)(2,1)S(1)}, bf16[1040,128]{1,0:T(8,128)(2,1)S(1)}) custom-call(bf16[576,128]{1,0:T(8,128)(2,1)S(1)} %collective-permute-done.5.refs_0_.refs_2_, bf16[576,128]{1,0:T(8,128)(2,1)S(1)} %collective-permute-done.6.refs_1_, bf16[2048,512]{1,0:T(8,128)(2,1)S(1)} %shard_map.97.refs_1_.refs_2_, ...), custom_call_target="tpu_custom_call" | custom-call | flops 6442450944 | tf_op jit(solution)/shard_map/pallas_call | solution.py:23
  28.0 0.6 %collective-permute-start.10 = (bf16[1040,128]{1,0:T(8,128)(2,1)S(1)}, bf16[1040,128]{1,0:T(8,128)(2,1)S(1)}, u32[]{:S(2)}, u32[]{:S(2)}) collective-permute-start(bf16[1040,128]{1,0:T(8,128)(2,1)S(1)} %get-tuple-element.23.refs_7_.refs_5_), channel_id=1, source_target_pairs={{0,8},{8,0},{16,24},{24,16},{1,9},{9,1},{17,25},{25,17},{2,10},{10... | collective-permute-start | bytes 798728 | tf_op jit(solution)/shard_map/ppermute | solution.py:455
  28.6 1.3 %collective-permute-start.9 = (bf16[1040,128]{1,0:T(8,128)(2,1)S(1)}, bf16[1040,128]{1,0:T(8,128)(2,1)S(1)}, u32[]{:S(2)}, u32[]{:S(2)}) collective-permute-start(bf16[1040,128]{1,0:T(8,128)(2,1)S(1)} %get-tuple-element.22.refs_6_.refs_4_), channel_id=1, source_target_pairs={{0,16},{8,24},{16,0},{24,8},{1,17},{9,25},{17,1},{25,9},{2,18},{10... | collective-permute-start | bytes 798728 | tf_op jit(solution)/shard_map/ppermute | solution.py:455
  30.0 2.9 %shard_map.101 = (f32[1040,128]{1,0:T(8,128)S(1)}, bf16[2048,512]{1,0:T(8,128)(2,1)}) custom-call(bf16[576,128]{1,0:T(8,128)(2,1)S(1)} %shard_map.96.refs_0_, bf16[2048,512]{1,0:T(8,128)(2,1)S(1)} %shard_map.97.refs_1_.refs_2_, bf16[2048,512]{1,0:T(8,128)(2,1)S(1)} %shard_map.98.refs_2_.refs_3_, s32[1,2048]{1,0:T(1,128)S(1)} %bitcast.11, ...), custom_call_target="tpu_custom_call" | custom-call | flops 3221225472 | tf_op jit(solution)/shard_map/pallas_call | solution.py:23
  32.9 1.6 %collective-permute-done.10.refs_3_ = bf16[1040,128]{1,0:T(8,128)(2,1)S(1)} collective-permute-done((bf16[1040,128]{1,0:T(8,128)(2,1)S(1)}, bf16[1040,128]{1,0:T(8,128)(2,1)S(1)}, u32[]{:S(2)}, u32[]{:S(2)}) %collective-permute-start.10) | collective-permute-done | bytes 266272 | tf_op jit(solution)/shard_map/ppermute | solution.py:455
  34.5 0.8 %collective-permute-done.9.refs_2_ = bf16[1040,128]{1,0:T(8,128)(2,1)S(1)} collective-permute-done((bf16[1040,128]{1,0:T(8,128)(2,1)S(1)}, bf16[1040,128]{1,0:T(8,128)(2,1)S(1)}, u32[]{:S(2)}, u32[]{:S(2)}) %collective-permute-start.9) | collective-permute-done | bytes 266272 | tf_op jit(solution)/shard_map/ppermute | solution.py:455
  35.4 0.1 shard_map.103
  35.5 2.0 %collective-permute-start.12 = (bf16[272,128]{1,0:T(8,128)(2,1)S(1)}, bf16[272,128]{1,0:T(8,128)(2,1)S(1)}, u32[]{:S(2)}, u32[]{:S(2)}) collective-permute-start(bf16[272,128]{1,0:T(8,128)(2,1)S(1)} %get-tuple-element.26), channel_id=1, source_target_pairs={{0,6},{1,7},{2,4},{3,5},{4,2},{5,3},{6,0},{7,1},{8,14},{9,15},{10,... | collective-permute-start | bytes 208904 | tf_op jit(solution)/shard_map/ppermute | solution.py:457
  37.5 0.1 collective-permute-start.13
  37.6 2.3 %collective-permute-start.14 = (bf16[272,128]{1,0:T(8,128)(2,1)S(1)}, bf16[272,128]{1,0:T(8,128)(2,1)S(1)}, u32[]{:S(2)}, u32[]{:S(2)}) collective-permute-start(bf16[272,128]{1,0:T(8,128)(2,1)S(1)} %get-tuple-element.28), channel_id=1, source_target_pairs={{0,2},{1,3},{2,0},{3,1},{4,6},{5,7},{6,4},{7,5},{8,10},{9,11},{10,... | collective-permute-start | bytes 208904 | tf_op jit(solution)/shard_map/ppermute | solution.py:457
  40.0 1.2 %shard_map.105 = (bf16[2048,512]{1,0:T(8,128)(2,1)}, s32[16,128]{1,0:T(8,128)}) custom-call(s32[1]{0:T(128)S(6)} %copy.12.step_ref, bf16[2048,512]{1,0:T(8,128)(2,1)} %get-tuple-element.33.stored_ref, s32[16,128]{1,0:T(8,128)S(1)} %bitcast.8, bf16[144,128]{1,0:T(8,128)(2,1)S(1)} %shard_map.102.refs_4_.refs_0_, ...), custom_call_target="tpu_custom_call", output_to_operand_aliasing={{0}: (1, {})} | custom-call | tf_op jit(solution)/shard_map/pallas_call | solution.py:23
  41.2 0.5 %collective-permute-done.12.refs_1_ = bf16[272,128]{1,0:T(8,128)(2,1)S(1)} collective-permute-done((bf16[272,128]{1,0:T(8,128)(2,1)S(1)}, bf16[272,128]{1,0:T(8,128)(2,1)S(1)}, u32[]{:S(2)}, u32[]{:S(2)}) %collective-permute-start.12) | collective-permute-done | bytes 69664 | tf_op jit(solution)/shard_map/ppermute | solution.py:457
  41.7 1.8 %collective-permute-done.13.refs_2_ = bf16[272,128]{1,0:T(8,128)(2,1)S(1)} collective-permute-done((bf16[272,128]{1,0:T(8,128)(2,1)S(1)}, bf16[272,128]{1,0:T(8,128)(2,1)S(1)}, u32[]{:S(2)}, u32[]{:S(2)}) %collective-permute-start.13) | collective-permute-done | bytes 69664 | tf_op jit(solution)/shard_map/ppermute | solution.py:457
  43.5 0.9 %shard_map.104 = (f32[32,512]{1,0:T(8,128)}, f32[1,32]{1,0:T(1,128)}) custom-call(f32[272,128]{1,0:T(8,128)S(1)} %get-tuple-element.25.refs_0_, bf16[272,128]{1,0:T(8,128)(2,1)S(1)} %collective-permute-done.12.refs_1_, bf16[272,128]{1,0:T(8,128)(2,1)S(1)} %collective-permute-done.13.refs_2_, bf16[272,128]{1,0:T(8,128)(2,1)S(1)} %collective-permute-done.14.refs_3_, ...), custom_call_target="tpu_custom_call" | custom-call | tf_op jit(solution)/shard_map/pallas_call | solution.py:23
  (15 shorter events, 0.1 us)
Async XLA Ops:
  1.5 7.1 %collective-permute-start = (bf16[144,128]{1,0:T(8,128)(2,1)S(1)}, bf16[144,128]{1,0:T(8,128)(2,1)S(1)}, u32[]{:S(2)}, u32[]{:S(2)}) collective-permute-start(bf16[144,128]{1,0:T(8,128)(2,1)S(1)} %get-tuple-element.20.refs_0_), channel_id=1, source_target_pairs={{0,6},{1,7},{2,4},{3,5},{4,2},{5,3},{6,0},{7,1},{8,14},{9,15},{10,... | collective-permute-start | bytes 110600 | tf_op jit(solution)/shard_map/ppermute | solution.py:457
  6.6 4.9 %collective-permute-start.1 = (bf16[144,128]{1,0:T(8,128)(2,1)S(1)}, bf16[144,128]{1,0:T(8,128)(2,1)S(1)}, u32[]{:S(2)}, u32[]{:S(2)}) collective-permute-start(bf16[144,128]{1,0:T(8,128)(2,1)S(1)} %get-tuple-element.20.refs_0_), channel_id=1, source_target_pairs={{0,4},{1,5},{2,6},{3,7},{4,0},{5,1},{6,2},{7,3},{8,12},{9,13},{10,... | collective-permute-start | bytes 110600 | tf_op jit(solution)/shard_map/ppermute | solution.py:457
  6.6 4.9 %collective-permute-start.2 = (bf16[144,128]{1,0:T(8,128)(2,1)S(1)}, bf16[144,128]{1,0:T(8,128)(2,1)S(1)}, u32[]{:S(2)}, u32[]{:S(2)}) collective-permute-start(bf16[144,128]{1,0:T(8,128)(2,1)S(1)} %get-tuple-element.20.refs_0_), channel_id=1, source_target_pairs={{0,2},{1,3},{2,0},{3,1},{4,6},{5,7},{6,4},{7,5},{8,10},{9,11},{10,... | collective-permute-start | bytes 110600 | tf_op jit(solution)/shard_map/ppermute | solution.py:457
  7.3 4.2 %collective-permute-start.3 = (s32[16,128]{1,0:T(8,128)S(1)}, s32[16,128]{1,0:T(8,128)S(1)}, u32[]{:S(2)}, u32[]{:S(2)}) collective-permute-start(s32[16,128]{1,0:T(8,128)S(1)} %get-tuple-element.21.refs_2_), channel_id=1, source_target_pairs={{0,1},{1,0},{2,3},{3,2},{4,5},{5,4},{6,7},{7,6},{8,9},{9,8},{10,11... | collective-permute-start | bytes 24584 | tf_op jit(solution)/shard_map/ppermute | solution.py:457
  7.3 10.1 %collective-permute-start.4 = (bf16[2048,512]{1,0:T(8,128)(2,1)}, bf16[2048,512]{1,0:T(8,128)(2,1)S(1)}, u32[]{:S(2)}, u32[]{:S(2)}) collective-permute-start(bf16[2048,512]{1,0:T(8,128)(2,1)} %refs_5_.1), channel_id=1, source_target_pairs={{0,1},{1,0},{2,3},{3,2},{4,5},{5,4},{6,7},{7,6},{8,9},{9,8},{10,11... | collective-permute-start | bytes 6291464 | tf_op jit(solution)/shard_map/ppermute | solution.py:457
  11.5 7.7 %collective-permute-start.7 = (bf16[576,128]{1,0:T(8,128)(2,1)S(1)}, bf16[576,128]{1,0:T(8,128)(2,1)S(1)}, u32[]{:S(2)}, u32[]{:S(2)}) collective-permute-start(bf16[576,128]{1,0:T(8,128)(2,1)S(1)} %shard_map.96.refs_0_), channel_id=1, source_target_pairs={{0,24},{8,16},{16,8},{24,0},{1,25},{9,17},{17,9},{25,1},{2,26},{10... | collective-permute-start | bytes 442376 | tf_op jit(solution)/shard_map/ppermute | solution.py:455
  14.1 9.8 %collective-permute-start.5 = (bf16[576,128]{1,0:T(8,128)(2,1)S(1)}, bf16[576,128]{1,0:T(8,128)(2,1)S(1)}, u32[]{:S(2)}, u32[]{:S(2)}) collective-permute-start(bf16[576,128]{1,0:T(8,128)(2,1)S(1)} %shard_map.96.refs_0_), channel_id=1, source_target_pairs={{0,16},{8,24},{16,0},{24,8},{1,17},{9,25},{17,1},{25,9},{2,18},{10... | collective-permute-start | bytes 442376 | tf_op jit(solution)/shard_map/ppermute | solution.py:455
  14.6 9.3 %collective-permute-start.6 = (bf16[576,128]{1,0:T(8,128)(2,1)S(1)}, bf16[576,128]{1,0:T(8,128)(2,1)S(1)}, u32[]{:S(2)}, u32[]{:S(2)}) collective-permute-start(bf16[576,128]{1,0:T(8,128)(2,1)S(1)} %shard_map.96.refs_0_), channel_id=1, source_target_pairs={{0,8},{8,0},{16,24},{24,16},{1,9},{9,1},{17,25},{25,17},{2,10},{10... | collective-permute-start | bytes 442376 | tf_op jit(solution)/shard_map/ppermute | solution.py:455
  22.1 7.9 %copy-start.1 = (bf16[2048,512]{1,0:T(8,128)(2,1)S(1)}, bf16[2048,512]{1,0:T(8,128)(2,1)}, u32[]{:S(2)}) copy-start(bf16[2048,512]{1,0:T(8,128)(2,1)} %refs_5_.1) | copy-start | bytes 6291460
  22.1 13.2 %collective-permute-start.8 = (bf16[1040,128]{1,0:T(8,128)(2,1)S(1)}, bf16[1040,128]{1,0:T(8,128)(2,1)S(1)}, u32[]{:S(2)}, u32[]{:S(2)}) collective-permute-start(bf16[1040,128]{1,0:T(8,128)(2,1)S(1)} %shard_map.99.refs_6_), channel_id=1, source_target_pairs={{0,24},{8,16},{16,8},{24,0},{1,25},{9,17},{17,9},{25,1},{2,26},{10... | collective-permute-start | bytes 798728 | tf_op jit(solution)/shard_map/ppermute | solution.py:455
  28.0 6.5 %collective-permute-start.10 = (bf16[1040,128]{1,0:T(8,128)(2,1)S(1)}, bf16[1040,128]{1,0:T(8,128)(2,1)S(1)}, u32[]{:S(2)}, u32[]{:S(2)}) collective-permute-start(bf16[1040,128]{1,0:T(8,128)(2,1)S(1)} %get-tuple-element.23.refs_7_.refs_5_), channel_id=1, source_target_pairs={{0,8},{8,0},{16,24},{24,16},{1,9},{9,1},{17,25},{25,17},{2,10},{10... | collective-permute-start | bytes 798728 | tf_op jit(solution)/shard_map/ppermute | solution.py:455
  28.6 6.7 %collective-permute-start.9 = (bf16[1040,128]{1,0:T(8,128)(2,1)S(1)}, bf16[1040,128]{1,0:T(8,128)(2,1)S(1)}, u32[]{:S(2)}, u32[]{:S(2)}) collective-permute-start(bf16[1040,128]{1,0:T(8,128)(2,1)S(1)} %get-tuple-element.22.refs_6_.refs_4_), channel_id=1, source_target_pairs={{0,16},{8,24},{16,0},{24,8},{1,17},{9,25},{17,1},{25,9},{2,18},{10... | collective-permute-start | bytes 798728 | tf_op jit(solution)/shard_map/ppermute | solution.py:455
  30.0 10.0 %copy-start = (s32[2048]{0:T(1024)S(1)}, s32[2048]{0:T(1024)}, u32[]{:S(2)}) copy-start(s32[2048]{0:T(1024)} %param.9) | copy-start | bytes 24580
  30.0 2.9 %collective-permute-start.11 = (bf16[144,128]{1,0:T(8,128)(2,1)S(1)}, bf16[144,128]{1,0:T(8,128)(2,1)S(1)}, u32[]{:S(2)}, u32[]{:S(2)}) collective-permute-start(bf16[144,128]{1,0:T(8,128)(2,1)S(1)} %shard_map.102.refs_4_.refs_0_), channel_id=1, source_target_pairs={{0,1},{1,0},{2,3},{3,2},{4,5},{5,4},{6,7},{7,6},{8,9},{9,8},{10,11... | collective-permute-start | bytes 110600 | tf_op jit(solution)/shard_map/ppermute | solution.py:457
  35.5 6.2 %collective-permute-start.12 = (bf16[272,128]{1,0:T(8,128)(2,1)S(1)}, bf16[272,128]{1,0:T(8,128)(2,1)S(1)}, u32[]{:S(2)}, u32[]{:S(2)}) collective-permute-start(bf16[272,128]{1,0:T(8,128)(2,1)S(1)} %get-tuple-element.26), channel_id=1, source_target_pairs={{0,6},{1,7},{2,4},{3,5},{4,2},{5,3},{6,0},{7,1},{8,14},{9,15},{10,... | collective-permute-start | bytes 208904 | tf_op jit(solution)/shard_map/ppermute | solution.py:457
  37.5 6.0 %collective-permute-start.13 = (bf16[272,128]{1,0:T(8,128)(2,1)S(1)}, bf16[272,128]{1,0:T(8,128)(2,1)S(1)}, u32[]{:S(2)}, u32[]{:S(2)}) collective-permute-start(bf16[272,128]{1,0:T(8,128)(2,1)S(1)} %get-tuple-element.27), channel_id=1, source_target_pairs={{0,4},{1,5},{2,6},{3,7},{4,0},{5,1},{6,2},{7,3},{8,12},{9,13},{10,... | collective-permute-start | bytes 208904 | tf_op jit(solution)/shard_map/ppermute | solution.py:457
  37.6 5.9 %collective-permute-start.14 = (bf16[272,128]{1,0:T(8,128)(2,1)S(1)}, bf16[272,128]{1,0:T(8,128)(2,1)S(1)}, u32[]{:S(2)}, u32[]{:S(2)}) collective-permute-start(bf16[272,128]{1,0:T(8,128)(2,1)S(1)} %get-tuple-element.28), channel_id=1, source_target_pairs={{0,2},{1,3},{2,0},{3,1},{4,6},{5,7},{6,4},{7,5},{8,10},{9,11},{10,... | collective-permute-start | bytes 208904 | tf_op jit(solution)/shard_map/ppermute | solution.py:457
